TPU v7x, 128 devices: a whole 4x4x4 slice. The times are simulated.
128 devices in a mesh: rows: 32 (over z_hi, x, y), cols: 4 (over z_lo, core).
Axes of the slice: x: 4, y: 4, z: 4 (z_hi: 2, z_lo: 2; z = z_hi * 2 + z_lo), core: 2. Of those that a mesh axis runs over, the one named last changes fastest.
Arguments:
- gradient: bfloat16 [8192, 7168], P('rows', 'cols'), may hold values from -0.21484375 to 0.21484375
- stat_old: float32 [8192, 8192], P('cols', 'rows'), may hold values from -4 to 6, as said below
Outputs:
- stat_new: float32 [8192, 8192], P('cols', 'rows')
Inputs may be any that keep to these rules, and one draw needn't show every extreme that they name: `stat_old`: symmetric.
All inputs are finite; a program needn't handle non-finite values.
Results may differ from a plain program's by a relative error of at most 0.0003.
Values may be sent and summed in bfloat16 or wider, within the bound.
No kernel may reach another device: no remote copies, remote signals or barrier semaphores. Data moves between devices by JAX's collectives and lax.ppermute only.
A program may use at most 128 MiB of HBM per device.

v0:
```python
import jax
import jax.numpy as jnp
from jax import lax
from jax.sharding import PartitionSpec as P


def row_products(left_rows, right_rows):
    return lax.dot_general(
        left_rows, right_rows, (((1,), (1,)), ((), ())), preferred_element_type=jnp.float32
    )


def body(gradient, stat_old):
    gathered = lax.all_gather(gradient, "rows", axis=0, tiled=True)
    gram = lax.psum_scatter(
        row_products(gathered, gradient), "cols", scatter_dimension=0, tiled=True
    )
    return 0.9 * stat_old + 0.1 * gram


def solution(mesh):
    placed = (P("rows", "cols"), P("cols", "rows"))
    return jax.shard_map(
        body, mesh=mesh, in_specs=placed, out_specs=P("cols", "rows"), check_vma=False
    )
```

profile of v0, /device:TPU:33, one launch (start us, length us, event | category | flops | bytes accessed | tf_op | source)
XLA Modules:
  0.0 349.2 jit_solution(17443727280684728864)
XLA Ops:
  6.5 0.0 all-gather.2.cloned.1.call-start
  6.5 0.7 all-gather.2.cloned.1.call-update
  7.3 0.0 reduce-scatter.2.cloned.1.call-start
  7.3 239.0 %all-gather.2.cloned.1.call-done = bf16[8192,1792]{1,0:T(8,128)(2,1)} async-done(((bf16[256,1792]{1,0:T(8,128)(2,1)}), bf16[8192,1792]{1,0:T(8,128)(2,1)}) %all-gather.2.cloned.1.call-update) | async-done | bytes 29360144 | tf_op jit(solution)/shard_map/all_gather | solution.py:14
  246.3 15.7 %fusion = f32[8192,256]{1,0:T(8,128)} fusion(bf16[8192,1792]{1,0:T(8,128)(2,1)} %all-gather.2.cloned.1.call-done, bf16[256,1792]{1,0:T(8,128)(2,1)} %param.2), kind=kOutput, calls=%fused_computation.1 | convolution fusion | flops 7516192768 | bytes 38666240 | tf_op jit(solution)/shard_map/dot_general | solution.py:8
  262.0 0.0 copy-start
  262.0 0.0 reduce-scatter.2.cloned.1.call-update
  262.0 77.1 %reduce-scatter.2.cloned.1.call-done = f32[2048,256]{1,0:T(8,128)} async-done(((f32[8192,256]{1,0:T(8,128)}), f32[2048,256]{1,0:T(8,128)}) %reduce-scatter.2.cloned.1.call-update) | async-done | bytes 2097168 | tf_op jit(solution)/shard_map/reduce_scatter | solution.py:15
  339.1 0.0 copy-done
  339.1 3.2 multiply_add_fusion
Async XLA Ops:
  6.5 239.7 %all-gather.2.cloned.1.call-start = ((), (), s32[]{:S(2)}) async-start(), calls=%async_computation.1 | async-start | bytes 30277632 | tf_op jit(solution)/shard_map/all_gather | solution.py:14
  7.3 331.9 %reduce-scatter.2.cloned.1.call-start = ((), (), s32[]{:S(2)}) async-start(), calls=%async_computation.2 | async-start | bytes 10485760 | tf_op jit(solution)/shard_map/reduce_scatter | solution.py:15
  262.0 77.2 %copy-start = (f32[2048,256]{1,0:T(8,128)S(1)}, f32[2048,256]{1,0:T(8,128)}, u32[]{:S(2)}) copy-start(f32[2048,256]{1,0:T(8,128)} %param.3) | copy-start | bytes 6291460
Sparse Core Ops, SparseCore 0:
  10.5 235.7 all-gather.1
  262.1 76.9 reduce-scatter.1
where the time goes:
time: 352 us; the launch traced here: 349 us
  waiting for transfers between devices  317 us (90%)
  matrix products  15.7 us (4%)
  between operations  13.4 us (4%)
    all_gather x1, waiting for transfers between devices, body(): gathered = lax.all_gather(gradient, 'rows', axis=0, tiled=True)  239 us
    reduce_scatter x1, waiting for transfers between devices, body(): lax.psum_scatter(row_products(gathered, gradient), 'cols', scatter_dimens...  77.1 us
    dot_general x1, matrix products, row_products(): lax.dot_general(left_rows, right_rows, (((1,), (1,)), ((), ())), preferre...  15.7 us
  transfers between devices with their start and end apart: 2, of which 2 were waited for; matrix products, arithmetic and copies ran while one was open for 0% of the time, Pallas kernels for 0%

commit v1 on v0

v1 whole, which is shorter than its diff:
```python
import functools

import jax
import jax.numpy as jnp
import numpy as np
from jax import lax
from jax.experimental import pallas as pl
from jax.experimental.pallas import tpu as pltpu
from jax.sharding import PartitionSpec as P

AXES = ("rows", "cols")
SIZES = (2, 4, 4, 2, 2)
WIRE = jnp.float16
SCALE = 128.0

NEAR = (("s", "s"), ("r1", "s"), ("c3", "s"), ("r1", "c1"), ("r3", "c1"))
FAR = (("r2", "s"), ("c2", "s"), ("c3", "r2"), ("r3", "c2"), ("r2", "c2"))
OFFSET = {"s": (0, 0), "r1": (1, 0), "r2": (2, 0), "r3": (3, 0), "c1": (0, 1), "c2": (0, 2), "c3": (0, 3)}


def route(move):
    pairs = []
    for source in range(int(np.prod(SIZES))):
        place = [int(i) for i in np.unravel_index(source, SIZES)]
        pairs.append((source, int(np.ravel_multi_index(move(*place), SIZES))))
    return pairs


def send(value, move):
    return lax.ppermute(value, AXES, route(move))


def shift(dx, dy, swap=False):
    def move(zh, x, y, zl, core):
        if swap:
            zh, zl = zl, zh
        return zh, (x + dx) % 4, (y + dy) % 4, zl, core

    return move


def other_core(zh, x, y, zl, core):
    return zh, x, y, zl, 1 - core


def other_high(zh, x, y, zl, core):
    return 1 - zh, x, y, zl, core


def first_partner(zh, x, y, zl, core):
    return (zh, x, y, 1 - zl, core) if core == 0 else (1 - zh, x, y, 1 - zl, core)


def second_partner(zh, x, y, zl, core):
    return first_partner(zh, x, y, zl, 1 - core)[:4] + (core,)


def products(blocks, pairs, half):
    out = {}
    for right in dict.fromkeys(r for _, r in pairs):
        lefts = [l for l, r in pairs if r == right]
        rows = [
            lax.dynamic_slice_in_dim(blocks[l][kind], half * 128, 128, 0) for l in lefts for kind in (0, 1)
        ]
        full = lax.dot_general(
            jnp.concatenate(rows),
            jnp.concatenate(blocks[right]),
            (((1,), (1,)), ((), ())),
            preferred_element_type=jnp.float32,
        ).reshape(len(lefts), 2, 128, 2, 256)
        for i, l in enumerate(lefts):
            out[l, right] = full[i]
    return jnp.stack([out[p] for p in pairs])


def summed(blocks, pairs, straight, core):
    away = send(products(blocks, pairs, 1 - core), other_core)
    whole = (products(blocks, pairs, core) + away) * SCALE
    q0 = jnp.where(straight, whole[:, 0], whole[:, 1])
    q1 = jnp.where(straight, whole[:, 1], whole[:, 0])
    q1_early = jnp.where(core == 0, q1[:, :, 0], q1[:, :, 1])
    q1_late = jnp.where(core == 0, q1[:, :, 1], q1[:, :, 0])
    got = send(jnp.stack([q1_early, q0[:, :, 1]]).astype(WIRE), first_partner).astype(jnp.float32)
    late = send((q1_late + got[1]).astype(WIRE), second_partner).astype(jnp.float32)
    return (q0[:, :, 0] + got[0] + late) * (1.0 / SCALE)


def delivered(totals, pairs):
    by_rows, by_columns = {}, {}
    moves = {}
    for i, (left, right) in enumerate(pairs):
        to = OFFSET[right]
        rows = tuple((a - b) % 4 for a, b in zip(OFFSET[left], to))
        moves.setdefault((to, False), []).append((i, rows))
        twice = left == right or (left, right) in (("r2", "s"), ("c2", "s"), ("r2", "c2"))
        if not twice:
            to = OFFSET[left]
            rows = tuple((a - b) % 4 for a, b in zip(OFFSET[right], to))
            moves.setdefault((to, True), []).append((i, rows))
    for (to, swap), tiles in moves.items():
        picked = jnp.stack([totals[i] for i, _ in tiles])
        if to != (0, 0):
            picked = send(picked, shift(*to, swap))
        for n, (_, rows) in enumerate(tiles):
            if swap:
                by_columns[rows] = picked[n].T
            else:
                by_rows[rows] = picked[n]
    return by_rows, by_columns


def both_halves(by_rows, by_columns, core):
    mine = jnp.stack([*by_rows.values()])
    turned = jnp.stack([*by_columns.values()])
    far, far_turned = send(mine, other_core), send(turned, other_core)
    low = jnp.where(core == 0, mine, far)
    high = jnp.where(core == 0, far, mine)
    whole = jnp.concatenate([low, high], axis=1)
    low = jnp.where(core == 0, turned, far_turned)
    high = jnp.where(core == 0, far_turned, turned)
    whole_turned = jnp.concatenate([low, high], axis=2)
    tiles = {rows: whole[i] for i, rows in enumerate(by_rows)}
    tiles.update({rows: whole_turned[i] for i, rows in enumerate(by_columns)})
    return tiles


def update(index, tile, old, new):
    new[...] = 0.9 * old[...] + 0.1 * tile[0]


def body(gradient, stat_old):
    device, column = lax.axis_index("rows"), lax.axis_index("cols")
    zh, x, y = device // 16, (device // 4) % 4, device % 4
    zl, core = column // 2, column % 2
    straight = zh == zl
    keep = lax.dynamic_slice_in_dim(gradient, zh * 896, 896, 1)
    give = lax.dynamic_slice_in_dim(gradient, (1 - zh) * 896, 896, 1)
    moves = {"r1": (-1, 0), "r3": (1, 0), "c1": (0, -1), "c3": (0, 1)}
    own = {"s": keep}
    other = {"s": send(give, other_high)}
    for name, move in moves.items():
        own[name] = send(keep, shift(*move))
    for name, move in moves.items():
        other[name] = send(other["s"], shift(*move))
    own["r2"] = send(own["r1"], shift(*moves["r1"]))
    own["c2"] = send(own["c1"], shift(*moves["c1"]))
    other["r2"] = send(other["r3"], shift(*moves["r3"]))
    other["c2"] = send(other["c3"], shift(*moves["c3"]))
    blocks = {name: (own[name], other[name]) for name in own}
    tiles = {}
    for pairs in (NEAR, FAR):
        totals = summed(blocks, pairs, straight, core)
        tiles.update(both_halves(*delivered(totals, pairs), core))
    stacked = jnp.stack([tiles[dx, dy] for dx in range(4) for dy in range(4)])
    block = jnp.arange(8)
    index = ((block // 4 + 2 * core - x) % 4) * 4 + (block % 4 - y) % 4
    return pl.pallas_call(
        update,
        out_shape=jax.ShapeDtypeStruct((2048, 256), jnp.float32),
        grid_spec=pltpu.PrefetchScalarGridSpec(
            num_scalar_prefetch=1,
            grid=(8,),
            in_specs=[
                pl.BlockSpec((1, 256, 256), lambda i, index: (index[i], 0, 0)),
                pl.BlockSpec((256, 256), lambda i, index: (i, 0)),
            ],
            out_specs=pl.BlockSpec((256, 256), lambda i, index: (i, 0)),
        ),
    )(index.astype(jnp.int32), stacked, stat_old)


def solution(mesh):
    placed = (P("rows", "cols"), P("cols", "rows"))
    return jax.shard_map(
        body, mesh=mesh, in_specs=placed, out_specs=P("cols", "rows"), check_vma=False
    )
```

time: 352 us -> 214 us (0.61)
  waiting for transfers between devices: 317 us -> 30.7 us
  local copies, waits for them, and re-layouts: 0.01 us -> 77.7 us
  starting transfers between devices: 0.04 us -> 57.8 us
  other arithmetic: 3.25 us -> 23.5 us
  between operations: 13.4 us -> 0.88 us
  Pallas kernels: 0 us -> 6.78 us
    all_gather x1 -> x0, waiting for transfers between devices: 239 us -> none  [body(): gathered = lax.all_gather(gradient, 'rows', axis=0, tiled=True)]
    reduce_scatter x1 -> x0, waiting for transfers between devices: 77.1 us -> none  [body(): lax.psum_scatter(row_products(gathered, gradient), 'cols', scatter_dimens...]
    ppermute x0 -> x31, starting transfers between devices: none -> 57.8 us  [send(): return lax.ppermute(value, AXES, route(move))]
    ppermute x0 -> x31, waiting for transfers between devices: none -> 30.7 us  [send(): return lax.ppermute(value, AXES, route(move))]
    slice x0 -> x35, local copies, waits for them, and re-layouts: none -> 29.3 us  [the longest x26 28.5 us: products(): out[l, right] = full[i]]
    unnamed x2 -> x113, local copies, waits for them, and re-layouts: 0.01 us -> 28.3 us
    dynamic_slice x0 -> x7, local copies, waits for them, and re-layouts: none -> 11.7 us  [the longest x6 10.3 us: products(): lax.dynamic_slice_in_dim(blocks[l][kind], half * 128, 128, 0)]
    pallas_call x0 -> x1, Pallas kernels: none -> 6.78 us  [body(): pl.pallas_call(update, out_shape=jax.ShapeDtypeStruct((2048, 256), jnp.fl...]
  transfers between devices with their start and end apart: 2 -> 31, of which waited for: 2 -> 8; matrix products, arithmetic and copies ran while one was open for 0% -> 46% of each run, Pallas kernels for 0% -> 0%
where the time goes in v1:
time: 214 us; the launch traced here: 212 us
  local copies, waits for them, and re-layouts  77.7 us (36%)
  starting transfers between devices  57.8 us (27%)
  waiting for transfers between devices  30.7 us (14%)
  other arithmetic  23.5 us (11%)
  matrix products  15 us (7%)
  Pallas kernels  6.78 us (3%)
    ppermute x31, starting transfers between devices, send(): return lax.ppermute(value, AXES, route(move))  57.8 us
    ppermute x31, waiting for transfers between devices, send(): return lax.ppermute(value, AXES, route(move))  30.7 us
    slice x26, local copies, waits for them, and re-layouts, products(): out[l, right] = full[i]  28.5 us
    unnamed x113, local copies, waits for them, and re-layouts  28.3 us
    dot_general x10, matrix products, products(): lax.dot_general(jnp.concatenate(rows), jnp.concatenate(blocks[right]), ((...  15 us
    dynamic_slice x6, local copies, waits for them, and re-layouts, products(): lax.dynamic_slice_in_dim(blocks[l][kind], half * 128, 128, 0)  10.3 us
    pallas_call x1, Pallas kernels, body(): pl.pallas_call(update, out_shape=jax.ShapeDtypeStruct((2048, 256), jnp.fl...  6.78 us
    unnamed x9, other arithmetic  6.48 us
  transfers between devices with their start and end apart: 31, of which 8 were waited for; matrix products, arithmetic and copies ran while one was open for 46% of the time, Pallas kernels for 0%

profile of v1, /device:TPU:33, one launch (start us, length us, event | category | flops | bytes accessed | tf_op | source)
XLA Modules:
  0.0 212.3 jit_solution(16745403706237904814)
XLA Ops:
  1.3 2.8 %collective-permute-start = (bf16[256,896]{1,0:T(8,128)(2,1)S(1)}, bf16[256,896]{1,0:T(8,128)(2,1)S(1)}, u32[]{:S(2)}, u32[]{:S(2)}) collective-permute-start(bf16[256,896]{1,0:T(8,128)(2,1)S(1)} %get-tuple-element.54), channel_id=1, source_target_pairs={{0,64},{1,65},{2,66},{3,67},{4,68},{5,69},{6,70},{7,71},{8,72},{9,... | collective-permute-start | bytes 1376264 | tf_op jit(solution)/shard_map/ppermute | solution.py:30
  4.1 2.7 %collective-permute-start.7 = (bf16[256,896]{1,0:T(8,128)(2,1)S(1)}, bf16[256,896]{1,0:T(8,128)(2,1)}, u32[]{:S(2)}, u32[]{:S(2)}) collective-permute-start(bf16[256,896]{1,0:T(8,128)(2,1)S(1)} %get-tuple-element.53), channel_id=1, source_target_pairs={{0,12},{1,13},{2,14},{3,15},{4,0},{5,1},{6,2},{7,3},{8,4},{9,5},{1... | collective-permute-start | bytes 1376264 | tf_op jit(solution)/shard_map/ppermute | solution.py:30
  9.8 4.5 %collective-permute-done = bf16[256,896]{1,0:T(8,128)(2,1)S(1)} collective-permute-done((bf16[256,896]{1,0:T(8,128)(2,1)S(1)}, bf16[256,896]{1,0:T(8,128)(2,1)S(1)}, u32[]{:S(2)}, u32[]{:S(2)}) %collective-permute-start) | collective-permute-done | bytes 458784 | tf_op jit(solution)/shard_map/ppermute | solution.py:30
  14.3 2.6 %collective-permute-start.2 = (bf16[256,896]{1,0:T(8,128)(2,1)S(1)}, bf16[256,896]{1,0:T(8,128)(2,1)S(1)}, u32[]{:S(2)}, u32[]{:S(2)}) collective-permute-start(bf16[256,896]{1,0:T(8,128)(2,1)S(1)} %collective-permute-done), channel_id=1, source_target_pairs={{0,48},{1,49},{2,50},{3,51},{4,52},{5,53},{6,54},{7,55},{8,56},{9,... | collective-permute-start | bytes 1376264 | tf_op jit(solution)/shard_map/ppermute | solution.py:30
  25.2 3.3 %collective-permute-done.2 = bf16[256,896]{1,0:T(8,128)(2,1)S(1)} collective-permute-done((bf16[256,896]{1,0:T(8,128)(2,1)S(1)}, bf16[256,896]{1,0:T(8,128)(2,1)S(1)}, u32[]{:S(2)}, u32[]{:S(2)}) %collective-permute-start.2) | collective-permute-done | bytes 458784 | tf_op jit(solution)/shard_map/ppermute | solution.py:30
  28.5 2.7 %collective-permute-start.18 = (bf16[256,896]{1,0:T(8,128)(2,1)}, bf16[256,896]{1,0:T(8,128)(2,1)}, u32[]{:S(2)}, u32[]{:S(2)}) collective-permute-start(bf16[256,896]{1,0:T(8,128)(2,1)} %collective-permute-done.1), channel_id=1, source_target_pairs={{0,48},{1,49},{2,50},{3,51},{4,52},{5,53},{6,54},{7,55},{8,56},{9,... | collective-permute-start | bytes 1376264 | tf_op jit(solution)/shard_map/ppermute | solution.py:30
  46.8 2.7 %collective-permute-start.9 = (f32[5,2,128,2,256]{4,2,0,3,1:T(8,128)}, f32[5,2,128,2,256]{4,2,0,3,1:T(8,128)}, u32[]{:S(2)}, u32[]{:S(2)}) collective-permute-start(f32[5,2,128,2,256]{4,2,0,3,1:T(8,128)} %copy_dynamic-update-slice_fusion.10), channel_id=1, source_target_pairs={{0,1},{1,0},{2,3},{3,2},{4,5},{5,4},{6,7},{7,6},{8,9},{9,8},{10,11... | collective-permute-start | bytes 7864328 | tf_op jit(solution)/shard_map/ppermute | solution.py:30
  53.3 2.0 fusion
  66.9 4.5 %collective-permute-done.19 = bf16[256,896]{1,0:T(8,128)(2,1)S(1)} collective-permute-done((bf16[256,896]{1,0:T(8,128)(2,1)}, bf16[256,896]{1,0:T(8,128)(2,1)S(1)}, u32[]{:S(2)}, u32[]{:S(2)}) %collective-permute-start.19) | collective-permute-done | bytes 458784 | tf_op jit(solution)/shard_map/ppermute | solution.py:30
  81.4 2.2 %slice.307 = f32[1,2,128,2,256]{4,3,2,1,0:T(2,128)} reshape(f32[256,512]{1,0:T(8,128)} %get-tuple-element.40) | data formatting | bytes 1048576 | tf_op jit(solution)/shard_map/slice | solution.py:72
  85.5 2.2 %slice.309 = f32[1,2,128,2,256]{4,3,2,1,0:T(2,128)} reshape(f32[256,512]{1,0:T(8,128)} %get-tuple-element.39) | data formatting | bytes 1048576 | tf_op jit(solution)/shard_map/slice | solution.py:72
  89.5 2.3 %fusion.40 = f32[512,512]{1,0:T(8,128)S(1)} fusion(bf16[512,896]{1,0:T(8,128)(2,1)} %constant_dynamic-update-slice_fusion.12, bf16[128,896]{1,0:T(8,128)(2,1)} %copy-done.39, bf16[128,896]{1,0:T(8,128)(2,1)} %get-tuple-element.67, bf16[128,896]{1,0:T(8,128)(2,1)} %copy-done.36, bf16[128,896]{1,0:T(8,128)(2,1)} %get-tuple-element.75), kind=kOutput, calls=%fused_computation.63 | convolution fusion | flops 473432064 | bytes 2883584 | tf_op jit(solution)/shard_map/dot_general | solution.py:65
  92.9 2.2 %slice.311 = f32[1,2,128,2,256]{4,3,2,1,0:T(2,128)} reshape(f32[256,512]{1,0:T(8,128)} %get-tuple-element.38) | data formatting | bytes 1048576 | tf_op jit(solution)/shard_map/slice | solution.py:72
  95.0 2.1 %slice.313 = f32[1,2,128,2,256]{4,3,2,1,0:T(2,128)} reshape(f32[256,512]{1,0:T(8,128)} %get-tuple-element.37) | data formatting | bytes 1048576 | tf_op jit(solution)/shard_map/slice | solution.py:72
  97.2 2.0 copy_dynamic-update-slice_fusion.3
  105.2 2.3 %fusion.16 = f32[512,512]{1,0:T(8,128)S(1)} fusion(bf16[128,896]{1,0:T(8,128)(2,1)} %get-tuple-element.74, bf16[128,896]{1,0:T(8,128)(2,1)} %get-tuple-element.72, bf16[128,896]{1,0:T(8,128)(2,1)} %get-tuple-element.70, bf16[128,896]{1,0:T(8,128)(2,1)} %get-tuple-element.68, bf16[256,896]{1,0:T(8,128)(2,1)} %copy-done.20, bf16[256,896]{1,0:T(8,128)(2,1)} %copy-done.18), kind=kOutput, calls=%fused_computation.39 | convolution fusion | flops 475267072 | bytes 2883584 | tf_op jit(solution)/shard_map/dot_general | solution.py:65
  108.5 2.2 %slice.299 = f32[1,2,128,2,256]{4,3,2,1,0:T(2,128)} reshape(f32[256,512]{1,0:T(8,128)} %get-tuple-element.44) | data formatting | bytes 1048576 | tf_op jit(solution)/shard_map/slice | solution.py:72
  110.7 2.2 %slice.301 = f32[1,2,128,2,256]{4,3,2,1,0:T(2,128)} reshape(f32[256,512]{1,0:T(8,128)} %get-tuple-element.43) | data formatting | bytes 1048576 | tf_op jit(solution)/shard_map/slice | solution.py:72
  112.9 2.3 %fusion.24 = f32[512,512]{1,0:T(8,128)S(1)} fusion(bf16[512,896]{1,0:T(8,128)(2,1)} %constant_dynamic-update-slice_fusion.12, bf16[128,896]{1,0:T(8,128)(2,1)} %get-tuple-element.70, bf16[128,896]{1,0:T(8,128)(2,1)} %get-tuple-element.68, bf16[128,896]{1,0:T(8,128)(2,1)} %get-tuple-element.78, bf16[128,896]{1,0:T(8,128)(2,1)S(1)} %copy-done.34), kind=kOutput, calls=%fused_computation.47 | convolution fusion | flops 473432064 | bytes 2883584 | tf_op jit(solution)/shard_map/dot_general | solution.py:65
  116.2 2.2 %slice.303 = f32[1,2,128,2,256]{4,3,2,1,0:T(2,128)} reshape(f32[256,512]{1,0:T(8,128)} %get-tuple-element.42) | data formatting | bytes 1048576 | tf_op jit(solution)/shard_map/slice | solution.py:72
  118.4 2.2 %slice.305 = f32[1,2,128,2,256]{4,3,2,1,0:T(2,128)} reshape(f32[256,512]{1,0:T(8,128)} %get-tuple-element.41) | data formatting | bytes 1048576 | tf_op jit(solution)/shard_map/slice | solution.py:72
  123.0 2.1 add_multiply_fusion.1
  125.1 2.1 add_multiply_fusion
  131.1 8.1 %collective-permute-done.23 = f16[2,5,128,256]{3,2,1,0:T(8,128)(2,1)} collective-permute-done((f16[2,5,128,256]{3,2,1,0:T(8,128)(2,1)}, f16[2,5,128,256]{3,2,1,0:T(8,128)(2,1)}, u32[]{:S(2)}, u32[]{:S(2)}) %collective-permute-start.23) | collective-permute-done | bytes 655392 | tf_op jit(solution)/shard_map/ppermute | solution.py:30
  142.9 4.7 %collective-permute-done.10 = f16[2,5,128,256]{3,2,1,0:T(8,128)(2,1)} collective-permute-done((f16[2,5,128,256]{3,2,1,0:T(8,128)(2,1)S(1)}, f16[2,5,128,256]{3,2,1,0:T(8,128)(2,1)}, u32[]{:S(2)}, u32[]{:S(2)}) %collective-permute-start.10) | collective-permute-done | bytes 655392 | tf_op jit(solution)/shard_map/ppermute | solution.py:30
  151.0 2.4 %collective-permute-start.28 = (f32[1,128,256]{2,1,0:T(8,128)S(1)}, f32[1,128,256]{2,1,0:T(8,128)S(1)}, u32[]{:S(2)}, u32[]{:S(2)}) collective-permute-start(f32[1,128,256]{2,1,0:T(8,128)S(1)} %get-tuple-element.56), channel_id=1, source_target_pairs={{0,12},{1,13},{2,76},{3,77},{4,0},{5,1},{6,64},{7,65},{8,4},{9,5},... | collective-permute-start | bytes 393224 | tf_op jit(solution)/shard_map/ppermute | solution.py:30
  153.5 2.2 %collective-permute-done.11 = f16[5,128,256]{2,1,0:T(8,128)(2,1)S(1)} collective-permute-done((f16[5,128,256]{2,1,0:T(8,128)(2,1)S(1)}, f16[5,128,256]{2,1,0:T(8,128)(2,1)S(1)}, u32[]{:S(2)}, u32[]{:S(2)}) %collective-permute-start.11) | collective-permute-done | bytes 327712 | tf_op jit(solution)/shard_map/ppermute | solution.py:30
  158.2 3.5 %collective-permute-start.29 = (f32[1,128,256]{2,1,0:T(8,128)S(1)}, f32[1,128,256]{2,1,0:T(8,128)S(1)}, u32[]{:S(2)}, u32[]{:S(2)}) collective-permute-start(f32[1,128,256]{2,1,0:T(8,128)S(1)} %get-tuple-element.55), channel_id=1, source_target_pairs={{0,48},{1,49},{2,112},{3,113},{4,52},{5,53},{6,116},{7,117},{8,56}... | collective-permute-start | bytes 393224 | tf_op jit(solution)/shard_map/ppermute | solution.py:30
  161.8 2.9 %collective-permute-done.29 = f32[1,128,256]{2,1,0:T(8,128)S(1)} collective-permute-done((f32[1,128,256]{2,1,0:T(8,128)S(1)}, f32[1,128,256]{2,1,0:T(8,128)S(1)}, u32[]{:S(2)}, u32[]{:S(2)}) %collective-permute-start.29) | collective-permute-done | bytes 131104 | tf_op jit(solution)/shard_map/ppermute | solution.py:30
  166.9 13.4 %collective-permute-start.30 = (f32[2,256,128]{1,2,0:T(8,128)S(1)}, f32[2,256,128]{1,2,0:T(8,128)S(1)}, u32[]{:S(2)}, u32[]{:S(2)}) collective-permute-start(f32[2,256,128]{1,2,0:T(8,128)S(1)} %pad_maximum_fusion.13), channel_id=1, source_target_pairs={{0,1},{1,0},{2,3},{3,2},{4,5},{5,4},{6,7},{7,6},{8,9},{9,8},{10,11... | collective-permute-start | bytes 786440 | tf_op jit(solution)/shard_map/ppermute | solution.py:30
  182.1 5.2 %collective-permute-start.27 = (f32[5,128,256]{2,1,0:T(8,128)}, f32[5,128,256]{2,1,0:T(8,128)}, u32[]{:S(2)}, u32[]{:S(2)}) collective-permute-start(f32[5,128,256]{2,1,0:T(8,128)} %pad_maximum_fusion.4), channel_id=1, source_target_pairs={{0,1},{1,0},{2,3},{3,2},{4,5},{5,4},{6,7},{7,6},{8,9},{9,8},{10,11... | collective-permute-start | bytes 1966088 | tf_op jit(solution)/shard_map/ppermute | solution.py:30
  205.5 6.8 %shard_map.28 = f32[2048,256]{1,0:T(8,128)} custom-call(s32[8]{0:T(128)} %fusion.90.index, f32[16,256,256]{2,1,0:T(8,128)} %fusion.87.tile, f32[2048,256]{1,0:T(8,128)} %old.1), custom_call_target="tpu_custom_call" | custom-call | tf_op jit(solution)/shard_map/pallas_call | solution.py:157
  (246 shorter events, 104.0 us)
Async XLA Ops:
  1.3 48.2 %copy-start.18 = (bf16[256,896]{1,0:T(8,128)(2,1)}, bf16[256,896]{1,0:T(8,128)(2,1)S(1)}, u32[]{:S(2)}) copy-start(bf16[256,896]{1,0:T(8,128)(2,1)S(1)} %get-tuple-element.53) | copy-start | bytes 1376260
  1.3 13.0 %collective-permute-start = (bf16[256,896]{1,0:T(8,128)(2,1)S(1)}, bf16[256,896]{1,0:T(8,128)(2,1)S(1)}, u32[]{:S(2)}, u32[]{:S(2)}) collective-permute-start(bf16[256,896]{1,0:T(8,128)(2,1)S(1)} %get-tuple-element.54), channel_id=1, source_target_pairs={{0,64},{1,65},{2,66},{3,67},{4,68},{5,69},{6,70},{7,71},{8,72},{9,... | collective-permute-start | bytes 1376264 | tf_op jit(solution)/shard_map/ppermute | solution.py:30
  4.1 12.8 %collective-permute-start.7 = (bf16[256,896]{1,0:T(8,128)(2,1)S(1)}, bf16[256,896]{1,0:T(8,128)(2,1)}, u32[]{:S(2)}, u32[]{:S(2)}) collective-permute-start(bf16[256,896]{1,0:T(8,128)(2,1)S(1)} %get-tuple-element.53), channel_id=1, source_target_pairs={{0,12},{1,13},{2,14},{3,15},{4,0},{5,1},{6,2},{7,3},{8,4},{9,5},{1... | collective-permute-start | bytes 1376264 | tf_op jit(solution)/shard_map/ppermute | solution.py:30
  6.8 13.2 %collective-permute-start.5 = (bf16[256,896]{1,0:T(8,128)(2,1)S(1)}, bf16[256,896]{1,0:T(8,128)(2,1)S(1)}, u32[]{:S(2)}, u32[]{:S(2)}) collective-permute-start(bf16[256,896]{1,0:T(8,128)(2,1)S(1)} %get-tuple-element.53), channel_id=1, source_target_pairs={{0,16},{1,17},{2,18},{3,19},{4,20},{5,21},{6,22},{7,23},{8,24},{9,... | collective-permute-start | bytes 1376264 | tf_op jit(solution)/shard_map/ppermute | solution.py:30
  8.1 14.4 %collective-permute-start.1 = (bf16[256,896]{1,0:T(8,128)(2,1)S(1)}, bf16[256,896]{1,0:T(8,128)(2,1)}, u32[]{:S(2)}, u32[]{:S(2)}) collective-permute-start(bf16[256,896]{1,0:T(8,128)(2,1)S(1)} %get-tuple-element.53), channel_id=1, source_target_pairs={{0,48},{1,49},{2,50},{3,51},{4,52},{5,53},{6,54},{7,55},{8,56},{9,... | collective-permute-start | bytes 1376264 | tf_op jit(solution)/shard_map/ppermute | solution.py:30
  9.5 22.5 %collective-permute-start.3 = (bf16[256,896]{1,0:T(8,128)(2,1)S(1)}, bf16[256,896]{1,0:T(8,128)(2,1)S(1)}, u32[]{:S(2)}, u32[]{:S(2)}) collective-permute-start(bf16[256,896]{1,0:T(8,128)(2,1)S(1)} %get-tuple-element.53), channel_id=1, source_target_pairs={{0,4},{1,5},{2,6},{3,7},{4,8},{5,9},{6,10},{7,11},{8,12},{9,13},{1... | collective-permute-start | bytes 1376264 | tf_op jit(solution)/shard_map/ppermute | solution.py:30
  14.3 14.2 %collective-permute-start.2 = (bf16[256,896]{1,0:T(8,128)(2,1)S(1)}, bf16[256,896]{1,0:T(8,128)(2,1)S(1)}, u32[]{:S(2)}, u32[]{:S(2)}) collective-permute-start(bf16[256,896]{1,0:T(8,128)(2,1)S(1)} %collective-permute-done), channel_id=1, source_target_pairs={{0,48},{1,49},{2,50},{3,51},{4,52},{5,53},{6,54},{7,55},{8,56},{9,... | collective-permute-start | bytes 1376264 | tf_op jit(solution)/shard_map/ppermute | solution.py:30
  16.9 16.6 %collective-permute-start.4 = (bf16[256,896]{1,0:T(8,128)(2,1)S(1)}, bf16[256,896]{1,0:T(8,128)(2,1)}, u32[]{:S(2)}, u32[]{:S(2)}) collective-permute-start(bf16[256,896]{1,0:T(8,128)(2,1)S(1)} %collective-permute-done), channel_id=1, source_target_pairs={{0,4},{1,5},{2,6},{3,7},{4,8},{5,9},{6,10},{7,11},{8,12},{9,13},{1... | collective-permute-start | bytes 1376264 | tf_op jit(solution)/shard_map/ppermute | solution.py:30
  20.1 21.5 %collective-permute-start.8 = (bf16[256,896]{1,0:T(8,128)(2,1)S(1)}, bf16[256,896]{1,0:T(8,128)(2,1)S(1)}, u32[]{:S(2)}, u32[]{:S(2)}) collective-permute-start(bf16[256,896]{1,0:T(8,128)(2,1)S(1)} %collective-permute-done), channel_id=1, source_target_pairs={{0,12},{1,13},{2,14},{3,15},{4,0},{5,1},{6,2},{7,3},{8,4},{9,5},{1... | collective-permute-start | bytes 1376264 | tf_op jit(solution)/shard_map/ppermute | solution.py:30
  22.4 16.3 %collective-permute-start.6 = (bf16[256,896]{1,0:T(8,128)(2,1)S(1)}, bf16[256,896]{1,0:T(8,128)(2,1)}, u32[]{:S(2)}, u32[]{:S(2)}) collective-permute-start(bf16[256,896]{1,0:T(8,128)(2,1)S(1)} %collective-permute-done), channel_id=1, source_target_pairs={{0,16},{1,17},{2,18},{3,19},{4,20},{5,21},{6,22},{7,23},{8,24},{9,... | collective-permute-start | bytes 1376264 | tf_op jit(solution)/shard_map/ppermute | solution.py:30
  28.5 31.3 %collective-permute-start.18 = (bf16[256,896]{1,0:T(8,128)(2,1)}, bf16[256,896]{1,0:T(8,128)(2,1)}, u32[]{:S(2)}, u32[]{:S(2)}) collective-permute-start(bf16[256,896]{1,0:T(8,128)(2,1)} %collective-permute-done.1), channel_id=1, source_target_pairs={{0,48},{1,49},{2,50},{3,51},{4,52},{5,53},{6,54},{7,55},{8,56},{9,... | collective-permute-start | bytes 1376264 | tf_op jit(solution)/shard_map/ppermute | solution.py:30
  32.0 30.8 %collective-permute-start.20 = (bf16[256,896]{1,0:T(8,128)(2,1)}, bf16[256,896]{1,0:T(8,128)(2,1)}, u32[]{:S(2)}, u32[]{:S(2)}) collective-permute-start(bf16[256,896]{1,0:T(8,128)(2,1)} %collective-permute-done.7), channel_id=1, source_target_pairs={{0,12},{1,13},{2,14},{3,15},{4,0},{5,1},{6,2},{7,3},{8,4},{9,5},{1... | collective-permute-start | bytes 1376264 | tf_op jit(solution)/shard_map/ppermute | solution.py:30
  46.8 76.2 %collective-permute-start.9 = (f32[5,2,128,2,256]{4,2,0,3,1:T(8,128)}, f32[5,2,128,2,256]{4,2,0,3,1:T(8,128)}, u32[]{:S(2)}, u32[]{:S(2)}) collective-permute-start(f32[5,2,128,2,256]{4,2,0,3,1:T(8,128)} %copy_dynamic-update-slice_fusion.10), channel_id=1, source_target_pairs={{0,1},{1,0},{2,3},{3,2},{4,5},{5,4},{6,7},{7,6},{8,9},{9,8},{10,11... | collective-permute-start | bytes 7864328 | tf_op jit(solution)/shard_map/ppermute | solution.py:30
  57.7 13.7 %collective-permute-start.19 = (bf16[256,896]{1,0:T(8,128)(2,1)}, bf16[256,896]{1,0:T(8,128)(2,1)S(1)}, u32[]{:S(2)}, u32[]{:S(2)}) collective-permute-start(bf16[256,896]{1,0:T(8,128)(2,1)} %collective-permute-done.6), channel_id=1, source_target_pairs={{0,16},{1,17},{2,18},{3,19},{4,20},{5,21},{6,22},{7,23},{8,24},{9,... | collective-permute-start | bytes 1376264 | tf_op jit(solution)/shard_map/ppermute | solution.py:30
  57.7 20.0 %collective-permute-start.21 = (bf16[256,896]{1,0:T(8,128)(2,1)}, bf16[256,896]{1,0:T(8,128)(2,1)}, u32[]{:S(2)}, u32[]{:S(2)}) collective-permute-start(bf16[256,896]{1,0:T(8,128)(2,1)} %collective-permute-done.4), channel_id=1, source_target_pairs={{0,4},{1,5},{2,6},{3,7},{4,8},{5,9},{6,10},{7,11},{8,12},{9,13},{1... | collective-permute-start | bytes 1376264 | tf_op jit(solution)/shard_map/ppermute | solution.py:30
  101.8 23.3 %collective-permute-start.22 = (f32[5,2,128,2,256]{4,2,0,3,1:T(8,128)}, f32[5,2,128,2,256]{4,2,0,3,1:T(8,128)}, u32[]{:S(2)}, u32[]{:S(2)}) collective-permute-start(f32[5,2,128,2,256]{4,2,0,3,1:T(8,128)} %copy_dynamic-update-slice_fusion), channel_id=1, source_target_pairs={{0,1},{1,0},{2,3},{3,2},{4,5},{5,4},{6,7},{7,6},{8,9},{9,8},{10,11... | collective-permute-start | bytes 7864328 | tf_op jit(solution)/shard_map/ppermute | solution.py:30
  129.2 10.0 %collective-permute-start.23 = (f16[2,5,128,256]{3,2,1,0:T(8,128)(2,1)}, f16[2,5,128,256]{3,2,1,0:T(8,128)(2,1)}, u32[]{:S(2)}, u32[]{:S(2)}) collective-permute-start(f16[2,5,128,256]{3,2,1,0:T(8,128)(2,1)} %pad_maximum_fusion.3), channel_id=1, source_target_pairs={{0,2},{1,67},{2,0},{3,65},{4,6},{5,71},{6,4},{7,69},{8,10},{9,75},... | collective-permute-start | bytes 1966088 | tf_op jit(solution)/shard_map/ppermute | solution.py:30
  130.9 16.7 %collective-permute-start.10 = (f16[2,5,128,256]{3,2,1,0:T(8,128)(2,1)S(1)}, f16[2,5,128,256]{3,2,1,0:T(8,128)(2,1)}, u32[]{:S(2)}, u32[]{:S(2)}) collective-permute-start(f16[2,5,128,256]{3,2,1,0:T(8,128)(2,1)S(1)} %pad_maximum_fusion.1), channel_id=1, source_target_pairs={{0,2},{1,67},{2,0},{3,65},{4,6},{5,71},{6,4},{7,69},{8,10},{9,75},... | collective-permute-start | bytes 1966088 | tf_op jit(solution)/shard_map/ppermute | solution.py:30
  140.6 10.3 %collective-permute-start.24 = (f16[5,128,256]{2,1,0:T(8,128)(2,1)S(1)}, f16[5,128,256]{2,1,0:T(8,128)(2,1)S(1)}, u32[]{:S(2)}, u32[]{:S(2)}) collective-permute-start(f16[5,128,256]{2,1,0:T(8,128)(2,1)S(1)} %fusion.49), channel_id=1, source_target_pairs={{0,66},{1,3},{2,64},{3,1},{4,70},{5,7},{6,68},{7,5},{8,74},{9,11},... | collective-permute-start | bytes 983048 | tf_op jit(solution)/shard_map/ppermute | solution.py:30
  149.0 6.7 %collective-permute-start.11 = (f16[5,128,256]{2,1,0:T(8,128)(2,1)S(1)}, f16[5,128,256]{2,1,0:T(8,128)(2,1)S(1)}, u32[]{:S(2)}, u32[]{:S(2)}) collective-permute-start(f16[5,128,256]{2,1,0:T(8,128)(2,1)S(1)} %fusion.54), channel_id=1, source_target_pairs={{0,66},{1,3},{2,64},{3,1},{4,70},{5,7},{6,68},{7,5},{8,74},{9,11},... | collective-permute-start | bytes 983048 | tf_op jit(solution)/shard_map/ppermute | solution.py:30
  151.0 10.7 %collective-permute-start.28 = (f32[1,128,256]{2,1,0:T(8,128)S(1)}, f32[1,128,256]{2,1,0:T(8,128)S(1)}, u32[]{:S(2)}, u32[]{:S(2)}) collective-permute-start(f32[1,128,256]{2,1,0:T(8,128)S(1)} %get-tuple-element.56), channel_id=1, source_target_pairs={{0,12},{1,13},{2,76},{3,77},{4,0},{5,1},{6,64},{7,65},{8,4},{9,5},... | collective-permute-start | bytes 393224 | tf_op jit(solution)/shard_map/ppermute | solution.py:30
  153.5 27.8 %collective-permute-start.25 = (f32[1,128,256]{2,1,0:T(8,128)S(1)}, f32[1,128,256]{2,1,0:T(8,128)S(1)}, u32[]{:S(2)}, u32[]{:S(2)}) collective-permute-start(f32[1,128,256]{2,1,0:T(8,128)S(1)} %get-tuple-element.56), channel_id=1, source_target_pairs={{0,32},{1,33},{2,34},{3,35},{4,36},{5,37},{6,38},{7,39},{8,40},{9,... | collective-permute-start | bytes 393224 | tf_op jit(solution)/shard_map/ppermute | solution.py:30
  155.9 9.5 %collective-permute-start.14 = (f32[2,128,256]{2,1,0:T(8,128)S(1)}, f32[2,128,256]{2,1,0:T(8,128)S(1)}, u32[]{:S(2)}, u32[]{:S(2)}) collective-permute-start(f32[2,128,256]{2,1,0:T(8,128)S(1)} %pad_maximum_fusion.12), channel_id=1, source_target_pairs={{0,16},{1,17},{2,80},{3,81},{4,20},{5,21},{6,84},{7,85},{8,24},{9,... | collective-permute-start | bytes 786440 | tf_op jit(solution)/shard_map/ppermute | solution.py:30
  156.4 10.5 %collective-permute-start.15 = (f32[1,128,256]{2,1,0:T(8,128)S(1)}, f32[1,128,256]{2,1,0:T(8,128)S(1)}, u32[]{:S(2)}, u32[]{:S(2)}) collective-permute-start(f32[1,128,256]{2,1,0:T(8,128)S(1)} %get-tuple-element.61), channel_id=1, source_target_pairs={{0,12},{1,13},{2,76},{3,77},{4,0},{5,1},{6,64},{7,65},{8,4},{9,5},... | collective-permute-start | bytes 393224 | tf_op jit(solution)/shard_map/ppermute | solution.py:30
  158.2 6.5 %collective-permute-start.29 = (f32[1,128,256]{2,1,0:T(8,128)S(1)}, f32[1,128,256]{2,1,0:T(8,128)S(1)}, u32[]{:S(2)}, u32[]{:S(2)}) collective-permute-start(f32[1,128,256]{2,1,0:T(8,128)S(1)} %get-tuple-element.55), channel_id=1, source_target_pairs={{0,48},{1,49},{2,112},{3,113},{4,52},{5,53},{6,116},{7,117},{8,56}... | collective-permute-start | bytes 393224 | tf_op jit(solution)/shard_map/ppermute | solution.py:30
  161.7 18.6 %collective-permute-start.16 = (f32[1,128,256]{2,1,0:T(8,128)S(1)}, f32[1,128,256]{2,1,0:T(8,128)S(1)}, u32[]{:S(2)}, u32[]{:S(2)}) collective-permute-start(f32[1,128,256]{2,1,0:T(8,128)S(1)} %get-tuple-element.60), channel_id=1, source_target_pairs={{0,48},{1,49},{2,112},{3,113},{4,52},{5,53},{6,116},{7,117},{8,56}... | collective-permute-start | bytes 393224 | tf_op jit(solution)/shard_map/ppermute | solution.py:30
  164.7 16.6 %collective-permute-start.26 = (f32[2,128,256]{2,1,0:T(8,128)S(1)}, f32[2,128,256]{2,1,0:T(8,128)S(1)}, u32[]{:S(2)}, u32[]{:S(2)}) collective-permute-start(f32[2,128,256]{2,1,0:T(8,128)S(1)} %get-tuple-element.58), channel_id=1, source_target_pairs={{0,8},{1,9},{2,10},{3,11},{4,12},{5,13},{6,14},{7,15},{8,0},{9,1},... | collective-permute-start | bytes 786440 | tf_op jit(solution)/shard_map/ppermute | solution.py:30
  165.5 21.8 %collective-permute-start.12 = (f32[2,128,256]{2,1,0:T(8,128)S(1)}, f32[2,128,256]{2,1,0:T(8,128)S(1)}, u32[]{:S(2)}, u32[]{:S(2)}) collective-permute-start(f32[2,128,256]{2,1,0:T(8,128)S(1)} %stack.86), channel_id=1, source_target_pairs={{0,4},{1,5},{2,6},{3,7},{4,8},{5,9},{6,10},{7,11},{8,12},{9,13},{1... | collective-permute-start | bytes 786440 | tf_op jit(solution)/shard_map/ppermute | solution.py:30
  166.9 23.1 %collective-permute-start.30 = (f32[2,256,128]{1,2,0:T(8,128)S(1)}, f32[2,256,128]{1,2,0:T(8,128)S(1)}, u32[]{:S(2)}, u32[]{:S(2)}) collective-permute-start(f32[2,256,128]{1,2,0:T(8,128)S(1)} %pad_maximum_fusion.13), channel_id=1, source_target_pairs={{0,1},{1,0},{2,3},{3,2},{4,5},{5,4},{6,7},{7,6},{8,9},{9,8},{10,11... | collective-permute-start | bytes 786440 | tf_op jit(solution)/shard_map/ppermute | solution.py:30
  181.2 9.2 %collective-permute-start.17 = (f32[4,256,128]{1,2,0:T(8,128)}, f32[4,256,128]{1,2,0:T(8,128)S(1)}, u32[]{:S(2)}, u32[]{:S(2)}) collective-permute-start(f32[4,256,128]{1,2,0:T(8,128)} %pad_maximum_fusion.6), channel_id=1, source_target_pairs={{0,1},{1,0},{2,3},{3,2},{4,5},{5,4},{6,7},{7,6},{8,9},{9,8},{10,11... | collective-permute-start | bytes 1572872 | tf_op jit(solution)/shard_map/ppermute | solution.py:30
  182.1 12.7 %collective-permute-start.27 = (f32[5,128,256]{2,1,0:T(8,128)}, f32[5,128,256]{2,1,0:T(8,128)}, u32[]{:S(2)}, u32[]{:S(2)}) collective-permute-start(f32[5,128,256]{2,1,0:T(8,128)} %pad_maximum_fusion.4), channel_id=1, source_target_pairs={{0,1},{1,0},{2,3},{3,2},{4,5},{5,4},{6,7},{7,6},{8,9},{9,8},{10,11... | collective-permute-start | bytes 1966088 | tf_op jit(solution)/shard_map/ppermute | solution.py:30
  188.2 3.9 %collective-permute-start.13 = (f32[5,128,256]{2,1,0:T(8,128)}, f32[5,128,256]{2,1,0:T(8,128)}, u32[]{:S(2)}, u32[]{:S(2)}) collective-permute-start(f32[5,128,256]{2,1,0:T(8,128)} %pad_maximum_fusion.2), channel_id=1, source_target_pairs={{0,1},{1,0},{2,3},{3,2},{4,5},{5,4},{6,7},{7,6},{8,9},{9,8},{10,11... | collective-permute-start | bytes 1966088 | tf_op jit(solution)/shard_map/ppermute | solution.py:30
  (41 other events, 205.7 us)

commit v2 on v0

v2 whole, which is shorter than its diff:
```python
import functools

import jax
import jax.numpy as jnp
import numpy as np
from jax import lax
from jax.experimental import pallas as pl
from jax.experimental.pallas import tpu as pltpu
from jax.sharding import PartitionSpec as P


AXES = ("rows", "cols")
SIZES = (2, 4, 4, 2, 2)
ALONG = {"s": (0, 0), "a1": (1, 0), "a2": (2, 0), "a3": (3, 0), "b1": (0, 1), "b2": (0, 2), "b3": (0, 3)}
SCALE = 128.0
NEAR = (
    ("a1", "s", ("right", "left"), False),
    ("a1", "a3", ("right",), False),
    ("a1", "b1", ("right", "left"), False),
    ("s", "s", ("right",), True),
)
FAR = (("a2", "b3", ("right", "left"), False), ("a2", "b2", ("right",), True))
VMEM = pl.BlockSpec(memory_space=pltpu.VMEM)
SMEM = pl.BlockSpec(memory_space=pltpu.SMEM)


def offset(name, core):
    dx, dy = ALONG[name]
    return (dx, dy) if core == 0 else (-dy % 4, dx)


def gap(name, start, core):
    return tuple((a - b) % 4 for a, b in zip(offset(name, core), offset(start, core)))


def send(value, move):
    pairs = []
    for source in range(int(np.prod(SIZES))):
        place = [int(i) for i in np.unravel_index(source, SIZES)]
        pairs.append((source, int(np.ravel_multi_index(move(*place), SIZES))))
    return lax.ppermute(value, AXES, pairs)


def to_place(name, swap=False):
    def move(zh, x, y, zl, core):
        dx, dy = offset(name, core)
        if swap:
            zh, zl = zl, zh
        return zh, (x + dx) % 4, (y + dy) % 4, zl, core

    return move


def other_core(zh, x, y, zl, core):
    return zh, x, y, zl, 1 - core


def other_high(zh, x, y, zl, core):
    return 1 - zh, x, y, zl, core


def first_partner(zh, x, y, zl, core):
    return (zh, x, y, 1 - zl, core) if core == 0 else (1 - zh, x, y, 1 - zl, core)


def second_partner(zh, x, y, zl, core):
    return first_partner(zh, x, y, zl, 1 - core)[:4] + (core,)


def after(value, *others):
    return lax.optimization_barrier((value, *others))[0]


def packed(value):
    return (value * SCALE).astype(jnp.float16)


def unpacked(value):
    return value.astype(jnp.float32) * (1.0 / SCALE)


def call(kernel, outs, *args, flops=0, scratch=()):
    size = sum(a.size * a.dtype.itemsize for a in args) + sum(int(np.prod(s)) * 4 for s in outs)
    return pl.pallas_call(
        kernel,
        out_shape=[jax.ShapeDtypeStruct(s, jnp.float32) for s in outs],
        in_specs=[SMEM] + [VMEM] * (len(args) - 1),
        out_specs=[VMEM] * len(outs),
        scratch_shapes=scratch,
        compiler_params=pltpu.CompilerParams(vmem_limit_bytes=48 * 2**20),
        cost_estimate=pl.CostEstimate(flops=flops, bytes_accessed=size, transcendentals=0),
    )(*args)


def spans(pairs):
    at, out = 0, []
    for *_, halved in pairs:
        out.append((at, 128 if halved else 256))
        at += out[-1][1]
    return out, at


def multiply(pairs, names, place, *refs):
    held = {}
    for name in names:
        parts = 4 if name[1:] == "2" else 2
        held[name], refs = refs[:parts], refs[parts:]
    out, line = refs
    core = place[3]
    straight = jnp.where(place[0] == place[2], 1, 0)
    mirror = pairs[0][1] if pairs[0][1][0] == "b" else "b1"

    @pl.when(core == 0)
    def _():
        for kind in (0, 1):
            line[kind] = held[mirror][kind][...]

    @pl.when(core == 1)
    def _():
        for kind in (0, 1):
            line[kind] = held["b3" if mirror == "b1" else "b1"][kind][...]

    def rows(name, kind):
        if name == mirror:
            return line[kind]
        if name[1:] == "2":
            return jnp.concatenate([held[name][2 * kind][...], held[name][2 * kind + 1][...]], axis=0)
        return held[name][kind][...]

    for (left, right, _, halved), (at, size) in zip(pairs, spans(pairs)[0], strict=True):
        for kind in (0, 1):
            if not halved:
                lhs = rows(left, kind)
            elif left == "a2":
                lhs = jnp.where(core == 0, held[left][2 * kind][...], held[left][2 * kind + 1][...])
            else:
                lhs = held[left][kind][pl.ds(pl.multiple_of(core * 128, 128), 128), :]
            ends = straight if kind == 0 else 1 - straight
            for col in (0, 1):
                slot = jnp.where(ends == 1, 1 if col else 2, jnp.where(core == col, 0, 3))
                out[slot, pl.ds(at, size)] = lax.dot_general(
                    lhs, rows(right, col), (((1,), (1,)), ((), ())), preferred_element_type=jnp.float32
                )


def finish(groups, place, stay, got, late, *outs):
    for parts, out in zip(groups, outs, strict=True):
        to = 0
        for at, size in parts:
            take = pl.ds(at, size)
            out[pl.ds(to, size)] = stay[2, take] + got[0, take] + late[take]
            to += size


def products(place, blocks, pairs):
    total = spans(pairs)[1]
    names = sorted({name for pair in pairs for name in pair[:2]} | {"b1", "b3"})
    return call(
        functools.partial(multiply, pairs, names),
        [(4, total, 256)],
        place,
        *[rows for name in names for rows in blocks[name]],
        flops=total * 4 * 2 * 256 * 1792,
        scratch=[pltpu.VMEM((2, 256, 1792), jnp.bfloat16)],
    )[0]


def summed(place, stay, leave, pairs):
    where = spans(pairs)[0]
    got = unpacked(send(leave, first_partner))
    late = unpacked(send(packed(stay[3] + got[1]), second_partner))
    messages = {}
    for (left, right, keepers, halved), span in zip(pairs, where, strict=True):
        for keeper in keepers:
            to, rows = (right, left) if keeper == "right" else (left, right)
            messages.setdefault((to, keeper == "left"), []).append((span, halved, [gap(rows, to, c) for c in (0, 1)]))
    groups = [[span for span, _, _ in parts] for parts in messages.values()]
    outs = call(
        functools.partial(finish, groups),
        [(sum(size for _, size in g), 256) for g in groups],
        place,
        stay,
        got,
        late,
    )
    delivered = []
    for ((to, turned), parts), out in zip(messages.items(), outs, strict=True):
        if to != "s":
            out = send(out, to_place(to, turned))
        layout = [(turned, halved, gaps) for _, halved, gaps in parts]
        delivered.append((layout, out, send(out, other_core)))
    return delivered


def update(layouts, place, old, *refs):
    new = refs[-1]
    core = place[3]
    for parts, mine, far in zip(layouts, refs[:-1:2], refs[1:-1:2], strict=True):
        for source, tiles in ((core, mine), (1 - core, far)):
            at = 0
            for turned, halved, gaps in parts:
                size = 128 if halved else 256
                dx = jnp.where(source == 0, gaps[0][0], gaps[1][0])
                dy = jnp.where(source == 0, gaps[0][1], gaps[1][1])
                x, y = (place[1] + dx) & 3, (place[4] + dy) & 3

                @pl.when((x >> 1) == core)
                def _():
                    tile = tiles[pl.ds(at, size)]
                    if turned:
                        tile = tile.T
                    to = ((x & 1) * 4 + y) * 256 + (source * 128 if halved else 0)
                    to = pl.ds(pl.multiple_of(to, 128), size)
                    new[to] = 0.9 * old[to] + 0.1 * tile

                at += size


def body(gradient, stat_old):
    device = lax.axis_index("rows").astype(jnp.int32)
    column = lax.axis_index("cols").astype(jnp.int32)
    zh, x, y = device >> 4, (device >> 2) & 3, device & 3
    zl, core = column >> 1, column & 1
    place = jnp.stack([zh, x, zl, core, y])

    def whole(rows):
        far = send(rows, other_core)
        first = jnp.where(core == 0, rows, far)
        return jnp.concatenate([first, jnp.where(core == 0, far, rows)], axis=1)

    keep = lax.dynamic_slice_in_dim(gradient, zh * 896, 896, 1)
    give = lax.dynamic_slice_in_dim(gradient, (1 - zh) * 896, 896, 1)
    own = {"s": whole(keep)}
    given = send(after(give, own["s"]), other_high)
    own["a1"], own["a3"] = send(own["s"], to_place("a3")), send(own["s"], to_place("a1"))
    other = {"s": whole(after(given, own["a1"], own["a3"]))}
    other["a1"], other["a3"] = send(other["s"], to_place("a3")), send(other["s"], to_place("a1"))
    for kind in (own, other):
        kind["b1"], kind["b3"] = send(kind["a1"], other_core), send(kind["a3"], other_core)
        upper, lower = send(kind["a1"][:128], to_place("a3")), send(kind["a3"][128:], to_place("a1"))
        kind["a2"] = upper, lower
        kind["b2"] = send(upper, other_core), send(lower, other_core)
    blocks = {name: (own[name], other[name]) for name in ("s", "a1", "a3", "b1", "b3")}
    blocks.update({name: own[name] + other[name] for name in ("a2", "b2")})
    near = products(place, blocks, NEAR)
    near_leave = packed(near[:2])
    far = products(after(place, near_leave), blocks, FAR)
    far_leave = packed(far[:2])
    delivered = summed(place, near, near_leave, NEAR) + summed(place, far, far_leave, FAR)
    (new,) = call(
        functools.partial(update, [layout for layout, _, _ in delivered]),
        [stat_old.shape],
        place,
        stat_old,
        *[tiles for _, mine, far in delivered for tiles in (mine, far)],
    )
    return new


def solution(mesh):
    placed = (P("rows", "cols"), P("cols", "rows"))
    return jax.shard_map(
        body, mesh=mesh, in_specs=placed, out_specs=P("cols", "rows"), check_vma=False
    )
```

time: 352 us -> 124 us (0.35)
  waiting for transfers between devices: 317 us -> 45 us
  starting transfers between devices: 0.04 us -> 47.7 us
  Pallas kernels: 0 us -> 20.7 us
  matrix products: 15.7 us -> 0 us
  between operations: 13.4 us -> 0.2 us
  local copies, waits for them, and re-layouts: 0.01 us -> 4.51 us
    all_gather x1 -> x0, waiting for transfers between devices: 239 us -> none  [body(): gathered = lax.all_gather(gradient, 'rows', axis=0, tiled=True)]
    reduce_scatter x1 -> x0, waiting for transfers between devices: 77.1 us -> none  [body(): lax.psum_scatter(row_products(gathered, gradient), 'cols', scatter_dimens...]
    ppermute x0 -> x36, starting transfers between devices: none -> 47.7 us  [send(): return lax.ppermute(value, AXES, pairs)]
    ppermute x0 -> x36, waiting for transfers between devices: none -> 45 us  [send(): return lax.ppermute(value, AXES, pairs)]
    pallas_call x0 -> x5, Pallas kernels: none -> 20.7 us  [call(): pl.pallas_call(kernel, out_shape=[jax.ShapeDtypeStruct(s, jnp.float32) fo...]
    dot_general x1 -> x0, matrix products: 15.7 us -> none  [row_products(): lax.dot_general(left_rows, right_rows, (((1,), (1,)), ((), ())), preferre...]
    convert_element_type x0 -> x4, other arithmetic: none -> 4.45 us  [packed(): return (value * SCALE).astype(jnp.float16)]
  transfers between devices with their start and end apart: 2 -> 36, of which waited for: 2 -> 15; matrix products, arithmetic and copies ran while one was open for 0% -> 7% of each run, Pallas kernels for 0% -> 14%
where the time goes in v2:
time: 124 us; the launch traced here: 123 us
  starting transfers between devices  47.7 us (38%)
  waiting for transfers between devices  45 us (36%)
  Pallas kernels  20.7 us (17%)
  other arithmetic  5.12 us (4%)
  local copies, waits for them, and re-layouts  4.51 us (4%)
    ppermute x36, starting transfers between devices, send(): return lax.ppermute(value, AXES, pairs)  47.7 us
    ppermute x36, waiting for transfers between devices, send(): return lax.ppermute(value, AXES, pairs)  45 us
    pallas_call x5, Pallas kernels, call(): pl.pallas_call(kernel, out_shape=[jax.ShapeDtypeStruct(s, jnp.float32) fo...  20.7 us
    convert_element_type x4, other arithmetic, packed(): return (value * SCALE).astype(jnp.float16)  4.45 us
  transfers between devices with their start and end apart: 36, of which 15 were waited for; matrix products, arithmetic and copies ran while one was open for 7% of the time, Pallas kernels for 14%

profile of v2, /device:TPU:33, one launch (start us, length us, event | category | flops | bytes accessed | tf_op | source)
XLA Modules:
  0.0 123.3 jit_solution(5136497245493329199)
XLA Ops:
  0.0 1.2 constant_dynamic-slice_fusion
  2.0 1.4 %collective-permute-done = bf16[256,896]{1,0:T(8,128)(2,1)S(1)} collective-permute-done((bf16[256,896]{1,0:T(8,128)(2,1)S(1)}, bf16[256,896]{1,0:T(8,128)(2,1)S(1)}, u32[]{:S(2)}, u32[]{:S(2)}) %collective-permute-start) | collective-permute-done | bytes 458784 | tf_op jit(solution)/shard_map/ppermute | solution.py:41
  3.6 2.8 %collective-permute-start.1 = (bf16[256,1792]{1,0:T(8,128)(2,1)S(1)}, bf16[256,1792]{1,0:T(8,128)(2,1)S(1)}, u32[]{:S(2)}, u32[]{:S(2)}) collective-permute-start(bf16[256,1792]{1,0:T(8,128)(2,1)S(1)} %pad_maximum_fusion.refs_8_), channel_id=1, source_target_pairs={{0,48},{1,13},{2,50},{3,15},{4,52},{5,1},{6,54},{7,3},{8,56},{9,5}... | collective-permute-start | bytes 2752520 | tf_op jit(solution)/shard_map/ppermute | solution.py:41
  6.4 2.7 %collective-permute-start.2 = (bf16[256,896]{1,0:T(8,128)(2,1)S(1)}, bf16[256,896]{1,0:T(8,128)(2,1)S(1)}, u32[]{:S(2)}, u32[]{:S(2)}) collective-permute-start(bf16[256,896]{1,0:T(8,128)(2,1)S(1)} %get-tuple-element.15), channel_id=1, source_target_pairs={{0,64},{1,65},{2,66},{3,67},{4,68},{5,69},{6,70},{7,71},{8,72},{9,... | collective-permute-start | bytes 1376264 | tf_op jit(solution)/shard_map/ppermute | solution.py:41
  9.1 10.6 %collective-permute-done.2 = bf16[256,896]{1,0:T(8,128)(2,1)S(1)} collective-permute-done((bf16[256,896]{1,0:T(8,128)(2,1)S(1)}, bf16[256,896]{1,0:T(8,128)(2,1)S(1)}, u32[]{:S(2)}, u32[]{:S(2)}) %collective-permute-start.2) | collective-permute-done | bytes 458784 | tf_op jit(solution)/shard_map/ppermute | solution.py:41
  20.3 1.3 %collective-permute-start.4 = (bf16[256,896]{1,0:T(8,128)(2,1)S(1)}, bf16[256,896]{1,0:T(8,128)(2,1)S(1)}, u32[]{:S(2)}, u32[]{:S(2)}) collective-permute-start(bf16[256,896]{1,0:T(8,128)(2,1)S(1)} %collective-permute-done.2), channel_id=1, source_target_pairs={{0,1},{1,0},{2,3},{3,2},{4,5},{5,4},{6,7},{7,6},{8,9},{9,8},{10,11... | collective-permute-start | bytes 1376264 | tf_op jit(solution)/shard_map/ppermute | solution.py:41
  21.5 1.4 %collective-permute-done.4 = bf16[256,896]{1,0:T(8,128)(2,1)S(1)} collective-permute-done((bf16[256,896]{1,0:T(8,128)(2,1)S(1)}, bf16[256,896]{1,0:T(8,128)(2,1)S(1)}, u32[]{:S(2)}, u32[]{:S(2)}) %collective-permute-start.4) | collective-permute-done | bytes 458784 | tf_op jit(solution)/shard_map/ppermute | solution.py:41
  23.2 1.4 %collective-permute-start.6 = (bf16[256,1792]{1,0:T(8,128)(2,1)S(1)}, bf16[256,1792]{1,0:T(8,128)(2,1)}, u32[]{:S(2)}, u32[]{:S(2)}) collective-permute-start(bf16[256,1792]{1,0:T(8,128)(2,1)S(1)} %pad_maximum_fusion.1.refs_9_), channel_id=1, source_target_pairs={{0,16},{1,5},{2,18},{3,7},{4,20},{5,9},{6,22},{7,11},{8,24},{9,13}... | collective-permute-start | bytes 2752520 | tf_op jit(solution)/shard_map/ppermute | solution.py:41
  24.5 1.5 %collective-permute-start.5 = (bf16[256,1792]{1,0:T(8,128)(2,1)S(1)}, bf16[256,1792]{1,0:T(8,128)(2,1)}, u32[]{:S(2)}, u32[]{:S(2)}) collective-permute-start(bf16[256,1792]{1,0:T(8,128)(2,1)S(1)} %pad_maximum_fusion.1.refs_9_), channel_id=1, source_target_pairs={{0,48},{1,13},{2,50},{3,15},{4,52},{5,1},{6,54},{7,3},{8,56},{9,5}... | collective-permute-start | bytes 2752520 | tf_op jit(solution)/shard_map/ppermute | solution.py:41
  26.8 10.3 %collective-permute-done.6.refs_3_ = bf16[256,1792]{1,0:T(8,128)(2,1)} collective-permute-done((bf16[256,1792]{1,0:T(8,128)(2,1)S(1)}, bf16[256,1792]{1,0:T(8,128)(2,1)}, u32[]{:S(2)}, u32[]{:S(2)}) %collective-permute-start.6) | collective-permute-done | bytes 917536 | tf_op jit(solution)/shard_map/ppermute | solution.py:41
  37.1 1.2 collective-permute-start.10
  38.5 2.8 %collective-permute-start.20 = (bf16[128,1792]{1,0:T(8,128)(2,1)S(1)}, bf16[128,1792]{1,0:T(8,128)(2,1)S(1)}, u32[]{:S(2)}, u32[]{:S(2)}) collective-permute-start(bf16[128,1792]{1,0:T(8,128)(2,1)S(1)} %slice.43), channel_id=1, source_target_pairs={{0,48},{1,13},{2,50},{3,15},{4,52},{5,1},{6,54},{7,3},{8,56},{9,5}... | collective-permute-start | bytes 1376264 | tf_op jit(solution)/shard_map/ppermute | solution.py:41
  44.6 2.7 %collective-permute-start.22 = (bf16[128,1792]{1,0:T(8,128)(2,1)S(1)}, bf16[128,1792]{1,0:T(8,128)(2,1)S(1)}, u32[]{:S(2)}, u32[]{:S(2)}) collective-permute-start(bf16[128,1792]{1,0:T(8,128)(2,1)S(1)} %slice.45), channel_id=1, source_target_pairs={{0,48},{1,13},{2,50},{3,15},{4,52},{5,1},{6,54},{7,3},{8,56},{9,5}... | collective-permute-start | bytes 1376264 | tf_op jit(solution)/shard_map/ppermute | solution.py:41
  47.3 8.9 %shard_map.28.stay = f32[4,896,256]{2,1,0:T(8,128)} custom-call(s32[5]{0:T(128)S(1)} %stack.23.place, bf16[256,1792]{1,0:T(8,128)(2,1)S(1)} %collective-permute-done.1.refs_0_, bf16[256,1792]{1,0:T(8,128)(2,1)} %collective-permute-done.5.refs_1_, bf16[256,1792]{1,0:T(8,128)(2,1)} %collective-permute-done.3.refs_2_, ...), custom_call_target="tpu_custom_call" | custom-call | flops 3288334336 | bytes 12845076 | tf_op jit(solution)/shard_map/pallas_call | solution.py:84
  56.2 1.7 %fusion = f16[2,896,256]{2,1,0:T(8,128)(2,1)S(1)} fusion(f32[4,896,256]{2,1,0:T(8,128)} %shard_map.28.stay), kind=kLoop, calls=%fused_computation.1 | loop fusion | flops 917504 | bytes 2752512 | tf_op jit(solution)/shard_map/convert_element_type | solution.py:75
  57.9 1.7 %collective-permute-start.11 = (f16[2,896,256]{2,1,0:T(8,128)(2,1)S(1)}, f16[2,896,256]{2,1,0:T(8,128)(2,1)S(1)}, u32[]{:S(2)}, u32[]{:S(2)}) collective-permute-start(f16[2,896,256]{2,1,0:T(8,128)(2,1)S(1)} %fusion), channel_id=1, source_target_pairs={{0,2},{1,67},{2,0},{3,65},{4,6},{5,71},{6,4},{7,69},{8,10},{9,75},... | collective-permute-start | bytes 2752520 | tf_op jit(solution)/shard_map/ppermute | solution.py:41
  63.4 5.2 %shard_map.30.stay = f32[4,384,256]{2,1,0:T(8,128)} custom-call(s32[5]{0:T(128)S(1)} %stack.23.place, bf16[128,1792]{1,0:T(8,128)(2,1)S(1)} %collective-permute-done.20.refs_0_, bf16[128,1792]{1,0:T(8,128)(2,1)S(1)} %collective-permute-done.21.refs_1_, bf16[128,1792]{1,0:T(8,128)(2,1)S(1)} %collective-permute-done.22.refs_2_, ...), custom_call_target="tpu_custom_call" | custom-call | flops 1409286144 | bytes 8912916 | tf_op jit(solution)/shard_map/pallas_call | solution.py:84
  68.6 1.2 fusion.3
  69.8 2.3 %collective-permute-start.28 = (f16[2,384,256]{2,1,0:T(8,128)(2,1)S(1)}, f16[2,384,256]{2,1,0:T(8,128)(2,1)S(1)}, u32[]{:S(2)}, u32[]{:S(2)}) collective-permute-start(f16[2,384,256]{2,1,0:T(8,128)(2,1)S(1)} %fusion.3), channel_id=1, source_target_pairs={{0,2},{1,67},{2,0},{3,65},{4,6},{5,71},{6,4},{7,69},{8,10},{9,75},... | collective-permute-start | bytes 1179656 | tf_op jit(solution)/shard_map/ppermute | solution.py:41
  72.3 1.5 %fusion.4 = f16[896,256]{1,0:T(8,128)(2,1)S(1)} fusion(f32[2,896,256]{2,1,0:T(8,128)S(1)} %convert_multiply_fusion.got, f32[4,896,256]{2,1,0:T(8,128)} %shard_map.28.stay), kind=kLoop, calls=%fused_computation.12 | loop fusion | flops 688128 | bytes 2293760 | tf_op jit(solution)/shard_map/convert_element_type | solution.py:75
  74.6 3.2 %collective-permute-done.28 = f16[2,384,256]{2,1,0:T(8,128)(2,1)S(1)} collective-permute-done((f16[2,384,256]{2,1,0:T(8,128)(2,1)S(1)}, f16[2,384,256]{2,1,0:T(8,128)(2,1)S(1)}, u32[]{:S(2)}, u32[]{:S(2)}) %collective-permute-start.28) | collective-permute-done | bytes 393248 | tf_op jit(solution)/shard_map/ppermute | solution.py:41
  78.0 3.0 %collective-permute-start.29 = (f16[384,256]{1,0:T(8,128)(2,1)S(1)}, f16[384,256]{1,0:T(8,128)(2,1)S(1)}, u32[]{:S(2)}, u32[]{:S(2)}) collective-permute-start(f16[384,256]{1,0:T(8,128)(2,1)S(1)} %fusion.7), channel_id=1, source_target_pairs={{0,66},{1,3},{2,64},{3,1},{4,70},{5,7},{6,68},{7,5},{8,74},{9,11},... | collective-permute-start | bytes 589832 | tf_op jit(solution)/shard_map/ppermute | solution.py:41
  81.0 1.5 %collective-permute-done.12 = f16[896,256]{1,0:T(8,128)(2,1)S(1)} collective-permute-done((f16[896,256]{1,0:T(8,128)(2,1)S(1)}, f16[896,256]{1,0:T(8,128)(2,1)S(1)}, u32[]{:S(2)}, u32[]{:S(2)}) %collective-permute-start.12) | collective-permute-done | bytes 458784 | tf_op jit(solution)/shard_map/ppermute | solution.py:41
  82.6 2.2 %shard_map.29 = (f32[384,256]{1,0:T(8,128)S(1)}, f32[512,256]{1,0:T(8,128)S(1)}, f32[256,256]{1,0:T(8,128)S(1)}, f32[256,256]{1,0:T(8,128)S(1)}) custom-call(s32[5]{0:T(128)S(1)} %stack.23.place, f32[4,896,256]{2,1,0:T(8,128)} %shard_map.28.stay, f32[2,896,256]{2,1,0:T(8,128)S(1)} %convert_multiply_fusion.got, f32[896,256]{1,0:T(8,128)S(1)} %convert_multiply_fusion.1.late), custom_call_target="tpu_custom_call" | custom-call | bytes 7864340 | tf_op jit(solution)/shard_map/pallas_call | solution.py:84
  84.8 3.1 %collective-permute-start.14 = (f32[512,256]{1,0:T(8,128)S(1)}, f32[512,256]{1,0:T(8,128)S(1)}, u32[]{:S(2)}, u32[]{:S(2)}) collective-permute-start(f32[512,256]{1,0:T(8,128)S(1)} %get-tuple-element.18), channel_id=1, source_target_pairs={{0,16},{1,5},{2,80},{3,69},{4,20},{5,9},{6,84},{7,73},{8,24},{9,13... | collective-permute-start | bytes 1572872 | tf_op jit(solution)/shard_map/ppermute | solution.py:41
  88.6 2.1 %collective-permute-start.32 = (f32[256,256]{1,0:T(8,128)S(1)}, f32[256,256]{1,0:T(8,128)S(1)}, u32[]{:S(2)}, u32[]{:S(2)}) collective-permute-start(f32[256,256]{1,0:T(8,128)S(1)} %get-tuple-element.23), channel_id=1, source_target_pairs={{0,32},{1,9},{2,96},{3,73},{4,36},{5,13},{6,100},{7,77},{8,40},{9,... | collective-permute-start | bytes 786440 | tf_op jit(solution)/shard_map/ppermute | solution.py:41
  90.8 3.7 %collective-permute-start.34 = (f32[128,256]{1,0:T(8,128)S(1)}, f32[128,256]{1,0:T(8,128)S(1)}, u32[]{:S(2)}, u32[]{:S(2)}) collective-permute-start(f32[128,256]{1,0:T(8,128)S(1)} %get-tuple-element.24), channel_id=1, source_target_pairs={{0,8},{1,33},{2,10},{3,35},{4,12},{5,37},{6,14},{7,39},{8,0},{9,41... | collective-permute-start | bytes 393224 | tf_op jit(solution)/shard_map/ppermute | solution.py:41
  94.4 10.6 %collective-permute-done.34.refs_12_ = f32[128,256]{1,0:T(8,128)S(1)} collective-permute-done((f32[128,256]{1,0:T(8,128)S(1)}, f32[128,256]{1,0:T(8,128)S(1)}, u32[]{:S(2)}, u32[]{:S(2)}) %collective-permute-start.34) | collective-permute-done | bytes 131104 | tf_op jit(solution)/shard_map/ppermute | solution.py:41
  105.6 3.1 %collective-permute-start.16 = (f32[256,256]{1,0:T(8,128)S(1)}, f32[256,256]{1,0:T(8,128)S(1)}, u32[]{:S(2)}, u32[]{:S(2)}) collective-permute-start(f32[256,256]{1,0:T(8,128)S(1)} %get-tuple-element.19), channel_id=1, source_target_pairs={{0,48},{1,13},{2,50},{3,15},{4,52},{5,1},{6,54},{7,3},{8,56},{9,5}... | collective-permute-start | bytes 786440 | tf_op jit(solution)/shard_map/ppermute | solution.py:41
  109.7 2.6 %collective-permute-start.15 = (f32[512,256]{1,0:T(8,128)S(1)}, f32[512,256]{1,0:T(8,128)S(1)}, u32[]{:S(2)}, u32[]{:S(2)}) collective-permute-start(f32[512,256]{1,0:T(8,128)S(1)} %collective-permute-done.14.refs_2_), channel_id=1, source_target_pairs={{0,1},{1,0},{2,3},{3,2},{4,5},{5,4},{6,7},{7,6},{8,9},{9,8},{10,11... | collective-permute-start | bytes 1572872 | tf_op jit(solution)/shard_map/ppermute | solution.py:41
  114.2 4.2 %collective-permute-start.19 = (f32[256,256]{1,0:T(8,128)S(1)}, f32[256,256]{1,0:T(8,128)S(1)}, u32[]{:S(2)}, u32[]{:S(2)}) collective-permute-start(f32[256,256]{1,0:T(8,128)S(1)} %collective-permute-done.18.refs_6_), channel_id=1, source_target_pairs={{0,1},{1,0},{2,3},{3,2},{4,5},{5,4},{6,7},{7,6},{8,9},{9,8},{10,11... | collective-permute-start | bytes 786440 | tf_op jit(solution)/shard_map/ppermute | solution.py:41
  119.6 3.8 %shard_map.32 = f32[2048,256]{1,0:T(8,128)} custom-call(s32[5]{0:T(128)S(1)} %stack.23.place, f32[2048,256]{1,0:T(8,128)} %old.1, f32[384,256]{1,0:T(8,128)S(1)} %get-tuple-element.17.refs_0_, f32[384,256]{1,0:T(8,128)S(1)} %collective-permute-done.13.refs_1_, f32[512,256]{1,0:T(8,128)S(1)} %collective-permute-done.14.refs_2_, ...), custom_call_target="tpu_custom_call" | custom-call | bytes 8388628 | tf_op jit(solution)/shard_map/pallas_call | solution.py:84
  (69 shorter events, 16.1 us)
Async XLA Ops:
  3.6 16.1 %collective-permute-start.1 = (bf16[256,1792]{1,0:T(8,128)(2,1)S(1)}, bf16[256,1792]{1,0:T(8,128)(2,1)S(1)}, u32[]{:S(2)}, u32[]{:S(2)}) collective-permute-start(bf16[256,1792]{1,0:T(8,128)(2,1)S(1)} %pad_maximum_fusion.refs_8_), channel_id=1, source_target_pairs={{0,48},{1,13},{2,50},{3,15},{4,52},{5,1},{6,54},{7,3},{8,56},{9,5}... | collective-permute-start | bytes 2752520 | tf_op jit(solution)/shard_map/ppermute | solution.py:41
  6.4 13.9 %collective-permute-start.3 = (bf16[256,1792]{1,0:T(8,128)(2,1)S(1)}, bf16[256,1792]{1,0:T(8,128)(2,1)}, u32[]{:S(2)}, u32[]{:S(2)}) collective-permute-start(bf16[256,1792]{1,0:T(8,128)(2,1)S(1)} %pad_maximum_fusion.refs_8_), channel_id=1, source_target_pairs={{0,16},{1,5},{2,18},{3,7},{4,20},{5,9},{6,22},{7,11},{8,24},{9,13}... | collective-permute-start | bytes 2752520 | tf_op jit(solution)/shard_map/ppermute | solution.py:41
  6.4 13.3 %collective-permute-start.2 = (bf16[256,896]{1,0:T(8,128)(2,1)S(1)}, bf16[256,896]{1,0:T(8,128)(2,1)S(1)}, u32[]{:S(2)}, u32[]{:S(2)}) collective-permute-start(bf16[256,896]{1,0:T(8,128)(2,1)S(1)} %get-tuple-element.15), channel_id=1, source_target_pairs={{0,64},{1,65},{2,66},{3,67},{4,68},{5,69},{6,70},{7,71},{8,72},{9,... | collective-permute-start | bytes 1376264 | tf_op jit(solution)/shard_map/ppermute | solution.py:41
  20.3 2.7 %collective-permute-start.4 = (bf16[256,896]{1,0:T(8,128)(2,1)S(1)}, bf16[256,896]{1,0:T(8,128)(2,1)S(1)}, u32[]{:S(2)}, u32[]{:S(2)}) collective-permute-start(bf16[256,896]{1,0:T(8,128)(2,1)S(1)} %collective-permute-done.2), channel_id=1, source_target_pairs={{0,1},{1,0},{2,3},{3,2},{4,5},{5,4},{6,7},{7,6},{8,9},{9,8},{10,11... | collective-permute-start | bytes 1376264 | tf_op jit(solution)/shard_map/ppermute | solution.py:41
  23.2 14.0 %collective-permute-start.6 = (bf16[256,1792]{1,0:T(8,128)(2,1)S(1)}, bf16[256,1792]{1,0:T(8,128)(2,1)}, u32[]{:S(2)}, u32[]{:S(2)}) collective-permute-start(bf16[256,1792]{1,0:T(8,128)(2,1)S(1)} %pad_maximum_fusion.1.refs_9_), channel_id=1, source_target_pairs={{0,16},{1,5},{2,18},{3,7},{4,20},{5,9},{6,22},{7,11},{8,24},{9,13}... | collective-permute-start | bytes 2752520 | tf_op jit(solution)/shard_map/ppermute | solution.py:41
  24.5 13.8 %collective-permute-start.5 = (bf16[256,1792]{1,0:T(8,128)(2,1)S(1)}, bf16[256,1792]{1,0:T(8,128)(2,1)}, u32[]{:S(2)}, u32[]{:S(2)}) collective-permute-start(bf16[256,1792]{1,0:T(8,128)(2,1)S(1)} %pad_maximum_fusion.1.refs_9_), channel_id=1, source_target_pairs={{0,48},{1,13},{2,50},{3,15},{4,52},{5,1},{6,54},{7,3},{8,56},{9,5}... | collective-permute-start | bytes 2752520 | tf_op jit(solution)/shard_map/ppermute | solution.py:41
  26.0 18.4 %collective-permute-start.7 = (bf16[256,1792]{1,0:T(8,128)(2,1)S(1)}, bf16[256,1792]{1,0:T(8,128)(2,1)S(1)}, u32[]{:S(2)}, u32[]{:S(2)}) collective-permute-start(bf16[256,1792]{1,0:T(8,128)(2,1)S(1)} %collective-permute-done.1.refs_0_), channel_id=1, source_target_pairs={{0,1},{1,0},{2,3},{3,2},{4,5},{5,4},{6,7},{7,6},{8,9},{9,8},{10,11... | collective-permute-start | bytes 2752520 | tf_op jit(solution)/shard_map/ppermute | solution.py:41
  26.8 17.7 %collective-permute-start.9 = (bf16[256,1792]{1,0:T(8,128)(2,1)}, bf16[256,1792]{1,0:T(8,128)(2,1)}, u32[]{:S(2)}, u32[]{:S(2)}) collective-permute-start(bf16[256,1792]{1,0:T(8,128)(2,1)} %collective-permute-done.3.refs_2_), channel_id=1, source_target_pairs={{0,1},{1,0},{2,3},{3,2},{4,5},{5,4},{6,7},{7,6},{8,9},{9,8},{10,11... | collective-permute-start | bytes 2752520 | tf_op jit(solution)/shard_map/ppermute | solution.py:41
  37.1 10.1 %collective-permute-start.10 = (bf16[256,1792]{1,0:T(8,128)(2,1)}, bf16[256,1792]{1,0:T(8,128)(2,1)}, u32[]{:S(2)}, u32[]{:S(2)}) collective-permute-start(bf16[256,1792]{1,0:T(8,128)(2,1)} %collective-permute-done.6.refs_3_), channel_id=1, source_target_pairs={{0,1},{1,0},{2,3},{3,2},{4,5},{5,4},{6,7},{7,6},{8,9},{9,8},{10,11... | collective-permute-start | bytes 2752520 | tf_op jit(solution)/shard_map/ppermute | solution.py:41
  38.3 8.9 %collective-permute-start.8 = (bf16[256,1792]{1,0:T(8,128)(2,1)}, bf16[256,1792]{1,0:T(8,128)(2,1)S(1)}, u32[]{:S(2)}, u32[]{:S(2)}) collective-permute-start(bf16[256,1792]{1,0:T(8,128)(2,1)} %collective-permute-done.5.refs_1_), channel_id=1, source_target_pairs={{0,1},{1,0},{2,3},{3,2},{4,5},{5,4},{6,7},{7,6},{8,9},{9,8},{10,11... | collective-permute-start | bytes 2752520 | tf_op jit(solution)/shard_map/ppermute | solution.py:41
  38.5 21.1 %collective-permute-start.20 = (bf16[128,1792]{1,0:T(8,128)(2,1)S(1)}, bf16[128,1792]{1,0:T(8,128)(2,1)S(1)}, u32[]{:S(2)}, u32[]{:S(2)}) collective-permute-start(bf16[128,1792]{1,0:T(8,128)(2,1)S(1)} %slice.43), channel_id=1, source_target_pairs={{0,48},{1,13},{2,50},{3,15},{4,52},{5,1},{6,54},{7,3},{8,56},{9,5}... | collective-permute-start | bytes 1376264 | tf_op jit(solution)/shard_map/ppermute | solution.py:41
  44.5 15.1 %collective-permute-start.21 = (bf16[128,1792]{1,0:T(8,128)(2,1)S(1)}, bf16[128,1792]{1,0:T(8,128)(2,1)S(1)}, u32[]{:S(2)}, u32[]{:S(2)}) collective-permute-start(bf16[128,1792]{1,0:T(8,128)(2,1)S(1)} %slice.44), channel_id=1, source_target_pairs={{0,16},{1,5},{2,18},{3,7},{4,20},{5,9},{6,22},{7,11},{8,24},{9,13}... | collective-permute-start | bytes 1376264 | tf_op jit(solution)/shard_map/ppermute | solution.py:41
  44.6 15.5 %collective-permute-start.22 = (bf16[128,1792]{1,0:T(8,128)(2,1)S(1)}, bf16[128,1792]{1,0:T(8,128)(2,1)S(1)}, u32[]{:S(2)}, u32[]{:S(2)}) collective-permute-start(bf16[128,1792]{1,0:T(8,128)(2,1)S(1)} %slice.45), channel_id=1, source_target_pairs={{0,48},{1,13},{2,50},{3,15},{4,52},{5,1},{6,54},{7,3},{8,56},{9,5}... | collective-permute-start | bytes 1376264 | tf_op jit(solution)/shard_map/ppermute | solution.py:41
  47.2 13.0 %collective-permute-start.23 = (bf16[128,1792]{1,0:T(8,128)(2,1)S(1)}, bf16[128,1792]{1,0:T(8,128)(2,1)S(1)}, u32[]{:S(2)}, u32[]{:S(2)}) collective-permute-start(bf16[128,1792]{1,0:T(8,128)(2,1)S(1)} %slice.46), channel_id=1, source_target_pairs={{0,16},{1,5},{2,18},{3,7},{4,20},{5,9},{6,22},{7,11},{8,24},{9,13}... | collective-permute-start | bytes 1376264 | tf_op jit(solution)/shard_map/ppermute | solution.py:41
  57.9 14.2 %collective-permute-start.11 = (f16[2,896,256]{2,1,0:T(8,128)(2,1)S(1)}, f16[2,896,256]{2,1,0:T(8,128)(2,1)S(1)}, u32[]{:S(2)}, u32[]{:S(2)}) collective-permute-start(f16[2,896,256]{2,1,0:T(8,128)(2,1)S(1)} %fusion), channel_id=1, source_target_pairs={{0,2},{1,67},{2,0},{3,65},{4,6},{5,71},{6,4},{7,69},{8,10},{9,75},... | collective-permute-start | bytes 2752520 | tf_op jit(solution)/shard_map/ppermute | solution.py:41
  60.2 3.2 %collective-permute-start.27 = (bf16[128,1792]{1,0:T(8,128)(2,1)S(1)}, bf16[128,1792]{1,0:T(8,128)(2,1)S(1)}, u32[]{:S(2)}, u32[]{:S(2)}) collective-permute-start(bf16[128,1792]{1,0:T(8,128)(2,1)S(1)} %collective-permute-done.23.refs_3_), channel_id=1, source_target_pairs={{0,1},{1,0},{2,3},{3,2},{4,5},{5,4},{6,7},{7,6},{8,9},{9,8},{10,11... | collective-permute-start | bytes 1376264 | tf_op jit(solution)/shard_map/ppermute | solution.py:41
  69.8 8.0 %collective-permute-start.28 = (f16[2,384,256]{2,1,0:T(8,128)(2,1)S(1)}, f16[2,384,256]{2,1,0:T(8,128)(2,1)S(1)}, u32[]{:S(2)}, u32[]{:S(2)}) collective-permute-start(f16[2,384,256]{2,1,0:T(8,128)(2,1)S(1)} %fusion.3), channel_id=1, source_target_pairs={{0,2},{1,67},{2,0},{3,65},{4,6},{5,71},{6,4},{7,69},{8,10},{9,75},... | collective-permute-start | bytes 1179656 | tf_op jit(solution)/shard_map/ppermute | solution.py:41
  73.8 8.7 %collective-permute-start.12 = (f16[896,256]{1,0:T(8,128)(2,1)S(1)}, f16[896,256]{1,0:T(8,128)(2,1)S(1)}, u32[]{:S(2)}, u32[]{:S(2)}) collective-permute-start(f16[896,256]{1,0:T(8,128)(2,1)S(1)} %fusion.4), channel_id=1, source_target_pairs={{0,66},{1,3},{2,64},{3,1},{4,70},{5,7},{6,68},{7,5},{8,74},{9,11},... | collective-permute-start | bytes 1376264 | tf_op jit(solution)/shard_map/ppermute | solution.py:41
  78.0 9.9 %collective-permute-start.29 = (f16[384,256]{1,0:T(8,128)(2,1)S(1)}, f16[384,256]{1,0:T(8,128)(2,1)S(1)}, u32[]{:S(2)}, u32[]{:S(2)}) collective-permute-start(f16[384,256]{1,0:T(8,128)(2,1)S(1)} %fusion.7), channel_id=1, source_target_pairs={{0,66},{1,3},{2,64},{3,1},{4,70},{5,7},{6,68},{7,5},{8,74},{9,11},... | collective-permute-start | bytes 589832 | tf_op jit(solution)/shard_map/ppermute | solution.py:41
  84.8 24.9 %collective-permute-start.14 = (f32[512,256]{1,0:T(8,128)S(1)}, f32[512,256]{1,0:T(8,128)S(1)}, u32[]{:S(2)}, u32[]{:S(2)}) collective-permute-start(f32[512,256]{1,0:T(8,128)S(1)} %get-tuple-element.18), channel_id=1, source_target_pairs={{0,16},{1,5},{2,80},{3,69},{4,20},{5,9},{6,84},{7,73},{8,24},{9,13... | collective-permute-start | bytes 1572872 | tf_op jit(solution)/shard_map/ppermute | solution.py:41
  88.6 16.6 %collective-permute-start.30 = (f32[256,256]{1,0:T(8,128)S(1)}, f32[256,256]{1,0:T(8,128)S(1)}, u32[]{:S(2)}, u32[]{:S(2)}) collective-permute-start(f32[256,256]{1,0:T(8,128)S(1)} %get-tuple-element.22), channel_id=1, source_target_pairs={{0,12},{1,17},{2,14},{3,19},{4,0},{5,21},{6,2},{7,23},{8,4},{9,25}... | collective-permute-start | bytes 786440 | tf_op jit(solution)/shard_map/ppermute | solution.py:41
  88.6 20.1 %collective-permute-start.32 = (f32[256,256]{1,0:T(8,128)S(1)}, f32[256,256]{1,0:T(8,128)S(1)}, u32[]{:S(2)}, u32[]{:S(2)}) collective-permute-start(f32[256,256]{1,0:T(8,128)S(1)} %get-tuple-element.23), channel_id=1, source_target_pairs={{0,32},{1,9},{2,96},{3,73},{4,36},{5,13},{6,100},{7,77},{8,40},{9,... | collective-permute-start | bytes 786440 | tf_op jit(solution)/shard_map/ppermute | solution.py:41
  90.8 14.3 %collective-permute-start.34 = (f32[128,256]{1,0:T(8,128)S(1)}, f32[128,256]{1,0:T(8,128)S(1)}, u32[]{:S(2)}, u32[]{:S(2)}) collective-permute-start(f32[128,256]{1,0:T(8,128)S(1)} %get-tuple-element.24), channel_id=1, source_target_pairs={{0,8},{1,33},{2,10},{3,35},{4,12},{5,37},{6,14},{7,39},{8,0},{9,41... | collective-permute-start | bytes 393224 | tf_op jit(solution)/shard_map/ppermute | solution.py:41
  105.1 7.2 %collective-permute-start.35 = (f32[128,256]{1,0:T(8,128)S(1)}, f32[128,256]{1,0:T(8,128)S(1)}, u32[]{:S(2)}, u32[]{:S(2)}) collective-permute-start(f32[128,256]{1,0:T(8,128)S(1)} %collective-permute-done.34.refs_12_), channel_id=1, source_target_pairs={{0,1},{1,0},{2,3},{3,2},{4,5},{5,4},{6,7},{7,6},{8,9},{9,8},{10,11... | collective-permute-start | bytes 393224 | tf_op jit(solution)/shard_map/ppermute | solution.py:41
  105.2 7.2 %collective-permute-start.31 = (f32[256,256]{1,0:T(8,128)S(1)}, f32[256,256]{1,0:T(8,128)S(1)}, u32[]{:S(2)}, u32[]{:S(2)}) collective-permute-start(f32[256,256]{1,0:T(8,128)S(1)} %collective-permute-done.30.refs_8_), channel_id=1, source_target_pairs={{0,1},{1,0},{2,3},{3,2},{4,5},{5,4},{6,7},{7,6},{8,9},{9,8},{10,11... | collective-permute-start | bytes 786440 | tf_op jit(solution)/shard_map/ppermute | solution.py:41
  105.6 8.1 %collective-permute-start.16 = (f32[256,256]{1,0:T(8,128)S(1)}, f32[256,256]{1,0:T(8,128)S(1)}, u32[]{:S(2)}, u32[]{:S(2)}) collective-permute-start(f32[256,256]{1,0:T(8,128)S(1)} %get-tuple-element.19), channel_id=1, source_target_pairs={{0,48},{1,13},{2,50},{3,15},{4,52},{5,1},{6,54},{7,3},{8,56},{9,5}... | collective-permute-start | bytes 786440 | tf_op jit(solution)/shard_map/ppermute | solution.py:41
  108.7 5.4 %collective-permute-start.18 = (f32[256,256]{1,0:T(8,128)S(1)}, f32[256,256]{1,0:T(8,128)S(1)}, u32[]{:S(2)}, u32[]{:S(2)}) collective-permute-start(f32[256,256]{1,0:T(8,128)S(1)} %get-tuple-element.20), channel_id=1, source_target_pairs={{0,4},{1,49},{2,6},{3,51},{4,8},{5,53},{6,10},{7,55},{8,12},{9,57}... | collective-permute-start | bytes 786440 | tf_op jit(solution)/shard_map/ppermute | solution.py:41
  109.7 9.9 %collective-permute-start.15 = (f32[512,256]{1,0:T(8,128)S(1)}, f32[512,256]{1,0:T(8,128)S(1)}, u32[]{:S(2)}, u32[]{:S(2)}) collective-permute-start(f32[512,256]{1,0:T(8,128)S(1)} %collective-permute-done.14.refs_2_), channel_id=1, source_target_pairs={{0,1},{1,0},{2,3},{3,2},{4,5},{5,4},{6,7},{7,6},{8,9},{9,8},{10,11... | collective-permute-start | bytes 1572872 | tf_op jit(solution)/shard_map/ppermute | solution.py:41
  112.3 6.1 %collective-permute-start.13 = (f32[384,256]{1,0:T(8,128)S(1)}, f32[384,256]{1,0:T(8,128)S(1)}, u32[]{:S(2)}, u32[]{:S(2)}) collective-permute-start(f32[384,256]{1,0:T(8,128)S(1)} %get-tuple-element.17.refs_0_), channel_id=1, source_target_pairs={{0,1},{1,0},{2,3},{3,2},{4,5},{5,4},{6,7},{7,6},{8,9},{9,8},{10,11... | collective-permute-start | bytes 1179656 | tf_op jit(solution)/shard_map/ppermute | solution.py:41
  112.4 6.1 %collective-permute-start.33 = (f32[256,256]{1,0:T(8,128)S(1)}, f32[256,256]{1,0:T(8,128)S(1)}, u32[]{:S(2)}, u32[]{:S(2)}) collective-permute-start(f32[256,256]{1,0:T(8,128)S(1)} %collective-permute-done.32.refs_10_), channel_id=1, source_target_pairs={{0,1},{1,0},{2,3},{3,2},{4,5},{5,4},{6,7},{7,6},{8,9},{9,8},{10,11... | collective-permute-start | bytes 786440 | tf_op jit(solution)/shard_map/ppermute | solution.py:41
  113.7 4.7 %collective-permute-start.17 = (f32[256,256]{1,0:T(8,128)S(1)}, f32[256,256]{1,0:T(8,128)S(1)}, u32[]{:S(2)}, u32[]{:S(2)}) collective-permute-start(f32[256,256]{1,0:T(8,128)S(1)} %collective-permute-done.16.refs_4_), channel_id=1, source_target_pairs={{0,1},{1,0},{2,3},{3,2},{4,5},{5,4},{6,7},{7,6},{8,9},{9,8},{10,11... | collective-permute-start | bytes 786440 | tf_op jit(solution)/shard_map/ppermute | solution.py:41
  114.2 5.4 %collective-permute-start.19 = (f32[256,256]{1,0:T(8,128)S(1)}, f32[256,256]{1,0:T(8,128)S(1)}, u32[]{:S(2)}, u32[]{:S(2)}) collective-permute-start(f32[256,256]{1,0:T(8,128)S(1)} %collective-permute-done.18.refs_6_), channel_id=1, source_target_pairs={{0,1},{1,0},{2,3},{3,2},{4,5},{5,4},{6,7},{7,6},{8,9},{9,8},{10,11... | collective-permute-start | bytes 786440 | tf_op jit(solution)/shard_map/ppermute | solution.py:41
  (7 other events, 49.4 us)

commit v3 on v2

v3 whole, which is shorter than its diff:
```python
import functools

import jax
import jax.numpy as jnp
import numpy as np
from jax import lax
from jax.experimental import pallas as pl
from jax.experimental.pallas import tpu as pltpu
from jax.sharding import PartitionSpec as P


AXES = ("rows", "cols")
SIZES = (2, 4, 4, 2, 2)
ALONG = {"s": (0, 0), "a1": (1, 0), "a2": (2, 0), "a3": (3, 0), "b1": (0, 1), "b2": (0, 2), "b3": (0, 3)}
ROWS = 64.0 * 2.0 ** (np.arange(1024) * 0.6180339887 % 1 / 2)
COLUMNS = 2.0 ** (np.arange(256) * 0.7548776662 % 1 / 2)
FIRST = (
    ("a1", "s", ("right", "left"), False),
    ("a1", "a3", ("right",), False),
    ("s", "s", ("right",), True),
    ("a1", "b1", ("right", "left"), False),
)
SECOND = (("a2", "b3", ("right", "left"), False), ("a2", "b2", ("left",), True))
VMEM = pl.BlockSpec(memory_space=pltpu.VMEM)
SMEM = pl.BlockSpec(memory_space=pltpu.SMEM)


def offset(name, core):
    dx, dy = ALONG[name]
    return (dx, dy) if core == 0 else (-dy % 4, dx)


def gap(name, start, core):
    return tuple((a - b) % 4 for a, b in zip(offset(name, core), offset(start, core)))


def send(value, move):
    pairs = []
    for source in range(int(np.prod(SIZES))):
        place = [int(i) for i in np.unravel_index(source, SIZES)]
        pairs.append((source, int(np.ravel_multi_index(move(*place), SIZES))))
    return lax.ppermute(value, AXES, pairs)


def to_place(name, swap=False):
    def move(zh, x, y, zl, core):
        dx, dy = offset(name, core)
        if swap:
            zh, zl = zl, zh
        return zh, (x + dx) % 4, (y + dy) % 4, zl, core

    return move


def other_core(zh, x, y, zl, core):
    return zh, x, y, zl, 1 - core


def other_high(zh, x, y, zl, core):
    return 1 - zh, x, y, zl, core


def first_partner(zh, x, y, zl, core):
    return (zh, x, y, 1 - zl, core) if core == 0 else (1 - zh, x, y, 1 - zl, core)


def second_partner(zh, x, y, zl, core):
    return first_partner(zh, x, y, zl, 1 - core)[:4] + (core,)


def after(value, *others):
    return lax.optimization_barrier((value, *others))[0]


def packed(value):
    rows, columns = np.float32(ROWS[: value.shape[-2], None]), np.float32(COLUMNS)
    return (value * rows * columns).astype(jnp.float16)


def unpacked(value):
    rows, columns = np.float32(1 / ROWS[: value.shape[-2], None]), np.float32(1 / COLUMNS)
    return value.astype(jnp.float32) * rows * columns


def call(kernel, outs, place, *args, keep=True, cost=2**21):
    return pl.pallas_call(
        kernel,
        out_shape=[pltpu.VMEM(s, jnp.float32) if keep else jax.ShapeDtypeStruct(s, jnp.float32) for s in outs],
        in_specs=[SMEM] + [VMEM] * len(args),
        out_specs=[VMEM] * len(outs),
        compiler_params=pltpu.CompilerParams(vmem_limit_bytes=8 * 2**20),
        cost_estimate=pl.CostEstimate(flops=0, bytes_accessed=cost, transcendentals=0),
    )(place, *[pltpu.with_memory_space_constraint(a, pltpu.VMEM) for a in args])


def spans(pairs):
    at, out = 0, []
    for *_, halved in pairs:
        out.append((at, 128 if halved else 256))
        at += out[-1][1]
    return out, at


def multiply(pairs, names, place, *refs):
    held = {name: refs[2 * i : 2 * i + 2] for i, name in enumerate(names)}
    out = refs[-1]
    core = place[3]
    straight = jnp.where(place[0] == place[2], 1, 0)

    def pair(left, right, halved, at):
        for kind in (0, 1):
            ends = straight if kind == 0 else 1 - straight
            size = 128 if halved else 256
            lhs = held[left][kind][pl.ds(pl.multiple_of(core * 128, 128), 128), :] if halved else held[left][kind][...]
            for col in (0, 1):
                slot = jnp.where(ends == 1, 1 if col else 2, jnp.where(core == col, 0, 3))
                out[slot, pl.ds(at, size)] = lax.dot_general(
                    lhs, held[right][col][...], (((1,), (1,)), ((), ())), preferred_element_type=jnp.float32
                )

    for (left, right, _, halved), (at, _) in zip(pairs, spans(pairs)[0], strict=True):
        if right in ("b1", "b3"):
            pl.when(core == 0)(functools.partial(pair, left, right, halved, at))
            pl.when(core == 1)(functools.partial(pair, left, {"b1": "b3", "b3": "b1"}[right], halved, at))
        else:
            pair(left, right, halved, at)


def finish(groups, place, stay, got, late, *outs):
    for parts, out in zip(groups, outs, strict=True):
        to = 0
        for at, size in parts:
            take = pl.ds(at, size)
            out[pl.ds(to, size)] = stay[2, take] + got[0, take] + late[take]
            to += size


def products(place, blocks, pairs):
    names = {name for pair in pairs for name in pair[:2]}
    names = sorted(names | {"b1", "b3"})
    return call(
        functools.partial(multiply, pairs, names),
        [(4, spans(pairs)[1], 256)],
        place,
        *[rows for name in names for rows in blocks[name]],
        cost=2**24,
    )[0]


def delivered(place, stay, got, late, pairs):
    where = spans(pairs)[0]
    messages = {}
    for (left, right, keepers, halved), span in zip(pairs, where, strict=True):
        for keeper in keepers:
            to, rows = (right, left) if keeper == "right" else (left, right)
            messages.setdefault((to, keeper == "left"), []).append((span, halved, [gap(rows, to, c) for c in (0, 1)]))
    groups = [[span for span, _, _ in parts] for parts in messages.values()]
    outs = call(
        functools.partial(finish, groups),
        [(sum(size for _, size in g), 256) for g in groups],
        place,
        stay,
        got,
        late,
    )
    tiles = []
    for ((to, turned), parts), out in zip(messages.items(), outs, strict=True):
        if turned:
            out = packed(out)
        if to != "s":
            out = send(out, to_place(to, turned))
        far = send(out, other_core)
        if turned:
            out, far = unpacked(out), unpacked(far)
        tiles.append(([(turned, halved, gaps) for _, halved, gaps in parts], out, far))
    return tiles, outs


def update(layouts, place, old, *refs):
    new = refs[-1]
    core = place[3]
    for parts, mine, far in zip(layouts, refs[:-1:2], refs[1:-1:2], strict=True):
        for source, tiles in ((core, mine), (1 - core, far)):
            at = 0
            for turned, halved, gaps in parts:
                size = 128 if halved else 256
                dx = jnp.where(source == 0, gaps[0][0], gaps[1][0])
                dy = jnp.where(source == 0, gaps[0][1], gaps[1][1])
                x, y = (place[1] + dx) & 3, (place[4] + dy) & 3

                @pl.when((x >> 1) == core)
                def _():
                    tile = tiles[pl.ds(at, size)]
                    half = pl.multiple_of(source * 128, 128)
                    to = pl.multiple_of(((x & 1) * 4 + y) * 256, 256)
                    if turned:
                        tile = tile.T
                        to = pl.ds(to, 256), pl.ds(half, 128) if halved else slice(None)
                    else:
                        to = pl.ds(to + half, 128) if halved else pl.ds(to, 256), slice(None)
                    new[to] = 0.9 * old[to] + 0.1 * tile

                at += size


def body(gradient, stat_old):
    device = lax.axis_index("rows").astype(jnp.int32)
    column = lax.axis_index("cols").astype(jnp.int32)
    zh, x, y = device >> 4, (device >> 2) & 3, device & 3
    zl, core = column >> 1, column & 1
    place = jnp.stack([zh, x, zl, core, y])

    def whole(rows, *others):
        far = after(send(rows, other_core), *others)
        first = jnp.where(core == 0, rows, far)
        return jnp.concatenate([first, jnp.where(core == 0, far, rows)], axis=1)

    keep = lax.dynamic_slice_in_dim(gradient, zh * 896, 896, 1)
    give = lax.dynamic_slice_in_dim(gradient, (1 - zh) * 896, 896, 1)
    given = send(give, other_high)
    own = {"s": whole(keep)}
    own["a1"], own["a3"] = send(own["s"], to_place("a3")), send(own["s"], to_place("a1"))
    own["b1"], own["b3"] = send(own["a1"], other_core), send(own["a3"], other_core)
    other = {"s": whole(given, own["a1"], own["a3"])}
    other["a1"], other["a3"] = send(other["s"], to_place("a3")), send(other["s"], to_place("a1"))
    own["a2"] = send(after(own["a1"], other["a1"], own["b1"]), to_place("a3"))
    other["a2"] = send(after(other["a3"], own["b3"]), to_place("a1"))
    other["b1"], other["b3"] = send(other["a1"], other_core), send(other["a3"], other_core)
    blocks = {name: (own[name], other[name]) for name in own}

    stay1 = products(place, blocks, FIRST)
    leave1 = packed(stay1[:2])
    blocks["a2"] = after(blocks["a2"], leave1)
    blocks["b2"] = tuple(send(rows, other_core) for rows in blocks["a2"])
    stay2 = products(place, blocks, SECOND)
    leave2 = packed(stay2[:2])
    got1 = unpacked(after(send(leave1, first_partner), leave2))
    late1 = packed(stay1[3] + got1[1])
    got2 = unpacked(after(send(leave2, first_partner), late1))
    late2 = packed(stay2[3] + got2[1])
    late1 = unpacked(after(send(late1, second_partner), late2))
    tiles1, outs = delivered(place, stay1, got1, late1, FIRST)
    late2 = unpacked(after(send(late2, second_partner), *outs))
    tiles2, _ = delivered(place, stay2, got2, late2, SECOND)
    tiles = tiles1 + tiles2
    (new,) = call(
        functools.partial(update, [layout for layout, _, _ in tiles]),
        [stat_old.shape],
        place,
        stat_old,
        *[part for _, mine, far in tiles for part in (mine, far)],
        keep=False,
    )
    return new


def solution(mesh):
    placed = (P("rows", "cols"), P("cols", "rows"))
    return jax.shard_map(
        body, mesh=mesh, in_specs=placed, out_specs=P("cols", "rows"), check_vma=False
    )
```

time: 124 us -> 102 us (0.82)
  starting transfers between devices: 47.7 us -> 34.1 us
  Pallas kernels: 20.7 us -> 14.8 us
  other arithmetic: 5.12 us -> 2.35 us
  local copies, waits for them, and re-layouts: 4.51 us -> 5.84 us
  waiting for transfers between devices: 45 us -> 43.7 us
    ppermute x36 -> x30, starting transfers between devices: 47.7 us -> 34.1 us  [send(): return lax.ppermute(value, AXES, pairs)]
    pallas_call x5, Pallas kernels: 20.7 us -> 14.8 us  [call(): pl.pallas_call(kernel, out_shape=[pltpu.VMEM(s, jnp.float32) if keep else...]
    unnamed x6 -> x30, local copies, waits for them, and re-layouts: 0.02 us -> 4.52 us
    convert_element_type x4 -> x6, other arithmetic: 4.45 us -> 1.03 us  [packed(): return (value * rows * columns).astype(jnp.float16)]
    slice x4 -> x0, local copies, waits for them, and re-layouts: 3.18 us -> none  [the longest x2 2.1 us: body(): kind['a3'][128:]]
    ppermute x36 -> x30, waiting for transfers between devices: 45 us -> 43.7 us  [send(): return lax.ppermute(value, AXES, pairs)]
  transfers between devices with their start and end apart: 36 -> 30, of which waited for: 15 -> 19; matrix products, arithmetic and copies ran while one was open for 7% -> 2% of each run, Pallas kernels for 14% -> 11%
where the time goes in v3:
time: 102 us; the launch traced here: 101 us
  waiting for transfers between devices  43.7 us (43%)
  starting transfers between devices  34.1 us (33%)
  Pallas kernels  14.8 us (15%)
  local copies, waits for them, and re-layouts  5.84 us (6%)
  other arithmetic  2.35 us (2%)
    ppermute x30, waiting for transfers between devices, send(): return lax.ppermute(value, AXES, pairs)  43.7 us
    ppermute x30, starting transfers between devices, send(): return lax.ppermute(value, AXES, pairs)  34.1 us
    pallas_call x5, Pallas kernels, call(): pl.pallas_call(kernel, out_shape=[pltpu.VMEM(s, jnp.float32) if keep else...  14.8 us
    unnamed x30, local copies, waits for them, and re-layouts  4.52 us
  transfers between devices with their start and end apart: 30, of which 19 were waited for; matrix products, arithmetic and copies ran while one was open for 2% of the time, Pallas kernels for 11%

profile of v3, /device:TPU:33, one launch (start us, length us, event | category | flops | bytes accessed | tf_op | source)
XLA Modules:
  0.0 101.0 jit_solution(2048770951843956911)
XLA Ops:
  0.0 1.2 %constant_dynamic-slice_fusion = (bf16[256,896]{1,0:T(8,128)(2,1)S(1)}, bf16[256,896]{1,0:T(8,128)(2,1)S(1)}) fusion(bf16[256,1792]{1,0:T(8,128)(2,1)} %param.30, s32[]{:T(128)S(6)} %select_n.30, s32[]{:T(128)S(6)} %select_n.27), kind=kLoop, calls=%fused_computation.32 | loop fusion | bytes 1835016 | tf_op jit(solution)/shard_map/dynamic_slice | solution.py:219
  2.0 2.7 %collective-permute-start.2 = (bf16[256,896]{1,0:T(8,128)(2,1)S(1)}, bf16[256,896]{1,0:T(8,128)(2,1)S(1)}, u32[]{:S(2)}, u32[]{:S(2)}) collective-permute-start(bf16[256,896]{1,0:T(8,128)(2,1)S(1)} %get-tuple-element.37), channel_id=1, source_target_pairs={{0,64},{1,65},{2,66},{3,67},{4,68},{5,69},{6,70},{7,71},{8,72},{9,... | collective-permute-start | bytes 1376264 | tf_op jit(solution)/shard_map/ppermute | solution.py:42
  4.9 2.8 %collective-permute-start.1 = (bf16[256,1792]{1,0:T(8,128)(2,1)S(1)}, bf16[256,1792]{1,0:T(8,128)(2,1)}, u32[]{:S(2)}, u32[]{:S(2)}) collective-permute-start(bf16[256,1792]{1,0:T(8,128)(2,1)S(1)} %pad_maximum_fusion.refs_8_), channel_id=1, source_target_pairs={{0,48},{1,13},{2,50},{3,15},{4,52},{5,1},{6,54},{7,3},{8,56},{9,5}... | collective-permute-start | bytes 2752520 | tf_op jit(solution)/shard_map/ppermute | solution.py:42
  7.7 7.9 %collective-permute-done.2 = bf16[256,896]{1,0:T(8,128)(2,1)S(1)} collective-permute-done((bf16[256,896]{1,0:T(8,128)(2,1)S(1)}, bf16[256,896]{1,0:T(8,128)(2,1)S(1)}, u32[]{:S(2)}, u32[]{:S(2)}) %collective-permute-start.2) | collective-permute-done | bytes 458784 | tf_op jit(solution)/shard_map/ppermute | solution.py:42
  16.4 1.4 %collective-permute-done.3 = bf16[256,896]{1,0:T(8,128)(2,1)S(1)} collective-permute-done((bf16[256,896]{1,0:T(8,128)(2,1)S(1)}, bf16[256,896]{1,0:T(8,128)(2,1)S(1)}, u32[]{:S(2)}, u32[]{:S(2)}) %collective-permute-start.3) | collective-permute-done | bytes 458784 | tf_op jit(solution)/shard_map/ppermute | solution.py:42
  18.0 3.4 %collective-permute-done.4.refs_2_ = bf16[256,1792]{1,0:T(8,128)(2,1)S(1)} collective-permute-done((bf16[256,1792]{1,0:T(8,128)(2,1)S(1)}, bf16[256,1792]{1,0:T(8,128)(2,1)S(1)}, u32[]{:S(2)}, u32[]{:S(2)}) %collective-permute-start.4) | collective-permute-done | bytes 917536 | tf_op jit(solution)/shard_map/ppermute | solution.py:42
  21.7 1.5 %collective-permute-start.6 = (bf16[256,1792]{1,0:T(8,128)(2,1)S(1)}, bf16[256,1792]{1,0:T(8,128)(2,1)}, u32[]{:S(2)}, u32[]{:S(2)}) collective-permute-start(bf16[256,1792]{1,0:T(8,128)(2,1)S(1)} %pad_maximum_fusion.1.refs_9_), channel_id=1, source_target_pairs={{0,16},{1,5},{2,18},{3,7},{4,20},{5,9},{6,22},{7,11},{8,24},{9,13}... | collective-permute-start | bytes 2752520 | tf_op jit(solution)/shard_map/ppermute | solution.py:42
  24.1 1.8 %collective-permute-start.7 = (bf16[256,1792]{1,0:T(8,128)(2,1)}, bf16[256,1792]{1,0:T(8,128)(2,1)S(1)}, u32[]{:S(2)}, u32[]{:S(2)}) collective-permute-start(bf16[256,1792]{1,0:T(8,128)(2,1)} %collective-permute-done.1.refs_0_), channel_id=1, source_target_pairs={{0,1},{1,0},{2,3},{3,2},{4,5},{5,4},{6,7},{7,6},{8,9},{9,8},{10,11... | collective-permute-start | bytes 2752520 | tf_op jit(solution)/shard_map/ppermute | solution.py:42
  25.9 8.4 %collective-permute-done.5.refs_1_ = bf16[256,1792]{1,0:T(8,128)(2,1)} collective-permute-done((bf16[256,1792]{1,0:T(8,128)(2,1)S(1)}, bf16[256,1792]{1,0:T(8,128)(2,1)}, u32[]{:S(2)}, u32[]{:S(2)}) %collective-permute-start.5) | collective-permute-done | bytes 917536 | tf_op jit(solution)/shard_map/ppermute | solution.py:42
  34.3 2.1 %collective-permute-start.8 = (bf16[256,1792]{1,0:T(8,128)(2,1)}, bf16[256,1792]{1,0:T(8,128)(2,1)S(1)}, u32[]{:S(2)}, u32[]{:S(2)}) collective-permute-start(bf16[256,1792]{1,0:T(8,128)(2,1)} %collective-permute-done.5.refs_1_), channel_id=1, source_target_pairs={{0,1},{1,0},{2,3},{3,2},{4,5},{5,4},{6,7},{7,6},{8,9},{9,8},{10,11... | collective-permute-start | bytes 2752520 | tf_op jit(solution)/shard_map/ppermute | solution.py:42
  36.4 1.3 %collective-permute-start.10 = (bf16[256,1792]{1,0:T(8,128)(2,1)}, bf16[256,1792]{1,0:T(8,128)(2,1)}, u32[]{:S(2)}, u32[]{:S(2)}) collective-permute-start(bf16[256,1792]{1,0:T(8,128)(2,1)} %collective-permute-done.6.refs_3_), channel_id=1, source_target_pairs={{0,1},{1,0},{2,3},{3,2},{4,5},{5,4},{6,7},{7,6},{8,9},{9,8},{10,11... | collective-permute-start | bytes 2752520 | tf_op jit(solution)/shard_map/ppermute | solution.py:42
  37.8 2.7 %collective-permute-start.12 = (bf16[256,1792]{1,0:T(8,128)(2,1)}, bf16[256,1792]{1,0:T(8,128)(2,1)}, u32[]{:S(2)}, u32[]{:S(2)}) collective-permute-start(bf16[256,1792]{1,0:T(8,128)(2,1)} %collective-permute-done.1.refs_0_), channel_id=1, source_target_pairs={{0,48},{1,13},{2,50},{3,15},{4,52},{5,1},{6,54},{7,3},{8,56},{9,5}... | collective-permute-start | bytes 2752520 | tf_op jit(solution)/shard_map/ppermute | solution.py:42
  41.8 1.2 %copy-done.3 = bf16[256,1792]{1,0:T(8,128)(2,1)S(1)} copy-done((bf16[256,1792]{1,0:T(8,128)(2,1)S(1)}, bf16[256,1792]{1,0:T(8,128)(2,1)}, u32[]{:S(2)}) %copy-start.3) | copy-done | bytes 917528
  44.1 6.4 %shard_map.280.stay = f32[4,896,256]{2,1,0:T(8,128)S(1)} custom-call(s32[5]{0:T(128)S(1)} %stack.23.place, bf16[256,1792]{1,0:T(8,128)(2,1)} %collective-permute-done.1.refs_0_, bf16[256,1792]{1,0:T(8,128)(2,1)} %collective-permute-done.5.refs_1_, bf16[256,1792]{1,0:T(8,128)(2,1)S(1)} %copy-done.6, bf16[256,1792]{1,0:T(8,128)(2,1)} %collective-permute-done.6.refs_3_, ...), custom_call_target="tpu_custom_call" | custom-call | bytes 16777216 | tf_op jit(solution)/shard_map/pallas_call | solution.py:86
  51.1 3.1 %collective-permute-done.13.refs_1_ = bf16[256,1792]{1,0:T(8,128)(2,1)} collective-permute-done((bf16[256,1792]{1,0:T(8,128)(2,1)}, bf16[256,1792]{1,0:T(8,128)(2,1)}, u32[]{:S(2)}, u32[]{:S(2)}) %collective-permute-start.13) | collective-permute-done | bytes 917536 | tf_op jit(solution)/shard_map/ppermute | solution.py:42
  55.2 1.8 %collective-permute-done.14.refs_4_ = bf16[256,1792]{1,0:T(8,128)(2,1)S(1)} collective-permute-done((bf16[256,1792]{1,0:T(8,128)(2,1)}, bf16[256,1792]{1,0:T(8,128)(2,1)S(1)}, u32[]{:S(2)}, u32[]{:S(2)}) %collective-permute-start.14) | collective-permute-done | bytes 917536 | tf_op jit(solution)/shard_map/ppermute | solution.py:42
  56.9 1.3 %collective-permute-done.15.refs_5_ = bf16[256,1792]{1,0:T(8,128)(2,1)S(1)} collective-permute-done((bf16[256,1792]{1,0:T(8,128)(2,1)}, bf16[256,1792]{1,0:T(8,128)(2,1)S(1)}, u32[]{:S(2)}, u32[]{:S(2)}) %collective-permute-start.15) | collective-permute-done | bytes 917536 | tf_op jit(solution)/shard_map/ppermute | solution.py:42
  58.3 4.2 %shard_map.281.stay = f32[4,384,256]{2,1,0:T(8,128)S(1)} custom-call(s32[5]{0:T(128)S(1)} %stack.23.place, bf16[256,1792]{1,0:T(8,128)(2,1)} %collective-permute-done.12.refs_0_, bf16[256,1792]{1,0:T(8,128)(2,1)} %collective-permute-done.13.refs_1_, bf16[256,1792]{1,0:T(8,128)(2,1)S(1)} %collective-permute-done.7.refs_4_.refs_2_, ...), custom_call_target="tpu_custom_call" | custom-call | bytes 16777216 | tf_op jit(solution)/shard_map/pallas_call | solution.py:86
  63.3 4.0 %collective-permute-done.11 = f16[2,896,256]{2,1,0:T(8,128)(2,1)S(1)} collective-permute-done((f16[2,896,256]{2,1,0:T(8,128)(2,1)S(1)}, f16[2,896,256]{2,1,0:T(8,128)(2,1)S(1)}, u32[]{:S(2)}, u32[]{:S(2)}) %collective-permute-start.11) | collective-permute-done | bytes 917536 | tf_op jit(solution)/shard_map/ppermute | solution.py:42
  67.8 1.7 %collective-permute-start.16 = (f16[896,256]{1,0:T(8,128)(2,1)S(1)}, f16[896,256]{1,0:T(8,128)(2,1)S(1)}, u32[]{:S(2)}, u32[]{:S(2)}) collective-permute-start(f16[896,256]{1,0:T(8,128)(2,1)S(1)} %fusion.5), channel_id=1, source_target_pairs={{0,66},{1,3},{2,64},{3,1},{4,70},{5,7},{6,68},{7,5},{8,74},{9,11},... | collective-permute-start | bytes 1376264 | tf_op jit(solution)/shard_map/ppermute | solution.py:42
  69.5 2.0 %collective-permute-done.17 = f16[2,384,256]{2,1,0:T(8,128)(2,1)S(1)} collective-permute-done((f16[2,384,256]{2,1,0:T(8,128)(2,1)S(1)}, f16[2,384,256]{2,1,0:T(8,128)(2,1)S(1)}, u32[]{:S(2)}, u32[]{:S(2)}) %collective-permute-start.17) | collective-permute-done | bytes 393248 | tf_op jit(solution)/shard_map/ppermute | solution.py:42
  71.8 1.7 %collective-permute-start.25 = (f16[384,256]{1,0:T(8,128)(2,1)S(1)}, f16[384,256]{1,0:T(8,128)(2,1)S(1)}, u32[]{:S(2)}, u32[]{:S(2)}) collective-permute-start(f16[384,256]{1,0:T(8,128)(2,1)S(1)} %fusion.11), channel_id=1, source_target_pairs={{0,66},{1,3},{2,64},{3,1},{4,70},{5,7},{6,68},{7,5},{8,74},{9,11},... | collective-permute-start | bytes 589832 | tf_op jit(solution)/shard_map/ppermute | solution.py:42
  73.5 3.3 %collective-permute-done.16 = f16[896,256]{1,0:T(8,128)(2,1)S(1)} collective-permute-done((f16[896,256]{1,0:T(8,128)(2,1)S(1)}, f16[896,256]{1,0:T(8,128)(2,1)S(1)}, u32[]{:S(2)}, u32[]{:S(2)}) %collective-permute-start.16) | collective-permute-done | bytes 458784 | tf_op jit(solution)/shard_map/ppermute | solution.py:42
  77.8 1.2 %collective-permute-done.25 = f16[384,256]{1,0:T(8,128)(2,1)S(1)} collective-permute-done((f16[384,256]{1,0:T(8,128)(2,1)S(1)}, f16[384,256]{1,0:T(8,128)(2,1)S(1)}, u32[]{:S(2)}, u32[]{:S(2)}) %collective-permute-start.25) | collective-permute-done | bytes 196640 | tf_op jit(solution)/shard_map/ppermute | solution.py:42
  79.9 2.0 %collective-permute-start.28 = (f16[384,256]{1,0:T(8,128)(2,1)S(1)}, f16[384,256]{1,0:T(8,128)(2,1)S(1)}, u32[]{:S(2)}, u32[]{:S(2)}) collective-permute-start(f16[384,256]{1,0:T(8,128)(2,1)S(1)} %multiply_convert_fusion.1), channel_id=1, source_target_pairs={{0,32},{1,9},{2,96},{3,73},{4,36},{5,13},{6,100},{7,77},{8,40},{9,... | collective-permute-start | bytes 589832 | tf_op jit(solution)/shard_map/ppermute | solution.py:42
  82.1 1.3 %collective-permute-start.19 = (f16[512,256]{1,0:T(8,128)(2,1)S(1)}, f16[512,256]{1,0:T(8,128)(2,1)S(1)}, u32[]{:S(2)}, u32[]{:S(2)}) collective-permute-start(f16[512,256]{1,0:T(8,128)(2,1)S(1)} %multiply_convert_fusion), channel_id=1, source_target_pairs={{0,16},{1,5},{2,80},{3,69},{4,20},{5,9},{6,84},{7,73},{8,24},{9,13... | collective-permute-start | bytes 786440 | tf_op jit(solution)/shard_map/ppermute | solution.py:42
  83.3 2.3 %collective-permute-start.21 = (f32[256,256]{1,0:T(8,128)S(1)}, f32[256,256]{1,0:T(8,128)S(1)}, u32[]{:S(2)}, u32[]{:S(2)}) collective-permute-start(f32[256,256]{1,0:T(8,128)S(1)} %get-tuple-element.30), channel_id=1, source_target_pairs={{0,48},{1,13},{2,50},{3,15},{4,52},{5,1},{6,54},{7,3},{8,56},{9,5}... | collective-permute-start | bytes 786440 | tf_op jit(solution)/shard_map/ppermute | solution.py:42
  85.6 1.5 %collective-permute-start.26 = (f32[256,256]{1,0:T(8,128)S(1)}, f32[256,256]{1,0:T(8,128)S(1)}, u32[]{:S(2)}, u32[]{:S(2)}) collective-permute-start(f32[256,256]{1,0:T(8,128)S(1)} %get-tuple-element.33), channel_id=1, source_target_pairs={{0,12},{1,17},{2,14},{3,19},{4,0},{5,21},{6,2},{7,23},{8,4},{9,25}... | collective-permute-start | bytes 786440 | tf_op jit(solution)/shard_map/ppermute | solution.py:42
  88.1 2.8 %collective-permute-start.29 = (f16[384,256]{1,0:T(8,128)(2,1)S(1)}, f16[384,256]{1,0:T(8,128)(2,1)S(1)}, u32[]{:S(2)}, u32[]{:S(2)}) collective-permute-start(f16[384,256]{1,0:T(8,128)(2,1)S(1)} %collective-permute-done.28), channel_id=1, source_target_pairs={{0,1},{1,0},{2,3},{3,2},{4,5},{5,4},{6,7},{7,6},{8,9},{9,8},{10,11... | collective-permute-start | bytes 589832 | tf_op jit(solution)/shard_map/ppermute | solution.py:42
  90.8 2.8 %collective-permute-done.19 = f16[512,256]{1,0:T(8,128)(2,1)S(1)} collective-permute-done((f16[512,256]{1,0:T(8,128)(2,1)S(1)}, f16[512,256]{1,0:T(8,128)(2,1)S(1)}, u32[]{:S(2)}, u32[]{:S(2)}) %collective-permute-start.19) | collective-permute-done | bytes 262176 | tf_op jit(solution)/shard_map/ppermute | solution.py:42
  93.7 1.7 %collective-permute-start.20 = (f16[512,256]{1,0:T(8,128)(2,1)S(1)}, f16[512,256]{1,0:T(8,128)(2,1)S(1)}, u32[]{:S(2)}, u32[]{:S(2)}) collective-permute-start(f16[512,256]{1,0:T(8,128)(2,1)S(1)} %collective-permute-done.19), channel_id=1, source_target_pairs={{0,1},{1,0},{2,3},{3,2},{4,5},{5,4},{6,7},{7,6},{8,9},{9,8},{10,11... | collective-permute-start | bytes 786440 | tf_op jit(solution)/shard_map/ppermute | solution.py:42
  98.2 2.8 %shard_map.284 = f32[2048,256]{1,0:T(8,128)} custom-call(s32[5]{0:T(128)S(1)} %stack.23.place, f32[2048,256]{1,0:T(8,128)S(1)} %copy-done.4, f32[384,256]{1,0:T(8,128)S(1)} %get-tuple-element.28.refs_0_, f32[384,256]{1,0:T(8,128)S(1)} %collective-permute-done.18.refs_1_, f32[512,256]{1,0:T(8,128)S(1)} %get-tuple-element.44.refs_2_, ...), custom_call_target="tpu_custom_call" | custom-call | bytes 2097152 | tf_op jit(solution)/shard_map/pallas_call | solution.py:86
  (81 shorter events, 14.3 us)
Async XLA Ops:
  1.2 3.5 %collective-permute-start = (bf16[256,896]{1,0:T(8,128)(2,1)S(1)}, bf16[256,896]{1,0:T(8,128)(2,1)S(1)}, u32[]{:S(2)}, u32[]{:S(2)}) collective-permute-start(bf16[256,896]{1,0:T(8,128)(2,1)S(1)} %get-tuple-element.38), channel_id=1, source_target_pairs={{0,1},{1,0},{2,3},{3,2},{4,5},{5,4},{6,7},{7,6},{8,9},{9,8},{10,11... | collective-permute-start | bytes 1376264 | tf_op jit(solution)/shard_map/ppermute | solution.py:42
  2.0 13.6 %collective-permute-start.2 = (bf16[256,896]{1,0:T(8,128)(2,1)S(1)}, bf16[256,896]{1,0:T(8,128)(2,1)S(1)}, u32[]{:S(2)}, u32[]{:S(2)}) collective-permute-start(bf16[256,896]{1,0:T(8,128)(2,1)S(1)} %get-tuple-element.37), channel_id=1, source_target_pairs={{0,64},{1,65},{2,66},{3,67},{4,68},{5,69},{6,70},{7,71},{8,72},{9,... | collective-permute-start | bytes 1376264 | tf_op jit(solution)/shard_map/ppermute | solution.py:42
  4.9 13.1 %collective-permute-start.1 = (bf16[256,1792]{1,0:T(8,128)(2,1)S(1)}, bf16[256,1792]{1,0:T(8,128)(2,1)}, u32[]{:S(2)}, u32[]{:S(2)}) collective-permute-start(bf16[256,1792]{1,0:T(8,128)(2,1)S(1)} %pad_maximum_fusion.refs_8_), channel_id=1, source_target_pairs={{0,48},{1,13},{2,50},{3,15},{4,52},{5,1},{6,54},{7,3},{8,56},{9,5}... | collective-permute-start | bytes 2752520 | tf_op jit(solution)/shard_map/ppermute | solution.py:42
  7.7 13.8 %collective-permute-start.4 = (bf16[256,1792]{1,0:T(8,128)(2,1)S(1)}, bf16[256,1792]{1,0:T(8,128)(2,1)S(1)}, u32[]{:S(2)}, u32[]{:S(2)}) collective-permute-start(bf16[256,1792]{1,0:T(8,128)(2,1)S(1)} %pad_maximum_fusion.refs_8_), channel_id=1, source_target_pairs={{0,16},{1,5},{2,18},{3,7},{4,20},{5,9},{6,22},{7,11},{8,24},{9,13}... | collective-permute-start | bytes 2752520 | tf_op jit(solution)/shard_map/ppermute | solution.py:42
  15.6 2.3 %collective-permute-start.3 = (bf16[256,896]{1,0:T(8,128)(2,1)S(1)}, bf16[256,896]{1,0:T(8,128)(2,1)S(1)}, u32[]{:S(2)}, u32[]{:S(2)}) collective-permute-start(bf16[256,896]{1,0:T(8,128)(2,1)S(1)} %collective-permute-done.2), channel_id=1, source_target_pairs={{0,1},{1,0},{2,3},{3,2},{4,5},{5,4},{6,7},{7,6},{8,9},{9,8},{10,11... | collective-permute-start | bytes 1376264 | tf_op jit(solution)/shard_map/ppermute | solution.py:42
  21.6 12.7 %collective-permute-start.5 = (bf16[256,1792]{1,0:T(8,128)(2,1)S(1)}, bf16[256,1792]{1,0:T(8,128)(2,1)}, u32[]{:S(2)}, u32[]{:S(2)}) collective-permute-start(bf16[256,1792]{1,0:T(8,128)(2,1)S(1)} %pad_maximum_fusion.1.refs_9_), channel_id=1, source_target_pairs={{0,48},{1,13},{2,50},{3,15},{4,52},{5,1},{6,54},{7,3},{8,56},{9,5}... | collective-permute-start | bytes 2752520 | tf_op jit(solution)/shard_map/ppermute | solution.py:42
  21.7 14.7 %collective-permute-start.6 = (bf16[256,1792]{1,0:T(8,128)(2,1)S(1)}, bf16[256,1792]{1,0:T(8,128)(2,1)}, u32[]{:S(2)}, u32[]{:S(2)}) collective-permute-start(bf16[256,1792]{1,0:T(8,128)(2,1)S(1)} %pad_maximum_fusion.1.refs_9_), channel_id=1, source_target_pairs={{0,16},{1,5},{2,18},{3,7},{4,20},{5,9},{6,22},{7,11},{8,24},{9,13}... | collective-permute-start | bytes 2752520 | tf_op jit(solution)/shard_map/ppermute | solution.py:42
  24.1 13.7 %collective-permute-start.7 = (bf16[256,1792]{1,0:T(8,128)(2,1)}, bf16[256,1792]{1,0:T(8,128)(2,1)S(1)}, u32[]{:S(2)}, u32[]{:S(2)}) collective-permute-start(bf16[256,1792]{1,0:T(8,128)(2,1)} %collective-permute-done.1.refs_0_), channel_id=1, source_target_pairs={{0,1},{1,0},{2,3},{3,2},{4,5},{5,4},{6,7},{7,6},{8,9},{9,8},{10,11... | collective-permute-start | bytes 2752520 | tf_op jit(solution)/shard_map/ppermute | solution.py:42
  25.9 14.6 %collective-permute-start.9 = (bf16[256,1792]{1,0:T(8,128)(2,1)S(1)}, bf16[256,1792]{1,0:T(8,128)(2,1)S(1)}, u32[]{:S(2)}, u32[]{:S(2)}) collective-permute-start(bf16[256,1792]{1,0:T(8,128)(2,1)S(1)} %collective-permute-done.4.refs_2_), channel_id=1, source_target_pairs={{0,1},{1,0},{2,3},{3,2},{4,5},{5,4},{6,7},{7,6},{8,9},{9,8},{10,11... | collective-permute-start | bytes 2752520 | tf_op jit(solution)/shard_map/ppermute | solution.py:42
  34.3 6.3 %collective-permute-start.8 = (bf16[256,1792]{1,0:T(8,128)(2,1)}, bf16[256,1792]{1,0:T(8,128)(2,1)S(1)}, u32[]{:S(2)}, u32[]{:S(2)}) collective-permute-start(bf16[256,1792]{1,0:T(8,128)(2,1)} %collective-permute-done.5.refs_1_), channel_id=1, source_target_pairs={{0,1},{1,0},{2,3},{3,2},{4,5},{5,4},{6,7},{7,6},{8,9},{9,8},{10,11... | collective-permute-start | bytes 2752520 | tf_op jit(solution)/shard_map/ppermute | solution.py:42
  36.4 4.2 %collective-permute-start.10 = (bf16[256,1792]{1,0:T(8,128)(2,1)}, bf16[256,1792]{1,0:T(8,128)(2,1)}, u32[]{:S(2)}, u32[]{:S(2)}) collective-permute-start(bf16[256,1792]{1,0:T(8,128)(2,1)} %collective-permute-done.6.refs_3_), channel_id=1, source_target_pairs={{0,1},{1,0},{2,3},{3,2},{4,5},{5,4},{6,7},{7,6},{8,9},{9,8},{10,11... | collective-permute-start | bytes 2752520 | tf_op jit(solution)/shard_map/ppermute | solution.py:42
  37.8 13.4 %collective-permute-start.12 = (bf16[256,1792]{1,0:T(8,128)(2,1)}, bf16[256,1792]{1,0:T(8,128)(2,1)}, u32[]{:S(2)}, u32[]{:S(2)}) collective-permute-start(bf16[256,1792]{1,0:T(8,128)(2,1)} %collective-permute-done.1.refs_0_), channel_id=1, source_target_pairs={{0,48},{1,13},{2,50},{3,15},{4,52},{5,1},{6,54},{7,3},{8,56},{9,5}... | collective-permute-start | bytes 2752520 | tf_op jit(solution)/shard_map/ppermute | solution.py:42
  40.5 13.8 %collective-permute-start.13 = (bf16[256,1792]{1,0:T(8,128)(2,1)}, bf16[256,1792]{1,0:T(8,128)(2,1)}, u32[]{:S(2)}, u32[]{:S(2)}) collective-permute-start(bf16[256,1792]{1,0:T(8,128)(2,1)} %collective-permute-done.6.refs_3_), channel_id=1, source_target_pairs={{0,16},{1,5},{2,18},{3,7},{4,20},{5,9},{6,22},{7,11},{8,24},{9,13}... | collective-permute-start | bytes 2752520 | tf_op jit(solution)/shard_map/ppermute | solution.py:42
  54.3 2.7 %collective-permute-start.14 = (bf16[256,1792]{1,0:T(8,128)(2,1)}, bf16[256,1792]{1,0:T(8,128)(2,1)S(1)}, u32[]{:S(2)}, u32[]{:S(2)}) collective-permute-start(bf16[256,1792]{1,0:T(8,128)(2,1)} %collective-permute-done.12.refs_0_), channel_id=1, source_target_pairs={{0,1},{1,0},{2,3},{3,2},{4,5},{5,4},{6,7},{7,6},{8,9},{9,8},{10,11... | collective-permute-start | bytes 2752520 | tf_op jit(solution)/shard_map/ppermute | solution.py:42
  54.3 4.0 %collective-permute-start.15 = (bf16[256,1792]{1,0:T(8,128)(2,1)}, bf16[256,1792]{1,0:T(8,128)(2,1)S(1)}, u32[]{:S(2)}, u32[]{:S(2)}) collective-permute-start(bf16[256,1792]{1,0:T(8,128)(2,1)} %collective-permute-done.13.refs_1_), channel_id=1, source_target_pairs={{0,1},{1,0},{2,3},{3,2},{4,5},{5,4},{6,7},{7,6},{8,9},{9,8},{10,11... | collective-permute-start | bytes 2752520 | tf_op jit(solution)/shard_map/ppermute | solution.py:42
  54.8 12.5 %collective-permute-start.11 = (f16[2,896,256]{2,1,0:T(8,128)(2,1)S(1)}, f16[2,896,256]{2,1,0:T(8,128)(2,1)S(1)}, u32[]{:S(2)}, u32[]{:S(2)}) collective-permute-start(f16[2,896,256]{2,1,0:T(8,128)(2,1)S(1)} %fusion.1), channel_id=1, source_target_pairs={{0,2},{1,67},{2,0},{3,65},{4,6},{5,71},{6,4},{7,69},{8,10},{9,75},... | collective-permute-start | bytes 2752520 | tf_op jit(solution)/shard_map/ppermute | solution.py:42
  62.6 8.9 %collective-permute-start.17 = (f16[2,384,256]{2,1,0:T(8,128)(2,1)S(1)}, f16[2,384,256]{2,1,0:T(8,128)(2,1)S(1)}, u32[]{:S(2)}, u32[]{:S(2)}) collective-permute-start(f16[2,384,256]{2,1,0:T(8,128)(2,1)S(1)} %fusion.7), channel_id=1, source_target_pairs={{0,2},{1,67},{2,0},{3,65},{4,6},{5,71},{6,4},{7,69},{8,10},{9,75},... | collective-permute-start | bytes 1179656 | tf_op jit(solution)/shard_map/ppermute | solution.py:42
  67.8 9.0 %collective-permute-start.16 = (f16[896,256]{1,0:T(8,128)(2,1)S(1)}, f16[896,256]{1,0:T(8,128)(2,1)S(1)}, u32[]{:S(2)}, u32[]{:S(2)}) collective-permute-start(f16[896,256]{1,0:T(8,128)(2,1)S(1)} %fusion.5), channel_id=1, source_target_pairs={{0,66},{1,3},{2,64},{3,1},{4,70},{5,7},{6,68},{7,5},{8,74},{9,11},... | collective-permute-start | bytes 1376264 | tf_op jit(solution)/shard_map/ppermute | solution.py:42
  71.8 7.2 %collective-permute-start.25 = (f16[384,256]{1,0:T(8,128)(2,1)S(1)}, f16[384,256]{1,0:T(8,128)(2,1)S(1)}, u32[]{:S(2)}, u32[]{:S(2)}) collective-permute-start(f16[384,256]{1,0:T(8,128)(2,1)S(1)} %fusion.11), channel_id=1, source_target_pairs={{0,66},{1,3},{2,64},{3,1},{4,70},{5,7},{6,68},{7,5},{8,74},{9,11},... | collective-permute-start | bytes 589832 | tf_op jit(solution)/shard_map/ppermute | solution.py:42
  79.8 16.8 %copy-start.13 = (f32[512]{0:T(512)S(1)}, f32[512]{0:T(512)}, u32[]{:S(2)}) copy-start(f32[512]{0:T(512)} %constant.52) | copy-start | bytes 6148
  79.9 18.3 %copy-start.4 = (f32[2048,256]{1,0:T(8,128)S(1)}, f32[2048,256]{1,0:T(8,128)}, u32[]{:S(2)}) copy-start(f32[2048,256]{1,0:T(8,128)} %old.1) | copy-start | bytes 6291460
  79.9 8.2 %collective-permute-start.28 = (f16[384,256]{1,0:T(8,128)(2,1)S(1)}, f16[384,256]{1,0:T(8,128)(2,1)S(1)}, u32[]{:S(2)}, u32[]{:S(2)}) collective-permute-start(f16[384,256]{1,0:T(8,128)(2,1)S(1)} %multiply_convert_fusion.1), channel_id=1, source_target_pairs={{0,32},{1,9},{2,96},{3,73},{4,36},{5,13},{6,100},{7,77},{8,40},{9,... | collective-permute-start | bytes 589832 | tf_op jit(solution)/shard_map/ppermute | solution.py:42
  82.1 11.6 %collective-permute-start.19 = (f16[512,256]{1,0:T(8,128)(2,1)S(1)}, f16[512,256]{1,0:T(8,128)(2,1)S(1)}, u32[]{:S(2)}, u32[]{:S(2)}) collective-permute-start(f16[512,256]{1,0:T(8,128)(2,1)S(1)} %multiply_convert_fusion), channel_id=1, source_target_pairs={{0,16},{1,5},{2,80},{3,69},{4,20},{5,9},{6,84},{7,73},{8,24},{9,13... | collective-permute-start | bytes 786440 | tf_op jit(solution)/shard_map/ppermute | solution.py:42
  83.3 12.0 %collective-permute-start.21 = (f32[256,256]{1,0:T(8,128)S(1)}, f32[256,256]{1,0:T(8,128)S(1)}, u32[]{:S(2)}, u32[]{:S(2)}) collective-permute-start(f32[256,256]{1,0:T(8,128)S(1)} %get-tuple-element.30), channel_id=1, source_target_pairs={{0,48},{1,13},{2,50},{3,15},{4,52},{5,1},{6,54},{7,3},{8,56},{9,5}... | collective-permute-start | bytes 786440 | tf_op jit(solution)/shard_map/ppermute | solution.py:42
  85.6 9.7 %collective-permute-start.23 = (f32[256,256]{1,0:T(8,128)S(1)}, f32[256,256]{1,0:T(8,128)S(1)}, u32[]{:S(2)}, u32[]{:S(2)}) collective-permute-start(f32[256,256]{1,0:T(8,128)S(1)} %get-tuple-element.31), channel_id=1, source_target_pairs={{0,4},{1,49},{2,6},{3,51},{4,8},{5,53},{6,10},{7,55},{8,12},{9,57}... | collective-permute-start | bytes 786440 | tf_op jit(solution)/shard_map/ppermute | solution.py:42
  85.6 10.2 %collective-permute-start.26 = (f32[256,256]{1,0:T(8,128)S(1)}, f32[256,256]{1,0:T(8,128)S(1)}, u32[]{:S(2)}, u32[]{:S(2)}) collective-permute-start(f32[256,256]{1,0:T(8,128)S(1)} %get-tuple-element.33), channel_id=1, source_target_pairs={{0,12},{1,17},{2,14},{3,19},{4,0},{5,21},{6,2},{7,23},{8,4},{9,25}... | collective-permute-start | bytes 786440 | tf_op jit(solution)/shard_map/ppermute | solution.py:42
  88.1 7.8 %collective-permute-start.29 = (f16[384,256]{1,0:T(8,128)(2,1)S(1)}, f16[384,256]{1,0:T(8,128)(2,1)S(1)}, u32[]{:S(2)}, u32[]{:S(2)}) collective-permute-start(f16[384,256]{1,0:T(8,128)(2,1)S(1)} %collective-permute-done.28), channel_id=1, source_target_pairs={{0,1},{1,0},{2,3},{3,2},{4,5},{5,4},{6,7},{7,6},{8,9},{9,8},{10,11... | collective-permute-start | bytes 589832 | tf_op jit(solution)/shard_map/ppermute | solution.py:42
  93.7 2.8 %collective-permute-start.20 = (f16[512,256]{1,0:T(8,128)(2,1)S(1)}, f16[512,256]{1,0:T(8,128)(2,1)S(1)}, u32[]{:S(2)}, u32[]{:S(2)}) collective-permute-start(f16[512,256]{1,0:T(8,128)(2,1)S(1)} %collective-permute-done.19), channel_id=1, source_target_pairs={{0,1},{1,0},{2,3},{3,2},{4,5},{5,4},{6,7},{7,6},{8,9},{9,8},{10,11... | collective-permute-start | bytes 786440 | tf_op jit(solution)/shard_map/ppermute | solution.py:42
  95.3 1.7 %collective-permute-start.18 = (f32[384,256]{1,0:T(8,128)S(1)}, f32[384,256]{1,0:T(8,128)S(1)}, u32[]{:S(2)}, u32[]{:S(2)}) collective-permute-start(f32[384,256]{1,0:T(8,128)S(1)} %get-tuple-element.28.refs_0_), channel_id=1, source_target_pairs={{0,1},{1,0},{2,3},{3,2},{4,5},{5,4},{6,7},{7,6},{8,9},{9,8},{10,11... | collective-permute-start | bytes 1179656 | tf_op jit(solution)/shard_map/ppermute | solution.py:42
  95.3 2.1 %collective-permute-start.22 = (f32[256,256]{1,0:T(8,128)S(1)}, f32[256,256]{1,0:T(8,128)S(1)}, u32[]{:S(2)}, u32[]{:S(2)}) collective-permute-start(f32[256,256]{1,0:T(8,128)S(1)} %collective-permute-done.21.refs_4_), channel_id=1, source_target_pairs={{0,1},{1,0},{2,3},{3,2},{4,5},{5,4},{6,7},{7,6},{8,9},{9,8},{10,11... | collective-permute-start | bytes 786440 | tf_op jit(solution)/shard_map/ppermute | solution.py:42
  95.8 2.0 %collective-permute-start.24 = (f32[256,256]{1,0:T(8,128)S(1)}, f32[256,256]{1,0:T(8,128)S(1)}, u32[]{:S(2)}, u32[]{:S(2)}) collective-permute-start(f32[256,256]{1,0:T(8,128)S(1)} %collective-permute-done.23.refs_6_), channel_id=1, source_target_pairs={{0,1},{1,0},{2,3},{3,2},{4,5},{5,4},{6,7},{7,6},{8,9},{9,8},{10,11... | collective-permute-start | bytes 786440 | tf_op jit(solution)/shard_map/ppermute | solution.py:42
  95.9 2.2 %collective-permute-start.27 = (f32[256,256]{1,0:T(8,128)S(1)}, f32[256,256]{1,0:T(8,128)S(1)}, u32[]{:S(2)}, u32[]{:S(2)}) collective-permute-start(f32[256,256]{1,0:T(8,128)S(1)} %collective-permute-done.26.refs_8_), channel_id=1, source_target_pairs={{0,1},{1,0},{2,3},{3,2},{4,5},{5,4},{6,7},{7,6},{8,9},{9,8},{10,11... | collective-permute-start | bytes 786440 | tf_op jit(solution)/shard_map/ppermute | solution.py:42
  (13 other events, 93.6 us)

commit v4 on v3

v4 whole, which is shorter than its diff:
```python
import functools

import jax
import jax.numpy as jnp
import numpy as np
from jax import lax
from jax.experimental import pallas as pl
from jax.experimental.pallas import tpu as pltpu
from jax.sharding import PartitionSpec as P


AXES = ("rows", "cols")
SIZES = (2, 4, 4, 2, 2)
ALONG = {"s": (0, 0), "a1": (1, 0), "a2": (2, 0), "a3": (3, 0), "b1": (0, 1), "b2": (0, 2), "b3": (0, 3)}
ROWS = 64.0 * 2.0 ** (np.arange(1024) * 0.6180339887 % 1 / 2)
COLUMNS = 2.0 ** (np.arange(256) * 0.7548776662 % 1 / 2)
NEAR = (
    ("a1", "s", ("right", "left"), False),
    ("a1", "a3", ("right",), False),
    ("a1", "b1", ("right", "left"), False),
)
SELF = (("s", "s", ("right",), True),)
FAR = (("b3", "a2", ("right", "left"), False),)
OPPOSITE = (("b2", "a2", ("right",), True),)
VMEM = pl.BlockSpec(memory_space=pltpu.VMEM)
SMEM = pl.BlockSpec(memory_space=pltpu.SMEM)


def offset(name, core):
    dx, dy = ALONG[name]
    return (dx, dy) if core == 0 else (-dy % 4, dx)


def gap(name, start, core):
    return tuple((a - b) % 4 for a, b in zip(offset(name, core), offset(start, core)))


def send(value, move):
    pairs = []
    for source in range(int(np.prod(SIZES))):
        place = [int(i) for i in np.unravel_index(source, SIZES)]
        pairs.append((source, int(np.ravel_multi_index(move(*place), SIZES))))
    return lax.ppermute(value, AXES, pairs)


def to_place(name, swap=False):
    def move(zh, x, y, zl, core):
        dx, dy = offset(name, core)
        if swap:
            zh, zl = zl, zh
        return zh, (x + dx) % 4, (y + dy) % 4, zl, core

    return move


def other_core(zh, x, y, zl, core):
    return zh, x, y, zl, 1 - core


def other_high(zh, x, y, zl, core):
    return 1 - zh, x, y, zl, core


def first_partner(zh, x, y, zl, core):
    return (zh, x, y, 1 - zl, core) if core == 0 else (1 - zh, x, y, 1 - zl, core)


def second_partner(zh, x, y, zl, core):
    return first_partner(zh, x, y, zl, 1 - core)[:4] + (core,)


def after(value, *others):
    return lax.optimization_barrier((value, *others))[0]


def packed(value):
    rows, columns = np.float32(ROWS[: value.shape[-2], None]), np.float32(COLUMNS)
    return (value * rows * columns).astype(jnp.float16)


def unpacked(value):
    rows, columns = np.float32(1 / ROWS[: value.shape[-2], None]), np.float32(1 / COLUMNS)
    return value.astype(jnp.float32) * rows * columns


def call(kernel, outs, place, *args, keep=True, cost=2**21):
    return pl.pallas_call(
        kernel,
        out_shape=[pltpu.VMEM(s, jnp.float32) if keep else jax.ShapeDtypeStruct(s, jnp.float32) for s in outs],
        in_specs=[SMEM] + [VMEM] * len(args),
        out_specs=[VMEM] * len(outs),
        compiler_params=pltpu.CompilerParams(vmem_limit_bytes=8 * 2**20),
        cost_estimate=pl.CostEstimate(flops=0, bytes_accessed=cost, transcendentals=0),
    )(place, *[pltpu.with_memory_space_constraint(a, pltpu.VMEM) for a in args])


def multiply(pairs, names, place, *refs):
    held = {name: refs[2 * i : 2 * i + 2] for i, name in enumerate(names)}
    out = refs[-1]
    core = place[3]
    straight = jnp.where(place[0] == place[2], 1, 0)

    def pair(left, right, halved, at):
        for kind in (0, 1):
            ends = straight if kind == 0 else 1 - straight
            lhs = held[left][kind]
            if halved and lhs.shape[0] == 256:
                lhs = lhs.at[pl.ds(pl.multiple_of(core * 128, 128), 128)]
            for col in (0, 1):
                slot = jnp.where(ends == 1, 1 if col else 2, jnp.where(core == col, 0, 3))
                out[slot, pl.ds(at, lhs.shape[0])] = lax.dot_general(
                    lhs[...], held[right][col][...], (((1,), (1,)), ((), ())), preferred_element_type=jnp.float32
                )

    at = 0
    for left, right, _, halved in pairs:
        if {left, right} & {"b1", "b3"}:
            mirror = {"b1": "b3", "b3": "b1"}
            pl.when(core == 0)(functools.partial(pair, left, right, halved, at))
            pl.when(core == 1)(functools.partial(pair, mirror.get(left, left), mirror.get(right, right), halved, at))
        else:
            pair(left, right, halved, at)
        at += 128 if halved else 256


def products(place, blocks, pairs, cost=0):
    names = {name for pair in pairs for name in pair[:2]}
    names = sorted(names | {"b1", "b3"} if names & {"b1", "b3"} else names)
    return call(
        functools.partial(multiply, pairs, names),
        [(4, sum(128 if halved else 256 for *_, halved in pairs), 256)],
        place,
        *[rows for name in names for rows in blocks[name]],
        cost=cost,
    )[0]


def finish(messages, place, *refs):
    outs = refs[-len(messages) :]
    for tiles, out in zip(messages, outs, strict=True):
        to = 0
        for size, terms in tiles:
            parts = [refs[i][pl.ds(at, size)] if slot is None else refs[i][slot, pl.ds(at, size)] for i, slot, at in terms]
            out[pl.ds(to, size)] = sum(parts[1:], parts[0])
            to += size


def delivered(place, arrays, tiles):
    messages = {}
    for (left, right, keepers, halved), terms in tiles:
        for keeper in keepers:
            to, rows = (right, left) if keeper == "right" else (left, right)
            part = (halved, [gap(rows, to, c) for c in (0, 1)], (128 if halved else 256, terms))
            messages.setdefault((to, keeper == "left"), []).append(part)
    sums = [[part[2] for part in parts] for parts in messages.values()]
    outs = call(functools.partial(finish, sums), [(sum(size for size, _ in m), 256) for m in sums], place, *arrays)
    kept = []
    for ((to, turned), parts), out in zip(messages.items(), outs, strict=True):
        if turned:
            out = packed(out)
        if to != "s":
            out = send(out, to_place(to, turned))
        kept.append(([(turned, halved, gaps) for halved, gaps, _ in parts], out))
    return kept, outs


def with_halves(kept):
    both = []
    for _, mine in kept:
        far = send(mine, other_core)
        both += [unpacked(part) if mine.dtype == jnp.float16 else part for part in (mine, far)]
    return [layout for layout, _ in kept], [pltpu.with_memory_space_constraint(part, pltpu.VMEM) for part in both]


def places(layouts, place, tiles):
    core = place[3]
    for parts, pair in zip(layouts, zip(tiles[::2], tiles[1::2]), strict=True):
        for source, ref in zip((core, 1 - core), pair):
            at = 0
            for turned, halved, gaps in parts:
                size = 128 if halved else 256
                dx = jnp.where(source == 0, gaps[0][0], gaps[1][0])
                dy = jnp.where(source == 0, gaps[0][1], gaps[1][1])
                x, y = (place[1] + dx) & 3, (place[4] + dy) & 3
                to = ((x & 1) * 4 + y) * 256 + (source * 128 if halved else 0)

                def tile(ref=ref, at=at, size=size, turned=turned):
                    return ref[pl.ds(at, size)].T if turned else ref[pl.ds(at, size)]

                yield (x >> 1) == core, pl.ds(pl.multiple_of(to, 128), size), tile
                at += size


def begin(layouts, place, old, *refs):
    new, out, sem = refs[-3:]
    new[...] = 0.9 * old[...]
    for ours, to, tile in places(layouts, place, refs[:-3]):

        @pl.when(ours)
        def _():
            new[to] += 0.1 * tile()

    copy = pltpu.make_async_copy(new, out, sem)
    copy.start()
    copy.wait()


def end(layouts, place, base, *refs):
    out, rows, sems = refs[-3:]
    copies = []
    for n, (ours, to, tile) in enumerate(places(layouts, place, refs[:-4])):
        size = to.size
        copy = pltpu.make_async_copy(rows.at[n, pl.ds(0, size)], out.at[to], sems.at[n])

        @pl.when(ours)
        def _():
            rows[n, pl.ds(0, size)] = base[to] + 0.1 * tile()
            copy.start()

        copies.append((ours, copy))
    for ours, copy in copies:
        pl.when(ours)(copy.wait)


def body(gradient, stat_old):
    device = lax.axis_index("rows").astype(jnp.int32)
    column = lax.axis_index("cols").astype(jnp.int32)
    zh, x, y = device >> 4, (device >> 2) & 3, device & 3
    zl, core = column >> 1, column & 1
    place = jnp.stack([zh, x, zl, core, y])
    gradient, place, zh, core = lax.optimization_barrier((gradient, place, zh, core))
    first_core = core == 0

    def whole(rows, *others):
        far = after(send(rows, other_core), *others)
        first = jnp.where(first_core, rows, far)
        return jnp.concatenate([first, jnp.where(first_core, far, rows)], axis=1)

    keep = lax.dynamic_slice_in_dim(gradient, zh * 896, 896, 1)
    give = lax.dynamic_slice_in_dim(gradient, (1 - zh) * 896, 896, 1)
    given = send(give, other_high)
    own = {"s": whole(keep)}
    own["a1"], own["a3"] = send(own["s"], to_place("a3")), send(own["s"], to_place("a1"))
    own["b1"], own["b3"] = send(own["a1"], other_core), send(own["a3"], other_core)
    other = {"s": whole(given, own["a1"], own["a3"])}
    other["a1"], other["a3"] = send(other["s"], to_place("a3")), send(other["s"], to_place("a1"))
    made0 = products(place, {"s": (own["s"], other["s"])}, SELF)
    got0 = send(packed(made0[:2]), first_partner)
    late0 = send(packed(made0[3] + unpacked(got0[1])), second_partner)
    other["a1"], other["a3"] = after((other["a1"], other["a3"]), late0)
    own["a2"] = send(after(own["a1"], other["a1"], own["b1"]), to_place("a3"))
    other["a2"] = send(after(other["a3"], own["b3"]), to_place("a1"))
    other["b1"], other["b3"] = send(other["a1"], other_core), send(other["a3"], other_core)
    blocks = {name: (own[name], other[name]) for name in own}

    made1 = products(place, blocks, NEAR, 2**24)
    leave1 = packed(made1[0]), packed(made1[1])
    got1 = send(leave1[1], first_partner)
    a2 = after(blocks["a2"], got1)
    b2 = tuple(send(jnp.where(first_core, rows[128:], rows[:128]), other_core) for rows in a2)
    pass1 = packed(made1[3] + unpacked(got1))
    late1 = send(pass1, second_partner)
    rest1 = send(after(leave1[0], pass1), first_partner)
    made2 = products(after(place, pass1), {**blocks, "a2": a2}, FAR, 2**23)
    made3 = products(place, {"a2": a2, "b2": after(b2, made2)}, OPPOSITE, 2**23)
    leave2 = packed(jnp.concatenate([made2[:2], made3[:2]], axis=1))
    got2 = send(leave2, first_partner)
    at = [256 * i for i in range(4)]
    tiles1, _ = delivered(
        place,
        [made1, unpacked(after(rest1, leave2)), unpacked(after(late1, leave2)), made0, unpacked(got0[0]), unpacked(late0)],
        [(pair, [(0, 2, at[i]), (1, None, at[i]), (2, None, at[i])]) for i, pair in enumerate(NEAR)]
        + [(SELF[0], [(3, 2, 0), (4, None, 0), (5, None, 0)])],
    )
    pass2 = packed(jnp.concatenate([made2[3], made3[3]]) + unpacked(got2[1]))
    late2 = send(pass2, second_partner)
    tiles2, _ = delivered(
        place,
        [made2, made3, unpacked(got2[0]), unpacked(after(late2, *(mine for _, mine in tiles1)))],
        [
            (FAR[0], [(0, 2, 0), (2, None, 0), (3, None, 0)]),
            (OPPOSITE[0], [(1, 2, 0), (2, None, 256), (3, None, 256)]),
        ],
    )
    anywhere = pl.BlockSpec(memory_space=pl.ANY)
    params = pltpu.CompilerParams(vmem_limit_bytes=8 * 2**20)
    cost = pl.CostEstimate(flops=0, bytes_accessed=2**21, transcendentals=0)
    layouts, tiles = with_halves(tiles1)
    base, new = pl.pallas_call(
        functools.partial(begin, layouts),
        out_shape=[pltpu.VMEM(stat_old.shape, jnp.float32), jax.ShapeDtypeStruct(stat_old.shape, jnp.float32)],
        in_specs=[SMEM] + [VMEM] * (1 + len(tiles)),
        out_specs=[VMEM, anywhere],
        scratch_shapes=[pltpu.SemaphoreType.DMA],
        compiler_params=params,
        cost_estimate=cost,
    )(place, pltpu.with_memory_space_constraint(stat_old, pltpu.VMEM), *tiles)
    layouts, tiles = with_halves([(layout, after(mine, base)) for layout, mine in tiles2])
    count = 2 * sum(len(layout) for layout in layouts)
    return pl.pallas_call(
        functools.partial(end, layouts),
        out_shape=jax.ShapeDtypeStruct(stat_old.shape, jnp.float32),
        in_specs=[SMEM] + [VMEM] * (1 + len(tiles)) + [anywhere],
        out_specs=anywhere,
        scratch_shapes=[pltpu.VMEM((count, 256, 256), jnp.float32), pltpu.SemaphoreType.DMA((count,))],
        input_output_aliases={2 + len(tiles): 0},
        compiler_params=params,
        cost_estimate=cost,
    )(place, pltpu.with_memory_space_constraint(base, pltpu.VMEM), *tiles, new)


def solution(mesh):
    placed = (P("rows", "cols"), P("cols", "rows"))
    return jax.shard_map(
        body, mesh=mesh, in_specs=placed, out_specs=P("cols", "rows"), check_vma=False
    )
```

time: 102 us -> 97.7 us (0.958)
  local copies, waits for them, and re-layouts: 5.84 us -> 1.49 us
  waiting for transfers between devices: 43.7 us -> 41.5 us
    unnamed x30 -> x26, local copies, waits for them, and re-layouts: 4.52 us -> 0.09 us
    pallas_call x0 -> x2, Pallas kernels: none -> 4.24 us  [the longest x1 2.56 us: body(): pl.pallas_call(functools.partial(begin, layouts), out_shape=[pltpu.VMEM(s...]
    pallas_call x5 -> x6, Pallas kernels: 14.8 us -> 10.7 us  [call(): pl.pallas_call(kernel, out_shape=[pltpu.VMEM(s, jnp.float32) if keep else...]
    ppermute x30 -> x33, waiting for transfers between devices: 43.7 us -> 41.5 us  [send(): return lax.ppermute(value, AXES, pairs)]
    ppermute x30 -> x33, starting transfers between devices: 34.1 us -> 34.9 us  [send(): return lax.ppermute(value, AXES, pairs)]
  transfers between devices with their start and end apart: 30 -> 33, of which waited for: 19 -> 16; matrix products, arithmetic and copies ran while one was open for 2% -> 2% of each run, Pallas kernels for 11% -> 14%
where the time goes in v4:
time: 97.7 us; the launch traced here: 96 us
  waiting for transfers between devices  41.5 us (42%)
  starting transfers between devices  34.9 us (36%)
  Pallas kernels  15 us (15%)
  other arithmetic  2.44 us (2%)
  local copies, waits for them, and re-layouts  1.49 us (2%)
    ppermute x33, waiting for transfers between devices, send(): return lax.ppermute(value, AXES, pairs)  41.5 us
    ppermute x33, starting transfers between devices, send(): return lax.ppermute(value, AXES, pairs)  34.9 us
    pallas_call x6, Pallas kernels, call(): pl.pallas_call(kernel, out_shape=[pltpu.VMEM(s, jnp.float32) if keep else...  10.7 us
    pallas_call x1, Pallas kernels, body(): pl.pallas_call(functools.partial(begin, layouts), out_shape=[pltpu.VMEM(s...  2.56 us
  transfers between devices with their start and end apart: 33, of which 16 were waited for; matrix products, arithmetic and copies ran while one was open for 2% of the time, Pallas kernels for 14%

profile of v4, /device:TPU:33, one launch (start us, length us, event | category | flops | bytes accessed | tf_op | source)
XLA Modules:
  0.0 96.0 jit_solution(775318999081351436)
XLA Ops:
  0.1 1.2 %constant_dynamic-slice_fusion = (bf16[256,896]{1,0:T(8,128)(2,1)S(1)}, bf16[256,896]{1,0:T(8,128)(2,1)S(1)}) fusion(bf16[256,1792]{1,0:T(8,128)(2,1)} %param.46, s32[]{:T(128)S(6)} %select_n.42, s32[]{:T(128)S(6)} %select_n.39), kind=kLoop, calls=%fused_computation.60 | loop fusion | bytes 1835016 | tf_op jit(solution)/shard_map/dynamic_slice | solution.py:240
  2.1 2.7 %collective-permute-start.2 = (bf16[256,896]{1,0:T(8,128)(2,1)S(1)}, bf16[256,896]{1,0:T(8,128)(2,1)S(1)}, u32[]{:S(2)}, u32[]{:S(2)}) collective-permute-start(bf16[256,896]{1,0:T(8,128)(2,1)S(1)} %get-tuple-element.65), channel_id=1, source_target_pairs={{0,64},{1,65},{2,66},{3,67},{4,68},{5,69},{6,70},{7,71},{8,72},{9,... | collective-permute-start | bytes 1376264 | tf_op jit(solution)/shard_map/ppermute | solution.py:43
  5.0 2.8 %collective-permute-start.1 = (bf16[256,1792]{1,0:T(8,128)(2,1)S(1)}, bf16[256,1792]{1,0:T(8,128)(2,1)S(1)}, u32[]{:S(2)}, u32[]{:S(2)}) collective-permute-start(bf16[256,1792]{1,0:T(8,128)(2,1)S(1)} %pad_maximum_fusion.refs_0_.refs_8_), channel_id=1, source_target_pairs={{0,48},{1,13},{2,50},{3,15},{4,52},{5,1},{6,54},{7,3},{8,56},{9,5}... | collective-permute-start | bytes 2752520 | tf_op jit(solution)/shard_map/ppermute | solution.py:43
  7.8 7.9 %collective-permute-done.2 = bf16[256,896]{1,0:T(8,128)(2,1)S(1)} collective-permute-done((bf16[256,896]{1,0:T(8,128)(2,1)S(1)}, bf16[256,896]{1,0:T(8,128)(2,1)S(1)}, u32[]{:S(2)}, u32[]{:S(2)}) %collective-permute-start.2) | collective-permute-done | bytes 458784 | tf_op jit(solution)/shard_map/ppermute | solution.py:43
  16.5 1.4 %collective-permute-done.3 = bf16[256,896]{1,0:T(8,128)(2,1)S(1)} collective-permute-done((bf16[256,896]{1,0:T(8,128)(2,1)S(1)}, bf16[256,896]{1,0:T(8,128)(2,1)S(1)}, u32[]{:S(2)}, u32[]{:S(2)}) %collective-permute-start.3) | collective-permute-done | bytes 458784 | tf_op jit(solution)/shard_map/ppermute | solution.py:43
  18.1 3.4 %collective-permute-done.4.refs_2_ = bf16[256,1792]{1,0:T(8,128)(2,1)S(1)} collective-permute-done((bf16[256,1792]{1,0:T(8,128)(2,1)S(1)}, bf16[256,1792]{1,0:T(8,128)(2,1)S(1)}, u32[]{:S(2)}, u32[]{:S(2)}) %collective-permute-start.4) | collective-permute-done | bytes 917536 | tf_op jit(solution)/shard_map/ppermute | solution.py:43
  21.8 1.5 %collective-permute-start.6 = (bf16[256,1792]{1,0:T(8,128)(2,1)S(1)}, bf16[256,1792]{1,0:T(8,128)(2,1)S(1)}, u32[]{:S(2)}, u32[]{:S(2)}) collective-permute-start(bf16[256,1792]{1,0:T(8,128)(2,1)S(1)} %pad_maximum_fusion.1.refs_1_.refs_9_), channel_id=1, source_target_pairs={{0,16},{1,5},{2,18},{3,7},{4,20},{5,9},{6,22},{7,11},{8,24},{9,13}... | collective-permute-start | bytes 2752520 | tf_op jit(solution)/shard_map/ppermute | solution.py:43
  23.3 1.8 %shard_map.424.refs_3_ = f32[4,128,256]{2,1,0:T(8,128)S(1)} custom-call(s32[5]{0:T(128)S(1)} %stack.23.place, bf16[256,1792]{1,0:T(8,128)(2,1)S(1)} %pad_maximum_fusion.refs_0_.refs_8_, bf16[256,1792]{1,0:T(8,128)(2,1)S(1)} %pad_maximum_fusion.1.refs_1_.refs_9_), custom_call_target="tpu_custom_call" | custom-call | tf_op jit(solution)/shard_map/pallas_call | solution.py:87
  25.7 2.4 %collective-permute-start.9 = (bf16[256,1792]{1,0:T(8,128)(2,1)S(1)}, bf16[256,1792]{1,0:T(8,128)(2,1)S(1)}, u32[]{:S(2)}, u32[]{:S(2)}) collective-permute-start(bf16[256,1792]{1,0:T(8,128)(2,1)S(1)} %collective-permute-done.1.refs_0_), channel_id=1, source_target_pairs={{0,1},{1,0},{2,3},{3,2},{4,5},{5,4},{6,7},{7,6},{8,9},{9,8},{10,11... | collective-permute-start | bytes 2752520 | tf_op jit(solution)/shard_map/ppermute | solution.py:43
  28.1 1.3 %collective-permute-done.7 = f16[2,128,256]{2,1,0:T(8,128)(2,1)S(1)} collective-permute-done((f16[2,128,256]{2,1,0:T(8,128)(2,1)S(1)}, f16[2,128,256]{2,1,0:T(8,128)(2,1)S(1)}, u32[]{:S(2)}, u32[]{:S(2)}) %collective-permute-start.7) | collective-permute-done | bytes 131104 | tf_op jit(solution)/shard_map/ppermute | solution.py:43
  29.6 2.0 %collective-permute-start.8 = (f16[128,256]{1,0:T(8,128)(2,1)S(1)}, f16[128,256]{1,0:T(8,128)(2,1)S(1)}, u32[]{:S(2)}, u32[]{:S(2)}) collective-permute-start(f16[128,256]{1,0:T(8,128)(2,1)S(1)} %get-tuple-element.72), channel_id=1, source_target_pairs={{0,66},{1,3},{2,64},{3,1},{4,70},{5,7},{6,68},{7,5},{8,74},{9,11},... | collective-permute-start | bytes 196616 | tf_op jit(solution)/shard_map/ppermute | solution.py:43
  31.6 2.0 %collective-permute-done.8 = f16[128,256]{1,0:T(8,128)(2,1)S(1)} collective-permute-done((f16[128,256]{1,0:T(8,128)(2,1)S(1)}, f16[128,256]{1,0:T(8,128)(2,1)S(1)}, u32[]{:S(2)}, u32[]{:S(2)}) %collective-permute-start.8) | collective-permute-done | bytes 65568 | tf_op jit(solution)/shard_map/ppermute | solution.py:43
  34.3 1.3 %collective-permute-done.6.refs_3_ = bf16[256,1792]{1,0:T(8,128)(2,1)S(1)} collective-permute-done((bf16[256,1792]{1,0:T(8,128)(2,1)S(1)}, bf16[256,1792]{1,0:T(8,128)(2,1)S(1)}, u32[]{:S(2)}, u32[]{:S(2)}) %collective-permute-start.6) | collective-permute-done | bytes 917536 | tf_op jit(solution)/shard_map/ppermute | solution.py:43
  35.6 2.1 %collective-permute-start.10 = (bf16[256,1792]{1,0:T(8,128)(2,1)S(1)}, bf16[256,1792]{1,0:T(8,128)(2,1)S(1)}, u32[]{:S(2)}, u32[]{:S(2)}) collective-permute-start(bf16[256,1792]{1,0:T(8,128)(2,1)S(1)} %collective-permute-done.5.refs_1_), channel_id=1, source_target_pairs={{0,1},{1,0},{2,3},{3,2},{4,5},{5,4},{6,7},{7,6},{8,9},{9,8},{10,11... | collective-permute-start | bytes 2752520 | tf_op jit(solution)/shard_map/ppermute | solution.py:43
  37.7 2.7 %collective-permute-start.15 = (bf16[256,1792]{1,0:T(8,128)(2,1)S(1)}, bf16[256,1792]{1,0:T(8,128)(2,1)S(1)}, u32[]{:S(2)}, u32[]{:S(2)}) collective-permute-start(bf16[256,1792]{1,0:T(8,128)(2,1)S(1)} %collective-permute-done.1.refs_0_), channel_id=1, source_target_pairs={{0,48},{1,13},{2,50},{3,15},{4,52},{5,1},{6,54},{7,3},{8,56},{9,5}... | collective-permute-start | bytes 2752520 | tf_op jit(solution)/shard_map/ppermute | solution.py:43
  41.1 3.8 %shard_map.425.refs_0_ = f32[4,768,256]{2,1,0:T(8,128)S(1)} custom-call(s32[5]{0:T(128)S(1)} %stack.23.place, bf16[256,1792]{1,0:T(8,128)(2,1)S(1)} %collective-permute-done.1.refs_0_, bf16[256,1792]{1,0:T(8,128)(2,1)S(1)} %collective-permute-done.5.refs_1_, bf16[256,1792]{1,0:T(8,128)(2,1)S(1)} %collective-permute-done.4.refs_2_, ...), custom_call_target="tpu_custom_call" | custom-call | bytes 16777216 | tf_op jit(solution)/shard_map/pallas_call | solution.py:87
  45.7 5.1 %collective-permute-done.15.refs_0_ = bf16[256,1792]{1,0:T(8,128)(2,1)S(1)} collective-permute-done((bf16[256,1792]{1,0:T(8,128)(2,1)S(1)}, bf16[256,1792]{1,0:T(8,128)(2,1)S(1)}, u32[]{:S(2)}, u32[]{:S(2)}) %collective-permute-start.15) | collective-permute-done | bytes 917536 | tf_op jit(solution)/shard_map/ppermute | solution.py:43
  50.8 3.1 %collective-permute-done.16.refs_1_ = bf16[256,1792]{1,0:T(8,128)(2,1)S(1)} collective-permute-done((bf16[256,1792]{1,0:T(8,128)(2,1)S(1)}, bf16[256,1792]{1,0:T(8,128)(2,1)S(1)}, u32[]{:S(2)}, u32[]{:S(2)}) %collective-permute-start.16) | collective-permute-done | bytes 917536 | tf_op jit(solution)/shard_map/ppermute | solution.py:43
  56.0 1.9 %shard_map.426.refs_0_ = f32[4,256,256]{2,1,0:T(8,128)S(1)} custom-call(s32[5]{0:T(128)S(1)} %stack.23.place, bf16[256,1792]{1,0:T(8,128)(2,1)S(1)} %collective-permute-done.15.refs_0_, bf16[256,1792]{1,0:T(8,128)(2,1)S(1)} %collective-permute-done.16.refs_1_, bf16[256,1792]{1,0:T(8,128)(2,1)S(1)} %collective-permute-done.9.refs_4_.refs_2_, ...), custom_call_target="tpu_custom_call" | custom-call | bytes 8388608 | tf_op jit(solution)/shard_map/pallas_call | solution.py:87
  57.9 1.1 %collective-permute-start.14 = (f16[768,256]{1,0:T(8,128)(2,1)S(1)}, f16[768,256]{1,0:T(8,128)(2,1)S(1)}, u32[]{:S(2)}, u32[]{:S(2)}) collective-permute-start(f16[768,256]{1,0:T(8,128)(2,1)S(1)} %get-tuple-element.40), channel_id=1, source_target_pairs={{0,2},{1,67},{2,0},{3,65},{4,6},{5,71},{6,4},{7,69},{8,10},{9,75},... | collective-permute-start | bytes 1179656 | tf_op jit(solution)/shard_map/ppermute | solution.py:43
  59.1 1.8 %shard_map.427.refs_1_ = f32[4,128,256]{2,1,0:T(8,128)S(1)} custom-call(s32[5]{0:T(128)S(1)} %stack.23.place, bf16[256,1792]{1,0:T(8,128)(2,1)S(1)} %collective-permute-done.15.refs_0_, bf16[256,1792]{1,0:T(8,128)(2,1)S(1)} %collective-permute-done.16.refs_1_, bf16[128,1792]{1,0:T(8,128)(2,1)S(1)} %collective-permute-done.17.refs_2_, ...), custom_call_target="tpu_custom_call" | custom-call | bytes 8388608 | tf_op jit(solution)/shard_map/pallas_call | solution.py:87
  62.6 4.2 %collective-permute-done.14 = f16[768,256]{1,0:T(8,128)(2,1)S(1)} collective-permute-done((f16[768,256]{1,0:T(8,128)(2,1)S(1)}, f16[768,256]{1,0:T(8,128)(2,1)S(1)}, u32[]{:S(2)}, u32[]{:S(2)}) %collective-permute-start.14) | collective-permute-done | bytes 393248 | tf_op jit(solution)/shard_map/ppermute | solution.py:43
  68.8 2.0 %collective-permute-start.23 = (f32[256,256]{1,0:T(8,128)S(1)}, f32[256,256]{1,0:T(8,128)S(1)}, u32[]{:S(2)}, u32[]{:S(2)}) collective-permute-start(f32[256,256]{1,0:T(8,128)S(1)} %get-tuple-element.52), channel_id=1, source_target_pairs={{0,48},{1,13},{2,50},{3,15},{4,52},{5,1},{6,54},{7,3},{8,56},{9,5}... | collective-permute-start | bytes 786440 | tf_op jit(solution)/shard_map/ppermute | solution.py:43
  71.1 2.7 %collective-permute-start.28 = (f16[384,256]{1,0:T(8,128)(2,1)S(1)}, f16[384,256]{1,0:T(8,128)(2,1)S(1)}, u32[]{:S(2)}, u32[]{:S(2)}) collective-permute-start(f16[384,256]{1,0:T(8,128)(2,1)S(1)} %get-tuple-element.69), channel_id=1, source_target_pairs={{0,66},{1,3},{2,64},{3,1},{4,70},{5,7},{6,68},{7,5},{8,74},{9,11},... | collective-permute-start | bytes 589832 | tf_op jit(solution)/shard_map/ppermute | solution.py:43
  73.9 3.9 %collective-permute-done.21 = f16[512,256]{1,0:T(8,128)(2,1)S(1)} collective-permute-done((f16[512,256]{1,0:T(8,128)(2,1)S(1)}, f16[512,256]{1,0:T(8,128)(2,1)S(1)}, u32[]{:S(2)}, u32[]{:S(2)}) %collective-permute-start.21) | collective-permute-done | bytes 262176 | tf_op jit(solution)/shard_map/ppermute | solution.py:43
  77.9 1.1 %collective-permute-start.22 = (f16[512,256]{1,0:T(8,128)(2,1)S(1)}, f16[512,256]{1,0:T(8,128)(2,1)S(1)}, u32[]{:S(2)}, u32[]{:S(2)}) collective-permute-start(f16[512,256]{1,0:T(8,128)(2,1)S(1)} %collective-permute-done.21), channel_id=1, source_target_pairs={{0,1},{1,0},{2,3},{3,2},{4,5},{5,4},{6,7},{7,6},{8,9},{9,8},{10,11... | collective-permute-start | bytes 786440 | tf_op jit(solution)/shard_map/ppermute | solution.py:43
  80.2 1.4 %collective-permute-start.29 = (f32[384,256]{1,0:T(8,128)S(1)}, f32[384,256]{1,0:T(8,128)S(1)}, u32[]{:S(2)}, u32[]{:S(2)}) collective-permute-start(f32[384,256]{1,0:T(8,128)S(1)} %get-tuple-element.56), channel_id=1, source_target_pairs={{0,32},{1,9},{2,34},{3,11},{4,36},{5,13},{6,38},{7,15},{8,40},{9,1... | collective-permute-start | bytes 1179656 | tf_op jit(solution)/shard_map/ppermute | solution.py:43
  82.4 2.6 %shard_map.429 = (f32[2048,256]{1,0:T(8,128)S(1)}, f32[2048,256]{1,0:T(8,128)}) custom-call(s32[5]{0:T(128)S(1)} %stack.23.place, f32[2048,256]{1,0:T(8,128)S(1)} %copy-done, f32[384,256]{1,0:T(8,128)S(1)} %get-tuple-element.50.refs_0_, f32[384,256]{1,0:T(8,128)S(1)} %collective-permute-done.20.refs_1_, f32[512,256]{1,0:T(8,128)S(1)} %get-tuple-element.76.refs_2_, ...), custom_call_target="tpu_custom_call" | custom-call | bytes 2097152 | tf_op jit(solution)/shard_map/pallas_call | solution.py:289
  84.9 3.8 %collective-permute-done.29.refs_0_ = f32[384,256]{1,0:T(8,128)S(1)} collective-permute-done((f32[384,256]{1,0:T(8,128)S(1)}, f32[384,256]{1,0:T(8,128)S(1)}, u32[]{:S(2)}, u32[]{:S(2)}) %collective-permute-start.29) | collective-permute-done | bytes 393248 | tf_op jit(solution)/shard_map/ppermute | solution.py:43
  88.7 3.7 %collective-permute-start.30 = (f32[384,256]{1,0:T(8,128)S(1)}, f32[384,256]{1,0:T(8,128)S(1)}, u32[]{:S(2)}, u32[]{:S(2)}) collective-permute-start(f32[384,256]{1,0:T(8,128)S(1)} %collective-permute-done.29.refs_0_), channel_id=1, source_target_pairs={{0,1},{1,0},{2,3},{3,2},{4,5},{5,4},{6,7},{7,6},{8,9},{9,8},{10,11... | collective-permute-start | bytes 1179656 | tf_op jit(solution)/shard_map/ppermute | solution.py:43
  92.5 1.5 %collective-permute-done.32 = f16[256,256]{1,0:T(8,128)(2,1)S(1)} collective-permute-done((f16[256,256]{1,0:T(8,128)(2,1)S(1)}, f16[256,256]{1,0:T(8,128)(2,1)S(1)}, u32[]{:S(2)}, u32[]{:S(2)}) %collective-permute-start.32) | collective-permute-done | bytes 131104 | tf_op jit(solution)/shard_map/ppermute | solution.py:43
  94.1 1.7 %shard_map.431 = f32[2048,256]{1,0:T(8,128)} custom-call(s32[5]{0:T(128)S(1)} %stack.23.place, f32[2048,256]{1,0:T(8,128)S(1)} %get-tuple-element.54.base, f32[384,256]{1,0:T(8,128)S(1)} %collective-permute-done.29.refs_0_, f32[384,256]{1,0:T(8,128)S(1)} %collective-permute-done.30.refs_1_, ...), custom_call_target="tpu_custom_call", output_to_operand_aliasing={{}: (6, {})} | custom-call | bytes 2097152 | tf_op jit(solution)/shard_map/pallas_call | solution.py:300
  (93 shorter events, 13.3 us)
Async XLA Ops:
  1.3 3.5 %collective-permute-start = (bf16[256,896]{1,0:T(8,128)(2,1)S(1)}, bf16[256,896]{1,0:T(8,128)(2,1)S(1)}, u32[]{:S(2)}, u32[]{:S(2)}) collective-permute-start(bf16[256,896]{1,0:T(8,128)(2,1)S(1)} %get-tuple-element.66), channel_id=1, source_target_pairs={{0,1},{1,0},{2,3},{3,2},{4,5},{5,4},{6,7},{7,6},{8,9},{9,8},{10,11... | collective-permute-start | bytes 1376264 | tf_op jit(solution)/shard_map/ppermute | solution.py:43
  2.1 13.6 %collective-permute-start.2 = (bf16[256,896]{1,0:T(8,128)(2,1)S(1)}, bf16[256,896]{1,0:T(8,128)(2,1)S(1)}, u32[]{:S(2)}, u32[]{:S(2)}) collective-permute-start(bf16[256,896]{1,0:T(8,128)(2,1)S(1)} %get-tuple-element.65), channel_id=1, source_target_pairs={{0,64},{1,65},{2,66},{3,67},{4,68},{5,69},{6,70},{7,71},{8,72},{9,... | collective-permute-start | bytes 1376264 | tf_op jit(solution)/shard_map/ppermute | solution.py:43
  5.0 13.1 %collective-permute-start.1 = (bf16[256,1792]{1,0:T(8,128)(2,1)S(1)}, bf16[256,1792]{1,0:T(8,128)(2,1)S(1)}, u32[]{:S(2)}, u32[]{:S(2)}) collective-permute-start(bf16[256,1792]{1,0:T(8,128)(2,1)S(1)} %pad_maximum_fusion.refs_0_.refs_8_), channel_id=1, source_target_pairs={{0,48},{1,13},{2,50},{3,15},{4,52},{5,1},{6,54},{7,3},{8,56},{9,5}... | collective-permute-start | bytes 2752520 | tf_op jit(solution)/shard_map/ppermute | solution.py:43
  7.8 13.8 %collective-permute-start.4 = (bf16[256,1792]{1,0:T(8,128)(2,1)S(1)}, bf16[256,1792]{1,0:T(8,128)(2,1)S(1)}, u32[]{:S(2)}, u32[]{:S(2)}) collective-permute-start(bf16[256,1792]{1,0:T(8,128)(2,1)S(1)} %pad_maximum_fusion.refs_0_.refs_8_), channel_id=1, source_target_pairs={{0,16},{1,5},{2,18},{3,7},{4,20},{5,9},{6,22},{7,11},{8,24},{9,13}... | collective-permute-start | bytes 2752520 | tf_op jit(solution)/shard_map/ppermute | solution.py:43
  15.7 2.3 %collective-permute-start.3 = (bf16[256,896]{1,0:T(8,128)(2,1)S(1)}, bf16[256,896]{1,0:T(8,128)(2,1)S(1)}, u32[]{:S(2)}, u32[]{:S(2)}) collective-permute-start(bf16[256,896]{1,0:T(8,128)(2,1)S(1)} %collective-permute-done.2), channel_id=1, source_target_pairs={{0,1},{1,0},{2,3},{3,2},{4,5},{5,4},{6,7},{7,6},{8,9},{9,8},{10,11... | collective-permute-start | bytes 1376264 | tf_op jit(solution)/shard_map/ppermute | solution.py:43
  21.7 12.6 %collective-permute-start.5 = (bf16[256,1792]{1,0:T(8,128)(2,1)S(1)}, bf16[256,1792]{1,0:T(8,128)(2,1)S(1)}, u32[]{:S(2)}, u32[]{:S(2)}) collective-permute-start(bf16[256,1792]{1,0:T(8,128)(2,1)S(1)} %pad_maximum_fusion.1.refs_1_.refs_9_), channel_id=1, source_target_pairs={{0,48},{1,13},{2,50},{3,15},{4,52},{5,1},{6,54},{7,3},{8,56},{9,5}... | collective-permute-start | bytes 2752520 | tf_op jit(solution)/shard_map/ppermute | solution.py:43
  21.8 13.8 %collective-permute-start.6 = (bf16[256,1792]{1,0:T(8,128)(2,1)S(1)}, bf16[256,1792]{1,0:T(8,128)(2,1)S(1)}, u32[]{:S(2)}, u32[]{:S(2)}) collective-permute-start(bf16[256,1792]{1,0:T(8,128)(2,1)S(1)} %pad_maximum_fusion.1.refs_1_.refs_9_), channel_id=1, source_target_pairs={{0,16},{1,5},{2,18},{3,7},{4,20},{5,9},{6,22},{7,11},{8,24},{9,13}... | collective-permute-start | bytes 2752520 | tf_op jit(solution)/shard_map/ppermute | solution.py:43
  25.2 4.2 %collective-permute-start.7 = (f16[2,128,256]{2,1,0:T(8,128)(2,1)S(1)}, f16[2,128,256]{2,1,0:T(8,128)(2,1)S(1)}, u32[]{:S(2)}, u32[]{:S(2)}) collective-permute-start(f16[2,128,256]{2,1,0:T(8,128)(2,1)S(1)} %fusion.18), channel_id=1, source_target_pairs={{0,2},{1,67},{2,0},{3,65},{4,6},{5,71},{6,4},{7,69},{8,10},{9,75},... | collective-permute-start | bytes 393224 | tf_op jit(solution)/shard_map/ppermute | solution.py:43
  25.7 12.0 %collective-permute-start.9 = (bf16[256,1792]{1,0:T(8,128)(2,1)S(1)}, bf16[256,1792]{1,0:T(8,128)(2,1)S(1)}, u32[]{:S(2)}, u32[]{:S(2)}) collective-permute-start(bf16[256,1792]{1,0:T(8,128)(2,1)S(1)} %collective-permute-done.1.refs_0_), channel_id=1, source_target_pairs={{0,1},{1,0},{2,3},{3,2},{4,5},{5,4},{6,7},{7,6},{8,9},{9,8},{10,11... | collective-permute-start | bytes 2752520 | tf_op jit(solution)/shard_map/ppermute | solution.py:43
  28.1 12.3 %collective-permute-start.11 = (bf16[256,1792]{1,0:T(8,128)(2,1)S(1)}, bf16[256,1792]{1,0:T(8,128)(2,1)S(1)}, u32[]{:S(2)}, u32[]{:S(2)}) collective-permute-start(bf16[256,1792]{1,0:T(8,128)(2,1)S(1)} %collective-permute-done.4.refs_2_), channel_id=1, source_target_pairs={{0,1},{1,0},{2,3},{3,2},{4,5},{5,4},{6,7},{7,6},{8,9},{9,8},{10,11... | collective-permute-start | bytes 2752520 | tf_op jit(solution)/shard_map/ppermute | solution.py:43
  29.6 4.0 %collective-permute-start.8 = (f16[128,256]{1,0:T(8,128)(2,1)S(1)}, f16[128,256]{1,0:T(8,128)(2,1)S(1)}, u32[]{:S(2)}, u32[]{:S(2)}) collective-permute-start(f16[128,256]{1,0:T(8,128)(2,1)S(1)} %get-tuple-element.72), channel_id=1, source_target_pairs={{0,66},{1,3},{2,64},{3,1},{4,70},{5,7},{6,68},{7,5},{8,74},{9,11},... | collective-permute-start | bytes 196616 | tf_op jit(solution)/shard_map/ppermute | solution.py:43
  35.6 4.8 %collective-permute-start.10 = (bf16[256,1792]{1,0:T(8,128)(2,1)S(1)}, bf16[256,1792]{1,0:T(8,128)(2,1)S(1)}, u32[]{:S(2)}, u32[]{:S(2)}) collective-permute-start(bf16[256,1792]{1,0:T(8,128)(2,1)S(1)} %collective-permute-done.5.refs_1_), channel_id=1, source_target_pairs={{0,1},{1,0},{2,3},{3,2},{4,5},{5,4},{6,7},{7,6},{8,9},{9,8},{10,11... | collective-permute-start | bytes 2752520 | tf_op jit(solution)/shard_map/ppermute | solution.py:43
  37.7 3.4 %collective-permute-start.12 = (bf16[256,1792]{1,0:T(8,128)(2,1)S(1)}, bf16[256,1792]{1,0:T(8,128)(2,1)S(1)}, u32[]{:S(2)}, u32[]{:S(2)}) collective-permute-start(bf16[256,1792]{1,0:T(8,128)(2,1)S(1)} %collective-permute-done.6.refs_3_), channel_id=1, source_target_pairs={{0,1},{1,0},{2,3},{3,2},{4,5},{5,4},{6,7},{7,6},{8,9},{9,8},{10,11... | collective-permute-start | bytes 2752520 | tf_op jit(solution)/shard_map/ppermute | solution.py:43
  37.7 13.1 %collective-permute-start.15 = (bf16[256,1792]{1,0:T(8,128)(2,1)S(1)}, bf16[256,1792]{1,0:T(8,128)(2,1)S(1)}, u32[]{:S(2)}, u32[]{:S(2)}) collective-permute-start(bf16[256,1792]{1,0:T(8,128)(2,1)S(1)} %collective-permute-done.1.refs_0_), channel_id=1, source_target_pairs={{0,48},{1,13},{2,50},{3,15},{4,52},{5,1},{6,54},{7,3},{8,56},{9,5}... | collective-permute-start | bytes 2752520 | tf_op jit(solution)/shard_map/ppermute | solution.py:43
  40.5 13.5 %collective-permute-start.16 = (bf16[256,1792]{1,0:T(8,128)(2,1)S(1)}, bf16[256,1792]{1,0:T(8,128)(2,1)S(1)}, u32[]{:S(2)}, u32[]{:S(2)}) collective-permute-start(bf16[256,1792]{1,0:T(8,128)(2,1)S(1)} %collective-permute-done.6.refs_3_), channel_id=1, source_target_pairs={{0,16},{1,5},{2,18},{3,7},{4,20},{5,9},{6,22},{7,11},{8,24},{9,13}... | collective-permute-start | bytes 2752520 | tf_op jit(solution)/shard_map/ppermute | solution.py:43
  45.1 8.8 %collective-permute-start.13 = (f16[768,256]{1,0:T(8,128)(2,1)S(1)}, f16[768,256]{1,0:T(8,128)(2,1)S(1)}, u32[]{:S(2)}, u32[]{:S(2)}) collective-permute-start(f16[768,256]{1,0:T(8,128)(2,1)S(1)} %fusion.2), channel_id=1, source_target_pairs={{0,2},{1,67},{2,0},{3,65},{4,6},{5,71},{6,4},{7,69},{8,10},{9,75},... | collective-permute-start | bytes 1179656 | tf_op jit(solution)/shard_map/ppermute | solution.py:43
  54.0 5.1 %collective-permute-start.17 = (bf16[128,1792]{1,0:T(8,128)(2,1)S(1)}, bf16[128,1792]{1,0:T(8,128)(2,1)S(1)}, u32[]{:S(2)}, u32[]{:S(2)}) collective-permute-start(bf16[128,1792]{1,0:T(8,128)(2,1)S(1)} %slice_select_fusion.1), channel_id=1, source_target_pairs={{0,1},{1,0},{2,3},{3,2},{4,5},{5,4},{6,7},{7,6},{8,9},{9,8},{10,11... | collective-permute-start | bytes 1376264 | tf_op jit(solution)/shard_map/ppermute | solution.py:43
  54.1 4.9 %collective-permute-start.18 = (bf16[128,1792]{1,0:T(8,128)(2,1)S(1)}, bf16[128,1792]{1,0:T(8,128)(2,1)S(1)}, u32[]{:S(2)}, u32[]{:S(2)}) collective-permute-start(bf16[128,1792]{1,0:T(8,128)(2,1)S(1)} %slice_select_fusion), channel_id=1, source_target_pairs={{0,1},{1,0},{2,3},{3,2},{4,5},{5,4},{6,7},{7,6},{8,9},{9,8},{10,11... | collective-permute-start | bytes 1376264 | tf_op jit(solution)/shard_map/ppermute | solution.py:43
  55.1 7.5 %collective-permute-start.19 = (f16[768,256]{1,0:T(8,128)(2,1)S(1)}, f16[768,256]{1,0:T(8,128)(2,1)S(1)}, u32[]{:S(2)}, u32[]{:S(2)}) collective-permute-start(f16[768,256]{1,0:T(8,128)(2,1)S(1)} %get-tuple-element.61), channel_id=1, source_target_pairs={{0,66},{1,3},{2,64},{3,1},{4,70},{5,7},{6,68},{7,5},{8,74},{9,11},... | collective-permute-start | bytes 1179656 | tf_op jit(solution)/shard_map/ppermute | solution.py:43
  57.9 8.8 %collective-permute-start.14 = (f16[768,256]{1,0:T(8,128)(2,1)S(1)}, f16[768,256]{1,0:T(8,128)(2,1)S(1)}, u32[]{:S(2)}, u32[]{:S(2)}) collective-permute-start(f16[768,256]{1,0:T(8,128)(2,1)S(1)} %get-tuple-element.40), channel_id=1, source_target_pairs={{0,2},{1,67},{2,0},{3,65},{4,6},{5,71},{6,4},{7,69},{8,10},{9,75},... | collective-permute-start | bytes 1179656 | tf_op jit(solution)/shard_map/ppermute | solution.py:43
  61.1 9.7 %collective-permute-start.27 = (f16[2,384,256]{2,1,0:T(8,128)(2,1)S(1)}, f16[2,384,256]{2,1,0:T(8,128)(2,1)S(1)}, u32[]{:S(2)}, u32[]{:S(2)}) collective-permute-start(f16[2,384,256]{2,1,0:T(8,128)(2,1)S(1)} %fusion.11), channel_id=1, source_target_pairs={{0,2},{1,67},{2,0},{3,65},{4,6},{5,71},{6,4},{7,69},{8,10},{9,75},... | collective-permute-start | bytes 1179656 | tf_op jit(solution)/shard_map/ppermute | solution.py:43
  67.9 9.9 %collective-permute-start.21 = (f16[512,256]{1,0:T(8,128)(2,1)S(1)}, f16[512,256]{1,0:T(8,128)(2,1)S(1)}, u32[]{:S(2)}, u32[]{:S(2)}) collective-permute-start(f16[512,256]{1,0:T(8,128)(2,1)S(1)} %multiply_convert_fusion), channel_id=1, source_target_pairs={{0,16},{1,5},{2,80},{3,69},{4,20},{5,9},{6,84},{7,73},{8,24},{9,13... | collective-permute-start | bytes 786440 | tf_op jit(solution)/shard_map/ppermute | solution.py:43
  68.8 10.2 %collective-permute-start.23 = (f32[256,256]{1,0:T(8,128)S(1)}, f32[256,256]{1,0:T(8,128)S(1)}, u32[]{:S(2)}, u32[]{:S(2)}) collective-permute-start(f32[256,256]{1,0:T(8,128)S(1)} %get-tuple-element.52), channel_id=1, source_target_pairs={{0,48},{1,13},{2,50},{3,15},{4,52},{5,1},{6,54},{7,3},{8,56},{9,5}... | collective-permute-start | bytes 786440 | tf_op jit(solution)/shard_map/ppermute | solution.py:43
  70.8 8.2 %collective-permute-start.25 = (f32[256,256]{1,0:T(8,128)S(1)}, f32[256,256]{1,0:T(8,128)S(1)}, u32[]{:S(2)}, u32[]{:S(2)}) collective-permute-start(f32[256,256]{1,0:T(8,128)S(1)} %get-tuple-element.53), channel_id=1, source_target_pairs={{0,4},{1,49},{2,6},{3,51},{4,8},{5,53},{6,10},{7,55},{8,12},{9,57}... | collective-permute-start | bytes 786440 | tf_op jit(solution)/shard_map/ppermute | solution.py:43
  71.1 8.4 %collective-permute-start.28 = (f16[384,256]{1,0:T(8,128)(2,1)S(1)}, f16[384,256]{1,0:T(8,128)(2,1)S(1)}, u32[]{:S(2)}, u32[]{:S(2)}) collective-permute-start(f16[384,256]{1,0:T(8,128)(2,1)S(1)} %get-tuple-element.69), channel_id=1, source_target_pairs={{0,66},{1,3},{2,64},{3,1},{4,70},{5,7},{6,68},{7,5},{8,74},{9,11},... | collective-permute-start | bytes 589832 | tf_op jit(solution)/shard_map/ppermute | solution.py:43
  73.8 8.5 %collective-permute-start.20 = (f32[384,256]{1,0:T(8,128)S(1)}, f32[384,256]{1,0:T(8,128)S(1)}, u32[]{:S(2)}, u32[]{:S(2)}) collective-permute-start(f32[384,256]{1,0:T(8,128)S(1)} %get-tuple-element.50.refs_0_), channel_id=1, source_target_pairs={{0,1},{1,0},{2,3},{3,2},{4,5},{5,4},{6,7},{7,6},{8,9},{9,8},{10,11... | collective-permute-start | bytes 1179656 | tf_op jit(solution)/shard_map/ppermute | solution.py:43
  77.9 3.8 %collective-permute-start.22 = (f16[512,256]{1,0:T(8,128)(2,1)S(1)}, f16[512,256]{1,0:T(8,128)(2,1)S(1)}, u32[]{:S(2)}, u32[]{:S(2)}) collective-permute-start(f16[512,256]{1,0:T(8,128)(2,1)S(1)} %collective-permute-done.21), channel_id=1, source_target_pairs={{0,1},{1,0},{2,3},{3,2},{4,5},{5,4},{6,7},{7,6},{8,9},{9,8},{10,11... | collective-permute-start | bytes 786440 | tf_op jit(solution)/shard_map/ppermute | solution.py:43
  78.9 3.4 %collective-permute-start.24 = (f32[256,256]{1,0:T(8,128)S(1)}, f32[256,256]{1,0:T(8,128)S(1)}, u32[]{:S(2)}, u32[]{:S(2)}) collective-permute-start(f32[256,256]{1,0:T(8,128)S(1)} %collective-permute-done.23.refs_4_), channel_id=1, source_target_pairs={{0,1},{1,0},{2,3},{3,2},{4,5},{5,4},{6,7},{7,6},{8,9},{9,8},{10,11... | collective-permute-start | bytes 786440 | tf_op jit(solution)/shard_map/ppermute | solution.py:43
  78.9 3.4 %collective-permute-start.26 = (f32[256,256]{1,0:T(8,128)S(1)}, f32[256,256]{1,0:T(8,128)S(1)}, u32[]{:S(2)}, u32[]{:S(2)}) collective-permute-start(f32[256,256]{1,0:T(8,128)S(1)} %collective-permute-done.25.refs_6_), channel_id=1, source_target_pairs={{0,1},{1,0},{2,3},{3,2},{4,5},{5,4},{6,7},{7,6},{8,9},{9,8},{10,11... | collective-permute-start | bytes 786440 | tf_op jit(solution)/shard_map/ppermute | solution.py:43
  80.2 8.5 %collective-permute-start.29 = (f32[384,256]{1,0:T(8,128)S(1)}, f32[384,256]{1,0:T(8,128)S(1)}, u32[]{:S(2)}, u32[]{:S(2)}) collective-permute-start(f32[384,256]{1,0:T(8,128)S(1)} %get-tuple-element.56), channel_id=1, source_target_pairs={{0,32},{1,9},{2,34},{3,11},{4,36},{5,13},{6,38},{7,15},{8,40},{9,1... | collective-permute-start | bytes 1179656 | tf_op jit(solution)/shard_map/ppermute | solution.py:43
  81.7 10.8 %collective-permute-start.31 = (f16[256,256]{1,0:T(8,128)(2,1)S(1)}, f16[256,256]{1,0:T(8,128)(2,1)S(1)}, u32[]{:S(2)}, u32[]{:S(2)}) collective-permute-start(f16[256,256]{1,0:T(8,128)(2,1)S(1)} %multiply_convert_fusion.1), channel_id=1, source_target_pairs={{0,12},{1,17},{2,76},{3,81},{4,0},{5,21},{6,64},{7,85},{8,4},{9,25... | collective-permute-start | bytes 393224 | tf_op jit(solution)/shard_map/ppermute | solution.py:43
  88.7 5.4 %collective-permute-start.30 = (f32[384,256]{1,0:T(8,128)S(1)}, f32[384,256]{1,0:T(8,128)S(1)}, u32[]{:S(2)}, u32[]{:S(2)}) collective-permute-start(f32[384,256]{1,0:T(8,128)S(1)} %collective-permute-done.29.refs_0_), channel_id=1, source_target_pairs={{0,1},{1,0},{2,3},{3,2},{4,5},{5,4},{6,7},{7,6},{8,9},{9,8},{10,11... | collective-permute-start | bytes 1179656 | tf_op jit(solution)/shard_map/ppermute | solution.py:43
  (14 other events, 93.5 us)

commit v5 on v4

--- a/solution.py
+++ b/solution.py
@@ -156,7 +156,7 @@
     outs = call(functools.partial(finish, sums), [(sum(size for size, _ in m), 256) for m in sums], place, *arrays)
     kept = []
     for ((to, turned), parts), out in zip(messages.items(), outs, strict=True):
-        if turned:
+        if turned or to == "a2":
             out = packed(out)
         if to != "s":
             out = send(out, to_place(to, turned))

time: 97.7 us -> 95.2 us (0.974)
  starting transfers between devices: 34.9 us -> 31.9 us
    ppermute x33, starting transfers between devices: 34.9 us -> 31.9 us  [send(): return lax.ppermute(value, AXES, pairs)]
  transfers between devices with their start and end apart: 33 -> 33, of which waited for: 16 -> 17; matrix products, arithmetic and copies ran while one was open for 2% -> 3% of each run, Pallas kernels for 14% -> 14%
where the time goes in v5:
time: 95.2 us; the launch traced here: 93.5 us
  waiting for transfers between devices  41.9 us (44%)
  starting transfers between devices  31.9 us (34%)
  Pallas kernels  15 us (16%)
  other arithmetic  2.7 us (3%)
  local copies, waits for them, and re-layouts  1.49 us (2%)
    ppermute x33, waiting for transfers between devices, send(): return lax.ppermute(value, AXES, pairs)  41.9 us
    ppermute x33, starting transfers between devices, send(): return lax.ppermute(value, AXES, pairs)  31.9 us
    pallas_call x6, Pallas kernels, call(): pl.pallas_call(kernel, out_shape=[pltpu.VMEM(s, jnp.float32) if keep else...  10.7 us
    pallas_call x1, Pallas kernels, body(): pl.pallas_call(functools.partial(begin, layouts), out_shape=[pltpu.VMEM(s...  2.56 us
  transfers between devices with their start and end apart: 33, of which 17 were waited for; matrix products, arithmetic and copies ran while one was open for 3% of the time, Pallas kernels for 14%

profile of v5, /device:TPU:33, one launch (start us, length us, event | category | flops | bytes accessed | tf_op | source)
XLA Modules:
  0.0 93.5 jit_solution(13130844461871797459)
XLA Ops:
  0.1 1.2 %constant_dynamic-slice_fusion = (bf16[256,896]{1,0:T(8,128)(2,1)S(1)}, bf16[256,896]{1,0:T(8,128)(2,1)S(1)}) fusion(bf16[256,1792]{1,0:T(8,128)(2,1)} %param.52, s32[]{:T(128)S(6)} %select_n.42, s32[]{:T(128)S(6)} %select_n.39), kind=kLoop, calls=%fused_computation.63 | loop fusion | bytes 1835016 | tf_op jit(solution)/shard_map/dynamic_slice | solution.py:240
  2.1 2.7 %collective-permute-start.2 = (bf16[256,896]{1,0:T(8,128)(2,1)S(1)}, bf16[256,896]{1,0:T(8,128)(2,1)S(1)}, u32[]{:S(2)}, u32[]{:S(2)}) collective-permute-start(bf16[256,896]{1,0:T(8,128)(2,1)S(1)} %get-tuple-element.65), channel_id=1, source_target_pairs={{0,64},{1,65},{2,66},{3,67},{4,68},{5,69},{6,70},{7,71},{8,72},{9,... | collective-permute-start | bytes 1376264 | tf_op jit(solution)/shard_map/ppermute | solution.py:43
  5.0 2.8 %collective-permute-start.1 = (bf16[256,1792]{1,0:T(8,128)(2,1)S(1)}, bf16[256,1792]{1,0:T(8,128)(2,1)S(1)}, u32[]{:S(2)}, u32[]{:S(2)}) collective-permute-start(bf16[256,1792]{1,0:T(8,128)(2,1)S(1)} %pad_maximum_fusion.refs_0_.refs_8_), channel_id=1, source_target_pairs={{0,48},{1,13},{2,50},{3,15},{4,52},{5,1},{6,54},{7,3},{8,56},{9,5}... | collective-permute-start | bytes 2752520 | tf_op jit(solution)/shard_map/ppermute | solution.py:43
  7.8 7.9 %collective-permute-done.2 = bf16[256,896]{1,0:T(8,128)(2,1)S(1)} collective-permute-done((bf16[256,896]{1,0:T(8,128)(2,1)S(1)}, bf16[256,896]{1,0:T(8,128)(2,1)S(1)}, u32[]{:S(2)}, u32[]{:S(2)}) %collective-permute-start.2) | collective-permute-done | bytes 458784 | tf_op jit(solution)/shard_map/ppermute | solution.py:43
  16.5 1.4 %collective-permute-done.3 = bf16[256,896]{1,0:T(8,128)(2,1)S(1)} collective-permute-done((bf16[256,896]{1,0:T(8,128)(2,1)S(1)}, bf16[256,896]{1,0:T(8,128)(2,1)S(1)}, u32[]{:S(2)}, u32[]{:S(2)}) %collective-permute-start.3) | collective-permute-done | bytes 458784 | tf_op jit(solution)/shard_map/ppermute | solution.py:43
  18.1 3.4 %collective-permute-done.4.refs_2_ = bf16[256,1792]{1,0:T(8,128)(2,1)S(1)} collective-permute-done((bf16[256,1792]{1,0:T(8,128)(2,1)S(1)}, bf16[256,1792]{1,0:T(8,128)(2,1)S(1)}, u32[]{:S(2)}, u32[]{:S(2)}) %collective-permute-start.4) | collective-permute-done | bytes 917536 | tf_op jit(solution)/shard_map/ppermute | solution.py:43
  21.8 1.5 %collective-permute-start.6 = (bf16[256,1792]{1,0:T(8,128)(2,1)S(1)}, bf16[256,1792]{1,0:T(8,128)(2,1)S(1)}, u32[]{:S(2)}, u32[]{:S(2)}) collective-permute-start(bf16[256,1792]{1,0:T(8,128)(2,1)S(1)} %pad_maximum_fusion.1.refs_1_.refs_9_), channel_id=1, source_target_pairs={{0,16},{1,5},{2,18},{3,7},{4,20},{5,9},{6,22},{7,11},{8,24},{9,13}... | collective-permute-start | bytes 2752520 | tf_op jit(solution)/shard_map/ppermute | solution.py:43
  23.3 1.8 %shard_map.478.refs_3_ = f32[4,128,256]{2,1,0:T(8,128)S(1)} custom-call(s32[5]{0:T(128)S(1)} %stack.23.place, bf16[256,1792]{1,0:T(8,128)(2,1)S(1)} %pad_maximum_fusion.refs_0_.refs_8_, bf16[256,1792]{1,0:T(8,128)(2,1)S(1)} %pad_maximum_fusion.1.refs_1_.refs_9_), custom_call_target="tpu_custom_call" | custom-call | tf_op jit(solution)/shard_map/pallas_call | solution.py:87
  25.7 2.4 %collective-permute-start.9 = (bf16[256,1792]{1,0:T(8,128)(2,1)S(1)}, bf16[256,1792]{1,0:T(8,128)(2,1)S(1)}, u32[]{:S(2)}, u32[]{:S(2)}) collective-permute-start(bf16[256,1792]{1,0:T(8,128)(2,1)S(1)} %collective-permute-done.1.refs_0_), channel_id=1, source_target_pairs={{0,1},{1,0},{2,3},{3,2},{4,5},{5,4},{6,7},{7,6},{8,9},{9,8},{10,11... | collective-permute-start | bytes 2752520 | tf_op jit(solution)/shard_map/ppermute | solution.py:43
  28.1 1.3 %collective-permute-done.7 = f16[2,128,256]{2,1,0:T(8,128)(2,1)S(1)} collective-permute-done((f16[2,128,256]{2,1,0:T(8,128)(2,1)S(1)}, f16[2,128,256]{2,1,0:T(8,128)(2,1)S(1)}, u32[]{:S(2)}, u32[]{:S(2)}) %collective-permute-start.7) | collective-permute-done | bytes 131104 | tf_op jit(solution)/shard_map/ppermute | solution.py:43
  29.6 2.0 %collective-permute-start.8 = (f16[128,256]{1,0:T(8,128)(2,1)S(1)}, f16[128,256]{1,0:T(8,128)(2,1)S(1)}, u32[]{:S(2)}, u32[]{:S(2)}) collective-permute-start(f16[128,256]{1,0:T(8,128)(2,1)S(1)} %get-tuple-element.72), channel_id=1, source_target_pairs={{0,66},{1,3},{2,64},{3,1},{4,70},{5,7},{6,68},{7,5},{8,74},{9,11},... | collective-permute-start | bytes 196616 | tf_op jit(solution)/shard_map/ppermute | solution.py:43
  31.6 2.0 %collective-permute-done.8 = f16[128,256]{1,0:T(8,128)(2,1)S(1)} collective-permute-done((f16[128,256]{1,0:T(8,128)(2,1)S(1)}, f16[128,256]{1,0:T(8,128)(2,1)S(1)}, u32[]{:S(2)}, u32[]{:S(2)}) %collective-permute-start.8) | collective-permute-done | bytes 65568 | tf_op jit(solution)/shard_map/ppermute | solution.py:43
  34.3 1.3 %collective-permute-done.6.refs_3_ = bf16[256,1792]{1,0:T(8,128)(2,1)S(1)} collective-permute-done((bf16[256,1792]{1,0:T(8,128)(2,1)S(1)}, bf16[256,1792]{1,0:T(8,128)(2,1)S(1)}, u32[]{:S(2)}, u32[]{:S(2)}) %collective-permute-start.6) | collective-permute-done | bytes 917536 | tf_op jit(solution)/shard_map/ppermute | solution.py:43
  35.6 2.1 %collective-permute-start.10 = (bf16[256,1792]{1,0:T(8,128)(2,1)S(1)}, bf16[256,1792]{1,0:T(8,128)(2,1)S(1)}, u32[]{:S(2)}, u32[]{:S(2)}) collective-permute-start(bf16[256,1792]{1,0:T(8,128)(2,1)S(1)} %collective-permute-done.5.refs_1_), channel_id=1, source_target_pairs={{0,1},{1,0},{2,3},{3,2},{4,5},{5,4},{6,7},{7,6},{8,9},{9,8},{10,11... | collective-permute-start | bytes 2752520 | tf_op jit(solution)/shard_map/ppermute | solution.py:43
  37.7 2.7 %collective-permute-start.15 = (bf16[256,1792]{1,0:T(8,128)(2,1)S(1)}, bf16[256,1792]{1,0:T(8,128)(2,1)S(1)}, u32[]{:S(2)}, u32[]{:S(2)}) collective-permute-start(bf16[256,1792]{1,0:T(8,128)(2,1)S(1)} %collective-permute-done.1.refs_0_), channel_id=1, source_target_pairs={{0,48},{1,13},{2,50},{3,15},{4,52},{5,1},{6,54},{7,3},{8,56},{9,5}... | collective-permute-start | bytes 2752520 | tf_op jit(solution)/shard_map/ppermute | solution.py:43
  41.1 3.8 %shard_map.479.refs_0_ = f32[4,768,256]{2,1,0:T(8,128)S(1)} custom-call(s32[5]{0:T(128)S(1)} %stack.23.place, bf16[256,1792]{1,0:T(8,128)(2,1)S(1)} %collective-permute-done.1.refs_0_, bf16[256,1792]{1,0:T(8,128)(2,1)S(1)} %collective-permute-done.5.refs_1_, bf16[256,1792]{1,0:T(8,128)(2,1)S(1)} %collective-permute-done.4.refs_2_, ...), custom_call_target="tpu_custom_call" | custom-call | bytes 16777216 | tf_op jit(solution)/shard_map/pallas_call | solution.py:87
  45.7 5.1 %collective-permute-done.15.refs_0_ = bf16[256,1792]{1,0:T(8,128)(2,1)S(1)} collective-permute-done((bf16[256,1792]{1,0:T(8,128)(2,1)S(1)}, bf16[256,1792]{1,0:T(8,128)(2,1)S(1)}, u32[]{:S(2)}, u32[]{:S(2)}) %collective-permute-start.15) | collective-permute-done | bytes 917536 | tf_op jit(solution)/shard_map/ppermute | solution.py:43
  50.8 3.1 %collective-permute-done.16.refs_1_ = bf16[256,1792]{1,0:T(8,128)(2,1)S(1)} collective-permute-done((bf16[256,1792]{1,0:T(8,128)(2,1)S(1)}, bf16[256,1792]{1,0:T(8,128)(2,1)S(1)}, u32[]{:S(2)}, u32[]{:S(2)}) %collective-permute-start.16) | collective-permute-done | bytes 917536 | tf_op jit(solution)/shard_map/ppermute | solution.py:43
  55.1 0.9 %collective-permute-start.19 = (f16[768,256]{1,0:T(8,128)(2,1)S(1)}, f16[768,256]{1,0:T(8,128)(2,1)S(1)}, u32[]{:S(2)}, u32[]{:S(2)}) collective-permute-start(f16[768,256]{1,0:T(8,128)(2,1)S(1)} %get-tuple-element.61), channel_id=1, source_target_pairs={{0,66},{1,3},{2,64},{3,1},{4,70},{5,7},{6,68},{7,5},{8,74},{9,11},... | collective-permute-start | bytes 1179656 | tf_op jit(solution)/shard_map/ppermute | solution.py:43
  56.0 1.9 %shard_map.480.refs_0_ = f32[4,256,256]{2,1,0:T(8,128)S(1)} custom-call(s32[5]{0:T(128)S(1)} %stack.23.place, bf16[256,1792]{1,0:T(8,128)(2,1)S(1)} %collective-permute-done.15.refs_0_, bf16[256,1792]{1,0:T(8,128)(2,1)S(1)} %collective-permute-done.16.refs_1_, bf16[256,1792]{1,0:T(8,128)(2,1)S(1)} %collective-permute-done.9.refs_4_.refs_2_, ...), custom_call_target="tpu_custom_call" | custom-call | bytes 8388608 | tf_op jit(solution)/shard_map/pallas_call | solution.py:87
  57.9 1.1 %collective-permute-start.14 = (f16[768,256]{1,0:T(8,128)(2,1)S(1)}, f16[768,256]{1,0:T(8,128)(2,1)S(1)}, u32[]{:S(2)}, u32[]{:S(2)}) collective-permute-start(f16[768,256]{1,0:T(8,128)(2,1)S(1)} %get-tuple-element.40), channel_id=1, source_target_pairs={{0,2},{1,67},{2,0},{3,65},{4,6},{5,71},{6,4},{7,69},{8,10},{9,75},... | collective-permute-start | bytes 1179656 | tf_op jit(solution)/shard_map/ppermute | solution.py:43
  59.1 1.8 %shard_map.481.refs_1_ = f32[4,128,256]{2,1,0:T(8,128)S(1)} custom-call(s32[5]{0:T(128)S(1)} %stack.23.place, bf16[256,1792]{1,0:T(8,128)(2,1)S(1)} %collective-permute-done.15.refs_0_, bf16[256,1792]{1,0:T(8,128)(2,1)S(1)} %collective-permute-done.16.refs_1_, bf16[128,1792]{1,0:T(8,128)(2,1)S(1)} %collective-permute-done.17.refs_2_, ...), custom_call_target="tpu_custom_call" | custom-call | bytes 8388608 | tf_op jit(solution)/shard_map/pallas_call | solution.py:87
  61.7 0.9 collective-permute-done.19
  62.6 4.2 %collective-permute-done.14 = f16[768,256]{1,0:T(8,128)(2,1)S(1)} collective-permute-done((f16[768,256]{1,0:T(8,128)(2,1)S(1)}, f16[768,256]{1,0:T(8,128)(2,1)S(1)}, u32[]{:S(2)}, u32[]{:S(2)}) %collective-permute-start.14) | collective-permute-done | bytes 393248 | tf_op jit(solution)/shard_map/ppermute | solution.py:43
  68.8 2.0 %collective-permute-start.23 = (f32[256,256]{1,0:T(8,128)S(1)}, f32[256,256]{1,0:T(8,128)S(1)}, u32[]{:S(2)}, u32[]{:S(2)}) collective-permute-start(f32[256,256]{1,0:T(8,128)S(1)} %get-tuple-element.52), channel_id=1, source_target_pairs={{0,48},{1,13},{2,50},{3,15},{4,52},{5,1},{6,54},{7,3},{8,56},{9,5}... | collective-permute-start | bytes 786440 | tf_op jit(solution)/shard_map/ppermute | solution.py:43
  71.1 2.7 %collective-permute-start.28 = (f16[384,256]{1,0:T(8,128)(2,1)S(1)}, f16[384,256]{1,0:T(8,128)(2,1)S(1)}, u32[]{:S(2)}, u32[]{:S(2)}) collective-permute-start(f16[384,256]{1,0:T(8,128)(2,1)S(1)} %get-tuple-element.69), channel_id=1, source_target_pairs={{0,66},{1,3},{2,64},{3,1},{4,70},{5,7},{6,68},{7,5},{8,74},{9,11},... | collective-permute-start | bytes 589832 | tf_op jit(solution)/shard_map/ppermute | solution.py:43
  73.9 3.9 %collective-permute-done.21 = f16[512,256]{1,0:T(8,128)(2,1)S(1)} collective-permute-done((f16[512,256]{1,0:T(8,128)(2,1)S(1)}, f16[512,256]{1,0:T(8,128)(2,1)S(1)}, u32[]{:S(2)}, u32[]{:S(2)}) %collective-permute-start.21) | collective-permute-done | bytes 262176 | tf_op jit(solution)/shard_map/ppermute | solution.py:43
  77.9 1.1 %collective-permute-start.22 = (f16[512,256]{1,0:T(8,128)(2,1)S(1)}, f16[512,256]{1,0:T(8,128)(2,1)S(1)}, u32[]{:S(2)}, u32[]{:S(2)}) collective-permute-start(f16[512,256]{1,0:T(8,128)(2,1)S(1)} %collective-permute-done.21), channel_id=1, source_target_pairs={{0,1},{1,0},{2,3},{3,2},{4,5},{5,4},{6,7},{7,6},{8,9},{9,8},{10,11... | collective-permute-start | bytes 786440 | tf_op jit(solution)/shard_map/ppermute | solution.py:43
  80.4 1.4 %collective-permute-start.29 = (f16[384,256]{1,0:T(8,128)(2,1)S(1)}, f16[384,256]{1,0:T(8,128)(2,1)S(1)}, u32[]{:S(2)}, u32[]{:S(2)}) collective-permute-start(f16[384,256]{1,0:T(8,128)(2,1)S(1)} %multiply_convert_fusion.1), channel_id=1, source_target_pairs={{0,32},{1,9},{2,34},{3,11},{4,36},{5,13},{6,38},{7,15},{8,40},{9,1... | collective-permute-start | bytes 589832 | tf_op jit(solution)/shard_map/ppermute | solution.py:43
  82.5 2.6 %shard_map.483 = (f32[2048,256]{1,0:T(8,128)S(1)}, f32[2048,256]{1,0:T(8,128)}) custom-call(s32[5]{0:T(128)S(1)} %stack.23.place, f32[2048,256]{1,0:T(8,128)S(1)} %copy-done, f32[384,256]{1,0:T(8,128)S(1)} %get-tuple-element.50.refs_0_, f32[384,256]{1,0:T(8,128)S(1)} %collective-permute-done.20.refs_1_, f32[512,256]{1,0:T(8,128)S(1)} %get-tuple-element.78.refs_2_, ...), custom_call_target="tpu_custom_call" | custom-call | bytes 2097152 | tf_op jit(solution)/shard_map/pallas_call | solution.py:289
  85.1 4.7 %collective-permute-done.31 = f16[256,256]{1,0:T(8,128)(2,1)S(1)} collective-permute-done((f16[256,256]{1,0:T(8,128)(2,1)S(1)}, f16[256,256]{1,0:T(8,128)(2,1)S(1)}, u32[]{:S(2)}, u32[]{:S(2)}) %collective-permute-start.31) | collective-permute-done | bytes 131104 | tf_op jit(solution)/shard_map/ppermute | solution.py:43
  91.7 1.7 %shard_map.485 = f32[2048,256]{1,0:T(8,128)} custom-call(s32[5]{0:T(128)S(1)} %stack.23.place, f32[2048,256]{1,0:T(8,128)S(1)} %get-tuple-element.54.base, f32[384,256]{1,0:T(8,128)S(1)} %get-tuple-element.76.refs_0_, f32[384,256]{1,0:T(8,128)S(1)} %get-tuple-element.75.refs_1_, ...), custom_call_target="tpu_custom_call", output_to_operand_aliasing={{}: (6, {})} | custom-call | bytes 2097152 | tf_op jit(solution)/shard_map/pallas_call | solution.py:300
  (95 shorter events, 13.4 us)
Async XLA Ops:
  1.3 3.5 %collective-permute-start = (bf16[256,896]{1,0:T(8,128)(2,1)S(1)}, bf16[256,896]{1,0:T(8,128)(2,1)S(1)}, u32[]{:S(2)}, u32[]{:S(2)}) collective-permute-start(bf16[256,896]{1,0:T(8,128)(2,1)S(1)} %get-tuple-element.66), channel_id=1, source_target_pairs={{0,1},{1,0},{2,3},{3,2},{4,5},{5,4},{6,7},{7,6},{8,9},{9,8},{10,11... | collective-permute-start | bytes 1376264 | tf_op jit(solution)/shard_map/ppermute | solution.py:43
  2.1 13.6 %collective-permute-start.2 = (bf16[256,896]{1,0:T(8,128)(2,1)S(1)}, bf16[256,896]{1,0:T(8,128)(2,1)S(1)}, u32[]{:S(2)}, u32[]{:S(2)}) collective-permute-start(bf16[256,896]{1,0:T(8,128)(2,1)S(1)} %get-tuple-element.65), channel_id=1, source_target_pairs={{0,64},{1,65},{2,66},{3,67},{4,68},{5,69},{6,70},{7,71},{8,72},{9,... | collective-permute-start | bytes 1376264 | tf_op jit(solution)/shard_map/ppermute | solution.py:43
  5.0 13.1 %collective-permute-start.1 = (bf16[256,1792]{1,0:T(8,128)(2,1)S(1)}, bf16[256,1792]{1,0:T(8,128)(2,1)S(1)}, u32[]{:S(2)}, u32[]{:S(2)}) collective-permute-start(bf16[256,1792]{1,0:T(8,128)(2,1)S(1)} %pad_maximum_fusion.refs_0_.refs_8_), channel_id=1, source_target_pairs={{0,48},{1,13},{2,50},{3,15},{4,52},{5,1},{6,54},{7,3},{8,56},{9,5}... | collective-permute-start | bytes 2752520 | tf_op jit(solution)/shard_map/ppermute | solution.py:43
  7.8 13.8 %collective-permute-start.4 = (bf16[256,1792]{1,0:T(8,128)(2,1)S(1)}, bf16[256,1792]{1,0:T(8,128)(2,1)S(1)}, u32[]{:S(2)}, u32[]{:S(2)}) collective-permute-start(bf16[256,1792]{1,0:T(8,128)(2,1)S(1)} %pad_maximum_fusion.refs_0_.refs_8_), channel_id=1, source_target_pairs={{0,16},{1,5},{2,18},{3,7},{4,20},{5,9},{6,22},{7,11},{8,24},{9,13}... | collective-permute-start | bytes 2752520 | tf_op jit(solution)/shard_map/ppermute | solution.py:43
  15.7 2.3 %collective-permute-start.3 = (bf16[256,896]{1,0:T(8,128)(2,1)S(1)}, bf16[256,896]{1,0:T(8,128)(2,1)S(1)}, u32[]{:S(2)}, u32[]{:S(2)}) collective-permute-start(bf16[256,896]{1,0:T(8,128)(2,1)S(1)} %collective-permute-done.2), channel_id=1, source_target_pairs={{0,1},{1,0},{2,3},{3,2},{4,5},{5,4},{6,7},{7,6},{8,9},{9,8},{10,11... | collective-permute-start | bytes 1376264 | tf_op jit(solution)/shard_map/ppermute | solution.py:43
  21.7 12.6 %collective-permute-start.5 = (bf16[256,1792]{1,0:T(8,128)(2,1)S(1)}, bf16[256,1792]{1,0:T(8,128)(2,1)S(1)}, u32[]{:S(2)}, u32[]{:S(2)}) collective-permute-start(bf16[256,1792]{1,0:T(8,128)(2,1)S(1)} %pad_maximum_fusion.1.refs_1_.refs_9_), channel_id=1, source_target_pairs={{0,48},{1,13},{2,50},{3,15},{4,52},{5,1},{6,54},{7,3},{8,56},{9,5}... | collective-permute-start | bytes 2752520 | tf_op jit(solution)/shard_map/ppermute | solution.py:43
  21.8 13.8 %collective-permute-start.6 = (bf16[256,1792]{1,0:T(8,128)(2,1)S(1)}, bf16[256,1792]{1,0:T(8,128)(2,1)S(1)}, u32[]{:S(2)}, u32[]{:S(2)}) collective-permute-start(bf16[256,1792]{1,0:T(8,128)(2,1)S(1)} %pad_maximum_fusion.1.refs_1_.refs_9_), channel_id=1, source_target_pairs={{0,16},{1,5},{2,18},{3,7},{4,20},{5,9},{6,22},{7,11},{8,24},{9,13}... | collective-permute-start | bytes 2752520 | tf_op jit(solution)/shard_map/ppermute | solution.py:43
  25.2 4.2 %collective-permute-start.7 = (f16[2,128,256]{2,1,0:T(8,128)(2,1)S(1)}, f16[2,128,256]{2,1,0:T(8,128)(2,1)S(1)}, u32[]{:S(2)}, u32[]{:S(2)}) collective-permute-start(f16[2,128,256]{2,1,0:T(8,128)(2,1)S(1)} %fusion.18), channel_id=1, source_target_pairs={{0,2},{1,67},{2,0},{3,65},{4,6},{5,71},{6,4},{7,69},{8,10},{9,75},... | collective-permute-start | bytes 393224 | tf_op jit(solution)/shard_map/ppermute | solution.py:43
  25.7 12.0 %collective-permute-start.9 = (bf16[256,1792]{1,0:T(8,128)(2,1)S(1)}, bf16[256,1792]{1,0:T(8,128)(2,1)S(1)}, u32[]{:S(2)}, u32[]{:S(2)}) collective-permute-start(bf16[256,1792]{1,0:T(8,128)(2,1)S(1)} %collective-permute-done.1.refs_0_), channel_id=1, source_target_pairs={{0,1},{1,0},{2,3},{3,2},{4,5},{5,4},{6,7},{7,6},{8,9},{9,8},{10,11... | collective-permute-start | bytes 2752520 | tf_op jit(solution)/shard_map/ppermute | solution.py:43
  28.1 12.3 %collective-permute-start.11 = (bf16[256,1792]{1,0:T(8,128)(2,1)S(1)}, bf16[256,1792]{1,0:T(8,128)(2,1)S(1)}, u32[]{:S(2)}, u32[]{:S(2)}) collective-permute-start(bf16[256,1792]{1,0:T(8,128)(2,1)S(1)} %collective-permute-done.4.refs_2_), channel_id=1, source_target_pairs={{0,1},{1,0},{2,3},{3,2},{4,5},{5,4},{6,7},{7,6},{8,9},{9,8},{10,11... | collective-permute-start | bytes 2752520 | tf_op jit(solution)/shard_map/ppermute | solution.py:43
  29.6 4.0 %collective-permute-start.8 = (f16[128,256]{1,0:T(8,128)(2,1)S(1)}, f16[128,256]{1,0:T(8,128)(2,1)S(1)}, u32[]{:S(2)}, u32[]{:S(2)}) collective-permute-start(f16[128,256]{1,0:T(8,128)(2,1)S(1)} %get-tuple-element.72), channel_id=1, source_target_pairs={{0,66},{1,3},{2,64},{3,1},{4,70},{5,7},{6,68},{7,5},{8,74},{9,11},... | collective-permute-start | bytes 196616 | tf_op jit(solution)/shard_map/ppermute | solution.py:43
  35.6 4.8 %collective-permute-start.10 = (bf16[256,1792]{1,0:T(8,128)(2,1)S(1)}, bf16[256,1792]{1,0:T(8,128)(2,1)S(1)}, u32[]{:S(2)}, u32[]{:S(2)}) collective-permute-start(bf16[256,1792]{1,0:T(8,128)(2,1)S(1)} %collective-permute-done.5.refs_1_), channel_id=1, source_target_pairs={{0,1},{1,0},{2,3},{3,2},{4,5},{5,4},{6,7},{7,6},{8,9},{9,8},{10,11... | collective-permute-start | bytes 2752520 | tf_op jit(solution)/shard_map/ppermute | solution.py:43
  37.7 3.4 %collective-permute-start.12 = (bf16[256,1792]{1,0:T(8,128)(2,1)S(1)}, bf16[256,1792]{1,0:T(8,128)(2,1)S(1)}, u32[]{:S(2)}, u32[]{:S(2)}) collective-permute-start(bf16[256,1792]{1,0:T(8,128)(2,1)S(1)} %collective-permute-done.6.refs_3_), channel_id=1, source_target_pairs={{0,1},{1,0},{2,3},{3,2},{4,5},{5,4},{6,7},{7,6},{8,9},{9,8},{10,11... | collective-permute-start | bytes 2752520 | tf_op jit(solution)/shard_map/ppermute | solution.py:43
  37.7 13.1 %collective-permute-start.15 = (bf16[256,1792]{1,0:T(8,128)(2,1)S(1)}, bf16[256,1792]{1,0:T(8,128)(2,1)S(1)}, u32[]{:S(2)}, u32[]{:S(2)}) collective-permute-start(bf16[256,1792]{1,0:T(8,128)(2,1)S(1)} %collective-permute-done.1.refs_0_), channel_id=1, source_target_pairs={{0,48},{1,13},{2,50},{3,15},{4,52},{5,1},{6,54},{7,3},{8,56},{9,5}... | collective-permute-start | bytes 2752520 | tf_op jit(solution)/shard_map/ppermute | solution.py:43
  40.5 13.5 %collective-permute-start.16 = (bf16[256,1792]{1,0:T(8,128)(2,1)S(1)}, bf16[256,1792]{1,0:T(8,128)(2,1)S(1)}, u32[]{:S(2)}, u32[]{:S(2)}) collective-permute-start(bf16[256,1792]{1,0:T(8,128)(2,1)S(1)} %collective-permute-done.6.refs_3_), channel_id=1, source_target_pairs={{0,16},{1,5},{2,18},{3,7},{4,20},{5,9},{6,22},{7,11},{8,24},{9,13}... | collective-permute-start | bytes 2752520 | tf_op jit(solution)/shard_map/ppermute | solution.py:43
  45.1 8.8 %collective-permute-start.13 = (f16[768,256]{1,0:T(8,128)(2,1)S(1)}, f16[768,256]{1,0:T(8,128)(2,1)S(1)}, u32[]{:S(2)}, u32[]{:S(2)}) collective-permute-start(f16[768,256]{1,0:T(8,128)(2,1)S(1)} %fusion.2), channel_id=1, source_target_pairs={{0,2},{1,67},{2,0},{3,65},{4,6},{5,71},{6,4},{7,69},{8,10},{9,75},... | collective-permute-start | bytes 1179656 | tf_op jit(solution)/shard_map/ppermute | solution.py:43
  54.0 5.1 %collective-permute-start.17 = (bf16[128,1792]{1,0:T(8,128)(2,1)S(1)}, bf16[128,1792]{1,0:T(8,128)(2,1)S(1)}, u32[]{:S(2)}, u32[]{:S(2)}) collective-permute-start(bf16[128,1792]{1,0:T(8,128)(2,1)S(1)} %slice_select_fusion.1), channel_id=1, source_target_pairs={{0,1},{1,0},{2,3},{3,2},{4,5},{5,4},{6,7},{7,6},{8,9},{9,8},{10,11... | collective-permute-start | bytes 1376264 | tf_op jit(solution)/shard_map/ppermute | solution.py:43
  54.1 4.9 %collective-permute-start.18 = (bf16[128,1792]{1,0:T(8,128)(2,1)S(1)}, bf16[128,1792]{1,0:T(8,128)(2,1)S(1)}, u32[]{:S(2)}, u32[]{:S(2)}) collective-permute-start(bf16[128,1792]{1,0:T(8,128)(2,1)S(1)} %slice_select_fusion), channel_id=1, source_target_pairs={{0,1},{1,0},{2,3},{3,2},{4,5},{5,4},{6,7},{7,6},{8,9},{9,8},{10,11... | collective-permute-start | bytes 1376264 | tf_op jit(solution)/shard_map/ppermute | solution.py:43
  55.1 7.5 %collective-permute-start.19 = (f16[768,256]{1,0:T(8,128)(2,1)S(1)}, f16[768,256]{1,0:T(8,128)(2,1)S(1)}, u32[]{:S(2)}, u32[]{:S(2)}) collective-permute-start(f16[768,256]{1,0:T(8,128)(2,1)S(1)} %get-tuple-element.61), channel_id=1, source_target_pairs={{0,66},{1,3},{2,64},{3,1},{4,70},{5,7},{6,68},{7,5},{8,74},{9,11},... | collective-permute-start | bytes 1179656 | tf_op jit(solution)/shard_map/ppermute | solution.py:43
  57.9 8.8 %collective-permute-start.14 = (f16[768,256]{1,0:T(8,128)(2,1)S(1)}, f16[768,256]{1,0:T(8,128)(2,1)S(1)}, u32[]{:S(2)}, u32[]{:S(2)}) collective-permute-start(f16[768,256]{1,0:T(8,128)(2,1)S(1)} %get-tuple-element.40), channel_id=1, source_target_pairs={{0,2},{1,67},{2,0},{3,65},{4,6},{5,71},{6,4},{7,69},{8,10},{9,75},... | collective-permute-start | bytes 1179656 | tf_op jit(solution)/shard_map/ppermute | solution.py:43
  61.1 9.7 %collective-permute-start.27 = (f16[2,384,256]{2,1,0:T(8,128)(2,1)S(1)}, f16[2,384,256]{2,1,0:T(8,128)(2,1)S(1)}, u32[]{:S(2)}, u32[]{:S(2)}) collective-permute-start(f16[2,384,256]{2,1,0:T(8,128)(2,1)S(1)} %fusion.11), channel_id=1, source_target_pairs={{0,2},{1,67},{2,0},{3,65},{4,6},{5,71},{6,4},{7,69},{8,10},{9,75},... | collective-permute-start | bytes 1179656 | tf_op jit(solution)/shard_map/ppermute | solution.py:43
  67.9 9.9 %collective-permute-start.21 = (f16[512,256]{1,0:T(8,128)(2,1)S(1)}, f16[512,256]{1,0:T(8,128)(2,1)S(1)}, u32[]{:S(2)}, u32[]{:S(2)}) collective-permute-start(f16[512,256]{1,0:T(8,128)(2,1)S(1)} %multiply_convert_fusion), channel_id=1, source_target_pairs={{0,16},{1,5},{2,80},{3,69},{4,20},{5,9},{6,84},{7,73},{8,24},{9,13... | collective-permute-start | bytes 786440 | tf_op jit(solution)/shard_map/ppermute | solution.py:43
  68.8 10.2 %collective-permute-start.23 = (f32[256,256]{1,0:T(8,128)S(1)}, f32[256,256]{1,0:T(8,128)S(1)}, u32[]{:S(2)}, u32[]{:S(2)}) collective-permute-start(f32[256,256]{1,0:T(8,128)S(1)} %get-tuple-element.52), channel_id=1, source_target_pairs={{0,48},{1,13},{2,50},{3,15},{4,52},{5,1},{6,54},{7,3},{8,56},{9,5}... | collective-permute-start | bytes 786440 | tf_op jit(solution)/shard_map/ppermute | solution.py:43
  70.8 8.2 %collective-permute-start.25 = (f32[256,256]{1,0:T(8,128)S(1)}, f32[256,256]{1,0:T(8,128)S(1)}, u32[]{:S(2)}, u32[]{:S(2)}) collective-permute-start(f32[256,256]{1,0:T(8,128)S(1)} %get-tuple-element.53), channel_id=1, source_target_pairs={{0,4},{1,49},{2,6},{3,51},{4,8},{5,53},{6,10},{7,55},{8,12},{9,57}... | collective-permute-start | bytes 786440 | tf_op jit(solution)/shard_map/ppermute | solution.py:43
  71.1 8.4 %collective-permute-start.28 = (f16[384,256]{1,0:T(8,128)(2,1)S(1)}, f16[384,256]{1,0:T(8,128)(2,1)S(1)}, u32[]{:S(2)}, u32[]{:S(2)}) collective-permute-start(f16[384,256]{1,0:T(8,128)(2,1)S(1)} %get-tuple-element.69), channel_id=1, source_target_pairs={{0,66},{1,3},{2,64},{3,1},{4,70},{5,7},{6,68},{7,5},{8,74},{9,11},... | collective-permute-start | bytes 589832 | tf_op jit(solution)/shard_map/ppermute | solution.py:43
  73.8 8.6 %collective-permute-start.20 = (f32[384,256]{1,0:T(8,128)S(1)}, f32[384,256]{1,0:T(8,128)S(1)}, u32[]{:S(2)}, u32[]{:S(2)}) collective-permute-start(f32[384,256]{1,0:T(8,128)S(1)} %get-tuple-element.50.refs_0_), channel_id=1, source_target_pairs={{0,1},{1,0},{2,3},{3,2},{4,5},{5,4},{6,7},{7,6},{8,9},{9,8},{10,11... | collective-permute-start | bytes 1179656 | tf_op jit(solution)/shard_map/ppermute | solution.py:43
  77.9 4.0 %collective-permute-start.22 = (f16[512,256]{1,0:T(8,128)(2,1)S(1)}, f16[512,256]{1,0:T(8,128)(2,1)S(1)}, u32[]{:S(2)}, u32[]{:S(2)}) collective-permute-start(f16[512,256]{1,0:T(8,128)(2,1)S(1)} %collective-permute-done.21), channel_id=1, source_target_pairs={{0,1},{1,0},{2,3},{3,2},{4,5},{5,4},{6,7},{7,6},{8,9},{9,8},{10,11... | collective-permute-start | bytes 786440 | tf_op jit(solution)/shard_map/ppermute | solution.py:43
  78.9 3.5 %collective-permute-start.24 = (f32[256,256]{1,0:T(8,128)S(1)}, f32[256,256]{1,0:T(8,128)S(1)}, u32[]{:S(2)}, u32[]{:S(2)}) collective-permute-start(f32[256,256]{1,0:T(8,128)S(1)} %collective-permute-done.23.refs_4_), channel_id=1, source_target_pairs={{0,1},{1,0},{2,3},{3,2},{4,5},{5,4},{6,7},{7,6},{8,9},{9,8},{10,11... | collective-permute-start | bytes 786440 | tf_op jit(solution)/shard_map/ppermute | solution.py:43
  78.9 3.5 %collective-permute-start.26 = (f32[256,256]{1,0:T(8,128)S(1)}, f32[256,256]{1,0:T(8,128)S(1)}, u32[]{:S(2)}, u32[]{:S(2)}) collective-permute-start(f32[256,256]{1,0:T(8,128)S(1)} %collective-permute-done.25.refs_6_), channel_id=1, source_target_pairs={{0,1},{1,0},{2,3},{3,2},{4,5},{5,4},{6,7},{7,6},{8,9},{9,8},{10,11... | collective-permute-start | bytes 786440 | tf_op jit(solution)/shard_map/ppermute | solution.py:43
  80.4 9.4 %collective-permute-start.29 = (f16[384,256]{1,0:T(8,128)(2,1)S(1)}, f16[384,256]{1,0:T(8,128)(2,1)S(1)}, u32[]{:S(2)}, u32[]{:S(2)}) collective-permute-start(f16[384,256]{1,0:T(8,128)(2,1)S(1)} %multiply_convert_fusion.1), channel_id=1, source_target_pairs={{0,32},{1,9},{2,34},{3,11},{4,36},{5,13},{6,38},{7,15},{8,40},{9,1... | collective-permute-start | bytes 589832 | tf_op jit(solution)/shard_map/ppermute | solution.py:43
  81.8 7.9 %collective-permute-start.31 = (f16[256,256]{1,0:T(8,128)(2,1)S(1)}, f16[256,256]{1,0:T(8,128)(2,1)S(1)}, u32[]{:S(2)}, u32[]{:S(2)}) collective-permute-start(f16[256,256]{1,0:T(8,128)(2,1)S(1)} %multiply_convert_fusion.2), channel_id=1, source_target_pairs={{0,12},{1,17},{2,76},{3,81},{4,0},{5,21},{6,64},{7,85},{8,4},{9,25... | collective-permute-start | bytes 393224 | tf_op jit(solution)/shard_map/ppermute | solution.py:43
  89.8 1.8 %collective-permute-start.30 = (f16[384,256]{1,0:T(8,128)(2,1)S(1)}, f16[384,256]{1,0:T(8,128)(2,1)S(1)}, u32[]{:S(2)}, u32[]{:S(2)}) collective-permute-start(f16[384,256]{1,0:T(8,128)(2,1)S(1)} %collective-permute-done.29), channel_id=1, source_target_pairs={{0,1},{1,0},{2,3},{3,2},{4,5},{5,4},{6,7},{7,6},{8,9},{9,8},{10,11... | collective-permute-start | bytes 589832 | tf_op jit(solution)/shard_map/ppermute | solution.py:43
  (14 other events, 90.2 us)

commit v6 on v5

--- a/solution.py
+++ b/solution.py
@@ -12,8 +12,6 @@
 AXES = ("rows", "cols")
 SIZES = (2, 4, 4, 2, 2)
 ALONG = {"s": (0, 0), "a1": (1, 0), "a2": (2, 0), "a3": (3, 0), "b1": (0, 1), "b2": (0, 2), "b3": (0, 3)}
-ROWS = 64.0 * 2.0 ** (np.arange(1024) * 0.6180339887 % 1 / 2)
-COLUMNS = 2.0 ** (np.arange(256) * 0.7548776662 % 1 / 2)
 NEAR = (
     ("a1", "s", ("right", "left"), False),
     ("a1", "a3", ("right",), False),
@@ -74,13 +72,11 @@
 
 
 def packed(value):
-    rows, columns = np.float32(ROWS[: value.shape[-2], None]), np.float32(COLUMNS)
-    return (value * rows * columns).astype(jnp.float16)
+    return value
 
 
 def unpacked(value):
-    rows, columns = np.float32(1 / ROWS[: value.shape[-2], None]), np.float32(1 / COLUMNS)
-    return value.astype(jnp.float32) * rows * columns
+    return value
 
 
 def call(kernel, outs, place, *args, keep=True, cost=2**21):
@@ -168,7 +164,7 @@
     both = []
     for _, mine in kept:
         far = send(mine, other_core)
-        both += [unpacked(part) if mine.dtype == jnp.float16 else part for part in (mine, far)]
+        both += [mine, far]
     return [layout for layout, _ in kept], [pltpu.with_memory_space_constraint(part, pltpu.VMEM) for part in both]
 
 

time: 95.2 us -> 128 us (1.34)
  waiting for transfers between devices: 41.9 us -> 72.9 us
  starting transfers between devices: 31.9 us -> 35.8 us
  other arithmetic: 2.7 us -> 0.65 us
    ppermute x33, waiting for transfers between devices: 41.9 us -> 72.9 us  [send(): return lax.ppermute(value, AXES, pairs)]
    ppermute x33, starting transfers between devices: 31.9 us -> 35.8 us  [send(): return lax.ppermute(value, AXES, pairs)]
    convert_element_type x8 -> x0, other arithmetic: 1.34 us -> none  [packed(): return (value * rows * columns).astype(jnp.float16)]
  transfers between devices with their start and end apart: 33 -> 33, of which waited for: 17 -> 21; matrix products, arithmetic and copies ran while one was open for 3% -> 1% of each run, Pallas kernels for 14% -> 11%
where the time goes in v6:
time: 128 us; the launch traced here: 126 us
  waiting for transfers between devices  72.9 us (57%)
  starting transfers between devices  35.8 us (28%)
  Pallas kernels  15 us (12%)
  local copies, waits for them, and re-layouts  1.55 us (1%)
    ppermute x33, waiting for transfers between devices, send(): return lax.ppermute(value, AXES, pairs)  72.9 us
    ppermute x33, starting transfers between devices, send(): return lax.ppermute(value, AXES, pairs)  35.8 us
    pallas_call x6, Pallas kernels, call(): pl.pallas_call(kernel, out_shape=[pltpu.VMEM(s, jnp.float32) if keep else...  10.7 us
    pallas_call x1, Pallas kernels, body(): pl.pallas_call(functools.partial(begin, layouts), out_shape=[pltpu.VMEM(s...  2.56 us
  transfers between devices with their start and end apart: 33, of which 21 were waited for; matrix products, arithmetic and copies ran while one was open for 1% of the time, Pallas kernels for 11%

profile of v6, /device:TPU:33, one launch (start us, length us, event | category | flops | bytes accessed | tf_op | source)
XLA Modules:
  0.0 126.3 jit_solution(7642018555857196382)
XLA Ops:
  2.1 2.7 %collective-permute-start.2 = (bf16[256,896]{1,0:T(8,128)(2,1)S(1)}, bf16[256,896]{1,0:T(8,128)(2,1)S(1)}, u32[]{:S(2)}, u32[]{:S(2)}) collective-permute-start(bf16[256,896]{1,0:T(8,128)(2,1)S(1)} %get-tuple-element.65), channel_id=1, source_target_pairs={{0,64},{1,65},{2,66},{3,67},{4,68},{5,69},{6,70},{7,71},{8,72},{9,... | collective-permute-start | bytes 1376264 | tf_op jit(solution)/shard_map/ppermute | solution.py:41
  5.0 2.8 %collective-permute-start.1 = (bf16[256,1792]{1,0:T(8,128)(2,1)S(1)}, bf16[256,1792]{1,0:T(8,128)(2,1)S(1)}, u32[]{:S(2)}, u32[]{:S(2)}) collective-permute-start(bf16[256,1792]{1,0:T(8,128)(2,1)S(1)} %pad_maximum_fusion.refs_0_.refs_8_), channel_id=1, source_target_pairs={{0,48},{1,13},{2,50},{3,15},{4,52},{5,1},{6,54},{7,3},{8,56},{9,5}... | collective-permute-start | bytes 2752520 | tf_op jit(solution)/shard_map/ppermute | solution.py:41
  7.8 7.9 %collective-permute-done.2 = bf16[256,896]{1,0:T(8,128)(2,1)S(1)} collective-permute-done((bf16[256,896]{1,0:T(8,128)(2,1)S(1)}, bf16[256,896]{1,0:T(8,128)(2,1)S(1)}, u32[]{:S(2)}, u32[]{:S(2)}) %collective-permute-start.2) | collective-permute-done | bytes 458784 | tf_op jit(solution)/shard_map/ppermute | solution.py:41
  16.5 1.4 %collective-permute-done.3 = bf16[256,896]{1,0:T(8,128)(2,1)S(1)} collective-permute-done((bf16[256,896]{1,0:T(8,128)(2,1)S(1)}, bf16[256,896]{1,0:T(8,128)(2,1)S(1)}, u32[]{:S(2)}, u32[]{:S(2)}) %collective-permute-start.3) | collective-permute-done | bytes 458784 | tf_op jit(solution)/shard_map/ppermute | solution.py:41
  18.1 3.4 %collective-permute-done.4.refs_2_ = bf16[256,1792]{1,0:T(8,128)(2,1)S(1)} collective-permute-done((bf16[256,1792]{1,0:T(8,128)(2,1)S(1)}, bf16[256,1792]{1,0:T(8,128)(2,1)S(1)}, u32[]{:S(2)}, u32[]{:S(2)}) %collective-permute-start.4) | collective-permute-done | bytes 917536 | tf_op jit(solution)/shard_map/ppermute | solution.py:41
  21.8 1.5 %collective-permute-start.6 = (bf16[256,1792]{1,0:T(8,128)(2,1)S(1)}, bf16[256,1792]{1,0:T(8,128)(2,1)S(1)}, u32[]{:S(2)}, u32[]{:S(2)}) collective-permute-start(bf16[256,1792]{1,0:T(8,128)(2,1)S(1)} %pad_maximum_fusion.1.refs_1_.refs_9_), channel_id=1, source_target_pairs={{0,16},{1,5},{2,18},{3,7},{4,20},{5,9},{6,22},{7,11},{8,24},{9,13}... | collective-permute-start | bytes 2752520 | tf_op jit(solution)/shard_map/ppermute | solution.py:41
  23.2 1.8 %shard_map.28.refs_3_ = f32[4,128,256]{2,1,0:T(8,128)S(1)} custom-call(s32[5]{0:T(128)S(1)} %stack.23.place, bf16[256,1792]{1,0:T(8,128)(2,1)S(1)} %pad_maximum_fusion.refs_0_.refs_8_, bf16[256,1792]{1,0:T(8,128)(2,1)S(1)} %pad_maximum_fusion.1.refs_1_.refs_9_), custom_call_target="tpu_custom_call" | custom-call | tf_op jit(solution)/shard_map/pallas_call | solution.py:83
  25.5 5.2 %collective-permute-done.7 = f32[2,128,256]{2,1,0:T(8,128)S(1)} collective-permute-done((f32[2,128,256]{2,1,0:T(8,128)S(1)}, f32[2,128,256]{2,1,0:T(8,128)S(1)}, u32[]{:S(2)}, u32[]{:S(2)}) %collective-permute-start.7) | collective-permute-done | bytes 262176 | tf_op jit(solution)/shard_map/ppermute | solution.py:41
  30.7 2.0 %collective-permute-start.8 = (f32[128,256]{1,0:T(8,128)S(1)}, f32[128,256]{1,0:T(8,128)S(1)}, u32[]{:S(2)}, u32[]{:S(2)}) collective-permute-start(f32[128,256]{1,0:T(8,128)S(1)} %get-tuple-element.70), channel_id=1, source_target_pairs={{0,66},{1,3},{2,64},{3,1},{4,70},{5,7},{6,68},{7,5},{8,74},{9,11},... | collective-permute-start | bytes 393224 | tf_op jit(solution)/shard_map/ppermute | solution.py:41
  32.7 1.4 %collective-permute-start.9 = (bf16[256,1792]{1,0:T(8,128)(2,1)S(1)}, bf16[256,1792]{1,0:T(8,128)(2,1)S(1)}, u32[]{:S(2)}, u32[]{:S(2)}) collective-permute-start(bf16[256,1792]{1,0:T(8,128)(2,1)S(1)} %collective-permute-done.1.refs_0_), channel_id=1, source_target_pairs={{0,1},{1,0},{2,3},{3,2},{4,5},{5,4},{6,7},{7,6},{8,9},{9,8},{10,11... | collective-permute-start | bytes 2752520 | tf_op jit(solution)/shard_map/ppermute | solution.py:41
  35.6 2.8 %collective-permute-start.10 = (bf16[256,1792]{1,0:T(8,128)(2,1)S(1)}, bf16[256,1792]{1,0:T(8,128)(2,1)S(1)}, u32[]{:S(2)}, u32[]{:S(2)}) collective-permute-start(bf16[256,1792]{1,0:T(8,128)(2,1)S(1)} %collective-permute-done.5.refs_1_), channel_id=1, source_target_pairs={{0,1},{1,0},{2,3},{3,2},{4,5},{5,4},{6,7},{7,6},{8,9},{9,8},{10,11... | collective-permute-start | bytes 2752520 | tf_op jit(solution)/shard_map/ppermute | solution.py:41
  38.5 3.1 %collective-permute-start.15 = (bf16[256,1792]{1,0:T(8,128)(2,1)S(1)}, bf16[256,1792]{1,0:T(8,128)(2,1)S(1)}, u32[]{:S(2)}, u32[]{:S(2)}) collective-permute-start(bf16[256,1792]{1,0:T(8,128)(2,1)S(1)} %collective-permute-done.1.refs_0_), channel_id=1, source_target_pairs={{0,48},{1,13},{2,50},{3,15},{4,52},{5,1},{6,54},{7,3},{8,56},{9,5}... | collective-permute-start | bytes 2752520 | tf_op jit(solution)/shard_map/ppermute | solution.py:41
  41.8 3.8 %shard_map.29.refs_0_ = f32[4,768,256]{2,1,0:T(8,128)S(1)} custom-call(s32[5]{0:T(128)S(1)} %stack.23.place, bf16[256,1792]{1,0:T(8,128)(2,1)S(1)} %collective-permute-done.1.refs_0_, bf16[256,1792]{1,0:T(8,128)(2,1)S(1)} %collective-permute-done.5.refs_1_, bf16[256,1792]{1,0:T(8,128)(2,1)S(1)} %collective-permute-done.4.refs_2_, ...), custom_call_target="tpu_custom_call" | custom-call | bytes 16777216 | tf_op jit(solution)/shard_map/pallas_call | solution.py:83
  46.2 5.7 %collective-permute-done.15.refs_0_ = bf16[256,1792]{1,0:T(8,128)(2,1)S(1)} collective-permute-done((bf16[256,1792]{1,0:T(8,128)(2,1)S(1)}, bf16[256,1792]{1,0:T(8,128)(2,1)S(1)}, u32[]{:S(2)}, u32[]{:S(2)}) %collective-permute-start.15) | collective-permute-done | bytes 917536 | tf_op jit(solution)/shard_map/ppermute | solution.py:41
  51.9 3.1 %collective-permute-done.16.refs_1_ = bf16[256,1792]{1,0:T(8,128)(2,1)S(1)} collective-permute-done((bf16[256,1792]{1,0:T(8,128)(2,1)S(1)}, bf16[256,1792]{1,0:T(8,128)(2,1)S(1)}, u32[]{:S(2)}, u32[]{:S(2)}) %collective-permute-start.16) | collective-permute-done | bytes 917536 | tf_op jit(solution)/shard_map/ppermute | solution.py:41
  55.0 1.9 %collective-permute-done.13 = f32[768,256]{1,0:T(8,128)S(1)} collective-permute-done((f32[768,256]{1,0:T(8,128)S(1)}, f32[768,256]{1,0:T(8,128)S(1)}, u32[]{:S(2)}, u32[]{:S(2)}) %collective-permute-start.13) | collective-permute-done | bytes 786464 | tf_op jit(solution)/shard_map/ppermute | solution.py:41
  57.0 1.5 %collective-permute-start.17 = (bf16[128,1792]{1,0:T(8,128)(2,1)S(1)}, bf16[128,1792]{1,0:T(8,128)(2,1)S(1)}, u32[]{:S(2)}, u32[]{:S(2)}) collective-permute-start(bf16[128,1792]{1,0:T(8,128)(2,1)S(1)} %slice_select_fusion.1), channel_id=1, source_target_pairs={{0,1},{1,0},{2,3},{3,2},{4,5},{5,4},{6,7},{7,6},{8,9},{9,8},{10,11... | collective-permute-start | bytes 1376264 | tf_op jit(solution)/shard_map/ppermute | solution.py:41
  59.8 2.6 %collective-permute-start.19 = (f32[768,256]{1,0:T(8,128)S(1)}, f32[768,256]{1,0:T(8,128)S(1)}, u32[]{:S(2)}, u32[]{:S(2)}) collective-permute-start(f32[768,256]{1,0:T(8,128)S(1)} %fusion), channel_id=1, source_target_pairs={{0,66},{1,3},{2,64},{3,1},{4,70},{5,7},{6,68},{7,5},{8,74},{9,11},... | collective-permute-start | bytes 2359304 | tf_op jit(solution)/shard_map/ppermute | solution.py:41
  62.4 1.9 %shard_map.30.refs_0_ = f32[4,256,256]{2,1,0:T(8,128)S(1)} custom-call(s32[5]{0:T(128)S(1)} %stack.23.place, bf16[256,1792]{1,0:T(8,128)(2,1)S(1)} %collective-permute-done.15.refs_0_, bf16[256,1792]{1,0:T(8,128)(2,1)S(1)} %collective-permute-done.16.refs_1_, bf16[256,1792]{1,0:T(8,128)(2,1)S(1)} %collective-permute-done.9.refs_4_.refs_2_, ...), custom_call_target="tpu_custom_call" | custom-call | bytes 8388608 | tf_op jit(solution)/shard_map/pallas_call | solution.py:83
  64.3 1.9 %shard_map.31.refs_1_ = f32[4,128,256]{2,1,0:T(8,128)S(1)} custom-call(s32[5]{0:T(128)S(1)} %stack.23.place, bf16[256,1792]{1,0:T(8,128)(2,1)S(1)} %collective-permute-done.15.refs_0_, bf16[256,1792]{1,0:T(8,128)(2,1)S(1)} %collective-permute-done.16.refs_1_, bf16[128,1792]{1,0:T(8,128)(2,1)S(1)} %collective-permute-done.17.refs_2_, ...), custom_call_target="tpu_custom_call" | custom-call | bytes 8388608 | tf_op jit(solution)/shard_map/pallas_call | solution.py:83
  66.8 8.5 %collective-permute-done.14.refs_1_ = f32[768,256]{1,0:T(8,128)S(1)} collective-permute-done((f32[768,256]{1,0:T(8,128)S(1)}, f32[768,256]{1,0:T(8,128)S(1)}, u32[]{:S(2)}, u32[]{:S(2)}) %collective-permute-start.14) | collective-permute-done | bytes 786464 | tf_op jit(solution)/shard_map/ppermute | solution.py:41
  75.3 5.1 %collective-permute-done.19.refs_2_ = f32[768,256]{1,0:T(8,128)S(1)} collective-permute-done((f32[768,256]{1,0:T(8,128)S(1)}, f32[768,256]{1,0:T(8,128)S(1)}, u32[]{:S(2)}, u32[]{:S(2)}) %collective-permute-start.19) | collective-permute-done | bytes 786464 | tf_op jit(solution)/shard_map/ppermute | solution.py:41
  81.2 1.5 %collective-permute-start.21 = (f32[512,256]{1,0:T(8,128)S(1)}, f32[512,256]{1,0:T(8,128)S(1)}, u32[]{:S(2)}, u32[]{:S(2)}) collective-permute-start(f32[512,256]{1,0:T(8,128)S(1)} %get-tuple-element.51), channel_id=1, source_target_pairs={{0,16},{1,5},{2,80},{3,69},{4,20},{5,9},{6,84},{7,73},{8,24},{9,13... | collective-permute-start | bytes 1572872 | tf_op jit(solution)/shard_map/ppermute | solution.py:41
  82.7 15.8 %collective-permute-done.27 = f32[2,384,256]{2,1,0:T(8,128)S(1)} collective-permute-done((f32[2,384,256]{2,1,0:T(8,128)S(1)}, f32[2,384,256]{2,1,0:T(8,128)S(1)}, u32[]{:S(2)}, u32[]{:S(2)}) %collective-permute-start.27) | collective-permute-done | bytes 786464 | tf_op jit(solution)/shard_map/ppermute | solution.py:41
  98.7 4.3 %collective-permute-start.23 = (f32[256,256]{1,0:T(8,128)S(1)}, f32[256,256]{1,0:T(8,128)S(1)}, u32[]{:S(2)}, u32[]{:S(2)}) collective-permute-start(f32[256,256]{1,0:T(8,128)S(1)} %get-tuple-element.52), channel_id=1, source_target_pairs={{0,48},{1,13},{2,50},{3,15},{4,52},{5,1},{6,54},{7,3},{8,56},{9,5}... | collective-permute-start | bytes 786440 | tf_op jit(solution)/shard_map/ppermute | solution.py:41
  104.3 2.0 %collective-permute-done.23.refs_4_ = f32[256,256]{1,0:T(8,128)S(1)} collective-permute-done((f32[256,256]{1,0:T(8,128)S(1)}, f32[256,256]{1,0:T(8,128)S(1)}, u32[]{:S(2)}, u32[]{:S(2)}) %collective-permute-start.23) | collective-permute-done | bytes 262176 | tf_op jit(solution)/shard_map/ppermute | solution.py:41
  106.3 2.9 %collective-permute-done.25.refs_6_ = f32[256,256]{1,0:T(8,128)S(1)} collective-permute-done((f32[256,256]{1,0:T(8,128)S(1)}, f32[256,256]{1,0:T(8,128)S(1)}, u32[]{:S(2)}, u32[]{:S(2)}) %collective-permute-start.25) | collective-permute-done | bytes 262176 | tf_op jit(solution)/shard_map/ppermute | solution.py:41
  109.9 2.4 %collective-permute-start.29 = (f32[384,256]{1,0:T(8,128)S(1)}, f32[384,256]{1,0:T(8,128)S(1)}, u32[]{:S(2)}, u32[]{:S(2)}) collective-permute-start(f32[384,256]{1,0:T(8,128)S(1)} %get-tuple-element.56), channel_id=1, source_target_pairs={{0,32},{1,9},{2,34},{3,11},{4,36},{5,13},{6,38},{7,15},{8,40},{9,1... | collective-permute-start | bytes 1179656 | tf_op jit(solution)/shard_map/ppermute | solution.py:41
  114.2 2.6 %shard_map.33 = (f32[2048,256]{1,0:T(8,128)S(1)}, f32[2048,256]{1,0:T(8,128)}) custom-call(s32[5]{0:T(128)S(1)} %stack.23.place, f32[2048,256]{1,0:T(8,128)S(1)} %copy-done, f32[384,256]{1,0:T(8,128)S(1)} %get-tuple-element.50.refs_0_, f32[384,256]{1,0:T(8,128)S(1)} %collective-permute-done.20.refs_1_, f32[512,256]{1,0:T(8,128)S(1)} %collective-permute-done.21.refs_2_, ...), custom_call_target="tpu_custom_call" | custom-call | bytes 2097152 | tf_op jit(solution)/shard_map/pallas_call | solution.py:285
  116.8 1.3 %collective-permute-done.29.refs_0_ = f32[384,256]{1,0:T(8,128)S(1)} collective-permute-done((f32[384,256]{1,0:T(8,128)S(1)}, f32[384,256]{1,0:T(8,128)S(1)}, u32[]{:S(2)}, u32[]{:S(2)}) %collective-permute-start.29) | collective-permute-done | bytes 393248 | tf_op jit(solution)/shard_map/ppermute | solution.py:41
  118.1 4.2 %collective-permute-done.31.refs_2_ = f32[256,256]{1,0:T(8,128)S(1)} collective-permute-done((f32[256,256]{1,0:T(8,128)S(1)}, f32[256,256]{1,0:T(8,128)S(1)}, u32[]{:S(2)}, u32[]{:S(2)}) %collective-permute-start.31) | collective-permute-done | bytes 262176 | tf_op jit(solution)/shard_map/ppermute | solution.py:41
  124.5 1.7 %shard_map.35 = f32[2048,256]{1,0:T(8,128)} custom-call(s32[5]{0:T(128)S(1)} %stack.23.place, f32[2048,256]{1,0:T(8,128)S(1)} %get-tuple-element.54.base, f32[384,256]{1,0:T(8,128)S(1)} %collective-permute-done.29.refs_0_, f32[384,256]{1,0:T(8,128)S(1)} %collective-permute-done.30.refs_1_, ...), custom_call_target="tpu_custom_call", output_to_operand_aliasing={{}: (6, {})} | custom-call | bytes 2097152 | tf_op jit(solution)/shard_map/pallas_call | solution.py:296
  (63 shorter events, 15.4 us)
Async XLA Ops:
  1.3 3.5 %collective-permute-start = (bf16[256,896]{1,0:T(8,128)(2,1)S(1)}, bf16[256,896]{1,0:T(8,128)(2,1)S(1)}, u32[]{:S(2)}, u32[]{:S(2)}) collective-permute-start(bf16[256,896]{1,0:T(8,128)(2,1)S(1)} %get-tuple-element.66), channel_id=1, source_target_pairs={{0,1},{1,0},{2,3},{3,2},{4,5},{5,4},{6,7},{7,6},{8,9},{9,8},{10,11... | collective-permute-start | bytes 1376264 | tf_op jit(solution)/shard_map/ppermute | solution.py:41
  2.1 13.6 %collective-permute-start.2 = (bf16[256,896]{1,0:T(8,128)(2,1)S(1)}, bf16[256,896]{1,0:T(8,128)(2,1)S(1)}, u32[]{:S(2)}, u32[]{:S(2)}) collective-permute-start(bf16[256,896]{1,0:T(8,128)(2,1)S(1)} %get-tuple-element.65), channel_id=1, source_target_pairs={{0,64},{1,65},{2,66},{3,67},{4,68},{5,69},{6,70},{7,71},{8,72},{9,... | collective-permute-start | bytes 1376264 | tf_op jit(solution)/shard_map/ppermute | solution.py:41
  5.0 13.1 %collective-permute-start.1 = (bf16[256,1792]{1,0:T(8,128)(2,1)S(1)}, bf16[256,1792]{1,0:T(8,128)(2,1)S(1)}, u32[]{:S(2)}, u32[]{:S(2)}) collective-permute-start(bf16[256,1792]{1,0:T(8,128)(2,1)S(1)} %pad_maximum_fusion.refs_0_.refs_8_), channel_id=1, source_target_pairs={{0,48},{1,13},{2,50},{3,15},{4,52},{5,1},{6,54},{7,3},{8,56},{9,5}... | collective-permute-start | bytes 2752520 | tf_op jit(solution)/shard_map/ppermute | solution.py:41
  7.8 13.8 %collective-permute-start.4 = (bf16[256,1792]{1,0:T(8,128)(2,1)S(1)}, bf16[256,1792]{1,0:T(8,128)(2,1)S(1)}, u32[]{:S(2)}, u32[]{:S(2)}) collective-permute-start(bf16[256,1792]{1,0:T(8,128)(2,1)S(1)} %pad_maximum_fusion.refs_0_.refs_8_), channel_id=1, source_target_pairs={{0,16},{1,5},{2,18},{3,7},{4,20},{5,9},{6,22},{7,11},{8,24},{9,13}... | collective-permute-start | bytes 2752520 | tf_op jit(solution)/shard_map/ppermute | solution.py:41
  15.7 2.3 %collective-permute-start.3 = (bf16[256,896]{1,0:T(8,128)(2,1)S(1)}, bf16[256,896]{1,0:T(8,128)(2,1)S(1)}, u32[]{:S(2)}, u32[]{:S(2)}) collective-permute-start(bf16[256,896]{1,0:T(8,128)(2,1)S(1)} %collective-permute-done.2), channel_id=1, source_target_pairs={{0,1},{1,0},{2,3},{3,2},{4,5},{5,4},{6,7},{7,6},{8,9},{9,8},{10,11... | collective-permute-start | bytes 1376264 | tf_op jit(solution)/shard_map/ppermute | solution.py:41
  21.7 13.7 %collective-permute-start.5 = (bf16[256,1792]{1,0:T(8,128)(2,1)S(1)}, bf16[256,1792]{1,0:T(8,128)(2,1)S(1)}, u32[]{:S(2)}, u32[]{:S(2)}) collective-permute-start(bf16[256,1792]{1,0:T(8,128)(2,1)S(1)} %pad_maximum_fusion.1.refs_1_.refs_9_), channel_id=1, source_target_pairs={{0,48},{1,13},{2,50},{3,15},{4,52},{5,1},{6,54},{7,3},{8,56},{9,5}... | collective-permute-start | bytes 2752520 | tf_op jit(solution)/shard_map/ppermute | solution.py:41
  21.8 13.8 %collective-permute-start.6 = (bf16[256,1792]{1,0:T(8,128)(2,1)S(1)}, bf16[256,1792]{1,0:T(8,128)(2,1)S(1)}, u32[]{:S(2)}, u32[]{:S(2)}) collective-permute-start(bf16[256,1792]{1,0:T(8,128)(2,1)S(1)} %pad_maximum_fusion.1.refs_1_.refs_9_), channel_id=1, source_target_pairs={{0,16},{1,5},{2,18},{3,7},{4,20},{5,9},{6,22},{7,11},{8,24},{9,13}... | collective-permute-start | bytes 2752520 | tf_op jit(solution)/shard_map/ppermute | solution.py:41
  25.1 5.6 %collective-permute-start.7 = (f32[2,128,256]{2,1,0:T(8,128)S(1)}, f32[2,128,256]{2,1,0:T(8,128)S(1)}, u32[]{:S(2)}, u32[]{:S(2)}) collective-permute-start(f32[2,128,256]{2,1,0:T(8,128)S(1)} %slice.69), channel_id=1, source_target_pairs={{0,2},{1,67},{2,0},{3,65},{4,6},{5,71},{6,4},{7,69},{8,10},{9,75},... | collective-permute-start | bytes 786440 | tf_op jit(solution)/shard_map/ppermute | solution.py:41
  30.7 4.7 %collective-permute-start.8 = (f32[128,256]{1,0:T(8,128)S(1)}, f32[128,256]{1,0:T(8,128)S(1)}, u32[]{:S(2)}, u32[]{:S(2)}) collective-permute-start(f32[128,256]{1,0:T(8,128)S(1)} %get-tuple-element.70), channel_id=1, source_target_pairs={{0,66},{1,3},{2,64},{3,1},{4,70},{5,7},{6,68},{7,5},{8,74},{9,11},... | collective-permute-start | bytes 393224 | tf_op jit(solution)/shard_map/ppermute | solution.py:41
  32.7 5.8 %collective-permute-start.9 = (bf16[256,1792]{1,0:T(8,128)(2,1)S(1)}, bf16[256,1792]{1,0:T(8,128)(2,1)S(1)}, u32[]{:S(2)}, u32[]{:S(2)}) collective-permute-start(bf16[256,1792]{1,0:T(8,128)(2,1)S(1)} %collective-permute-done.1.refs_0_), channel_id=1, source_target_pairs={{0,1},{1,0},{2,3},{3,2},{4,5},{5,4},{6,7},{7,6},{8,9},{9,8},{10,11... | collective-permute-start | bytes 2752520 | tf_op jit(solution)/shard_map/ppermute | solution.py:41
  34.1 7.5 %collective-permute-start.11 = (bf16[256,1792]{1,0:T(8,128)(2,1)S(1)}, bf16[256,1792]{1,0:T(8,128)(2,1)S(1)}, u32[]{:S(2)}, u32[]{:S(2)}) collective-permute-start(bf16[256,1792]{1,0:T(8,128)(2,1)S(1)} %collective-permute-done.4.refs_2_), channel_id=1, source_target_pairs={{0,1},{1,0},{2,3},{3,2},{4,5},{5,4},{6,7},{7,6},{8,9},{9,8},{10,11... | collective-permute-start | bytes 2752520 | tf_op jit(solution)/shard_map/ppermute | solution.py:41
  35.6 6.0 %collective-permute-start.10 = (bf16[256,1792]{1,0:T(8,128)(2,1)S(1)}, bf16[256,1792]{1,0:T(8,128)(2,1)S(1)}, u32[]{:S(2)}, u32[]{:S(2)}) collective-permute-start(bf16[256,1792]{1,0:T(8,128)(2,1)S(1)} %collective-permute-done.5.refs_1_), channel_id=1, source_target_pairs={{0,1},{1,0},{2,3},{3,2},{4,5},{5,4},{6,7},{7,6},{8,9},{9,8},{10,11... | collective-permute-start | bytes 2752520 | tf_op jit(solution)/shard_map/ppermute | solution.py:41
  38.4 3.4 %collective-permute-start.12 = (bf16[256,1792]{1,0:T(8,128)(2,1)S(1)}, bf16[256,1792]{1,0:T(8,128)(2,1)S(1)}, u32[]{:S(2)}, u32[]{:S(2)}) collective-permute-start(bf16[256,1792]{1,0:T(8,128)(2,1)S(1)} %collective-permute-done.6.refs_3_), channel_id=1, source_target_pairs={{0,1},{1,0},{2,3},{3,2},{4,5},{5,4},{6,7},{7,6},{8,9},{9,8},{10,11... | collective-permute-start | bytes 2752520 | tf_op jit(solution)/shard_map/ppermute | solution.py:41
  38.5 13.4 %collective-permute-start.15 = (bf16[256,1792]{1,0:T(8,128)(2,1)S(1)}, bf16[256,1792]{1,0:T(8,128)(2,1)S(1)}, u32[]{:S(2)}, u32[]{:S(2)}) collective-permute-start(bf16[256,1792]{1,0:T(8,128)(2,1)S(1)} %collective-permute-done.1.refs_0_), channel_id=1, source_target_pairs={{0,48},{1,13},{2,50},{3,15},{4,52},{5,1},{6,54},{7,3},{8,56},{9,5}... | collective-permute-start | bytes 2752520 | tf_op jit(solution)/shard_map/ppermute | solution.py:41
  41.6 13.5 %collective-permute-start.16 = (bf16[256,1792]{1,0:T(8,128)(2,1)S(1)}, bf16[256,1792]{1,0:T(8,128)(2,1)S(1)}, u32[]{:S(2)}, u32[]{:S(2)}) collective-permute-start(bf16[256,1792]{1,0:T(8,128)(2,1)S(1)} %collective-permute-done.6.refs_3_), channel_id=1, source_target_pairs={{0,16},{1,5},{2,18},{3,7},{4,20},{5,9},{6,22},{7,11},{8,24},{9,13}... | collective-permute-start | bytes 2752520 | tf_op jit(solution)/shard_map/ppermute | solution.py:41
  45.7 11.2 %collective-permute-start.13 = (f32[768,256]{1,0:T(8,128)S(1)}, f32[768,256]{1,0:T(8,128)S(1)}, u32[]{:S(2)}, u32[]{:S(2)}) collective-permute-start(f32[768,256]{1,0:T(8,128)S(1)} %get-tuple-element.61), channel_id=1, source_target_pairs={{0,2},{1,67},{2,0},{3,65},{4,6},{5,71},{6,4},{7,69},{8,10},{9,75},... | collective-permute-start | bytes 2359304 | tf_op jit(solution)/shard_map/ppermute | solution.py:41
  57.0 7.3 %collective-permute-start.17 = (bf16[128,1792]{1,0:T(8,128)(2,1)S(1)}, bf16[128,1792]{1,0:T(8,128)(2,1)S(1)}, u32[]{:S(2)}, u32[]{:S(2)}) collective-permute-start(bf16[128,1792]{1,0:T(8,128)(2,1)S(1)} %slice_select_fusion.1), channel_id=1, source_target_pairs={{0,1},{1,0},{2,3},{3,2},{4,5},{5,4},{6,7},{7,6},{8,9},{9,8},{10,11... | collective-permute-start | bytes 1376264 | tf_op jit(solution)/shard_map/ppermute | solution.py:41
  58.5 5.8 %collective-permute-start.18 = (bf16[128,1792]{1,0:T(8,128)(2,1)S(1)}, bf16[128,1792]{1,0:T(8,128)(2,1)S(1)}, u32[]{:S(2)}, u32[]{:S(2)}) collective-permute-start(bf16[128,1792]{1,0:T(8,128)(2,1)S(1)} %slice_select_fusion), channel_id=1, source_target_pairs={{0,1},{1,0},{2,3},{3,2},{4,5},{5,4},{6,7},{7,6},{8,9},{9,8},{10,11... | collective-permute-start | bytes 1376264 | tf_op jit(solution)/shard_map/ppermute | solution.py:41
  58.7 16.6 %collective-permute-start.14 = (f32[768,256]{1,0:T(8,128)S(1)}, f32[768,256]{1,0:T(8,128)S(1)}, u32[]{:S(2)}, u32[]{:S(2)}) collective-permute-start(f32[768,256]{1,0:T(8,128)S(1)} %get-tuple-element.40), channel_id=1, source_target_pairs={{0,2},{1,67},{2,0},{3,65},{4,6},{5,71},{6,4},{7,69},{8,10},{9,75},... | collective-permute-start | bytes 2359304 | tf_op jit(solution)/shard_map/ppermute | solution.py:41
  59.8 20.7 %collective-permute-start.19 = (f32[768,256]{1,0:T(8,128)S(1)}, f32[768,256]{1,0:T(8,128)S(1)}, u32[]{:S(2)}, u32[]{:S(2)}) collective-permute-start(f32[768,256]{1,0:T(8,128)S(1)} %fusion), channel_id=1, source_target_pairs={{0,66},{1,3},{2,64},{3,1},{4,70},{5,7},{6,68},{7,5},{8,74},{9,11},... | collective-permute-start | bytes 2359304 | tf_op jit(solution)/shard_map/ppermute | solution.py:41
  66.3 32.3 %collective-permute-start.27 = (f32[2,384,256]{2,1,0:T(8,128)S(1)}, f32[2,384,256]{2,1,0:T(8,128)S(1)}, u32[]{:S(2)}, u32[]{:S(2)}) collective-permute-start(f32[2,384,256]{2,1,0:T(8,128)S(1)} %pad_maximum_fusion.2), channel_id=1, source_target_pairs={{0,2},{1,67},{2,0},{3,65},{4,6},{5,71},{6,4},{7,69},{8,10},{9,75},... | collective-permute-start | bytes 2359304 | tf_op jit(solution)/shard_map/ppermute | solution.py:41
  81.2 22.5 %collective-permute-start.21 = (f32[512,256]{1,0:T(8,128)S(1)}, f32[512,256]{1,0:T(8,128)S(1)}, u32[]{:S(2)}, u32[]{:S(2)}) collective-permute-start(f32[512,256]{1,0:T(8,128)S(1)} %get-tuple-element.51), channel_id=1, source_target_pairs={{0,16},{1,5},{2,80},{3,69},{4,20},{5,9},{6,84},{7,73},{8,24},{9,13... | collective-permute-start | bytes 1572872 | tf_op jit(solution)/shard_map/ppermute | solution.py:41
  98.6 10.6 %collective-permute-start.28 = (f32[384,256]{1,0:T(8,128)S(1)}, f32[384,256]{1,0:T(8,128)S(1)}, u32[]{:S(2)}, u32[]{:S(2)}) collective-permute-start(f32[384,256]{1,0:T(8,128)S(1)} %fusion.1), channel_id=1, source_target_pairs={{0,66},{1,3},{2,64},{3,1},{4,70},{5,7},{6,68},{7,5},{8,74},{9,11},... | collective-permute-start | bytes 1179656 | tf_op jit(solution)/shard_map/ppermute | solution.py:41
  98.7 7.6 %collective-permute-start.23 = (f32[256,256]{1,0:T(8,128)S(1)}, f32[256,256]{1,0:T(8,128)S(1)}, u32[]{:S(2)}, u32[]{:S(2)}) collective-permute-start(f32[256,256]{1,0:T(8,128)S(1)} %get-tuple-element.52), channel_id=1, source_target_pairs={{0,48},{1,13},{2,50},{3,15},{4,52},{5,1},{6,54},{7,3},{8,56},{9,5}... | collective-permute-start | bytes 786440 | tf_op jit(solution)/shard_map/ppermute | solution.py:41
  103.0 6.2 %collective-permute-start.25 = (f32[256,256]{1,0:T(8,128)S(1)}, f32[256,256]{1,0:T(8,128)S(1)}, u32[]{:S(2)}, u32[]{:S(2)}) collective-permute-start(f32[256,256]{1,0:T(8,128)S(1)} %get-tuple-element.53), channel_id=1, source_target_pairs={{0,4},{1,49},{2,6},{3,51},{4,8},{5,53},{6,10},{7,55},{8,12},{9,57}... | collective-permute-start | bytes 786440 | tf_op jit(solution)/shard_map/ppermute | solution.py:41
  103.7 9.1 %collective-permute-start.20 = (f32[384,256]{1,0:T(8,128)S(1)}, f32[384,256]{1,0:T(8,128)S(1)}, u32[]{:S(2)}, u32[]{:S(2)}) collective-permute-start(f32[384,256]{1,0:T(8,128)S(1)} %get-tuple-element.50.refs_0_), channel_id=1, source_target_pairs={{0,1},{1,0},{2,3},{3,2},{4,5},{5,4},{6,7},{7,6},{8,9},{9,8},{10,11... | collective-permute-start | bytes 1179656 | tf_op jit(solution)/shard_map/ppermute | solution.py:41
  103.7 10.5 %collective-permute-start.22 = (f32[512,256]{1,0:T(8,128)S(1)}, f32[512,256]{1,0:T(8,128)S(1)}, u32[]{:S(2)}, u32[]{:S(2)}) collective-permute-start(f32[512,256]{1,0:T(8,128)S(1)} %collective-permute-done.21.refs_2_), channel_id=1, source_target_pairs={{0,1},{1,0},{2,3},{3,2},{4,5},{5,4},{6,7},{7,6},{8,9},{9,8},{10,11... | collective-permute-start | bytes 1572872 | tf_op jit(solution)/shard_map/ppermute | solution.py:41
  109.9 8.2 %collective-permute-start.29 = (f32[384,256]{1,0:T(8,128)S(1)}, f32[384,256]{1,0:T(8,128)S(1)}, u32[]{:S(2)}, u32[]{:S(2)}) collective-permute-start(f32[384,256]{1,0:T(8,128)S(1)} %get-tuple-element.56), channel_id=1, source_target_pairs={{0,32},{1,9},{2,34},{3,11},{4,36},{5,13},{6,38},{7,15},{8,40},{9,1... | collective-permute-start | bytes 1179656 | tf_op jit(solution)/shard_map/ppermute | solution.py:41
  112.3 1.9 %collective-permute-start.26 = (f32[256,256]{1,0:T(8,128)S(1)}, f32[256,256]{1,0:T(8,128)S(1)}, u32[]{:S(2)}, u32[]{:S(2)}) collective-permute-start(f32[256,256]{1,0:T(8,128)S(1)} %collective-permute-done.25.refs_6_), channel_id=1, source_target_pairs={{0,1},{1,0},{2,3},{3,2},{4,5},{5,4},{6,7},{7,6},{8,9},{9,8},{10,11... | collective-permute-start | bytes 786440 | tf_op jit(solution)/shard_map/ppermute | solution.py:41
  112.8 9.4 %collective-permute-start.31 = (f32[256,256]{1,0:T(8,128)S(1)}, f32[256,256]{1,0:T(8,128)S(1)}, u32[]{:S(2)}, u32[]{:S(2)}) collective-permute-start(f32[256,256]{1,0:T(8,128)S(1)} %get-tuple-element.58), channel_id=1, source_target_pairs={{0,12},{1,17},{2,76},{3,81},{4,0},{5,21},{6,64},{7,85},{8,4},{9,25... | collective-permute-start | bytes 786440 | tf_op jit(solution)/shard_map/ppermute | solution.py:41
  118.1 6.4 %collective-permute-start.30 = (f32[384,256]{1,0:T(8,128)S(1)}, f32[384,256]{1,0:T(8,128)S(1)}, u32[]{:S(2)}, u32[]{:S(2)}) collective-permute-start(f32[384,256]{1,0:T(8,128)S(1)} %collective-permute-done.29.refs_0_), channel_id=1, source_target_pairs={{0,1},{1,0},{2,3},{3,2},{4,5},{5,4},{6,7},{7,6},{8,9},{9,8},{10,11... | collective-permute-start | bytes 1179656 | tf_op jit(solution)/shard_map/ppermute | solution.py:41
  122.3 2.2 %collective-permute-start.32 = (f32[256,256]{1,0:T(8,128)S(1)}, f32[256,256]{1,0:T(8,128)S(1)}, u32[]{:S(2)}, u32[]{:S(2)}) collective-permute-start(f32[256,256]{1,0:T(8,128)S(1)} %collective-permute-done.31.refs_2_), channel_id=1, source_target_pairs={{0,1},{1,0},{2,3},{3,2},{4,5},{5,4},{6,7},{7,6},{8,9},{9,8},{10,11... | collective-permute-start | bytes 786440 | tf_op jit(solution)/shard_map/ppermute | solution.py:41
  (2 other events, 33.0 us)

commit v7 on v5

--- a/solution.py
+++ b/solution.py
@@ -248,7 +248,7 @@
     got0 = send(packed(made0[:2]), first_partner)
     late0 = send(packed(made0[3] + unpacked(got0[1])), second_partner)
     other["a1"], other["a3"] = after((other["a1"], other["a3"]), late0)
-    own["a2"] = send(after(own["a1"], other["a1"], own["b1"]), to_place("a3"))
+    own["a2"] = send(after(own["a1"], late0, own["b1"]), to_place("a3"))
     other["a2"] = send(after(other["a3"], own["b3"]), to_place("a1"))
     other["b1"], other["b3"] = send(other["a1"], other_core), send(other["a3"], other_core)
     blocks = {name: (own[name], other[name]) for name in own}
@@ -285,7 +285,8 @@
     anywhere = pl.BlockSpec(memory_space=pl.ANY)
     params = pltpu.CompilerParams(vmem_limit_bytes=8 * 2**20)
     cost = pl.CostEstimate(flops=0, bytes_accessed=2**21, transcendentals=0)
-    layouts, tiles = with_halves(tiles1)
+    received = [mine for _, mine in tiles1]
+    layouts, tiles = with_halves([(layout, after(mine, *received)) for layout, mine in tiles1])
     base, new = pl.pallas_call(
         functools.partial(begin, layouts),
         out_shape=[pltpu.VMEM(stat_old.shape, jnp.float32), jax.ShapeDtypeStruct(stat_old.shape, jnp.float32)],

time: 95.2 us -> 95.1 us (level)
  no operation moved by 1% of the time
where the time goes in v7:
time: 95.1 us; the launch traced here: 93.7 us
  waiting for transfers between devices  42 us (44%)
  starting transfers between devices  32 us (34%)
  Pallas kernels  15 us (16%)
  other arithmetic  2.7 us (3%)
  local copies, waits for them, and re-layouts  1.49 us (2%)
    ppermute x33, waiting for transfers between devices, send(): return lax.ppermute(value, AXES, pairs)  42 us
    ppermute x33, starting transfers between devices, send(): return lax.ppermute(value, AXES, pairs)  32 us
    pallas_call x6, Pallas kernels, call(): pl.pallas_call(kernel, out_shape=[pltpu.VMEM(s, jnp.float32) if keep else...  10.7 us
    pallas_call x1, Pallas kernels, body(): pl.pallas_call(functools.partial(begin, layouts), out_shape=[pltpu.VMEM(s...  2.56 us
  transfers between devices with their start and end apart: 33, of which 17 were waited for; matrix products, arithmetic and copies ran while one was open for 3% of the time, Pallas kernels for 14%

profile of v7, /device:TPU:33, one launch (start us, length us, event | category | flops | bytes accessed | tf_op | source)
XLA Modules:
  0.0 93.7 jit_solution(10616795972433233065)
XLA Ops:
  0.1 1.2 %constant_dynamic-slice_fusion = (bf16[256,896]{1,0:T(8,128)(2,1)S(1)}, bf16[256,896]{1,0:T(8,128)(2,1)S(1)}) fusion(bf16[256,1792]{1,0:T(8,128)(2,1)} %param.52, s32[]{:T(128)S(6)} %select_n.42, s32[]{:T(128)S(6)} %select_n.39), kind=kLoop, calls=%fused_computation.63 | loop fusion | bytes 1835016 | tf_op jit(solution)/shard_map/dynamic_slice | solution.py:240
  2.1 2.7 %collective-permute-start.2 = (bf16[256,896]{1,0:T(8,128)(2,1)S(1)}, bf16[256,896]{1,0:T(8,128)(2,1)S(1)}, u32[]{:S(2)}, u32[]{:S(2)}) collective-permute-start(bf16[256,896]{1,0:T(8,128)(2,1)S(1)} %get-tuple-element.73), channel_id=1, source_target_pairs={{0,64},{1,65},{2,66},{3,67},{4,68},{5,69},{6,70},{7,71},{8,72},{9,... | collective-permute-start | bytes 1376264 | tf_op jit(solution)/shard_map/ppermute | solution.py:43
  5.0 2.8 %collective-permute-start.1 = (bf16[256,1792]{1,0:T(8,128)(2,1)S(1)}, bf16[256,1792]{1,0:T(8,128)(2,1)S(1)}, u32[]{:S(2)}, u32[]{:S(2)}) collective-permute-start(bf16[256,1792]{1,0:T(8,128)(2,1)S(1)} %pad_maximum_fusion.refs_0_.refs_8_), channel_id=1, source_target_pairs={{0,48},{1,13},{2,50},{3,15},{4,52},{5,1},{6,54},{7,3},{8,56},{9,5}... | collective-permute-start | bytes 2752520 | tf_op jit(solution)/shard_map/ppermute | solution.py:43
  7.8 7.9 %collective-permute-done.2 = bf16[256,896]{1,0:T(8,128)(2,1)S(1)} collective-permute-done((bf16[256,896]{1,0:T(8,128)(2,1)S(1)}, bf16[256,896]{1,0:T(8,128)(2,1)S(1)}, u32[]{:S(2)}, u32[]{:S(2)}) %collective-permute-start.2) | collective-permute-done | bytes 458784 | tf_op jit(solution)/shard_map/ppermute | solution.py:43
  16.5 1.4 %collective-permute-done.3 = bf16[256,896]{1,0:T(8,128)(2,1)S(1)} collective-permute-done((bf16[256,896]{1,0:T(8,128)(2,1)S(1)}, bf16[256,896]{1,0:T(8,128)(2,1)S(1)}, u32[]{:S(2)}, u32[]{:S(2)}) %collective-permute-start.3) | collective-permute-done | bytes 458784 | tf_op jit(solution)/shard_map/ppermute | solution.py:43
  18.1 3.4 %collective-permute-done.4.refs_2_ = bf16[256,1792]{1,0:T(8,128)(2,1)S(1)} collective-permute-done((bf16[256,1792]{1,0:T(8,128)(2,1)S(1)}, bf16[256,1792]{1,0:T(8,128)(2,1)S(1)}, u32[]{:S(2)}, u32[]{:S(2)}) %collective-permute-start.4) | collective-permute-done | bytes 917536 | tf_op jit(solution)/shard_map/ppermute | solution.py:43
  21.8 1.5 %collective-permute-start.6 = (bf16[256,1792]{1,0:T(8,128)(2,1)S(1)}, bf16[256,1792]{1,0:T(8,128)(2,1)S(1)}, u32[]{:S(2)}, u32[]{:S(2)}) collective-permute-start(bf16[256,1792]{1,0:T(8,128)(2,1)S(1)} %pad_maximum_fusion.1.refs_1_.refs_9_), channel_id=1, source_target_pairs={{0,16},{1,5},{2,18},{3,7},{4,20},{5,9},{6,22},{7,11},{8,24},{9,13}... | collective-permute-start | bytes 2752520 | tf_op jit(solution)/shard_map/ppermute | solution.py:43
  23.3 1.8 %shard_map.478.refs_3_ = f32[4,128,256]{2,1,0:T(8,128)S(1)} custom-call(s32[5]{0:T(128)S(1)} %stack.23.place, bf16[256,1792]{1,0:T(8,128)(2,1)S(1)} %pad_maximum_fusion.refs_0_.refs_8_, bf16[256,1792]{1,0:T(8,128)(2,1)S(1)} %pad_maximum_fusion.1.refs_1_.refs_9_), custom_call_target="tpu_custom_call" | custom-call | tf_op jit(solution)/shard_map/pallas_call | solution.py:87
  25.7 2.4 %collective-permute-start.9 = (bf16[256,1792]{1,0:T(8,128)(2,1)S(1)}, bf16[256,1792]{1,0:T(8,128)(2,1)S(1)}, u32[]{:S(2)}, u32[]{:S(2)}) collective-permute-start(bf16[256,1792]{1,0:T(8,128)(2,1)S(1)} %collective-permute-done.1.refs_0_), channel_id=1, source_target_pairs={{0,1},{1,0},{2,3},{3,2},{4,5},{5,4},{6,7},{7,6},{8,9},{9,8},{10,11... | collective-permute-start | bytes 2752520 | tf_op jit(solution)/shard_map/ppermute | solution.py:43
  28.1 1.3 %collective-permute-done.7 = f16[2,128,256]{2,1,0:T(8,128)(2,1)S(1)} collective-permute-done((f16[2,128,256]{2,1,0:T(8,128)(2,1)S(1)}, f16[2,128,256]{2,1,0:T(8,128)(2,1)S(1)}, u32[]{:S(2)}, u32[]{:S(2)}) %collective-permute-start.7) | collective-permute-done | bytes 131104 | tf_op jit(solution)/shard_map/ppermute | solution.py:43
  29.6 2.0 %collective-permute-start.8 = (f16[128,256]{1,0:T(8,128)(2,1)S(1)}, f16[128,256]{1,0:T(8,128)(2,1)S(1)}, u32[]{:S(2)}, u32[]{:S(2)}) collective-permute-start(f16[128,256]{1,0:T(8,128)(2,1)S(1)} %get-tuple-element.80), channel_id=1, source_target_pairs={{0,66},{1,3},{2,64},{3,1},{4,70},{5,7},{6,68},{7,5},{8,74},{9,11},... | collective-permute-start | bytes 196616 | tf_op jit(solution)/shard_map/ppermute | solution.py:43
  31.6 2.0 %collective-permute-done.8 = f16[128,256]{1,0:T(8,128)(2,1)S(1)} collective-permute-done((f16[128,256]{1,0:T(8,128)(2,1)S(1)}, f16[128,256]{1,0:T(8,128)(2,1)S(1)}, u32[]{:S(2)}, u32[]{:S(2)}) %collective-permute-start.8) | collective-permute-done | bytes 65568 | tf_op jit(solution)/shard_map/ppermute | solution.py:43
  34.3 1.3 %collective-permute-done.6.refs_3_ = bf16[256,1792]{1,0:T(8,128)(2,1)S(1)} collective-permute-done((bf16[256,1792]{1,0:T(8,128)(2,1)S(1)}, bf16[256,1792]{1,0:T(8,128)(2,1)S(1)}, u32[]{:S(2)}, u32[]{:S(2)}) %collective-permute-start.6) | collective-permute-done | bytes 917536 | tf_op jit(solution)/shard_map/ppermute | solution.py:43
  35.6 2.1 %collective-permute-start.10 = (bf16[256,1792]{1,0:T(8,128)(2,1)S(1)}, bf16[256,1792]{1,0:T(8,128)(2,1)S(1)}, u32[]{:S(2)}, u32[]{:S(2)}) collective-permute-start(bf16[256,1792]{1,0:T(8,128)(2,1)S(1)} %collective-permute-done.5.refs_1_), channel_id=1, source_target_pairs={{0,1},{1,0},{2,3},{3,2},{4,5},{5,4},{6,7},{7,6},{8,9},{9,8},{10,11... | collective-permute-start | bytes 2752520 | tf_op jit(solution)/shard_map/ppermute | solution.py:43
  37.7 2.7 %collective-permute-start.15 = (bf16[256,1792]{1,0:T(8,128)(2,1)S(1)}, bf16[256,1792]{1,0:T(8,128)(2,1)S(1)}, u32[]{:S(2)}, u32[]{:S(2)}) collective-permute-start(bf16[256,1792]{1,0:T(8,128)(2,1)S(1)} %collective-permute-done.1.refs_0_), channel_id=1, source_target_pairs={{0,48},{1,13},{2,50},{3,15},{4,52},{5,1},{6,54},{7,3},{8,56},{9,5}... | collective-permute-start | bytes 2752520 | tf_op jit(solution)/shard_map/ppermute | solution.py:43
  41.1 3.8 %shard_map.479.refs_0_ = f32[4,768,256]{2,1,0:T(8,128)S(1)} custom-call(s32[5]{0:T(128)S(1)} %stack.23.place, bf16[256,1792]{1,0:T(8,128)(2,1)S(1)} %collective-permute-done.1.refs_0_, bf16[256,1792]{1,0:T(8,128)(2,1)S(1)} %collective-permute-done.5.refs_1_, bf16[256,1792]{1,0:T(8,128)(2,1)S(1)} %collective-permute-done.4.refs_2_, ...), custom_call_target="tpu_custom_call" | custom-call | bytes 16777216 | tf_op jit(solution)/shard_map/pallas_call | solution.py:87
  45.7 5.1 %collective-permute-done.15.refs_0_ = bf16[256,1792]{1,0:T(8,128)(2,1)S(1)} collective-permute-done((bf16[256,1792]{1,0:T(8,128)(2,1)S(1)}, bf16[256,1792]{1,0:T(8,128)(2,1)S(1)}, u32[]{:S(2)}, u32[]{:S(2)}) %collective-permute-start.15) | collective-permute-done | bytes 917536 | tf_op jit(solution)/shard_map/ppermute | solution.py:43
  50.8 3.1 %collective-permute-done.16.refs_1_ = bf16[256,1792]{1,0:T(8,128)(2,1)S(1)} collective-permute-done((bf16[256,1792]{1,0:T(8,128)(2,1)S(1)}, bf16[256,1792]{1,0:T(8,128)(2,1)S(1)}, u32[]{:S(2)}, u32[]{:S(2)}) %collective-permute-start.16) | collective-permute-done | bytes 917536 | tf_op jit(solution)/shard_map/ppermute | solution.py:43
  55.1 0.9 %collective-permute-start.19 = (f16[768,256]{1,0:T(8,128)(2,1)S(1)}, f16[768,256]{1,0:T(8,128)(2,1)S(1)}, u32[]{:S(2)}, u32[]{:S(2)}) collective-permute-start(f16[768,256]{1,0:T(8,128)(2,1)S(1)} %get-tuple-element.69), channel_id=1, source_target_pairs={{0,66},{1,3},{2,64},{3,1},{4,70},{5,7},{6,68},{7,5},{8,74},{9,11},... | collective-permute-start | bytes 1179656 | tf_op jit(solution)/shard_map/ppermute | solution.py:43
  56.0 1.9 %shard_map.480.refs_0_ = f32[4,256,256]{2,1,0:T(8,128)S(1)} custom-call(s32[5]{0:T(128)S(1)} %stack.23.place, bf16[256,1792]{1,0:T(8,128)(2,1)S(1)} %collective-permute-done.15.refs_0_, bf16[256,1792]{1,0:T(8,128)(2,1)S(1)} %collective-permute-done.16.refs_1_, bf16[256,1792]{1,0:T(8,128)(2,1)S(1)} %collective-permute-done.9.refs_4_.refs_2_, ...), custom_call_target="tpu_custom_call" | custom-call | bytes 8388608 | tf_op jit(solution)/shard_map/pallas_call | solution.py:87
  57.9 1.1 %collective-permute-start.14 = (f16[768,256]{1,0:T(8,128)(2,1)S(1)}, f16[768,256]{1,0:T(8,128)(2,1)S(1)}, u32[]{:S(2)}, u32[]{:S(2)}) collective-permute-start(f16[768,256]{1,0:T(8,128)(2,1)S(1)} %get-tuple-element.44), channel_id=1, source_target_pairs={{0,2},{1,67},{2,0},{3,65},{4,6},{5,71},{6,4},{7,69},{8,10},{9,75},... | collective-permute-start | bytes 1179656 | tf_op jit(solution)/shard_map/ppermute | solution.py:43
  59.1 1.8 %shard_map.481.refs_1_ = f32[4,128,256]{2,1,0:T(8,128)S(1)} custom-call(s32[5]{0:T(128)S(1)} %stack.23.place, bf16[256,1792]{1,0:T(8,128)(2,1)S(1)} %collective-permute-done.15.refs_0_, bf16[256,1792]{1,0:T(8,128)(2,1)S(1)} %collective-permute-done.16.refs_1_, bf16[128,1792]{1,0:T(8,128)(2,1)S(1)} %collective-permute-done.17.refs_2_, ...), custom_call_target="tpu_custom_call" | custom-call | bytes 8388608 | tf_op jit(solution)/shard_map/pallas_call | solution.py:87
  61.7 0.9 collective-permute-done.19
  62.6 4.2 %collective-permute-done.14 = f16[768,256]{1,0:T(8,128)(2,1)S(1)} collective-permute-done((f16[768,256]{1,0:T(8,128)(2,1)S(1)}, f16[768,256]{1,0:T(8,128)(2,1)S(1)}, u32[]{:S(2)}, u32[]{:S(2)}) %collective-permute-start.14) | collective-permute-done | bytes 393248 | tf_op jit(solution)/shard_map/ppermute | solution.py:43
  68.8 2.0 %collective-permute-start.21 = (f32[256,256]{1,0:T(8,128)S(1)}, f32[256,256]{1,0:T(8,128)S(1)}, u32[]{:S(2)}, u32[]{:S(2)}) collective-permute-start(f32[256,256]{1,0:T(8,128)S(1)} %get-tuple-element.56), channel_id=1, source_target_pairs={{0,48},{1,13},{2,50},{3,15},{4,52},{5,1},{6,54},{7,3},{8,56},{9,5}... | collective-permute-start | bytes 786440 | tf_op jit(solution)/shard_map/ppermute | solution.py:43
  71.1 2.7 %collective-permute-start.28 = (f16[384,256]{1,0:T(8,128)(2,1)S(1)}, f16[384,256]{1,0:T(8,128)(2,1)S(1)}, u32[]{:S(2)}, u32[]{:S(2)}) collective-permute-start(f16[384,256]{1,0:T(8,128)(2,1)S(1)} %get-tuple-element.77), channel_id=1, source_target_pairs={{0,66},{1,3},{2,64},{3,1},{4,70},{5,7},{6,68},{7,5},{8,74},{9,11},... | collective-permute-start | bytes 589832 | tf_op jit(solution)/shard_map/ppermute | solution.py:43
  73.8 4.0 %collective-permute-done.20 = f16[512,256]{1,0:T(8,128)(2,1)S(1)} collective-permute-done((f16[512,256]{1,0:T(8,128)(2,1)S(1)}, f16[512,256]{1,0:T(8,128)(2,1)S(1)}, u32[]{:S(2)}, u32[]{:S(2)}) %collective-permute-start.20) | collective-permute-done | bytes 262176 | tf_op jit(solution)/shard_map/ppermute | solution.py:43
  77.9 1.1 %collective-permute-start.23 = (f32[384,256]{1,0:T(8,128)S(1)}, f32[384,256]{1,0:T(8,128)S(1)}, u32[]{:S(2)}, u32[]{:S(2)}) collective-permute-start(f32[384,256]{1,0:T(8,128)S(1)} %get-tuple-element.58.refs_0_), channel_id=1, source_target_pairs={{0,1},{1,0},{2,3},{3,2},{4,5},{5,4},{6,7},{7,6},{8,9},{9,8},{10,11... | collective-permute-start | bytes 1179656 | tf_op jit(solution)/shard_map/ppermute | solution.py:43
  80.5 1.4 %collective-permute-start.29 = (f16[384,256]{1,0:T(8,128)(2,1)S(1)}, f16[384,256]{1,0:T(8,128)(2,1)S(1)}, u32[]{:S(2)}, u32[]{:S(2)}) collective-permute-start(f16[384,256]{1,0:T(8,128)(2,1)S(1)} %multiply_convert_fusion.1), channel_id=1, source_target_pairs={{0,32},{1,9},{2,34},{3,11},{4,36},{5,13},{6,38},{7,15},{8,40},{9,1... | collective-permute-start | bytes 589832 | tf_op jit(solution)/shard_map/ppermute | solution.py:43
  82.9 2.6 %shard_map.483 = (f32[2048,256]{1,0:T(8,128)S(1)}, f32[2048,256]{1,0:T(8,128)}) custom-call(s32[5]{0:T(128)S(1)} %stack.23.place, f32[2048,256]{1,0:T(8,128)S(1)} %copy-done, f32[384,256]{1,0:T(8,128)S(1)} %get-tuple-element.58.refs_0_, f32[384,256]{1,0:T(8,128)S(1)} %collective-permute-done.23.refs_1_, f32[512,256]{1,0:T(8,128)S(1)} %get-tuple-element.86.refs_2_, ...), custom_call_target="tpu_custom_call" | custom-call | bytes 2097152 | tf_op jit(solution)/shard_map/pallas_call | solution.py:290
  85.5 4.6 %collective-permute-done.31 = f16[256,256]{1,0:T(8,128)(2,1)S(1)} collective-permute-done((f16[256,256]{1,0:T(8,128)(2,1)S(1)}, f16[256,256]{1,0:T(8,128)(2,1)S(1)}, u32[]{:S(2)}, u32[]{:S(2)}) %collective-permute-start.31) | collective-permute-done | bytes 131104 | tf_op jit(solution)/shard_map/ppermute | solution.py:43
  91.9 1.7 %shard_map.485 = f32[2048,256]{1,0:T(8,128)} custom-call(s32[5]{0:T(128)S(1)} %stack.23.place, f32[2048,256]{1,0:T(8,128)S(1)} %get-tuple-element.62.base, f32[384,256]{1,0:T(8,128)S(1)} %get-tuple-element.84.refs_0_, f32[384,256]{1,0:T(8,128)S(1)} %get-tuple-element.83.refs_1_, ...), custom_call_target="tpu_custom_call", output_to_operand_aliasing={{}: (6, {})} | custom-call | bytes 2097152 | tf_op jit(solution)/shard_map/pallas_call | solution.py:301
  (95 shorter events, 13.5 us)
Async XLA Ops:
  1.3 3.5 %collective-permute-start = (bf16[256,896]{1,0:T(8,128)(2,1)S(1)}, bf16[256,896]{1,0:T(8,128)(2,1)S(1)}, u32[]{:S(2)}, u32[]{:S(2)}) collective-permute-start(bf16[256,896]{1,0:T(8,128)(2,1)S(1)} %get-tuple-element.74), channel_id=1, source_target_pairs={{0,1},{1,0},{2,3},{3,2},{4,5},{5,4},{6,7},{7,6},{8,9},{9,8},{10,11... | collective-permute-start | bytes 1376264 | tf_op jit(solution)/shard_map/ppermute | solution.py:43
  2.1 13.6 %collective-permute-start.2 = (bf16[256,896]{1,0:T(8,128)(2,1)S(1)}, bf16[256,896]{1,0:T(8,128)(2,1)S(1)}, u32[]{:S(2)}, u32[]{:S(2)}) collective-permute-start(bf16[256,896]{1,0:T(8,128)(2,1)S(1)} %get-tuple-element.73), channel_id=1, source_target_pairs={{0,64},{1,65},{2,66},{3,67},{4,68},{5,69},{6,70},{7,71},{8,72},{9,... | collective-permute-start | bytes 1376264 | tf_op jit(solution)/shard_map/ppermute | solution.py:43
  5.0 13.1 %collective-permute-start.1 = (bf16[256,1792]{1,0:T(8,128)(2,1)S(1)}, bf16[256,1792]{1,0:T(8,128)(2,1)S(1)}, u32[]{:S(2)}, u32[]{:S(2)}) collective-permute-start(bf16[256,1792]{1,0:T(8,128)(2,1)S(1)} %pad_maximum_fusion.refs_0_.refs_8_), channel_id=1, source_target_pairs={{0,48},{1,13},{2,50},{3,15},{4,52},{5,1},{6,54},{7,3},{8,56},{9,5}... | collective-permute-start | bytes 2752520 | tf_op jit(solution)/shard_map/ppermute | solution.py:43
  7.8 13.8 %collective-permute-start.4 = (bf16[256,1792]{1,0:T(8,128)(2,1)S(1)}, bf16[256,1792]{1,0:T(8,128)(2,1)S(1)}, u32[]{:S(2)}, u32[]{:S(2)}) collective-permute-start(bf16[256,1792]{1,0:T(8,128)(2,1)S(1)} %pad_maximum_fusion.refs_0_.refs_8_), channel_id=1, source_target_pairs={{0,16},{1,5},{2,18},{3,7},{4,20},{5,9},{6,22},{7,11},{8,24},{9,13}... | collective-permute-start | bytes 2752520 | tf_op jit(solution)/shard_map/ppermute | solution.py:43
  15.7 2.3 %collective-permute-start.3 = (bf16[256,896]{1,0:T(8,128)(2,1)S(1)}, bf16[256,896]{1,0:T(8,128)(2,1)S(1)}, u32[]{:S(2)}, u32[]{:S(2)}) collective-permute-start(bf16[256,896]{1,0:T(8,128)(2,1)S(1)} %collective-permute-done.2), channel_id=1, source_target_pairs={{0,1},{1,0},{2,3},{3,2},{4,5},{5,4},{6,7},{7,6},{8,9},{9,8},{10,11... | collective-permute-start | bytes 1376264 | tf_op jit(solution)/shard_map/ppermute | solution.py:43
  21.7 12.6 %collective-permute-start.5 = (bf16[256,1792]{1,0:T(8,128)(2,1)S(1)}, bf16[256,1792]{1,0:T(8,128)(2,1)S(1)}, u32[]{:S(2)}, u32[]{:S(2)}) collective-permute-start(bf16[256,1792]{1,0:T(8,128)(2,1)S(1)} %pad_maximum_fusion.1.refs_1_.refs_9_), channel_id=1, source_target_pairs={{0,48},{1,13},{2,50},{3,15},{4,52},{5,1},{6,54},{7,3},{8,56},{9,5}... | collective-permute-start | bytes 2752520 | tf_op jit(solution)/shard_map/ppermute | solution.py:43
  21.8 13.8 %collective-permute-start.6 = (bf16[256,1792]{1,0:T(8,128)(2,1)S(1)}, bf16[256,1792]{1,0:T(8,128)(2,1)S(1)}, u32[]{:S(2)}, u32[]{:S(2)}) collective-permute-start(bf16[256,1792]{1,0:T(8,128)(2,1)S(1)} %pad_maximum_fusion.1.refs_1_.refs_9_), channel_id=1, source_target_pairs={{0,16},{1,5},{2,18},{3,7},{4,20},{5,9},{6,22},{7,11},{8,24},{9,13}... | collective-permute-start | bytes 2752520 | tf_op jit(solution)/shard_map/ppermute | solution.py:43
  25.2 4.2 %collective-permute-start.7 = (f16[2,128,256]{2,1,0:T(8,128)(2,1)S(1)}, f16[2,128,256]{2,1,0:T(8,128)(2,1)S(1)}, u32[]{:S(2)}, u32[]{:S(2)}) collective-permute-start(f16[2,128,256]{2,1,0:T(8,128)(2,1)S(1)} %fusion.18), channel_id=1, source_target_pairs={{0,2},{1,67},{2,0},{3,65},{4,6},{5,71},{6,4},{7,69},{8,10},{9,75},... | collective-permute-start | bytes 393224 | tf_op jit(solution)/shard_map/ppermute | solution.py:43
  25.7 12.0 %collective-permute-start.9 = (bf16[256,1792]{1,0:T(8,128)(2,1)S(1)}, bf16[256,1792]{1,0:T(8,128)(2,1)S(1)}, u32[]{:S(2)}, u32[]{:S(2)}) collective-permute-start(bf16[256,1792]{1,0:T(8,128)(2,1)S(1)} %collective-permute-done.1.refs_0_), channel_id=1, source_target_pairs={{0,1},{1,0},{2,3},{3,2},{4,5},{5,4},{6,7},{7,6},{8,9},{9,8},{10,11... | collective-permute-start | bytes 2752520 | tf_op jit(solution)/shard_map/ppermute | solution.py:43
  28.1 12.3 %collective-permute-start.11 = (bf16[256,1792]{1,0:T(8,128)(2,1)S(1)}, bf16[256,1792]{1,0:T(8,128)(2,1)S(1)}, u32[]{:S(2)}, u32[]{:S(2)}) collective-permute-start(bf16[256,1792]{1,0:T(8,128)(2,1)S(1)} %collective-permute-done.4.refs_2_), channel_id=1, source_target_pairs={{0,1},{1,0},{2,3},{3,2},{4,5},{5,4},{6,7},{7,6},{8,9},{9,8},{10,11... | collective-permute-start | bytes 2752520 | tf_op jit(solution)/shard_map/ppermute | solution.py:43
  29.6 4.0 %collective-permute-start.8 = (f16[128,256]{1,0:T(8,128)(2,1)S(1)}, f16[128,256]{1,0:T(8,128)(2,1)S(1)}, u32[]{:S(2)}, u32[]{:S(2)}) collective-permute-start(f16[128,256]{1,0:T(8,128)(2,1)S(1)} %get-tuple-element.80), channel_id=1, source_target_pairs={{0,66},{1,3},{2,64},{3,1},{4,70},{5,7},{6,68},{7,5},{8,74},{9,11},... | collective-permute-start | bytes 196616 | tf_op jit(solution)/shard_map/ppermute | solution.py:43
  35.6 4.8 %collective-permute-start.10 = (bf16[256,1792]{1,0:T(8,128)(2,1)S(1)}, bf16[256,1792]{1,0:T(8,128)(2,1)S(1)}, u32[]{:S(2)}, u32[]{:S(2)}) collective-permute-start(bf16[256,1792]{1,0:T(8,128)(2,1)S(1)} %collective-permute-done.5.refs_1_), channel_id=1, source_target_pairs={{0,1},{1,0},{2,3},{3,2},{4,5},{5,4},{6,7},{7,6},{8,9},{9,8},{10,11... | collective-permute-start | bytes 2752520 | tf_op jit(solution)/shard_map/ppermute | solution.py:43
  37.7 3.4 %collective-permute-start.12 = (bf16[256,1792]{1,0:T(8,128)(2,1)S(1)}, bf16[256,1792]{1,0:T(8,128)(2,1)S(1)}, u32[]{:S(2)}, u32[]{:S(2)}) collective-permute-start(bf16[256,1792]{1,0:T(8,128)(2,1)S(1)} %collective-permute-done.6.refs_3_), channel_id=1, source_target_pairs={{0,1},{1,0},{2,3},{3,2},{4,5},{5,4},{6,7},{7,6},{8,9},{9,8},{10,11... | collective-permute-start | bytes 2752520 | tf_op jit(solution)/shard_map/ppermute | solution.py:43
  37.7 13.1 %collective-permute-start.15 = (bf16[256,1792]{1,0:T(8,128)(2,1)S(1)}, bf16[256,1792]{1,0:T(8,128)(2,1)S(1)}, u32[]{:S(2)}, u32[]{:S(2)}) collective-permute-start(bf16[256,1792]{1,0:T(8,128)(2,1)S(1)} %collective-permute-done.1.refs_0_), channel_id=1, source_target_pairs={{0,48},{1,13},{2,50},{3,15},{4,52},{5,1},{6,54},{7,3},{8,56},{9,5}... | collective-permute-start | bytes 2752520 | tf_op jit(solution)/shard_map/ppermute | solution.py:43
  40.5 13.5 %collective-permute-start.16 = (bf16[256,1792]{1,0:T(8,128)(2,1)S(1)}, bf16[256,1792]{1,0:T(8,128)(2,1)S(1)}, u32[]{:S(2)}, u32[]{:S(2)}) collective-permute-start(bf16[256,1792]{1,0:T(8,128)(2,1)S(1)} %collective-permute-done.6.refs_3_), channel_id=1, source_target_pairs={{0,16},{1,5},{2,18},{3,7},{4,20},{5,9},{6,22},{7,11},{8,24},{9,13}... | collective-permute-start | bytes 2752520 | tf_op jit(solution)/shard_map/ppermute | solution.py:43
  45.1 8.8 %collective-permute-start.13 = (f16[768,256]{1,0:T(8,128)(2,1)S(1)}, f16[768,256]{1,0:T(8,128)(2,1)S(1)}, u32[]{:S(2)}, u32[]{:S(2)}) collective-permute-start(f16[768,256]{1,0:T(8,128)(2,1)S(1)} %fusion.2), channel_id=1, source_target_pairs={{0,2},{1,67},{2,0},{3,65},{4,6},{5,71},{6,4},{7,69},{8,10},{9,75},... | collective-permute-start | bytes 1179656 | tf_op jit(solution)/shard_map/ppermute | solution.py:43
  54.0 5.1 %collective-permute-start.17 = (bf16[128,1792]{1,0:T(8,128)(2,1)S(1)}, bf16[128,1792]{1,0:T(8,128)(2,1)S(1)}, u32[]{:S(2)}, u32[]{:S(2)}) collective-permute-start(bf16[128,1792]{1,0:T(8,128)(2,1)S(1)} %slice_select_fusion.1), channel_id=1, source_target_pairs={{0,1},{1,0},{2,3},{3,2},{4,5},{5,4},{6,7},{7,6},{8,9},{9,8},{10,11... | collective-permute-start | bytes 1376264 | tf_op jit(solution)/shard_map/ppermute | solution.py:43
  54.1 4.9 %collective-permute-start.18 = (bf16[128,1792]{1,0:T(8,128)(2,1)S(1)}, bf16[128,1792]{1,0:T(8,128)(2,1)S(1)}, u32[]{:S(2)}, u32[]{:S(2)}) collective-permute-start(bf16[128,1792]{1,0:T(8,128)(2,1)S(1)} %slice_select_fusion), channel_id=1, source_target_pairs={{0,1},{1,0},{2,3},{3,2},{4,5},{5,4},{6,7},{7,6},{8,9},{9,8},{10,11... | collective-permute-start | bytes 1376264 | tf_op jit(solution)/shard_map/ppermute | solution.py:43
  55.1 7.5 %collective-permute-start.19 = (f16[768,256]{1,0:T(8,128)(2,1)S(1)}, f16[768,256]{1,0:T(8,128)(2,1)S(1)}, u32[]{:S(2)}, u32[]{:S(2)}) collective-permute-start(f16[768,256]{1,0:T(8,128)(2,1)S(1)} %get-tuple-element.69), channel_id=1, source_target_pairs={{0,66},{1,3},{2,64},{3,1},{4,70},{5,7},{6,68},{7,5},{8,74},{9,11},... | collective-permute-start | bytes 1179656 | tf_op jit(solution)/shard_map/ppermute | solution.py:43
  57.9 8.8 %collective-permute-start.14 = (f16[768,256]{1,0:T(8,128)(2,1)S(1)}, f16[768,256]{1,0:T(8,128)(2,1)S(1)}, u32[]{:S(2)}, u32[]{:S(2)}) collective-permute-start(f16[768,256]{1,0:T(8,128)(2,1)S(1)} %get-tuple-element.44), channel_id=1, source_target_pairs={{0,2},{1,67},{2,0},{3,65},{4,6},{5,71},{6,4},{7,69},{8,10},{9,75},... | collective-permute-start | bytes 1179656 | tf_op jit(solution)/shard_map/ppermute | solution.py:43
  61.1 9.7 %collective-permute-start.27 = (f16[2,384,256]{2,1,0:T(8,128)(2,1)S(1)}, f16[2,384,256]{2,1,0:T(8,128)(2,1)S(1)}, u32[]{:S(2)}, u32[]{:S(2)}) collective-permute-start(f16[2,384,256]{2,1,0:T(8,128)(2,1)S(1)} %fusion.11), channel_id=1, source_target_pairs={{0,2},{1,67},{2,0},{3,65},{4,6},{5,71},{6,4},{7,69},{8,10},{9,75},... | collective-permute-start | bytes 1179656 | tf_op jit(solution)/shard_map/ppermute | solution.py:43
  67.9 9.9 %collective-permute-start.20 = (f16[512,256]{1,0:T(8,128)(2,1)S(1)}, f16[512,256]{1,0:T(8,128)(2,1)S(1)}, u32[]{:S(2)}, u32[]{:S(2)}) collective-permute-start(f16[512,256]{1,0:T(8,128)(2,1)S(1)} %multiply_convert_fusion), channel_id=1, source_target_pairs={{0,16},{1,5},{2,80},{3,69},{4,20},{5,9},{6,84},{7,73},{8,24},{9,13... | collective-permute-start | bytes 786440 | tf_op jit(solution)/shard_map/ppermute | solution.py:43
  68.8 9.1 %collective-permute-start.21 = (f32[256,256]{1,0:T(8,128)S(1)}, f32[256,256]{1,0:T(8,128)S(1)}, u32[]{:S(2)}, u32[]{:S(2)}) collective-permute-start(f32[256,256]{1,0:T(8,128)S(1)} %get-tuple-element.56), channel_id=1, source_target_pairs={{0,48},{1,13},{2,50},{3,15},{4,52},{5,1},{6,54},{7,3},{8,56},{9,5}... | collective-permute-start | bytes 786440 | tf_op jit(solution)/shard_map/ppermute | solution.py:43
  70.8 7.1 %collective-permute-start.22 = (f32[256,256]{1,0:T(8,128)S(1)}, f32[256,256]{1,0:T(8,128)S(1)}, u32[]{:S(2)}, u32[]{:S(2)}) collective-permute-start(f32[256,256]{1,0:T(8,128)S(1)} %get-tuple-element.57), channel_id=1, source_target_pairs={{0,4},{1,49},{2,6},{3,51},{4,8},{5,53},{6,10},{7,55},{8,12},{9,57}... | collective-permute-start | bytes 786440 | tf_op jit(solution)/shard_map/ppermute | solution.py:43
  71.1 8.5 %collective-permute-start.28 = (f16[384,256]{1,0:T(8,128)(2,1)S(1)}, f16[384,256]{1,0:T(8,128)(2,1)S(1)}, u32[]{:S(2)}, u32[]{:S(2)}) collective-permute-start(f16[384,256]{1,0:T(8,128)(2,1)S(1)} %get-tuple-element.77), channel_id=1, source_target_pairs={{0,66},{1,3},{2,64},{3,1},{4,70},{5,7},{6,68},{7,5},{8,74},{9,11},... | collective-permute-start | bytes 589832 | tf_op jit(solution)/shard_map/ppermute | solution.py:43
  77.9 5.0 %collective-permute-start.23 = (f32[384,256]{1,0:T(8,128)S(1)}, f32[384,256]{1,0:T(8,128)S(1)}, u32[]{:S(2)}, u32[]{:S(2)}) collective-permute-start(f32[384,256]{1,0:T(8,128)S(1)} %get-tuple-element.58.refs_0_), channel_id=1, source_target_pairs={{0,1},{1,0},{2,3},{3,2},{4,5},{5,4},{6,7},{7,6},{8,9},{9,8},{10,11... | collective-permute-start | bytes 1179656 | tf_op jit(solution)/shard_map/ppermute | solution.py:43
  78.9 3.0 %collective-permute-start.24 = (f16[512,256]{1,0:T(8,128)(2,1)S(1)}, f16[512,256]{1,0:T(8,128)(2,1)S(1)}, u32[]{:S(2)}, u32[]{:S(2)}) collective-permute-start(f16[512,256]{1,0:T(8,128)(2,1)S(1)} %collective-permute-done.20), channel_id=1, source_target_pairs={{0,1},{1,0},{2,3},{3,2},{4,5},{5,4},{6,7},{7,6},{8,9},{9,8},{10,11... | collective-permute-start | bytes 786440 | tf_op jit(solution)/shard_map/ppermute | solution.py:43
  79.0 3.8 %collective-permute-start.25 = (f32[256,256]{1,0:T(8,128)S(1)}, f32[256,256]{1,0:T(8,128)S(1)}, u32[]{:S(2)}, u32[]{:S(2)}) collective-permute-start(f32[256,256]{1,0:T(8,128)S(1)} %collective-permute-done.21.refs_4_), channel_id=1, source_target_pairs={{0,1},{1,0},{2,3},{3,2},{4,5},{5,4},{6,7},{7,6},{8,9},{9,8},{10,11... | collective-permute-start | bytes 786440 | tf_op jit(solution)/shard_map/ppermute | solution.py:43
  79.5 3.4 %collective-permute-start.26 = (f32[256,256]{1,0:T(8,128)S(1)}, f32[256,256]{1,0:T(8,128)S(1)}, u32[]{:S(2)}, u32[]{:S(2)}) collective-permute-start(f32[256,256]{1,0:T(8,128)S(1)} %collective-permute-done.22.refs_6_), channel_id=1, source_target_pairs={{0,1},{1,0},{2,3},{3,2},{4,5},{5,4},{6,7},{7,6},{8,9},{9,8},{10,11... | collective-permute-start | bytes 786440 | tf_op jit(solution)/shard_map/ppermute | solution.py:43
  80.5 9.7 %collective-permute-start.29 = (f16[384,256]{1,0:T(8,128)(2,1)S(1)}, f16[384,256]{1,0:T(8,128)(2,1)S(1)}, u32[]{:S(2)}, u32[]{:S(2)}) collective-permute-start(f16[384,256]{1,0:T(8,128)(2,1)S(1)} %multiply_convert_fusion.1), channel_id=1, source_target_pairs={{0,32},{1,9},{2,34},{3,11},{4,36},{5,13},{6,38},{7,15},{8,40},{9,1... | collective-permute-start | bytes 589832 | tf_op jit(solution)/shard_map/ppermute | solution.py:43
  81.9 8.2 %collective-permute-start.31 = (f16[256,256]{1,0:T(8,128)(2,1)S(1)}, f16[256,256]{1,0:T(8,128)(2,1)S(1)}, u32[]{:S(2)}, u32[]{:S(2)}) collective-permute-start(f16[256,256]{1,0:T(8,128)(2,1)S(1)} %multiply_convert_fusion.2), channel_id=1, source_target_pairs={{0,12},{1,17},{2,76},{3,81},{4,0},{5,21},{6,64},{7,85},{8,4},{9,25... | collective-permute-start | bytes 393224 | tf_op jit(solution)/shard_map/ppermute | solution.py:43
  90.1 1.6 %collective-permute-start.30 = (f16[384,256]{1,0:T(8,128)(2,1)S(1)}, f16[384,256]{1,0:T(8,128)(2,1)S(1)}, u32[]{:S(2)}, u32[]{:S(2)}) collective-permute-start(f16[384,256]{1,0:T(8,128)(2,1)S(1)} %collective-permute-done.29), channel_id=1, source_target_pairs={{0,1},{1,0},{2,3},{3,2},{4,5},{5,4},{6,7},{7,6},{8,9},{9,8},{10,11... | collective-permute-start | bytes 589832 | tf_op jit(solution)/shard_map/ppermute | solution.py:43
  (14 other events, 90.9 us)

commit v8 on v5

--- a/solution.py
+++ b/solution.py
@@ -276,7 +276,7 @@
     late2 = send(pass2, second_partner)
     tiles2, _ = delivered(
         place,
-        [made2, made3, unpacked(got2[0]), unpacked(after(late2, *(mine for _, mine in tiles1)))],
+        [made2, made3, unpacked(got2[0]), unpacked(after(late2, *(mine for _, mine in tiles1 if mine.dtype == jnp.float32)))],
         [
             (FAR[0], [(0, 2, 0), (2, None, 0), (3, None, 0)]),
             (OPPOSITE[0], [(1, 2, 0), (2, None, 256), (3, None, 256)]),

time: 95.2 us -> 95.2 us (level)
  no operation moved by 1% of the time
where the time goes in v8:
time: 95.2 us; the launch traced here: 93.5 us
  waiting for transfers between devices  41.9 us (44%)
  starting transfers between devices  31.9 us (34%)
  Pallas kernels  15 us (16%)
  other arithmetic  2.7 us (3%)
  local copies, waits for them, and re-layouts  1.49 us (2%)
    ppermute x33, waiting for transfers between devices, send(): return lax.ppermute(value, AXES, pairs)  41.9 us
    ppermute x33, starting transfers between devices, send(): return lax.ppermute(value, AXES, pairs)  31.9 us
    pallas_call x6, Pallas kernels, call(): pl.pallas_call(kernel, out_shape=[pltpu.VMEM(s, jnp.float32) if keep else...  10.7 us
    pallas_call x1, Pallas kernels, body(): pl.pallas_call(functools.partial(begin, layouts), out_shape=[pltpu.VMEM(s...  2.56 us
  transfers between devices with their start and end apart: 33, of which 17 were waited for; matrix products, arithmetic and copies ran while one was open for 3% of the time, Pallas kernels for 14%

profile of v8, /device:TPU:33, one launch (start us, length us, event | category | flops | bytes accessed | tf_op | source)
XLA Modules:
  0.0 93.5 jit_solution(13130844461871797459)
XLA Ops:
  0.1 1.2 %constant_dynamic-slice_fusion = (bf16[256,896]{1,0:T(8,128)(2,1)S(1)}, bf16[256,896]{1,0:T(8,128)(2,1)S(1)}) fusion(bf16[256,1792]{1,0:T(8,128)(2,1)} %param.52, s32[]{:T(128)S(6)} %select_n.42, s32[]{:T(128)S(6)} %select_n.39), kind=kLoop, calls=%fused_computation.63 | loop fusion | bytes 1835016 | tf_op jit(solution)/shard_map/dynamic_slice | solution.py:240
  2.1 2.7 %collective-permute-start.2 = (bf16[256,896]{1,0:T(8,128)(2,1)S(1)}, bf16[256,896]{1,0:T(8,128)(2,1)S(1)}, u32[]{:S(2)}, u32[]{:S(2)}) collective-permute-start(bf16[256,896]{1,0:T(8,128)(2,1)S(1)} %get-tuple-element.65), channel_id=1, source_target_pairs={{0,64},{1,65},{2,66},{3,67},{4,68},{5,69},{6,70},{7,71},{8,72},{9,... | collective-permute-start | bytes 1376264 | tf_op jit(solution)/shard_map/ppermute | solution.py:43
  5.0 2.8 %collective-permute-start.1 = (bf16[256,1792]{1,0:T(8,128)(2,1)S(1)}, bf16[256,1792]{1,0:T(8,128)(2,1)S(1)}, u32[]{:S(2)}, u32[]{:S(2)}) collective-permute-start(bf16[256,1792]{1,0:T(8,128)(2,1)S(1)} %pad_maximum_fusion.refs_0_.refs_8_), channel_id=1, source_target_pairs={{0,48},{1,13},{2,50},{3,15},{4,52},{5,1},{6,54},{7,3},{8,56},{9,5}... | collective-permute-start | bytes 2752520 | tf_op jit(solution)/shard_map/ppermute | solution.py:43
  7.8 7.9 %collective-permute-done.2 = bf16[256,896]{1,0:T(8,128)(2,1)S(1)} collective-permute-done((bf16[256,896]{1,0:T(8,128)(2,1)S(1)}, bf16[256,896]{1,0:T(8,128)(2,1)S(1)}, u32[]{:S(2)}, u32[]{:S(2)}) %collective-permute-start.2) | collective-permute-done | bytes 458784 | tf_op jit(solution)/shard_map/ppermute | solution.py:43
  16.5 1.4 %collective-permute-done.3 = bf16[256,896]{1,0:T(8,128)(2,1)S(1)} collective-permute-done((bf16[256,896]{1,0:T(8,128)(2,1)S(1)}, bf16[256,896]{1,0:T(8,128)(2,1)S(1)}, u32[]{:S(2)}, u32[]{:S(2)}) %collective-permute-start.3) | collective-permute-done | bytes 458784 | tf_op jit(solution)/shard_map/ppermute | solution.py:43
  18.1 3.4 %collective-permute-done.4.refs_2_ = bf16[256,1792]{1,0:T(8,128)(2,1)S(1)} collective-permute-done((bf16[256,1792]{1,0:T(8,128)(2,1)S(1)}, bf16[256,1792]{1,0:T(8,128)(2,1)S(1)}, u32[]{:S(2)}, u32[]{:S(2)}) %collective-permute-start.4) | collective-permute-done | bytes 917536 | tf_op jit(solution)/shard_map/ppermute | solution.py:43
  21.8 1.5 %collective-permute-start.6 = (bf16[256,1792]{1,0:T(8,128)(2,1)S(1)}, bf16[256,1792]{1,0:T(8,128)(2,1)S(1)}, u32[]{:S(2)}, u32[]{:S(2)}) collective-permute-start(bf16[256,1792]{1,0:T(8,128)(2,1)S(1)} %pad_maximum_fusion.1.refs_1_.refs_9_), channel_id=1, source_target_pairs={{0,16},{1,5},{2,18},{3,7},{4,20},{5,9},{6,22},{7,11},{8,24},{9,13}... | collective-permute-start | bytes 2752520 | tf_op jit(solution)/shard_map/ppermute | solution.py:43
  23.3 1.8 %shard_map.478.refs_3_ = f32[4,128,256]{2,1,0:T(8,128)S(1)} custom-call(s32[5]{0:T(128)S(1)} %stack.23.place, bf16[256,1792]{1,0:T(8,128)(2,1)S(1)} %pad_maximum_fusion.refs_0_.refs_8_, bf16[256,1792]{1,0:T(8,128)(2,1)S(1)} %pad_maximum_fusion.1.refs_1_.refs_9_), custom_call_target="tpu_custom_call" | custom-call | tf_op jit(solution)/shard_map/pallas_call | solution.py:87
  25.7 2.4 %collective-permute-start.9 = (bf16[256,1792]{1,0:T(8,128)(2,1)S(1)}, bf16[256,1792]{1,0:T(8,128)(2,1)S(1)}, u32[]{:S(2)}, u32[]{:S(2)}) collective-permute-start(bf16[256,1792]{1,0:T(8,128)(2,1)S(1)} %collective-permute-done.1.refs_0_), channel_id=1, source_target_pairs={{0,1},{1,0},{2,3},{3,2},{4,5},{5,4},{6,7},{7,6},{8,9},{9,8},{10,11... | collective-permute-start | bytes 2752520 | tf_op jit(solution)/shard_map/ppermute | solution.py:43
  28.1 1.3 %collective-permute-done.7 = f16[2,128,256]{2,1,0:T(8,128)(2,1)S(1)} collective-permute-done((f16[2,128,256]{2,1,0:T(8,128)(2,1)S(1)}, f16[2,128,256]{2,1,0:T(8,128)(2,1)S(1)}, u32[]{:S(2)}, u32[]{:S(2)}) %collective-permute-start.7) | collective-permute-done | bytes 131104 | tf_op jit(solution)/shard_map/ppermute | solution.py:43
  29.6 2.0 %collective-permute-start.8 = (f16[128,256]{1,0:T(8,128)(2,1)S(1)}, f16[128,256]{1,0:T(8,128)(2,1)S(1)}, u32[]{:S(2)}, u32[]{:S(2)}) collective-permute-start(f16[128,256]{1,0:T(8,128)(2,1)S(1)} %get-tuple-element.72), channel_id=1, source_target_pairs={{0,66},{1,3},{2,64},{3,1},{4,70},{5,7},{6,68},{7,5},{8,74},{9,11},... | collective-permute-start | bytes 196616 | tf_op jit(solution)/shard_map/ppermute | solution.py:43
  31.6 2.0 %collective-permute-done.8 = f16[128,256]{1,0:T(8,128)(2,1)S(1)} collective-permute-done((f16[128,256]{1,0:T(8,128)(2,1)S(1)}, f16[128,256]{1,0:T(8,128)(2,1)S(1)}, u32[]{:S(2)}, u32[]{:S(2)}) %collective-permute-start.8) | collective-permute-done | bytes 65568 | tf_op jit(solution)/shard_map/ppermute | solution.py:43
  34.3 1.3 %collective-permute-done.6.refs_3_ = bf16[256,1792]{1,0:T(8,128)(2,1)S(1)} collective-permute-done((bf16[256,1792]{1,0:T(8,128)(2,1)S(1)}, bf16[256,1792]{1,0:T(8,128)(2,1)S(1)}, u32[]{:S(2)}, u32[]{:S(2)}) %collective-permute-start.6) | collective-permute-done | bytes 917536 | tf_op jit(solution)/shard_map/ppermute | solution.py:43
  35.6 2.1 %collective-permute-start.10 = (bf16[256,1792]{1,0:T(8,128)(2,1)S(1)}, bf16[256,1792]{1,0:T(8,128)(2,1)S(1)}, u32[]{:S(2)}, u32[]{:S(2)}) collective-permute-start(bf16[256,1792]{1,0:T(8,128)(2,1)S(1)} %collective-permute-done.5.refs_1_), channel_id=1, source_target_pairs={{0,1},{1,0},{2,3},{3,2},{4,5},{5,4},{6,7},{7,6},{8,9},{9,8},{10,11... | collective-permute-start | bytes 2752520 | tf_op jit(solution)/shard_map/ppermute | solution.py:43
  37.7 2.7 %collective-permute-start.15 = (bf16[256,1792]{1,0:T(8,128)(2,1)S(1)}, bf16[256,1792]{1,0:T(8,128)(2,1)S(1)}, u32[]{:S(2)}, u32[]{:S(2)}) collective-permute-start(bf16[256,1792]{1,0:T(8,128)(2,1)S(1)} %collective-permute-done.1.refs_0_), channel_id=1, source_target_pairs={{0,48},{1,13},{2,50},{3,15},{4,52},{5,1},{6,54},{7,3},{8,56},{9,5}... | collective-permute-start | bytes 2752520 | tf_op jit(solution)/shard_map/ppermute | solution.py:43
  41.1 3.8 %shard_map.479.refs_0_ = f32[4,768,256]{2,1,0:T(8,128)S(1)} custom-call(s32[5]{0:T(128)S(1)} %stack.23.place, bf16[256,1792]{1,0:T(8,128)(2,1)S(1)} %collective-permute-done.1.refs_0_, bf16[256,1792]{1,0:T(8,128)(2,1)S(1)} %collective-permute-done.5.refs_1_, bf16[256,1792]{1,0:T(8,128)(2,1)S(1)} %collective-permute-done.4.refs_2_, ...), custom_call_target="tpu_custom_call" | custom-call | bytes 16777216 | tf_op jit(solution)/shard_map/pallas_call | solution.py:87
  45.7 5.1 %collective-permute-done.15.refs_0_ = bf16[256,1792]{1,0:T(8,128)(2,1)S(1)} collective-permute-done((bf16[256,1792]{1,0:T(8,128)(2,1)S(1)}, bf16[256,1792]{1,0:T(8,128)(2,1)S(1)}, u32[]{:S(2)}, u32[]{:S(2)}) %collective-permute-start.15) | collective-permute-done | bytes 917536 | tf_op jit(solution)/shard_map/ppermute | solution.py:43
  50.8 3.1 %collective-permute-done.16.refs_1_ = bf16[256,1792]{1,0:T(8,128)(2,1)S(1)} collective-permute-done((bf16[256,1792]{1,0:T(8,128)(2,1)S(1)}, bf16[256,1792]{1,0:T(8,128)(2,1)S(1)}, u32[]{:S(2)}, u32[]{:S(2)}) %collective-permute-start.16) | collective-permute-done | bytes 917536 | tf_op jit(solution)/shard_map/ppermute | solution.py:43
  55.1 0.9 %collective-permute-start.19 = (f16[768,256]{1,0:T(8,128)(2,1)S(1)}, f16[768,256]{1,0:T(8,128)(2,1)S(1)}, u32[]{:S(2)}, u32[]{:S(2)}) collective-permute-start(f16[768,256]{1,0:T(8,128)(2,1)S(1)} %get-tuple-element.61), channel_id=1, source_target_pairs={{0,66},{1,3},{2,64},{3,1},{4,70},{5,7},{6,68},{7,5},{8,74},{9,11},... | collective-permute-start | bytes 1179656 | tf_op jit(solution)/shard_map/ppermute | solution.py:43
  56.0 1.9 %shard_map.480.refs_0_ = f32[4,256,256]{2,1,0:T(8,128)S(1)} custom-call(s32[5]{0:T(128)S(1)} %stack.23.place, bf16[256,1792]{1,0:T(8,128)(2,1)S(1)} %collective-permute-done.15.refs_0_, bf16[256,1792]{1,0:T(8,128)(2,1)S(1)} %collective-permute-done.16.refs_1_, bf16[256,1792]{1,0:T(8,128)(2,1)S(1)} %collective-permute-done.9.refs_4_.refs_2_, ...), custom_call_target="tpu_custom_call" | custom-call | bytes 8388608 | tf_op jit(solution)/shard_map/pallas_call | solution.py:87
  57.9 1.1 %collective-permute-start.14 = (f16[768,256]{1,0:T(8,128)(2,1)S(1)}, f16[768,256]{1,0:T(8,128)(2,1)S(1)}, u32[]{:S(2)}, u32[]{:S(2)}) collective-permute-start(f16[768,256]{1,0:T(8,128)(2,1)S(1)} %get-tuple-element.40), channel_id=1, source_target_pairs={{0,2},{1,67},{2,0},{3,65},{4,6},{5,71},{6,4},{7,69},{8,10},{9,75},... | collective-permute-start | bytes 1179656 | tf_op jit(solution)/shard_map/ppermute | solution.py:43
  59.1 1.8 %shard_map.481.refs_1_ = f32[4,128,256]{2,1,0:T(8,128)S(1)} custom-call(s32[5]{0:T(128)S(1)} %stack.23.place, bf16[256,1792]{1,0:T(8,128)(2,1)S(1)} %collective-permute-done.15.refs_0_, bf16[256,1792]{1,0:T(8,128)(2,1)S(1)} %collective-permute-done.16.refs_1_, bf16[128,1792]{1,0:T(8,128)(2,1)S(1)} %collective-permute-done.17.refs_2_, ...), custom_call_target="tpu_custom_call" | custom-call | bytes 8388608 | tf_op jit(solution)/shard_map/pallas_call | solution.py:87
  61.7 0.9 collective-permute-done.19
  62.6 4.2 %collective-permute-done.14 = f16[768,256]{1,0:T(8,128)(2,1)S(1)} collective-permute-done((f16[768,256]{1,0:T(8,128)(2,1)S(1)}, f16[768,256]{1,0:T(8,128)(2,1)S(1)}, u32[]{:S(2)}, u32[]{:S(2)}) %collective-permute-start.14) | collective-permute-done | bytes 393248 | tf_op jit(solution)/shard_map/ppermute | solution.py:43
  68.8 2.0 %collective-permute-start.23 = (f32[256,256]{1,0:T(8,128)S(1)}, f32[256,256]{1,0:T(8,128)S(1)}, u32[]{:S(2)}, u32[]{:S(2)}) collective-permute-start(f32[256,256]{1,0:T(8,128)S(1)} %get-tuple-element.52), channel_id=1, source_target_pairs={{0,48},{1,13},{2,50},{3,15},{4,52},{5,1},{6,54},{7,3},{8,56},{9,5}... | collective-permute-start | bytes 786440 | tf_op jit(solution)/shard_map/ppermute | solution.py:43
  71.1 2.7 %collective-permute-start.28 = (f16[384,256]{1,0:T(8,128)(2,1)S(1)}, f16[384,256]{1,0:T(8,128)(2,1)S(1)}, u32[]{:S(2)}, u32[]{:S(2)}) collective-permute-start(f16[384,256]{1,0:T(8,128)(2,1)S(1)} %get-tuple-element.69), channel_id=1, source_target_pairs={{0,66},{1,3},{2,64},{3,1},{4,70},{5,7},{6,68},{7,5},{8,74},{9,11},... | collective-permute-start | bytes 589832 | tf_op jit(solution)/shard_map/ppermute | solution.py:43
  73.9 3.9 %collective-permute-done.21 = f16[512,256]{1,0:T(8,128)(2,1)S(1)} collective-permute-done((f16[512,256]{1,0:T(8,128)(2,1)S(1)}, f16[512,256]{1,0:T(8,128)(2,1)S(1)}, u32[]{:S(2)}, u32[]{:S(2)}) %collective-permute-start.21) | collective-permute-done | bytes 262176 | tf_op jit(solution)/shard_map/ppermute | solution.py:43
  77.9 1.1 %collective-permute-start.22 = (f16[512,256]{1,0:T(8,128)(2,1)S(1)}, f16[512,256]{1,0:T(8,128)(2,1)S(1)}, u32[]{:S(2)}, u32[]{:S(2)}) collective-permute-start(f16[512,256]{1,0:T(8,128)(2,1)S(1)} %collective-permute-done.21), channel_id=1, source_target_pairs={{0,1},{1,0},{2,3},{3,2},{4,5},{5,4},{6,7},{7,6},{8,9},{9,8},{10,11... | collective-permute-start | bytes 786440 | tf_op jit(solution)/shard_map/ppermute | solution.py:43
  80.4 1.4 %collective-permute-start.29 = (f16[384,256]{1,0:T(8,128)(2,1)S(1)}, f16[384,256]{1,0:T(8,128)(2,1)S(1)}, u32[]{:S(2)}, u32[]{:S(2)}) collective-permute-start(f16[384,256]{1,0:T(8,128)(2,1)S(1)} %multiply_convert_fusion.1), channel_id=1, source_target_pairs={{0,32},{1,9},{2,34},{3,11},{4,36},{5,13},{6,38},{7,15},{8,40},{9,1... | collective-permute-start | bytes 589832 | tf_op jit(solution)/shard_map/ppermute | solution.py:43
  82.5 2.6 %shard_map.483 = (f32[2048,256]{1,0:T(8,128)S(1)}, f32[2048,256]{1,0:T(8,128)}) custom-call(s32[5]{0:T(128)S(1)} %stack.23.place, f32[2048,256]{1,0:T(8,128)S(1)} %copy-done, f32[384,256]{1,0:T(8,128)S(1)} %get-tuple-element.50.refs_0_, f32[384,256]{1,0:T(8,128)S(1)} %collective-permute-done.20.refs_1_, f32[512,256]{1,0:T(8,128)S(1)} %get-tuple-element.78.refs_2_, ...), custom_call_target="tpu_custom_call" | custom-call | bytes 2097152 | tf_op jit(solution)/shard_map/pallas_call | solution.py:289
  85.1 4.7 %collective-permute-done.31 = f16[256,256]{1,0:T(8,128)(2,1)S(1)} collective-permute-done((f16[256,256]{1,0:T(8,128)(2,1)S(1)}, f16[256,256]{1,0:T(8,128)(2,1)S(1)}, u32[]{:S(2)}, u32[]{:S(2)}) %collective-permute-start.31) | collective-permute-done | bytes 131104 | tf_op jit(solution)/shard_map/ppermute | solution.py:43
  91.7 1.7 %shard_map.485 = f32[2048,256]{1,0:T(8,128)} custom-call(s32[5]{0:T(128)S(1)} %stack.23.place, f32[2048,256]{1,0:T(8,128)S(1)} %get-tuple-element.54.base, f32[384,256]{1,0:T(8,128)S(1)} %get-tuple-element.76.refs_0_, f32[384,256]{1,0:T(8,128)S(1)} %get-tuple-element.75.refs_1_, ...), custom_call_target="tpu_custom_call", output_to_operand_aliasing={{}: (6, {})} | custom-call | bytes 2097152 | tf_op jit(solution)/shard_map/pallas_call | solution.py:300
  (95 shorter events, 13.4 us)
Async XLA Ops:
  1.3 3.5 %collective-permute-start = (bf16[256,896]{1,0:T(8,128)(2,1)S(1)}, bf16[256,896]{1,0:T(8,128)(2,1)S(1)}, u32[]{:S(2)}, u32[]{:S(2)}) collective-permute-start(bf16[256,896]{1,0:T(8,128)(2,1)S(1)} %get-tuple-element.66), channel_id=1, source_target_pairs={{0,1},{1,0},{2,3},{3,2},{4,5},{5,4},{6,7},{7,6},{8,9},{9,8},{10,11... | collective-permute-start | bytes 1376264 | tf_op jit(solution)/shard_map/ppermute | solution.py:43
  2.1 13.6 %collective-permute-start.2 = (bf16[256,896]{1,0:T(8,128)(2,1)S(1)}, bf16[256,896]{1,0:T(8,128)(2,1)S(1)}, u32[]{:S(2)}, u32[]{:S(2)}) collective-permute-start(bf16[256,896]{1,0:T(8,128)(2,1)S(1)} %get-tuple-element.65), channel_id=1, source_target_pairs={{0,64},{1,65},{2,66},{3,67},{4,68},{5,69},{6,70},{7,71},{8,72},{9,... | collective-permute-start | bytes 1376264 | tf_op jit(solution)/shard_map/ppermute | solution.py:43
  5.0 13.1 %collective-permute-start.1 = (bf16[256,1792]{1,0:T(8,128)(2,1)S(1)}, bf16[256,1792]{1,0:T(8,128)(2,1)S(1)}, u32[]{:S(2)}, u32[]{:S(2)}) collective-permute-start(bf16[256,1792]{1,0:T(8,128)(2,1)S(1)} %pad_maximum_fusion.refs_0_.refs_8_), channel_id=1, source_target_pairs={{0,48},{1,13},{2,50},{3,15},{4,52},{5,1},{6,54},{7,3},{8,56},{9,5}... | collective-permute-start | bytes 2752520 | tf_op jit(solution)/shard_map/ppermute | solution.py:43
  7.8 13.8 %collective-permute-start.4 = (bf16[256,1792]{1,0:T(8,128)(2,1)S(1)}, bf16[256,1792]{1,0:T(8,128)(2,1)S(1)}, u32[]{:S(2)}, u32[]{:S(2)}) collective-permute-start(bf16[256,1792]{1,0:T(8,128)(2,1)S(1)} %pad_maximum_fusion.refs_0_.refs_8_), channel_id=1, source_target_pairs={{0,16},{1,5},{2,18},{3,7},{4,20},{5,9},{6,22},{7,11},{8,24},{9,13}... | collective-permute-start | bytes 2752520 | tf_op jit(solution)/shard_map/ppermute | solution.py:43
  15.7 2.3 %collective-permute-start.3 = (bf16[256,896]{1,0:T(8,128)(2,1)S(1)}, bf16[256,896]{1,0:T(8,128)(2,1)S(1)}, u32[]{:S(2)}, u32[]{:S(2)}) collective-permute-start(bf16[256,896]{1,0:T(8,128)(2,1)S(1)} %collective-permute-done.2), channel_id=1, source_target_pairs={{0,1},{1,0},{2,3},{3,2},{4,5},{5,4},{6,7},{7,6},{8,9},{9,8},{10,11... | collective-permute-start | bytes 1376264 | tf_op jit(solution)/shard_map/ppermute | solution.py:43
  21.7 12.6 %collective-permute-start.5 = (bf16[256,1792]{1,0:T(8,128)(2,1)S(1)}, bf16[256,1792]{1,0:T(8,128)(2,1)S(1)}, u32[]{:S(2)}, u32[]{:S(2)}) collective-permute-start(bf16[256,1792]{1,0:T(8,128)(2,1)S(1)} %pad_maximum_fusion.1.refs_1_.refs_9_), channel_id=1, source_target_pairs={{0,48},{1,13},{2,50},{3,15},{4,52},{5,1},{6,54},{7,3},{8,56},{9,5}... | collective-permute-start | bytes 2752520 | tf_op jit(solution)/shard_map/ppermute | solution.py:43
  21.8 13.8 %collective-permute-start.6 = (bf16[256,1792]{1,0:T(8,128)(2,1)S(1)}, bf16[256,1792]{1,0:T(8,128)(2,1)S(1)}, u32[]{:S(2)}, u32[]{:S(2)}) collective-permute-start(bf16[256,1792]{1,0:T(8,128)(2,1)S(1)} %pad_maximum_fusion.1.refs_1_.refs_9_), channel_id=1, source_target_pairs={{0,16},{1,5},{2,18},{3,7},{4,20},{5,9},{6,22},{7,11},{8,24},{9,13}... | collective-permute-start | bytes 2752520 | tf_op jit(solution)/shard_map/ppermute | solution.py:43
  25.2 4.2 %collective-permute-start.7 = (f16[2,128,256]{2,1,0:T(8,128)(2,1)S(1)}, f16[2,128,256]{2,1,0:T(8,128)(2,1)S(1)}, u32[]{:S(2)}, u32[]{:S(2)}) collective-permute-start(f16[2,128,256]{2,1,0:T(8,128)(2,1)S(1)} %fusion.18), channel_id=1, source_target_pairs={{0,2},{1,67},{2,0},{3,65},{4,6},{5,71},{6,4},{7,69},{8,10},{9,75},... | collective-permute-start | bytes 393224 | tf_op jit(solution)/shard_map/ppermute | solution.py:43
  25.7 12.0 %collective-permute-start.9 = (bf16[256,1792]{1,0:T(8,128)(2,1)S(1)}, bf16[256,1792]{1,0:T(8,128)(2,1)S(1)}, u32[]{:S(2)}, u32[]{:S(2)}) collective-permute-start(bf16[256,1792]{1,0:T(8,128)(2,1)S(1)} %collective-permute-done.1.refs_0_), channel_id=1, source_target_pairs={{0,1},{1,0},{2,3},{3,2},{4,5},{5,4},{6,7},{7,6},{8,9},{9,8},{10,11... | collective-permute-start | bytes 2752520 | tf_op jit(solution)/shard_map/ppermute | solution.py:43
  28.1 12.3 %collective-permute-start.11 = (bf16[256,1792]{1,0:T(8,128)(2,1)S(1)}, bf16[256,1792]{1,0:T(8,128)(2,1)S(1)}, u32[]{:S(2)}, u32[]{:S(2)}) collective-permute-start(bf16[256,1792]{1,0:T(8,128)(2,1)S(1)} %collective-permute-done.4.refs_2_), channel_id=1, source_target_pairs={{0,1},{1,0},{2,3},{3,2},{4,5},{5,4},{6,7},{7,6},{8,9},{9,8},{10,11... | collective-permute-start | bytes 2752520 | tf_op jit(solution)/shard_map/ppermute | solution.py:43
  29.6 4.0 %collective-permute-start.8 = (f16[128,256]{1,0:T(8,128)(2,1)S(1)}, f16[128,256]{1,0:T(8,128)(2,1)S(1)}, u32[]{:S(2)}, u32[]{:S(2)}) collective-permute-start(f16[128,256]{1,0:T(8,128)(2,1)S(1)} %get-tuple-element.72), channel_id=1, source_target_pairs={{0,66},{1,3},{2,64},{3,1},{4,70},{5,7},{6,68},{7,5},{8,74},{9,11},... | collective-permute-start | bytes 196616 | tf_op jit(solution)/shard_map/ppermute | solution.py:43
  35.6 4.8 %collective-permute-start.10 = (bf16[256,1792]{1,0:T(8,128)(2,1)S(1)}, bf16[256,1792]{1,0:T(8,128)(2,1)S(1)}, u32[]{:S(2)}, u32[]{:S(2)}) collective-permute-start(bf16[256,1792]{1,0:T(8,128)(2,1)S(1)} %collective-permute-done.5.refs_1_), channel_id=1, source_target_pairs={{0,1},{1,0},{2,3},{3,2},{4,5},{5,4},{6,7},{7,6},{8,9},{9,8},{10,11... | collective-permute-start | bytes 2752520 | tf_op jit(solution)/shard_map/ppermute | solution.py:43
  37.7 3.4 %collective-permute-start.12 = (bf16[256,1792]{1,0:T(8,128)(2,1)S(1)}, bf16[256,1792]{1,0:T(8,128)(2,1)S(1)}, u32[]{:S(2)}, u32[]{:S(2)}) collective-permute-start(bf16[256,1792]{1,0:T(8,128)(2,1)S(1)} %collective-permute-done.6.refs_3_), channel_id=1, source_target_pairs={{0,1},{1,0},{2,3},{3,2},{4,5},{5,4},{6,7},{7,6},{8,9},{9,8},{10,11... | collective-permute-start | bytes 2752520 | tf_op jit(solution)/shard_map/ppermute | solution.py:43
  37.7 13.1 %collective-permute-start.15 = (bf16[256,1792]{1,0:T(8,128)(2,1)S(1)}, bf16[256,1792]{1,0:T(8,128)(2,1)S(1)}, u32[]{:S(2)}, u32[]{:S(2)}) collective-permute-start(bf16[256,1792]{1,0:T(8,128)(2,1)S(1)} %collective-permute-done.1.refs_0_), channel_id=1, source_target_pairs={{0,48},{1,13},{2,50},{3,15},{4,52},{5,1},{6,54},{7,3},{8,56},{9,5}... | collective-permute-start | bytes 2752520 | tf_op jit(solution)/shard_map/ppermute | solution.py:43
  40.5 13.5 %collective-permute-start.16 = (bf16[256,1792]{1,0:T(8,128)(2,1)S(1)}, bf16[256,1792]{1,0:T(8,128)(2,1)S(1)}, u32[]{:S(2)}, u32[]{:S(2)}) collective-permute-start(bf16[256,1792]{1,0:T(8,128)(2,1)S(1)} %collective-permute-done.6.refs_3_), channel_id=1, source_target_pairs={{0,16},{1,5},{2,18},{3,7},{4,20},{5,9},{6,22},{7,11},{8,24},{9,13}... | collective-permute-start | bytes 2752520 | tf_op jit(solution)/shard_map/ppermute | solution.py:43
  45.1 8.8 %collective-permute-start.13 = (f16[768,256]{1,0:T(8,128)(2,1)S(1)}, f16[768,256]{1,0:T(8,128)(2,1)S(1)}, u32[]{:S(2)}, u32[]{:S(2)}) collective-permute-start(f16[768,256]{1,0:T(8,128)(2,1)S(1)} %fusion.2), channel_id=1, source_target_pairs={{0,2},{1,67},{2,0},{3,65},{4,6},{5,71},{6,4},{7,69},{8,10},{9,75},... | collective-permute-start | bytes 1179656 | tf_op jit(solution)/shard_map/ppermute | solution.py:43
  54.0 5.1 %collective-permute-start.17 = (bf16[128,1792]{1,0:T(8,128)(2,1)S(1)}, bf16[128,1792]{1,0:T(8,128)(2,1)S(1)}, u32[]{:S(2)}, u32[]{:S(2)}) collective-permute-start(bf16[128,1792]{1,0:T(8,128)(2,1)S(1)} %slice_select_fusion.1), channel_id=1, source_target_pairs={{0,1},{1,0},{2,3},{3,2},{4,5},{5,4},{6,7},{7,6},{8,9},{9,8},{10,11... | collective-permute-start | bytes 1376264 | tf_op jit(solution)/shard_map/ppermute | solution.py:43
  54.1 4.9 %collective-permute-start.18 = (bf16[128,1792]{1,0:T(8,128)(2,1)S(1)}, bf16[128,1792]{1,0:T(8,128)(2,1)S(1)}, u32[]{:S(2)}, u32[]{:S(2)}) collective-permute-start(bf16[128,1792]{1,0:T(8,128)(2,1)S(1)} %slice_select_fusion), channel_id=1, source_target_pairs={{0,1},{1,0},{2,3},{3,2},{4,5},{5,4},{6,7},{7,6},{8,9},{9,8},{10,11... | collective-permute-start | bytes 1376264 | tf_op jit(solution)/shard_map/ppermute | solution.py:43
  55.1 7.5 %collective-permute-start.19 = (f16[768,256]{1,0:T(8,128)(2,1)S(1)}, f16[768,256]{1,0:T(8,128)(2,1)S(1)}, u32[]{:S(2)}, u32[]{:S(2)}) collective-permute-start(f16[768,256]{1,0:T(8,128)(2,1)S(1)} %get-tuple-element.61), channel_id=1, source_target_pairs={{0,66},{1,3},{2,64},{3,1},{4,70},{5,7},{6,68},{7,5},{8,74},{9,11},... | collective-permute-start | bytes 1179656 | tf_op jit(solution)/shard_map/ppermute | solution.py:43
  57.9 8.8 %collective-permute-start.14 = (f16[768,256]{1,0:T(8,128)(2,1)S(1)}, f16[768,256]{1,0:T(8,128)(2,1)S(1)}, u32[]{:S(2)}, u32[]{:S(2)}) collective-permute-start(f16[768,256]{1,0:T(8,128)(2,1)S(1)} %get-tuple-element.40), channel_id=1, source_target_pairs={{0,2},{1,67},{2,0},{3,65},{4,6},{5,71},{6,4},{7,69},{8,10},{9,75},... | collective-permute-start | bytes 1179656 | tf_op jit(solution)/shard_map/ppermute | solution.py:43
  61.1 9.7 %collective-permute-start.27 = (f16[2,384,256]{2,1,0:T(8,128)(2,1)S(1)}, f16[2,384,256]{2,1,0:T(8,128)(2,1)S(1)}, u32[]{:S(2)}, u32[]{:S(2)}) collective-permute-start(f16[2,384,256]{2,1,0:T(8,128)(2,1)S(1)} %fusion.11), channel_id=1, source_target_pairs={{0,2},{1,67},{2,0},{3,65},{4,6},{5,71},{6,4},{7,69},{8,10},{9,75},... | collective-permute-start | bytes 1179656 | tf_op jit(solution)/shard_map/ppermute | solution.py:43
  67.9 9.9 %collective-permute-start.21 = (f16[512,256]{1,0:T(8,128)(2,1)S(1)}, f16[512,256]{1,0:T(8,128)(2,1)S(1)}, u32[]{:S(2)}, u32[]{:S(2)}) collective-permute-start(f16[512,256]{1,0:T(8,128)(2,1)S(1)} %multiply_convert_fusion), channel_id=1, source_target_pairs={{0,16},{1,5},{2,80},{3,69},{4,20},{5,9},{6,84},{7,73},{8,24},{9,13... | collective-permute-start | bytes 786440 | tf_op jit(solution)/shard_map/ppermute | solution.py:43
  68.8 10.2 %collective-permute-start.23 = (f32[256,256]{1,0:T(8,128)S(1)}, f32[256,256]{1,0:T(8,128)S(1)}, u32[]{:S(2)}, u32[]{:S(2)}) collective-permute-start(f32[256,256]{1,0:T(8,128)S(1)} %get-tuple-element.52), channel_id=1, source_target_pairs={{0,48},{1,13},{2,50},{3,15},{4,52},{5,1},{6,54},{7,3},{8,56},{9,5}... | collective-permute-start | bytes 786440 | tf_op jit(solution)/shard_map/ppermute | solution.py:43
  70.8 8.2 %collective-permute-start.25 = (f32[256,256]{1,0:T(8,128)S(1)}, f32[256,256]{1,0:T(8,128)S(1)}, u32[]{:S(2)}, u32[]{:S(2)}) collective-permute-start(f32[256,256]{1,0:T(8,128)S(1)} %get-tuple-element.53), channel_id=1, source_target_pairs={{0,4},{1,49},{2,6},{3,51},{4,8},{5,53},{6,10},{7,55},{8,12},{9,57}... | collective-permute-start | bytes 786440 | tf_op jit(solution)/shard_map/ppermute | solution.py:43
  71.1 8.4 %collective-permute-start.28 = (f16[384,256]{1,0:T(8,128)(2,1)S(1)}, f16[384,256]{1,0:T(8,128)(2,1)S(1)}, u32[]{:S(2)}, u32[]{:S(2)}) collective-permute-start(f16[384,256]{1,0:T(8,128)(2,1)S(1)} %get-tuple-element.69), channel_id=1, source_target_pairs={{0,66},{1,3},{2,64},{3,1},{4,70},{5,7},{6,68},{7,5},{8,74},{9,11},... | collective-permute-start | bytes 589832 | tf_op jit(solution)/shard_map/ppermute | solution.py:43
  73.8 8.6 %collective-permute-start.20 = (f32[384,256]{1,0:T(8,128)S(1)}, f32[384,256]{1,0:T(8,128)S(1)}, u32[]{:S(2)}, u32[]{:S(2)}) collective-permute-start(f32[384,256]{1,0:T(8,128)S(1)} %get-tuple-element.50.refs_0_), channel_id=1, source_target_pairs={{0,1},{1,0},{2,3},{3,2},{4,5},{5,4},{6,7},{7,6},{8,9},{9,8},{10,11... | collective-permute-start | bytes 1179656 | tf_op jit(solution)/shard_map/ppermute | solution.py:43
  77.9 4.0 %collective-permute-start.22 = (f16[512,256]{1,0:T(8,128)(2,1)S(1)}, f16[512,256]{1,0:T(8,128)(2,1)S(1)}, u32[]{:S(2)}, u32[]{:S(2)}) collective-permute-start(f16[512,256]{1,0:T(8,128)(2,1)S(1)} %collective-permute-done.21), channel_id=1, source_target_pairs={{0,1},{1,0},{2,3},{3,2},{4,5},{5,4},{6,7},{7,6},{8,9},{9,8},{10,11... | collective-permute-start | bytes 786440 | tf_op jit(solution)/shard_map/ppermute | solution.py:43
  78.9 3.5 %collective-permute-start.24 = (f32[256,256]{1,0:T(8,128)S(1)}, f32[256,256]{1,0:T(8,128)S(1)}, u32[]{:S(2)}, u32[]{:S(2)}) collective-permute-start(f32[256,256]{1,0:T(8,128)S(1)} %collective-permute-done.23.refs_4_), channel_id=1, source_target_pairs={{0,1},{1,0},{2,3},{3,2},{4,5},{5,4},{6,7},{7,6},{8,9},{9,8},{10,11... | collective-permute-start | bytes 786440 | tf_op jit(solution)/shard_map/ppermute | solution.py:43
  78.9 3.5 %collective-permute-start.26 = (f32[256,256]{1,0:T(8,128)S(1)}, f32[256,256]{1,0:T(8,128)S(1)}, u32[]{:S(2)}, u32[]{:S(2)}) collective-permute-start(f32[256,256]{1,0:T(8,128)S(1)} %collective-permute-done.25.refs_6_), channel_id=1, source_target_pairs={{0,1},{1,0},{2,3},{3,2},{4,5},{5,4},{6,7},{7,6},{8,9},{9,8},{10,11... | collective-permute-start | bytes 786440 | tf_op jit(solution)/shard_map/ppermute | solution.py:43
  80.4 9.4 %collective-permute-start.29 = (f16[384,256]{1,0:T(8,128)(2,1)S(1)}, f16[384,256]{1,0:T(8,128)(2,1)S(1)}, u32[]{:S(2)}, u32[]{:S(2)}) collective-permute-start(f16[384,256]{1,0:T(8,128)(2,1)S(1)} %multiply_convert_fusion.1), channel_id=1, source_target_pairs={{0,32},{1,9},{2,34},{3,11},{4,36},{5,13},{6,38},{7,15},{8,40},{9,1... | collective-permute-start | bytes 589832 | tf_op jit(solution)/shard_map/ppermute | solution.py:43
  81.8 7.9 %collective-permute-start.31 = (f16[256,256]{1,0:T(8,128)(2,1)S(1)}, f16[256,256]{1,0:T(8,128)(2,1)S(1)}, u32[]{:S(2)}, u32[]{:S(2)}) collective-permute-start(f16[256,256]{1,0:T(8,128)(2,1)S(1)} %multiply_convert_fusion.2), channel_id=1, source_target_pairs={{0,12},{1,17},{2,76},{3,81},{4,0},{5,21},{6,64},{7,85},{8,4},{9,25... | collective-permute-start | bytes 393224 | tf_op jit(solution)/shard_map/ppermute | solution.py:43
  89.8 1.8 %collective-permute-start.30 = (f16[384,256]{1,0:T(8,128)(2,1)S(1)}, f16[384,256]{1,0:T(8,128)(2,1)S(1)}, u32[]{:S(2)}, u32[]{:S(2)}) collective-permute-start(f16[384,256]{1,0:T(8,128)(2,1)S(1)} %collective-permute-done.29), channel_id=1, source_target_pairs={{0,1},{1,0},{2,3},{3,2},{4,5},{5,4},{6,7},{7,6},{8,9},{9,8},{10,11... | collective-permute-start | bytes 589832 | tf_op jit(solution)/shard_map/ppermute | solution.py:43
  (14 other events, 90.2 us)

commit v9 on v8

--- a/solution.py
+++ b/solution.py
@@ -285,7 +285,8 @@
     anywhere = pl.BlockSpec(memory_space=pl.ANY)
     params = pltpu.CompilerParams(vmem_limit_bytes=8 * 2**20)
     cost = pl.CostEstimate(flops=0, bytes_accessed=2**21, transcendentals=0)
-    layouts, tiles = with_halves(tiles1)
+    received = [mine for _, mine in tiles1]
+    layouts, tiles = with_halves([(layout, after(mine, *received)) for layout, mine in tiles1])
     base, new = pl.pallas_call(
         functools.partial(begin, layouts),
         out_shape=[pltpu.VMEM(stat_old.shape, jnp.float32), jax.ShapeDtypeStruct(stat_old.shape, jnp.float32)],

time: 95.2 us -> 95.1 us (level)
  no operation moved by 1% of the time
where the time goes in v9:
time: 95.1 us; the launch traced here: 93.7 us
  waiting for transfers between devices  42 us (44%)
  starting transfers between devices  32 us (34%)
  Pallas kernels  15 us (16%)
  other arithmetic  2.7 us (3%)
  local copies, waits for them, and re-layouts  1.49 us (2%)
    ppermute x33, waiting for transfers between devices, send(): return lax.ppermute(value, AXES, pairs)  42 us
    ppermute x33, starting transfers between devices, send(): return lax.ppermute(value, AXES, pairs)  32 us
    pallas_call x6, Pallas kernels, call(): pl.pallas_call(kernel, out_shape=[pltpu.VMEM(s, jnp.float32) if keep else...  10.7 us
    pallas_call x1, Pallas kernels, body(): pl.pallas_call(functools.partial(begin, layouts), out_shape=[pltpu.VMEM(s...  2.56 us
  transfers between devices with their start and end apart: 33, of which 17 were waited for; matrix products, arithmetic and copies ran while one was open for 3% of the time, Pallas kernels for 14%

profile of v9, /device:TPU:33, one launch (start us, length us, event | category | flops | bytes accessed | tf_op | source)
XLA Modules:
  0.0 93.7 jit_solution(10616795972433233065)
XLA Ops:
  0.1 1.2 %constant_dynamic-slice_fusion = (bf16[256,896]{1,0:T(8,128)(2,1)S(1)}, bf16[256,896]{1,0:T(8,128)(2,1)S(1)}) fusion(bf16[256,1792]{1,0:T(8,128)(2,1)} %param.52, s32[]{:T(128)S(6)} %select_n.42, s32[]{:T(128)S(6)} %select_n.39), kind=kLoop, calls=%fused_computation.63 | loop fusion | bytes 1835016 | tf_op jit(solution)/shard_map/dynamic_slice | solution.py:240
  2.1 2.7 %collective-permute-start.2 = (bf16[256,896]{1,0:T(8,128)(2,1)S(1)}, bf16[256,896]{1,0:T(8,128)(2,1)S(1)}, u32[]{:S(2)}, u32[]{:S(2)}) collective-permute-start(bf16[256,896]{1,0:T(8,128)(2,1)S(1)} %get-tuple-element.73), channel_id=1, source_target_pairs={{0,64},{1,65},{2,66},{3,67},{4,68},{5,69},{6,70},{7,71},{8,72},{9,... | collective-permute-start | bytes 1376264 | tf_op jit(solution)/shard_map/ppermute | solution.py:43
  5.0 2.8 %collective-permute-start.1 = (bf16[256,1792]{1,0:T(8,128)(2,1)S(1)}, bf16[256,1792]{1,0:T(8,128)(2,1)S(1)}, u32[]{:S(2)}, u32[]{:S(2)}) collective-permute-start(bf16[256,1792]{1,0:T(8,128)(2,1)S(1)} %pad_maximum_fusion.refs_0_.refs_8_), channel_id=1, source_target_pairs={{0,48},{1,13},{2,50},{3,15},{4,52},{5,1},{6,54},{7,3},{8,56},{9,5}... | collective-permute-start | bytes 2752520 | tf_op jit(solution)/shard_map/ppermute | solution.py:43
  7.8 7.9 %collective-permute-done.2 = bf16[256,896]{1,0:T(8,128)(2,1)S(1)} collective-permute-done((bf16[256,896]{1,0:T(8,128)(2,1)S(1)}, bf16[256,896]{1,0:T(8,128)(2,1)S(1)}, u32[]{:S(2)}, u32[]{:S(2)}) %collective-permute-start.2) | collective-permute-done | bytes 458784 | tf_op jit(solution)/shard_map/ppermute | solution.py:43
  16.5 1.4 %collective-permute-done.3 = bf16[256,896]{1,0:T(8,128)(2,1)S(1)} collective-permute-done((bf16[256,896]{1,0:T(8,128)(2,1)S(1)}, bf16[256,896]{1,0:T(8,128)(2,1)S(1)}, u32[]{:S(2)}, u32[]{:S(2)}) %collective-permute-start.3) | collective-permute-done | bytes 458784 | tf_op jit(solution)/shard_map/ppermute | solution.py:43
  18.1 3.4 %collective-permute-done.4.refs_2_ = bf16[256,1792]{1,0:T(8,128)(2,1)S(1)} collective-permute-done((bf16[256,1792]{1,0:T(8,128)(2,1)S(1)}, bf16[256,1792]{1,0:T(8,128)(2,1)S(1)}, u32[]{:S(2)}, u32[]{:S(2)}) %collective-permute-start.4) | collective-permute-done | bytes 917536 | tf_op jit(solution)/shard_map/ppermute | solution.py:43
  21.8 1.5 %collective-permute-start.6 = (bf16[256,1792]{1,0:T(8,128)(2,1)S(1)}, bf16[256,1792]{1,0:T(8,128)(2,1)S(1)}, u32[]{:S(2)}, u32[]{:S(2)}) collective-permute-start(bf16[256,1792]{1,0:T(8,128)(2,1)S(1)} %pad_maximum_fusion.1.refs_1_.refs_9_), channel_id=1, source_target_pairs={{0,16},{1,5},{2,18},{3,7},{4,20},{5,9},{6,22},{7,11},{8,24},{9,13}... | collective-permute-start | bytes 2752520 | tf_op jit(solution)/shard_map/ppermute | solution.py:43
  23.3 1.8 %shard_map.478.refs_3_ = f32[4,128,256]{2,1,0:T(8,128)S(1)} custom-call(s32[5]{0:T(128)S(1)} %stack.23.place, bf16[256,1792]{1,0:T(8,128)(2,1)S(1)} %pad_maximum_fusion.refs_0_.refs_8_, bf16[256,1792]{1,0:T(8,128)(2,1)S(1)} %pad_maximum_fusion.1.refs_1_.refs_9_), custom_call_target="tpu_custom_call" | custom-call | tf_op jit(solution)/shard_map/pallas_call | solution.py:87
  25.7 2.4 %collective-permute-start.9 = (bf16[256,1792]{1,0:T(8,128)(2,1)S(1)}, bf16[256,1792]{1,0:T(8,128)(2,1)S(1)}, u32[]{:S(2)}, u32[]{:S(2)}) collective-permute-start(bf16[256,1792]{1,0:T(8,128)(2,1)S(1)} %collective-permute-done.1.refs_0_), channel_id=1, source_target_pairs={{0,1},{1,0},{2,3},{3,2},{4,5},{5,4},{6,7},{7,6},{8,9},{9,8},{10,11... | collective-permute-start | bytes 2752520 | tf_op jit(solution)/shard_map/ppermute | solution.py:43
  28.1 1.3 %collective-permute-done.7 = f16[2,128,256]{2,1,0:T(8,128)(2,1)S(1)} collective-permute-done((f16[2,128,256]{2,1,0:T(8,128)(2,1)S(1)}, f16[2,128,256]{2,1,0:T(8,128)(2,1)S(1)}, u32[]{:S(2)}, u32[]{:S(2)}) %collective-permute-start.7) | collective-permute-done | bytes 131104 | tf_op jit(solution)/shard_map/ppermute | solution.py:43
  29.6 2.0 %collective-permute-start.8 = (f16[128,256]{1,0:T(8,128)(2,1)S(1)}, f16[128,256]{1,0:T(8,128)(2,1)S(1)}, u32[]{:S(2)}, u32[]{:S(2)}) collective-permute-start(f16[128,256]{1,0:T(8,128)(2,1)S(1)} %get-tuple-element.80), channel_id=1, source_target_pairs={{0,66},{1,3},{2,64},{3,1},{4,70},{5,7},{6,68},{7,5},{8,74},{9,11},... | collective-permute-start | bytes 196616 | tf_op jit(solution)/shard_map/ppermute | solution.py:43
  31.6 2.0 %collective-permute-done.8 = f16[128,256]{1,0:T(8,128)(2,1)S(1)} collective-permute-done((f16[128,256]{1,0:T(8,128)(2,1)S(1)}, f16[128,256]{1,0:T(8,128)(2,1)S(1)}, u32[]{:S(2)}, u32[]{:S(2)}) %collective-permute-start.8) | collective-permute-done | bytes 65568 | tf_op jit(solution)/shard_map/ppermute | solution.py:43
  34.3 1.3 %collective-permute-done.6.refs_3_ = bf16[256,1792]{1,0:T(8,128)(2,1)S(1)} collective-permute-done((bf16[256,1792]{1,0:T(8,128)(2,1)S(1)}, bf16[256,1792]{1,0:T(8,128)(2,1)S(1)}, u32[]{:S(2)}, u32[]{:S(2)}) %collective-permute-start.6) | collective-permute-done | bytes 917536 | tf_op jit(solution)/shard_map/ppermute | solution.py:43
  35.6 2.1 %collective-permute-start.10 = (bf16[256,1792]{1,0:T(8,128)(2,1)S(1)}, bf16[256,1792]{1,0:T(8,128)(2,1)S(1)}, u32[]{:S(2)}, u32[]{:S(2)}) collective-permute-start(bf16[256,1792]{1,0:T(8,128)(2,1)S(1)} %collective-permute-done.5.refs_1_), channel_id=1, source_target_pairs={{0,1},{1,0},{2,3},{3,2},{4,5},{5,4},{6,7},{7,6},{8,9},{9,8},{10,11... | collective-permute-start | bytes 2752520 | tf_op jit(solution)/shard_map/ppermute | solution.py:43
  37.7 2.7 %collective-permute-start.15 = (bf16[256,1792]{1,0:T(8,128)(2,1)S(1)}, bf16[256,1792]{1,0:T(8,128)(2,1)S(1)}, u32[]{:S(2)}, u32[]{:S(2)}) collective-permute-start(bf16[256,1792]{1,0:T(8,128)(2,1)S(1)} %collective-permute-done.1.refs_0_), channel_id=1, source_target_pairs={{0,48},{1,13},{2,50},{3,15},{4,52},{5,1},{6,54},{7,3},{8,56},{9,5}... | collective-permute-start | bytes 2752520 | tf_op jit(solution)/shard_map/ppermute | solution.py:43
  41.1 3.8 %shard_map.479.refs_0_ = f32[4,768,256]{2,1,0:T(8,128)S(1)} custom-call(s32[5]{0:T(128)S(1)} %stack.23.place, bf16[256,1792]{1,0:T(8,128)(2,1)S(1)} %collective-permute-done.1.refs_0_, bf16[256,1792]{1,0:T(8,128)(2,1)S(1)} %collective-permute-done.5.refs_1_, bf16[256,1792]{1,0:T(8,128)(2,1)S(1)} %collective-permute-done.4.refs_2_, ...), custom_call_target="tpu_custom_call" | custom-call | bytes 16777216 | tf_op jit(solution)/shard_map/pallas_call | solution.py:87
  45.7 5.1 %collective-permute-done.15.refs_0_ = bf16[256,1792]{1,0:T(8,128)(2,1)S(1)} collective-permute-done((bf16[256,1792]{1,0:T(8,128)(2,1)S(1)}, bf16[256,1792]{1,0:T(8,128)(2,1)S(1)}, u32[]{:S(2)}, u32[]{:S(2)}) %collective-permute-start.15) | collective-permute-done | bytes 917536 | tf_op jit(solution)/shard_map/ppermute | solution.py:43
  50.8 3.1 %collective-permute-done.16.refs_1_ = bf16[256,1792]{1,0:T(8,128)(2,1)S(1)} collective-permute-done((bf16[256,1792]{1,0:T(8,128)(2,1)S(1)}, bf16[256,1792]{1,0:T(8,128)(2,1)S(1)}, u32[]{:S(2)}, u32[]{:S(2)}) %collective-permute-start.16) | collective-permute-done | bytes 917536 | tf_op jit(solution)/shard_map/ppermute | solution.py:43
  55.1 0.9 %collective-permute-start.19 = (f16[768,256]{1,0:T(8,128)(2,1)S(1)}, f16[768,256]{1,0:T(8,128)(2,1)S(1)}, u32[]{:S(2)}, u32[]{:S(2)}) collective-permute-start(f16[768,256]{1,0:T(8,128)(2,1)S(1)} %get-tuple-element.69), channel_id=1, source_target_pairs={{0,66},{1,3},{2,64},{3,1},{4,70},{5,7},{6,68},{7,5},{8,74},{9,11},... | collective-permute-start | bytes 1179656 | tf_op jit(solution)/shard_map/ppermute | solution.py:43
  56.0 1.9 %shard_map.480.refs_0_ = f32[4,256,256]{2,1,0:T(8,128)S(1)} custom-call(s32[5]{0:T(128)S(1)} %stack.23.place, bf16[256,1792]{1,0:T(8,128)(2,1)S(1)} %collective-permute-done.15.refs_0_, bf16[256,1792]{1,0:T(8,128)(2,1)S(1)} %collective-permute-done.16.refs_1_, bf16[256,1792]{1,0:T(8,128)(2,1)S(1)} %collective-permute-done.9.refs_4_.refs_2_, ...), custom_call_target="tpu_custom_call" | custom-call | bytes 8388608 | tf_op jit(solution)/shard_map/pallas_call | solution.py:87
  57.9 1.1 %collective-permute-start.14 = (f16[768,256]{1,0:T(8,128)(2,1)S(1)}, f16[768,256]{1,0:T(8,128)(2,1)S(1)}, u32[]{:S(2)}, u32[]{:S(2)}) collective-permute-start(f16[768,256]{1,0:T(8,128)(2,1)S(1)} %get-tuple-element.44), channel_id=1, source_target_pairs={{0,2},{1,67},{2,0},{3,65},{4,6},{5,71},{6,4},{7,69},{8,10},{9,75},... | collective-permute-start | bytes 1179656 | tf_op jit(solution)/shard_map/ppermute | solution.py:43
  59.1 1.8 %shard_map.481.refs_1_ = f32[4,128,256]{2,1,0:T(8,128)S(1)} custom-call(s32[5]{0:T(128)S(1)} %stack.23.place, bf16[256,1792]{1,0:T(8,128)(2,1)S(1)} %collective-permute-done.15.refs_0_, bf16[256,1792]{1,0:T(8,128)(2,1)S(1)} %collective-permute-done.16.refs_1_, bf16[128,1792]{1,0:T(8,128)(2,1)S(1)} %collective-permute-done.17.refs_2_, ...), custom_call_target="tpu_custom_call" | custom-call | bytes 8388608 | tf_op jit(solution)/shard_map/pallas_call | solution.py:87
  61.7 0.9 collective-permute-done.19
  62.6 4.2 %collective-permute-done.14 = f16[768,256]{1,0:T(8,128)(2,1)S(1)} collective-permute-done((f16[768,256]{1,0:T(8,128)(2,1)S(1)}, f16[768,256]{1,0:T(8,128)(2,1)S(1)}, u32[]{:S(2)}, u32[]{:S(2)}) %collective-permute-start.14) | collective-permute-done | bytes 393248 | tf_op jit(solution)/shard_map/ppermute | solution.py:43
  68.8 2.0 %collective-permute-start.21 = (f32[256,256]{1,0:T(8,128)S(1)}, f32[256,256]{1,0:T(8,128)S(1)}, u32[]{:S(2)}, u32[]{:S(2)}) collective-permute-start(f32[256,256]{1,0:T(8,128)S(1)} %get-tuple-element.56), channel_id=1, source_target_pairs={{0,48},{1,13},{2,50},{3,15},{4,52},{5,1},{6,54},{7,3},{8,56},{9,5}... | collective-permute-start | bytes 786440 | tf_op jit(solution)/shard_map/ppermute | solution.py:43
  71.1 2.7 %collective-permute-start.28 = (f16[384,256]{1,0:T(8,128)(2,1)S(1)}, f16[384,256]{1,0:T(8,128)(2,1)S(1)}, u32[]{:S(2)}, u32[]{:S(2)}) collective-permute-start(f16[384,256]{1,0:T(8,128)(2,1)S(1)} %get-tuple-element.77), channel_id=1, source_target_pairs={{0,66},{1,3},{2,64},{3,1},{4,70},{5,7},{6,68},{7,5},{8,74},{9,11},... | collective-permute-start | bytes 589832 | tf_op jit(solution)/shard_map/ppermute | solution.py:43
  73.8 4.0 %collective-permute-done.20 = f16[512,256]{1,0:T(8,128)(2,1)S(1)} collective-permute-done((f16[512,256]{1,0:T(8,128)(2,1)S(1)}, f16[512,256]{1,0:T(8,128)(2,1)S(1)}, u32[]{:S(2)}, u32[]{:S(2)}) %collective-permute-start.20) | collective-permute-done | bytes 262176 | tf_op jit(solution)/shard_map/ppermute | solution.py:43
  77.9 1.1 %collective-permute-start.23 = (f32[384,256]{1,0:T(8,128)S(1)}, f32[384,256]{1,0:T(8,128)S(1)}, u32[]{:S(2)}, u32[]{:S(2)}) collective-permute-start(f32[384,256]{1,0:T(8,128)S(1)} %get-tuple-element.58.refs_0_), channel_id=1, source_target_pairs={{0,1},{1,0},{2,3},{3,2},{4,5},{5,4},{6,7},{7,6},{8,9},{9,8},{10,11... | collective-permute-start | bytes 1179656 | tf_op jit(solution)/shard_map/ppermute | solution.py:43
  80.5 1.4 %collective-permute-start.29 = (f16[384,256]{1,0:T(8,128)(2,1)S(1)}, f16[384,256]{1,0:T(8,128)(2,1)S(1)}, u32[]{:S(2)}, u32[]{:S(2)}) collective-permute-start(f16[384,256]{1,0:T(8,128)(2,1)S(1)} %multiply_convert_fusion.1), channel_id=1, source_target_pairs={{0,32},{1,9},{2,34},{3,11},{4,36},{5,13},{6,38},{7,15},{8,40},{9,1... | collective-permute-start | bytes 589832 | tf_op jit(solution)/shard_map/ppermute | solution.py:43
  82.9 2.6 %shard_map.483 = (f32[2048,256]{1,0:T(8,128)S(1)}, f32[2048,256]{1,0:T(8,128)}) custom-call(s32[5]{0:T(128)S(1)} %stack.23.place, f32[2048,256]{1,0:T(8,128)S(1)} %copy-done, f32[384,256]{1,0:T(8,128)S(1)} %get-tuple-element.58.refs_0_, f32[384,256]{1,0:T(8,128)S(1)} %collective-permute-done.23.refs_1_, f32[512,256]{1,0:T(8,128)S(1)} %get-tuple-element.86.refs_2_, ...), custom_call_target="tpu_custom_call" | custom-call | bytes 2097152 | tf_op jit(solution)/shard_map/pallas_call | solution.py:290
  85.5 4.6 %collective-permute-done.31 = f16[256,256]{1,0:T(8,128)(2,1)S(1)} collective-permute-done((f16[256,256]{1,0:T(8,128)(2,1)S(1)}, f16[256,256]{1,0:T(8,128)(2,1)S(1)}, u32[]{:S(2)}, u32[]{:S(2)}) %collective-permute-start.31) | collective-permute-done | bytes 131104 | tf_op jit(solution)/shard_map/ppermute | solution.py:43
  91.9 1.7 %shard_map.485 = f32[2048,256]{1,0:T(8,128)} custom-call(s32[5]{0:T(128)S(1)} %stack.23.place, f32[2048,256]{1,0:T(8,128)S(1)} %get-tuple-element.62.base, f32[384,256]{1,0:T(8,128)S(1)} %get-tuple-element.84.refs_0_, f32[384,256]{1,0:T(8,128)S(1)} %get-tuple-element.83.refs_1_, ...), custom_call_target="tpu_custom_call", output_to_operand_aliasing={{}: (6, {})} | custom-call | bytes 2097152 | tf_op jit(solution)/shard_map/pallas_call | solution.py:301
  (95 shorter events, 13.5 us)
Async XLA Ops:
  1.3 3.5 %collective-permute-start = (bf16[256,896]{1,0:T(8,128)(2,1)S(1)}, bf16[256,896]{1,0:T(8,128)(2,1)S(1)}, u32[]{:S(2)}, u32[]{:S(2)}) collective-permute-start(bf16[256,896]{1,0:T(8,128)(2,1)S(1)} %get-tuple-element.74), channel_id=1, source_target_pairs={{0,1},{1,0},{2,3},{3,2},{4,5},{5,4},{6,7},{7,6},{8,9},{9,8},{10,11... | collective-permute-start | bytes 1376264 | tf_op jit(solution)/shard_map/ppermute | solution.py:43
  2.1 13.6 %collective-permute-start.2 = (bf16[256,896]{1,0:T(8,128)(2,1)S(1)}, bf16[256,896]{1,0:T(8,128)(2,1)S(1)}, u32[]{:S(2)}, u32[]{:S(2)}) collective-permute-start(bf16[256,896]{1,0:T(8,128)(2,1)S(1)} %get-tuple-element.73), channel_id=1, source_target_pairs={{0,64},{1,65},{2,66},{3,67},{4,68},{5,69},{6,70},{7,71},{8,72},{9,... | collective-permute-start | bytes 1376264 | tf_op jit(solution)/shard_map/ppermute | solution.py:43
  5.0 13.1 %collective-permute-start.1 = (bf16[256,1792]{1,0:T(8,128)(2,1)S(1)}, bf16[256,1792]{1,0:T(8,128)(2,1)S(1)}, u32[]{:S(2)}, u32[]{:S(2)}) collective-permute-start(bf16[256,1792]{1,0:T(8,128)(2,1)S(1)} %pad_maximum_fusion.refs_0_.refs_8_), channel_id=1, source_target_pairs={{0,48},{1,13},{2,50},{3,15},{4,52},{5,1},{6,54},{7,3},{8,56},{9,5}... | collective-permute-start | bytes 2752520 | tf_op jit(solution)/shard_map/ppermute | solution.py:43
  7.8 13.8 %collective-permute-start.4 = (bf16[256,1792]{1,0:T(8,128)(2,1)S(1)}, bf16[256,1792]{1,0:T(8,128)(2,1)S(1)}, u32[]{:S(2)}, u32[]{:S(2)}) collective-permute-start(bf16[256,1792]{1,0:T(8,128)(2,1)S(1)} %pad_maximum_fusion.refs_0_.refs_8_), channel_id=1, source_target_pairs={{0,16},{1,5},{2,18},{3,7},{4,20},{5,9},{6,22},{7,11},{8,24},{9,13}... | collective-permute-start | bytes 2752520 | tf_op jit(solution)/shard_map/ppermute | solution.py:43
  15.7 2.3 %collective-permute-start.3 = (bf16[256,896]{1,0:T(8,128)(2,1)S(1)}, bf16[256,896]{1,0:T(8,128)(2,1)S(1)}, u32[]{:S(2)}, u32[]{:S(2)}) collective-permute-start(bf16[256,896]{1,0:T(8,128)(2,1)S(1)} %collective-permute-done.2), channel_id=1, source_target_pairs={{0,1},{1,0},{2,3},{3,2},{4,5},{5,4},{6,7},{7,6},{8,9},{9,8},{10,11... | collective-permute-start | bytes 1376264 | tf_op jit(solution)/shard_map/ppermute | solution.py:43
  21.7 12.6 %collective-permute-start.5 = (bf16[256,1792]{1,0:T(8,128)(2,1)S(1)}, bf16[256,1792]{1,0:T(8,128)(2,1)S(1)}, u32[]{:S(2)}, u32[]{:S(2)}) collective-permute-start(bf16[256,1792]{1,0:T(8,128)(2,1)S(1)} %pad_maximum_fusion.1.refs_1_.refs_9_), channel_id=1, source_target_pairs={{0,48},{1,13},{2,50},{3,15},{4,52},{5,1},{6,54},{7,3},{8,56},{9,5}... | collective-permute-start | bytes 2752520 | tf_op jit(solution)/shard_map/ppermute | solution.py:43
  21.8 13.8 %collective-permute-start.6 = (bf16[256,1792]{1,0:T(8,128)(2,1)S(1)}, bf16[256,1792]{1,0:T(8,128)(2,1)S(1)}, u32[]{:S(2)}, u32[]{:S(2)}) collective-permute-start(bf16[256,1792]{1,0:T(8,128)(2,1)S(1)} %pad_maximum_fusion.1.refs_1_.refs_9_), channel_id=1, source_target_pairs={{0,16},{1,5},{2,18},{3,7},{4,20},{5,9},{6,22},{7,11},{8,24},{9,13}... | collective-permute-start | bytes 2752520 | tf_op jit(solution)/shard_map/ppermute | solution.py:43
  25.2 4.2 %collective-permute-start.7 = (f16[2,128,256]{2,1,0:T(8,128)(2,1)S(1)}, f16[2,128,256]{2,1,0:T(8,128)(2,1)S(1)}, u32[]{:S(2)}, u32[]{:S(2)}) collective-permute-start(f16[2,128,256]{2,1,0:T(8,128)(2,1)S(1)} %fusion.18), channel_id=1, source_target_pairs={{0,2},{1,67},{2,0},{3,65},{4,6},{5,71},{6,4},{7,69},{8,10},{9,75},... | collective-permute-start | bytes 393224 | tf_op jit(solution)/shard_map/ppermute | solution.py:43
  25.7 12.0 %collective-permute-start.9 = (bf16[256,1792]{1,0:T(8,128)(2,1)S(1)}, bf16[256,1792]{1,0:T(8,128)(2,1)S(1)}, u32[]{:S(2)}, u32[]{:S(2)}) collective-permute-start(bf16[256,1792]{1,0:T(8,128)(2,1)S(1)} %collective-permute-done.1.refs_0_), channel_id=1, source_target_pairs={{0,1},{1,0},{2,3},{3,2},{4,5},{5,4},{6,7},{7,6},{8,9},{9,8},{10,11... | collective-permute-start | bytes 2752520 | tf_op jit(solution)/shard_map/ppermute | solution.py:43
  28.1 12.3 %collective-permute-start.11 = (bf16[256,1792]{1,0:T(8,128)(2,1)S(1)}, bf16[256,1792]{1,0:T(8,128)(2,1)S(1)}, u32[]{:S(2)}, u32[]{:S(2)}) collective-permute-start(bf16[256,1792]{1,0:T(8,128)(2,1)S(1)} %collective-permute-done.4.refs_2_), channel_id=1, source_target_pairs={{0,1},{1,0},{2,3},{3,2},{4,5},{5,4},{6,7},{7,6},{8,9},{9,8},{10,11... | collective-permute-start | bytes 2752520 | tf_op jit(solution)/shard_map/ppermute | solution.py:43
  29.6 4.0 %collective-permute-start.8 = (f16[128,256]{1,0:T(8,128)(2,1)S(1)}, f16[128,256]{1,0:T(8,128)(2,1)S(1)}, u32[]{:S(2)}, u32[]{:S(2)}) collective-permute-start(f16[128,256]{1,0:T(8,128)(2,1)S(1)} %get-tuple-element.80), channel_id=1, source_target_pairs={{0,66},{1,3},{2,64},{3,1},{4,70},{5,7},{6,68},{7,5},{8,74},{9,11},... | collective-permute-start | bytes 196616 | tf_op jit(solution)/shard_map/ppermute | solution.py:43
  35.6 4.8 %collective-permute-start.10 = (bf16[256,1792]{1,0:T(8,128)(2,1)S(1)}, bf16[256,1792]{1,0:T(8,128)(2,1)S(1)}, u32[]{:S(2)}, u32[]{:S(2)}) collective-permute-start(bf16[256,1792]{1,0:T(8,128)(2,1)S(1)} %collective-permute-done.5.refs_1_), channel_id=1, source_target_pairs={{0,1},{1,0},{2,3},{3,2},{4,5},{5,4},{6,7},{7,6},{8,9},{9,8},{10,11... | collective-permute-start | bytes 2752520 | tf_op jit(solution)/shard_map/ppermute | solution.py:43
  37.7 3.4 %collective-permute-start.12 = (bf16[256,1792]{1,0:T(8,128)(2,1)S(1)}, bf16[256,1792]{1,0:T(8,128)(2,1)S(1)}, u32[]{:S(2)}, u32[]{:S(2)}) collective-permute-start(bf16[256,1792]{1,0:T(8,128)(2,1)S(1)} %collective-permute-done.6.refs_3_), channel_id=1, source_target_pairs={{0,1},{1,0},{2,3},{3,2},{4,5},{5,4},{6,7},{7,6},{8,9},{9,8},{10,11... | collective-permute-start | bytes 2752520 | tf_op jit(solution)/shard_map/ppermute | solution.py:43
  37.7 13.1 %collective-permute-start.15 = (bf16[256,1792]{1,0:T(8,128)(2,1)S(1)}, bf16[256,1792]{1,0:T(8,128)(2,1)S(1)}, u32[]{:S(2)}, u32[]{:S(2)}) collective-permute-start(bf16[256,1792]{1,0:T(8,128)(2,1)S(1)} %collective-permute-done.1.refs_0_), channel_id=1, source_target_pairs={{0,48},{1,13},{2,50},{3,15},{4,52},{5,1},{6,54},{7,3},{8,56},{9,5}... | collective-permute-start | bytes 2752520 | tf_op jit(solution)/shard_map/ppermute | solution.py:43
  40.5 13.5 %collective-permute-start.16 = (bf16[256,1792]{1,0:T(8,128)(2,1)S(1)}, bf16[256,1792]{1,0:T(8,128)(2,1)S(1)}, u32[]{:S(2)}, u32[]{:S(2)}) collective-permute-start(bf16[256,1792]{1,0:T(8,128)(2,1)S(1)} %collective-permute-done.6.refs_3_), channel_id=1, source_target_pairs={{0,16},{1,5},{2,18},{3,7},{4,20},{5,9},{6,22},{7,11},{8,24},{9,13}... | collective-permute-start | bytes 2752520 | tf_op jit(solution)/shard_map/ppermute | solution.py:43
  45.1 8.8 %collective-permute-start.13 = (f16[768,256]{1,0:T(8,128)(2,1)S(1)}, f16[768,256]{1,0:T(8,128)(2,1)S(1)}, u32[]{:S(2)}, u32[]{:S(2)}) collective-permute-start(f16[768,256]{1,0:T(8,128)(2,1)S(1)} %fusion.2), channel_id=1, source_target_pairs={{0,2},{1,67},{2,0},{3,65},{4,6},{5,71},{6,4},{7,69},{8,10},{9,75},... | collective-permute-start | bytes 1179656 | tf_op jit(solution)/shard_map/ppermute | solution.py:43
  54.0 5.1 %collective-permute-start.17 = (bf16[128,1792]{1,0:T(8,128)(2,1)S(1)}, bf16[128,1792]{1,0:T(8,128)(2,1)S(1)}, u32[]{:S(2)}, u32[]{:S(2)}) collective-permute-start(bf16[128,1792]{1,0:T(8,128)(2,1)S(1)} %slice_select_fusion.1), channel_id=1, source_target_pairs={{0,1},{1,0},{2,3},{3,2},{4,5},{5,4},{6,7},{7,6},{8,9},{9,8},{10,11... | collective-permute-start | bytes 1376264 | tf_op jit(solution)/shard_map/ppermute | solution.py:43
  54.1 4.9 %collective-permute-start.18 = (bf16[128,1792]{1,0:T(8,128)(2,1)S(1)}, bf16[128,1792]{1,0:T(8,128)(2,1)S(1)}, u32[]{:S(2)}, u32[]{:S(2)}) collective-permute-start(bf16[128,1792]{1,0:T(8,128)(2,1)S(1)} %slice_select_fusion), channel_id=1, source_target_pairs={{0,1},{1,0},{2,3},{3,2},{4,5},{5,4},{6,7},{7,6},{8,9},{9,8},{10,11... | collective-permute-start | bytes 1376264 | tf_op jit(solution)/shard_map/ppermute | solution.py:43
  55.1 7.5 %collective-permute-start.19 = (f16[768,256]{1,0:T(8,128)(2,1)S(1)}, f16[768,256]{1,0:T(8,128)(2,1)S(1)}, u32[]{:S(2)}, u32[]{:S(2)}) collective-permute-start(f16[768,256]{1,0:T(8,128)(2,1)S(1)} %get-tuple-element.69), channel_id=1, source_target_pairs={{0,66},{1,3},{2,64},{3,1},{4,70},{5,7},{6,68},{7,5},{8,74},{9,11},... | collective-permute-start | bytes 1179656 | tf_op jit(solution)/shard_map/ppermute | solution.py:43
  57.9 8.8 %collective-permute-start.14 = (f16[768,256]{1,0:T(8,128)(2,1)S(1)}, f16[768,256]{1,0:T(8,128)(2,1)S(1)}, u32[]{:S(2)}, u32[]{:S(2)}) collective-permute-start(f16[768,256]{1,0:T(8,128)(2,1)S(1)} %get-tuple-element.44), channel_id=1, source_target_pairs={{0,2},{1,67},{2,0},{3,65},{4,6},{5,71},{6,4},{7,69},{8,10},{9,75},... | collective-permute-start | bytes 1179656 | tf_op jit(solution)/shard_map/ppermute | solution.py:43
  61.1 9.7 %collective-permute-start.27 = (f16[2,384,256]{2,1,0:T(8,128)(2,1)S(1)}, f16[2,384,256]{2,1,0:T(8,128)(2,1)S(1)}, u32[]{:S(2)}, u32[]{:S(2)}) collective-permute-start(f16[2,384,256]{2,1,0:T(8,128)(2,1)S(1)} %fusion.11), channel_id=1, source_target_pairs={{0,2},{1,67},{2,0},{3,65},{4,6},{5,71},{6,4},{7,69},{8,10},{9,75},... | collective-permute-start | bytes 1179656 | tf_op jit(solution)/shard_map/ppermute | solution.py:43
  67.9 9.9 %collective-permute-start.20 = (f16[512,256]{1,0:T(8,128)(2,1)S(1)}, f16[512,256]{1,0:T(8,128)(2,1)S(1)}, u32[]{:S(2)}, u32[]{:S(2)}) collective-permute-start(f16[512,256]{1,0:T(8,128)(2,1)S(1)} %multiply_convert_fusion), channel_id=1, source_target_pairs={{0,16},{1,5},{2,80},{3,69},{4,20},{5,9},{6,84},{7,73},{8,24},{9,13... | collective-permute-start | bytes 786440 | tf_op jit(solution)/shard_map/ppermute | solution.py:43
  68.8 9.1 %collective-permute-start.21 = (f32[256,256]{1,0:T(8,128)S(1)}, f32[256,256]{1,0:T(8,128)S(1)}, u32[]{:S(2)}, u32[]{:S(2)}) collective-permute-start(f32[256,256]{1,0:T(8,128)S(1)} %get-tuple-element.56), channel_id=1, source_target_pairs={{0,48},{1,13},{2,50},{3,15},{4,52},{5,1},{6,54},{7,3},{8,56},{9,5}... | collective-permute-start | bytes 786440 | tf_op jit(solution)/shard_map/ppermute | solution.py:43
  70.8 7.1 %collective-permute-start.22 = (f32[256,256]{1,0:T(8,128)S(1)}, f32[256,256]{1,0:T(8,128)S(1)}, u32[]{:S(2)}, u32[]{:S(2)}) collective-permute-start(f32[256,256]{1,0:T(8,128)S(1)} %get-tuple-element.57), channel_id=1, source_target_pairs={{0,4},{1,49},{2,6},{3,51},{4,8},{5,53},{6,10},{7,55},{8,12},{9,57}... | collective-permute-start | bytes 786440 | tf_op jit(solution)/shard_map/ppermute | solution.py:43
  71.1 8.5 %collective-permute-start.28 = (f16[384,256]{1,0:T(8,128)(2,1)S(1)}, f16[384,256]{1,0:T(8,128)(2,1)S(1)}, u32[]{:S(2)}, u32[]{:S(2)}) collective-permute-start(f16[384,256]{1,0:T(8,128)(2,1)S(1)} %get-tuple-element.77), channel_id=1, source_target_pairs={{0,66},{1,3},{2,64},{3,1},{4,70},{5,7},{6,68},{7,5},{8,74},{9,11},... | collective-permute-start | bytes 589832 | tf_op jit(solution)/shard_map/ppermute | solution.py:43
  77.9 5.0 %collective-permute-start.23 = (f32[384,256]{1,0:T(8,128)S(1)}, f32[384,256]{1,0:T(8,128)S(1)}, u32[]{:S(2)}, u32[]{:S(2)}) collective-permute-start(f32[384,256]{1,0:T(8,128)S(1)} %get-tuple-element.58.refs_0_), channel_id=1, source_target_pairs={{0,1},{1,0},{2,3},{3,2},{4,5},{5,4},{6,7},{7,6},{8,9},{9,8},{10,11... | collective-permute-start | bytes 1179656 | tf_op jit(solution)/shard_map/ppermute | solution.py:43
  78.9 3.0 %collective-permute-start.24 = (f16[512,256]{1,0:T(8,128)(2,1)S(1)}, f16[512,256]{1,0:T(8,128)(2,1)S(1)}, u32[]{:S(2)}, u32[]{:S(2)}) collective-permute-start(f16[512,256]{1,0:T(8,128)(2,1)S(1)} %collective-permute-done.20), channel_id=1, source_target_pairs={{0,1},{1,0},{2,3},{3,2},{4,5},{5,4},{6,7},{7,6},{8,9},{9,8},{10,11... | collective-permute-start | bytes 786440 | tf_op jit(solution)/shard_map/ppermute | solution.py:43
  79.0 3.8 %collective-permute-start.25 = (f32[256,256]{1,0:T(8,128)S(1)}, f32[256,256]{1,0:T(8,128)S(1)}, u32[]{:S(2)}, u32[]{:S(2)}) collective-permute-start(f32[256,256]{1,0:T(8,128)S(1)} %collective-permute-done.21.refs_4_), channel_id=1, source_target_pairs={{0,1},{1,0},{2,3},{3,2},{4,5},{5,4},{6,7},{7,6},{8,9},{9,8},{10,11... | collective-permute-start | bytes 786440 | tf_op jit(solution)/shard_map/ppermute | solution.py:43
  79.5 3.4 %collective-permute-start.26 = (f32[256,256]{1,0:T(8,128)S(1)}, f32[256,256]{1,0:T(8,128)S(1)}, u32[]{:S(2)}, u32[]{:S(2)}) collective-permute-start(f32[256,256]{1,0:T(8,128)S(1)} %collective-permute-done.22.refs_6_), channel_id=1, source_target_pairs={{0,1},{1,0},{2,3},{3,2},{4,5},{5,4},{6,7},{7,6},{8,9},{9,8},{10,11... | collective-permute-start | bytes 786440 | tf_op jit(solution)/shard_map/ppermute | solution.py:43
  80.5 9.7 %collective-permute-start.29 = (f16[384,256]{1,0:T(8,128)(2,1)S(1)}, f16[384,256]{1,0:T(8,128)(2,1)S(1)}, u32[]{:S(2)}, u32[]{:S(2)}) collective-permute-start(f16[384,256]{1,0:T(8,128)(2,1)S(1)} %multiply_convert_fusion.1), channel_id=1, source_target_pairs={{0,32},{1,9},{2,34},{3,11},{4,36},{5,13},{6,38},{7,15},{8,40},{9,1... | collective-permute-start | bytes 589832 | tf_op jit(solution)/shard_map/ppermute | solution.py:43
  81.9 8.2 %collective-permute-start.31 = (f16[256,256]{1,0:T(8,128)(2,1)S(1)}, f16[256,256]{1,0:T(8,128)(2,1)S(1)}, u32[]{:S(2)}, u32[]{:S(2)}) collective-permute-start(f16[256,256]{1,0:T(8,128)(2,1)S(1)} %multiply_convert_fusion.2), channel_id=1, source_target_pairs={{0,12},{1,17},{2,76},{3,81},{4,0},{5,21},{6,64},{7,85},{8,4},{9,25... | collective-permute-start | bytes 393224 | tf_op jit(solution)/shard_map/ppermute | solution.py:43
  90.1 1.6 %collective-permute-start.30 = (f16[384,256]{1,0:T(8,128)(2,1)S(1)}, f16[384,256]{1,0:T(8,128)(2,1)S(1)}, u32[]{:S(2)}, u32[]{:S(2)}) collective-permute-start(f16[384,256]{1,0:T(8,128)(2,1)S(1)} %collective-permute-done.29), channel_id=1, source_target_pairs={{0,1},{1,0},{2,3},{3,2},{4,5},{5,4},{6,7},{7,6},{8,9},{9,8},{10,11... | collective-permute-start | bytes 589832 | tf_op jit(solution)/shard_map/ppermute | solution.py:43
  (14 other events, 90.9 us)
